TPU v7x, 32 devices: a whole 2x2x4 slice. The times are simulated.
32 devices in a mesh: feat: 2 (over x), rows: 16 (over z, y, core).
Axes of the slice: x: 2, y: 2, z: 4, core: 2. Of those that a mesh axis runs over, the one named last changes fastest.
Arguments:
- features: bfloat16 [16384, 4096], P('rows', 'feat'), may hold values from -6 to 6
- coeffs: float32 [4096, 96], P(('feat', 'rows')), may hold values from -0.09375 to 0.09375
- inverse: float32 [4096, 2048], P(('feat', 'rows')), as said below
- labels: int32 [16384], P('rows'), may hold values from 0 to 95
Outputs:
- new_coeffs: float32 [4096, 96], P(('feat', 'rows'))
- block_residuals: float32 [2, 16384, 96], P('feat', 'rows')
- residual_norms: float32 [2, 96], P('feat')
Inputs may be any that keep to these rules, and one draw needn't show every extreme that they name: Each block of 2048 rows of inverse is a symmetric matrix.
All inputs are finite; a program needn't handle non-finite values.
Results may differ from a plain program's by a relative error of at most 0.0036.
Values may be sent and summed in bfloat16 or wider, within the bound.
No kernel may reach another device: no remote copies, remote signals or barrier semaphores. Data moves between devices by JAX's collectives and lax.ppermute only.
A program may use at most 64 MiB of HBM per device.

v0:
```python
import jax
import jax.numpy as jnp
from jax import lax
from jax.sharding import PartitionSpec as P

FRONTS = 3


def passed_along(shard, axis, by):
    peers = lax.axis_size(axis)
    pairs = [(i, i + by) for i in range(peers) if 0 <= i + by < peers]
    return lax.ppermute(shard, axis, pairs)


def on_device(features, coeffs, inverse, labels):
    high = lax.Precision.HIGHEST
    nfeat = lax.axis_size("feat")
    block = lax.axis_index("feat")
    row_dev = features.shape[0]
    classes = coeffs.shape[1]
    front = classes // FRONTS
    partial_fit = jnp.dot(
        features,
        lax.all_gather(coeffs.astype(jnp.bfloat16), "rows", axis=0, tiled=True),
        preferred_element_type=jnp.float32,
    )
    fitted = lax.psum(partial_fit, "feat")
    targets = (labels[:, None] == jnp.arange(classes, dtype=jnp.int32)[None, :]).astype(jnp.float32)
    start_residual = targets - fitted
    contract = (((0,), (0,)), ((), ()))

    def step(turn, carry):
        received, new_coeffs, kept, norms = carry
        which = turn - block
        valid = jnp.logical_and(which >= 0, which < FRONTS)
        mask = valid.astype(jnp.float32)
        col_start = jnp.clip(which, 0, FRONTS - 1) * front
        seed = lax.dynamic_slice_in_dim(start_residual, col_start, front, 1)
        incoming = jnp.where(block == 0, seed, received)
        residual_low = incoming.astype(jnp.bfloat16)
        local_grad = lax.dot_general(
            features, residual_low, contract, preferred_element_type=jnp.float32
        )
        grad = lax.psum(local_grad, "rows")
        delta_mine = jnp.dot(inverse, grad, precision=high)
        delta_low = lax.all_gather(delta_mine.astype(jnp.bfloat16), "rows", axis=0, tiled=True)
        outgoing = incoming - jnp.dot(features, delta_low, preferred_element_type=jnp.float32)
        old_coeff = lax.dynamic_slice_in_dim(new_coeffs, col_start, front, 1)
        new_coeffs = lax.dynamic_update_slice_in_dim(
            new_coeffs, old_coeff + mask * delta_mine, col_start, 1
        )
        old_kept = lax.dynamic_slice_in_dim(kept, col_start, front, 1)
        kept = lax.dynamic_update_slice_in_dim(
            kept, jnp.where(valid, outgoing, old_kept), col_start, 1
        )
        squares = jnp.sum(outgoing * outgoing, axis=0)
        squares = lax.psum(squares, "rows")
        old_norm = lax.dynamic_slice_in_dim(norms, col_start, front, 0)
        norms = lax.dynamic_update_slice_in_dim(
            norms, jnp.where(valid, squares, old_norm), col_start, 0
        )
        received = passed_along(outgoing, "feat", 1)
        return (received, new_coeffs, kept, norms)

    initial = (
        jnp.zeros((row_dev, front), jnp.float32),
        coeffs,
        jnp.zeros((row_dev, classes), jnp.float32),
        jnp.zeros((classes,), jnp.float32),
    )
    received, new_coeffs, kept, norms = lax.fori_loop(0, nfeat + FRONTS - 1, step, initial)
    return (new_coeffs, kept[None], norms[None])


def solution(mesh):
    placed = (P("rows", "feat"), P(("feat", "rows"), None), P(("feat", "rows"), None), P("rows"))
    return jax.shard_map(
        on_device,
        mesh=mesh,
        in_specs=placed,
        out_specs=(P(("feat", "rows"), None), P("feat", "rows", None), P("feat", None)),
        check_vma=False,
    )
```

profile of v0, /device:TPU:0, one launch (start us, length us, event | category | flops | bytes accessed | tf_op | source)
XLA Modules:
  0.0 688.6 jit_solution(13991431327144313949)
XLA Ops:
  7.2 0.0 all-reduce.3.cloned.1.call-start
  7.2 0.9 copy.28
  8.1 24.1 %all_gather.11 = bf16[2048,96]{0,1:T(8,128)(2,1)S(1)} all-gather(bf16[128,96]{0,1:T(8,128)(2,1)S(1)} %convert_element_type.34), channel_id=1, replica_groups=mesh['feat'=2,'rows'=16] {'rows'}, dimensions={0}, use_global_device_ids=true | all-gather | bytes 417792 | tf_op jit(solution)/shard_map/all_gather | solution.py:24
  32.3 4.3 fusion.5
  36.6 0.0 all-reduce.3.cloned.1.call-update
  36.6 23.2 %all-reduce.3.cloned.1.call-done = f32[1024,96]{0,1:T(8,128)} async-done(((f32[1024,96]{0,1:T(8,128)}), f32[1024,96]{0,1:T(8,128)}) %all-reduce.3.cloned.1.call-update) | async-done | bytes 393232 | tf_op jit(solution)/shard_map/psum | solution.py:27
  59.8 1.0 convert_subtract_fusion
  60.9 620.4 %while.20 = (s32[]{:T(128)}, f32[1024,32]{0,1:T(8,128)S(1)}, f32[128,96]{0,1:T(8,128)S(1)}, f32[1024,96]{0,1:T(8,128)S(1)}, f32[96]{0:T(128)S(1)}, /*index=5*/pr...) while((s32[]{:T(128)}, f32[1024,32]{0,1:T(8,128)S(1)}, ...), condition=%wide.region_5.6_spmd, body=%wide.region_1.5_spmd.sunk | while | flops 369373248 | bytes 13223913 | solution.py:71
  60.9 0.0 all-reduce.5.cloned.1.call-start
  61.0 3.7 convolution_bitcast_fusion.3
  64.7 0.0 all-reduce.5.cloned.1.call-update
  64.8 90.1 %all-reduce.5.cloned.1.call-done = f32[2048,32]{0,1:T(8,128)} async-done(((f32[2048,32]{0,1:T(8,128)}), f32[2048,32]{0,1:T(8,128)}) %all-reduce.5.cloned.1.call-update) | async-done | bytes 262160 | tf_op jit(solution)/shard_map/while/body/eval_jaxpr/psum | solution.py:44
  154.9 2.1 fusion.27
  157.0 21.2 %all_gather.13 = bf16[2048,32]{0,1:T(8,128)(2,1)S(1)} all-gather(bf16[128,32]{0,1:T(8,128)(2,1)S(1)} %bitcast.39), channel_id=1, replica_groups=mesh['feat'=2,'rows'=16] {'rows'}, dimensions={0}, use_global_device_ids=true | all-gather | bytes 139264 | tf_op jit(solution)/shard_map/while/body/eval_jaxpr/all_gather | solution.py:46
  178.2 3.6 multiply_reduce_fusion.2
  181.9 29.8 %psum.35 = f32[32]{0:T(128)S(1)} all-reduce(f32[32]{0:T(128)S(1)} %get-tuple-element.300), channel_id=1, replica_groups=mesh['feat'=2,'rows'=16] {'rows'}, use_global_device_ids=true, to_apply=%region_4.4 | all-reduce | flops 32 | bytes 256 | tf_op jit(solution)/shard_map/while/body/eval_jaxpr/psum | solution.py:57
  211.7 3.4 collective-permute-start
  215.1 0.2 fusion.28
  215.2 2.3 collective-permute-done
  217.6 3.7 convolution_bitcast_fusion.3
  221.3 0.0 all-reduce.5.cloned.1.call-update
  221.3 88.4 %all-reduce.5.cloned.1.call-done = f32[2048,32]{0,1:T(8,128)} async-done(((f32[2048,32]{0,1:T(8,128)}), f32[2048,32]{0,1:T(8,128)}) %all-reduce.5.cloned.1.call-update) | async-done | bytes 262160 | tf_op jit(solution)/shard_map/while/body/eval_jaxpr/psum | solution.py:44
  309.7 2.1 fusion.27
  311.8 21.2 %all_gather.13 = bf16[2048,32]{0,1:T(8,128)(2,1)S(1)} all-gather(bf16[128,32]{0,1:T(8,128)(2,1)S(1)} %bitcast.39), channel_id=1, replica_groups=mesh['feat'=2,'rows'=16] {'rows'}, dimensions={0}, use_global_device_ids=true | all-gather | bytes 139264 | tf_op jit(solution)/shard_map/while/body/eval_jaxpr/all_gather | solution.py:46
  333.0 3.6 multiply_reduce_fusion.2
  336.7 29.8 %psum.35 = f32[32]{0:T(128)S(1)} all-reduce(f32[32]{0:T(128)S(1)} %get-tuple-element.300), channel_id=1, replica_groups=mesh['feat'=2,'rows'=16] {'rows'}, use_global_device_ids=true, to_apply=%region_4.4 | all-reduce | flops 32 | bytes 256 | tf_op jit(solution)/shard_map/while/body/eval_jaxpr/psum | solution.py:57
  366.5 3.4 collective-permute-start
  369.9 0.2 fusion.28
  370.0 2.3 collective-permute-done
  372.4 3.7 convolution_bitcast_fusion.3
  376.1 88.1 %all-reduce.5.cloned.1.call-done = f32[2048,32]{0,1:T(8,128)} async-done(((f32[2048,32]{0,1:T(8,128)}), f32[2048,32]{0,1:T(8,128)}) %all-reduce.5.cloned.1.call-update) | async-done | bytes 262160 | tf_op jit(solution)/shard_map/while/body/eval_jaxpr/psum | solution.py:44
  464.2 2.1 fusion.27
  466.3 21.2 %all_gather.13 = bf16[2048,32]{0,1:T(8,128)(2,1)S(1)} all-gather(bf16[128,32]{0,1:T(8,128)(2,1)S(1)} %bitcast.39), channel_id=1, replica_groups=mesh['feat'=2,'rows'=16] {'rows'}, dimensions={0}, use_global_device_ids=true | all-gather | bytes 139264 | tf_op jit(solution)/shard_map/while/body/eval_jaxpr/all_gather | solution.py:46
  487.5 3.6 multiply_reduce_fusion.2
  491.1 29.8 %psum.35 = f32[32]{0:T(128)S(1)} all-reduce(f32[32]{0:T(128)S(1)} %get-tuple-element.300), channel_id=1, replica_groups=mesh['feat'=2,'rows'=16] {'rows'}, use_global_device_ids=true, to_apply=%region_4.4 | all-reduce | flops 32 | bytes 256 | tf_op jit(solution)/shard_map/while/body/eval_jaxpr/psum | solution.py:57
  521.0 3.4 collective-permute-start
  524.3 0.2 fusion.28
  524.5 2.3 collective-permute-done
  526.8 3.7 convolution_bitcast_fusion.3
  530.6 88.1 %all-reduce.5.cloned.1.call-done = f32[2048,32]{0,1:T(8,128)} async-done(((f32[2048,32]{0,1:T(8,128)}), f32[2048,32]{0,1:T(8,128)}) %all-reduce.5.cloned.1.call-update) | async-done | bytes 262160 | tf_op jit(solution)/shard_map/while/body/eval_jaxpr/psum | solution.py:44
  618.7 2.1 fusion.27
  620.8 21.2 %all_gather.13 = bf16[2048,32]{0,1:T(8,128)(2,1)S(1)} all-gather(bf16[128,32]{0,1:T(8,128)(2,1)S(1)} %bitcast.39), channel_id=1, replica_groups=mesh['feat'=2,'rows'=16] {'rows'}, dimensions={0}, use_global_device_ids=true | all-gather | bytes 139264 | tf_op jit(solution)/shard_map/while/body/eval_jaxpr/all_gather | solution.py:46
  642.0 3.6 multiply_reduce_fusion.2
  645.6 29.8 %psum.35 = f32[32]{0:T(128)S(1)} all-reduce(f32[32]{0:T(128)S(1)} %get-tuple-element.300), channel_id=1, replica_groups=mesh['feat'=2,'rows'=16] {'rows'}, use_global_device_ids=true, to_apply=%region_4.4 | all-reduce | flops 32 | bytes 256 | tf_op jit(solution)/shard_map/while/body/eval_jaxpr/psum | solution.py:57
  675.5 3.4 collective-permute-start
  678.9 0.2 fusion.28
  679.0 2.3 collective-permute-done
  681.4 0.7 copy-done.1
  (18 shorter events, 0.1 us)
Async XLA Ops:
  7.2 53.8 %copy-start = (f32[128,2048]{1,0:T(8,128)S(1)}, f32[128,2048]{1,0:T(8,128)}, u32[]{:S(2)}) copy-start(f32[128,2048]{1,0:T(8,128)} %param.8) | copy-start | bytes 3145732
  7.2 52.6 %copy-start.4 = (s32[1024]{0:T(1024)S(1)}, s32[1024]{0:T(1024)}, u32[]{:S(2)}) copy-start(s32[1024]{0:T(1024)} %param.9) | copy-start | bytes 12292
  7.2 52.6 %all-reduce.3.cloned.1.call-start = ((), (), s32[]{:S(2)}) async-start(), calls=%async_computation | async-start | bytes 786432 | tf_op jit(solution)/shard_map/psum | solution.py:27
  60.9 94.0 %all-reduce.5.cloned.1.call-start = ((), (), s32[]{:S(2)}) async-start(), calls=%async_computation.1 | async-start | bytes 524288 | tf_op jit(solution)/shard_map/while/body/eval_jaxpr/psum | solution.py:44
  211.7 5.9 collective-permute-start
  217.6 92.2 %all-reduce.5.cloned.1.call-start = ((), (), s32[]{:S(2)}) async-start(), calls=%async_computation.1 | async-start | bytes 524288 | tf_op jit(solution)/shard_map/while/body/eval_jaxpr/psum | solution.py:44
  366.5 5.9 collective-permute-start
  372.4 91.8 %all-reduce.5.cloned.1.call-start = ((), (), s32[]{:S(2)}) async-start(), calls=%async_computation.1 | async-start | bytes 524288 | tf_op jit(solution)/shard_map/while/body/eval_jaxpr/psum | solution.py:44
  521.0 5.9 collective-permute-start
  526.8 91.9 %all-reduce.5.cloned.1.call-start = ((), (), s32[]{:S(2)}) async-start(), calls=%async_computation.1 | async-start | bytes 524288 | tf_op jit(solution)/shard_map/while/body/eval_jaxpr/psum | solution.py:44
  675.5 5.9 collective-permute-start
  681.4 0.7 copy-start.1
  681.4 0.7 copy-start.2
  681.4 0.7 copy-start.3
Sparse Core Ops, SparseCore 0:
  36.8 22.9 all-reduce.2
  66.1 88.7 all-reduce.4
  222.7 86.9 all-reduce.4
  377.2 86.9 all-reduce.4
  531.7 86.9 all-reduce.4
where the time goes:
time: 689 us
  waiting for transfers between devices  387 us (56%)
  blocking collectives  228 us (33%)
  matrix products  42.1 us (6%)
  between operations  13.8 us (2%)
  starting transfers between devices  13.5 us (2%)
    psum x4, waiting for transfers between devices, step(): grad = lax.psum(local_grad, 'rows')  355 us
    psum x4, blocking collectives, step(): squares = lax.psum(squares, 'rows')  119 us
    all_gather x4, blocking collectives, step(): lax.all_gather(delta_mine.astype(jnp.bfloat16), 'rows', axis=0, tiled=True)  84.9 us
    all_gather x1, blocking collectives, on_device(): lax.all_gather(coeffs.astype(jnp.bfloat16), 'rows', axis=0, tiled=True)  24.1 us
    psum x1, waiting for transfers between devices, on_device(): fitted = lax.psum(partial_fit, 'feat')  23.2 us
    dot_general x4, matrix products, step(): lax.dot_general(features, residual_low, contract, preferred_element_type=...  14.9 us
    dot_general x4, matrix products, step(): jnp.dot(features, delta_low, preferred_element_type=jnp.float32)  14.6 us
  transfers between devices with their start and end apart: 9, of which 9 were waited for; matrix products, arithmetic and copies ran while one was open for 0% of the time, Pallas kernels for 0%

commit v1 on v0

v1 whole, which is shorter than its diff:
```python
import jax
import jax.numpy as jnp
from jax import lax
from jax.sharding import PartitionSpec as P

LOW = jnp.bfloat16
WIDE = jnp.float32


def swapped(shard, axis, bit):
    peers = lax.axis_size(axis)
    return lax.ppermute(shard, axis, [(i, i ^ bit) for i in range(peers)])


def split(wide):
    high = lax.reduce_precision(wide, 8, 7)
    return high.astype(LOW), (wide - high).astype(LOW)


def on_device(features, coeffs, inverse, labels):
    nfeat = lax.axis_size("feat")
    nrows = lax.axis_size("rows")
    block = lax.axis_index("feat")
    me = lax.axis_index("rows")
    own, classes = coeffs.shape
    width = features.shape[1]
    inner = 4
    outer = nrows // inner
    low_bit, next_bit = me % 2, (me // 2) % 2
    same_low = [[bit + 2 * k for k in range(nrows // 2)] for bit in range(2)]
    same_inner = [[k + inner * z for z in range(outer)] for k in range(inner)]

    def both(mine, axis_at):
        other = swapped(mine, "rows", 1)
        first = jnp.where(low_bit == 0, mine, other)
        second = jnp.where(low_bit == 0, other, mine)
        return jnp.stack([first, second], axis=axis_at)

    def halves(whole, bit, axis_at):
        keep = lax.dynamic_index_in_dim(whole, bit, axis_at, keepdims=False)
        send = lax.dynamic_index_in_dim(whole, 1 - bit, axis_at, keepdims=False)
        return keep, send

    inverse_low = lax.all_gather(
        inverse.astype(LOW), "rows", axis=0, axis_index_groups=same_inner, tiled=True
    )

    coeffs_low = coeffs.astype(LOW)
    from_chips = lax.all_to_all(
        jnp.broadcast_to(coeffs_low[None], (nrows // 2, own, classes)),
        "rows", 0, 0, axis_index_groups=same_low, tiled=True,
    )
    all_coeffs = both(from_chips, 1).reshape(width, classes)
    fitted = jnp.dot(features, all_coeffs, preferred_element_type=WIDE)
    bits = [1 << k for k in range((nfeat - 1).bit_length())]
    for bit in bits[:-1]:
        fitted = fitted + swapped(fitted, "feat", bit)
    fit_high, fit_rest = split(fitted)
    targets = (labels[:, None] == jnp.arange(classes, dtype=jnp.int32)[None, :]).astype(WIDE)
    near = (targets - fitted) - swapped(fit_high, "feat", bits[-1]).astype(WIDE)
    incoming_low = near.astype(LOW)
    incoming = near - swapped(fit_rest, "feat", bits[-1]).astype(WIDE)

    contract = (((0,), (0,)), ((), ()))
    kept = jnp.zeros_like(incoming)
    delta_kept = jnp.zeros_like(coeffs)
    for turn in range(nfeat):
        grad = lax.dot_general(
            features, incoming_low, contract, preferred_element_type=WIDE
        ).reshape(outer, 2, 2, own, classes)
        keep, send = halves(grad, low_bit, 2)
        grad = keep + swapped(send, "rows", 1)
        keep, send = halves(grad, next_bit, 1)
        grad = keep + swapped(send.astype(LOW), "rows", 2).astype(WIDE)
        grad_low = grad.astype(LOW)
        for z in range(1, outer):
            grad = grad + swapped(grad_low, "rows", inner * z).astype(WIDE)
        pair = jnp.concatenate(split(grad.reshape(outer * own, classes)), axis=1)
        part = lax.dot_general(inverse_low, pair, contract, preferred_element_type=WIDE)
        part = (part[:, :classes] + part[:, classes:]).reshape(outer, 2, 2, own, classes)
        keep, send = halves(part, low_bit, 2)
        part = keep + swapped(send, "rows", 1)
        delta = part + swapped(part.astype(LOW), "rows", 2).astype(WIDE)
        delta_low = both(delta.astype(LOW), 2).reshape(width, classes)
        delta_mine = lax.dynamic_index_in_dim(
            delta.reshape(nrows // 2, own, classes), me // 2, 0, keepdims=False
        )
        outgoing = incoming - jnp.dot(features, delta_low, preferred_element_type=WIDE)
        active = block == turn
        kept = jnp.where(active, outgoing, kept)
        delta_kept = jnp.where(active, delta_mine, delta_kept)
        if turn < nfeat - 1:
            along = [(i, (i + 1) % nfeat) for i in range(nfeat)]
            high, rest = split(outgoing)
            incoming_low = lax.ppermute(high, "feat", along)
            incoming = incoming_low.astype(WIDE) + lax.ppermute(rest, "feat", along).astype(WIDE)

    squares = jnp.sum(kept * kept, axis=0, keepdims=True)
    squares = lax.all_to_all(
        jnp.broadcast_to(squares[None], (nrows, 1, classes)), "rows", 0, 0, tiled=True
    )
    return (coeffs + delta_kept, kept[None], jnp.sum(squares, axis=0))


def solution(mesh):
    placed = (P("rows", "feat"), P(("feat", "rows"), None), P(("feat", "rows"), None), P("rows"))
    return jax.shard_map(
        on_device,
        mesh=mesh,
        in_specs=placed,
        out_specs=(P(("feat", "rows"), None), P("feat", "rows", None), P("feat", None)),
        check_vma=False,
    )
```

time: 689 us -> 165 us (0.24)
  waiting for transfers between devices: 387 us -> 80.6 us
  blocking collectives: 228 us -> 0 us
  matrix products: 42.1 us -> 18.3 us
  starting transfers between devices: 13.5 us -> 32.2 us
  local copies, waits for them, and re-layouts: 1.67 us -> 11.4 us
    psum x5 -> x0, waiting for transfers between devices: 378 us -> none  [the longest x4 355 us: step(): grad = lax.psum(local_grad, 'rows')]
    psum x4 -> x0, blocking collectives: 119 us -> none  [step(): squares = lax.psum(squares, 'rows')]
    all_gather x5 -> x0, blocking collectives: 109 us -> none  [the longest x4 84.9 us: step(): lax.all_gather(delta_mine.astype(jnp.bfloat16), 'rows', axis=0, tiled=True)]
    ppermute x4 -> x21, waiting for transfers between devices: 9.29 us -> 65.3 us  [the longest x19 59 us: swapped(): return lax.ppermute(shard, axis, [(i, i ^ bit) for i in range(peers)])]
    dot_general x13 -> x7, matrix products: 42.1 us -> 18.3 us  [the longest x2 7.9 us: on_device(): jnp.dot(features, delta_low, preferred_element_type=WIDE)]
    all_to_all x0 -> x2, starting transfers between devices: none -> 10.8 us  [the longest x1 7.28 us: on_device(): lax.all_to_all(jnp.broadcast_to(coeffs_low[None], (nrows // 2, own, class...]
    all_to_all x0 -> x2, waiting for transfers between devices: none -> 10.8 us  [the longest x1 5.79 us: on_device(): lax.all_to_all(jnp.broadcast_to(coeffs_low[None], (nrows // 2, own, class...]
    ppermute x4 -> x21, starting transfers between devices: 13.5 us -> 21.4 us  [the longest x19 18.2 us: swapped(): return lax.ppermute(shard, axis, [(i, i ^ bit) for i in range(peers)])]
  transfers between devices with their start and end apart: 9 -> 24, of which waited for: 9 -> 20; matrix products, arithmetic and copies ran while one was open for 0% -> 11% of each run, Pallas kernels for 0% -> 0%
where the time goes in v1:
time: 165 us
  waiting for transfers between devices  80.6 us (49%)
  starting transfers between devices  32.2 us (20%)
  matrix products  18.3 us (11%)
  between operations  14.5 us (9%)
  local copies, waits for them, and re-layouts  11.4 us (7%)
  other arithmetic  7.75 us (5%)
    ppermute x19, waiting for transfers between devices, swapped(): return lax.ppermute(shard, axis, [(i, i ^ bit) for i in range(peers)])  59 us
    ppermute x19, starting transfers between devices, swapped(): return lax.ppermute(shard, axis, [(i, i ^ bit) for i in range(peers)])  18.2 us
    dot_general x2, matrix products, on_device(): jnp.dot(features, delta_low, preferred_element_type=WIDE)  7.9 us
    all_to_all x1, starting transfers between devices, on_device(): lax.all_to_all(jnp.broadcast_to(coeffs_low[None], (nrows // 2, own, class...  7.28 us
    all_to_all x1, waiting for transfers between devices, on_device(): lax.all_to_all(jnp.broadcast_to(coeffs_low[None], (nrows // 2, own, class...  5.79 us
    ppermute x1, waiting for transfers between devices, on_device(): incoming_low = lax.ppermute(high, 'feat', along)  5.06 us
    all_to_all x1, waiting for transfers between devices, on_device(): lax.all_to_all(jnp.broadcast_to(squares[None], (nrows, 1, classes)), 'row...  4.96 us
    all_gather x1, waiting for transfers between devices, on_device(): lax.all_gather(inverse.astype(LOW), 'rows', axis=0, axis_index_groups=sam...  4.56 us
  transfers between devices with their start and end apart: 24, of which 20 were waited for; matrix products, arithmetic and copies ran while one was open for 11% of the time, Pallas kernels for 0%

profile of v1, /device:TPU:0, one launch (start us, length us, event | category | flops | bytes accessed | tf_op | source)
XLA Modules:
  0.0 164.8 jit_solution(3337850115344626356)
XLA Ops:
  7.2 0.8 convert_element_type.109
  8.0 0.7 broadcast_in_dim.10
  8.7 7.3 %all-to-all-start = ((bf16[8,128,96]{1,2,0:T(8,128)(2,1)}), bf16[8,128,96]{1,2,0:T(8,128)(2,1)S(1)}, u32[]{:S(2)}, u32[]{:S(2)}) async-start(bf16[8,128,96]{1,2,0:T(8,128)(2,1)} %broadcast_in_dim.10), calls=%async_computation | async-start | bytes 393216 | tf_op jit(solution)/shard_map/all_to_all | solution.py:49
  16.0 2.1 %convert_element_type.124 = bf16[128,2048]{1,0:T(8,128)(2,1)} convert(f32[128,2048]{1,0:T(8,128)} %param.6) | non-fusion elementwise | flops 262144 | bytes 1572864 | tf_op jit(solution)/shard_map/convert_element_type | solution.py:45
  18.1 5.8 %all-to-all-done = bf16[8,128,96]{1,2,0:T(8,128)(2,1)S(1)} async-done(((bf16[8,128,96]{1,2,0:T(8,128)(2,1)}), bf16[8,128,96]{1,2,0:T(8,128)(2,1)S(1)}, u32[]{:S(2)}, u32[]{:S(2)}) %all-to-all-start) | async-done | bytes 196640 | tf_op jit(solution)/shard_map/all_to_all | solution.py:49
  23.9 1.4 collective-permute-done
  26.0 3.8 %fusion = (bf16[1024,96]{0,1:T(8,128)(2,1)S(1)}, bf16[1024,96]{0,1:T(8,128)(2,1)S(1)}, f32[1024,96]{0,1:T(8,128)S(1)}) fusion(bf16[2048,96]{0,1:T(8,128)(2,1)S(1)} %reshape.52, bf16[1024,2048]{1,0:T(8,128)(2,1)} %param.4), kind=kOutput, calls=%fused_computation.13 | convolution fusion | flops 403046400 | bytes 5373952 | tf_op jit(solution)/shard_map/dot_general | solution.py:54
  29.9 1.6 collective-permute-start.1
  31.5 5.4 %collective-permute-done.1 = bf16[1024,96]{0,1:T(8,128)(2,1)S(1)} collective-permute-done((bf16[1024,96]{0,1:T(8,128)(2,1)S(1)}, bf16[1024,96]{0,1:T(8,128)(2,1)S(1)}, u32[]{:S(2)}, u32[]{:S(2)}) %collective-permute-start.1) | collective-permute-done | bytes 196640 | tf_op jit(solution)/shard_map/ppermute | solution.py:12
  36.9 3.0 %convolution_bitcast_fusion.3 = f32[2048,96]{0,1:T(8,128)S(1)} fusion(bf16[1024,2048]{1,0:T(8,128)(2,1)} %param.4, bf16[1024,96]{0,1:T(8,128)(2,1)S(1)} %collective-permute-done.1, f32[1024,96]{0,1:T(8,128)S(1)} %get-tuple-element.31, s32[1024]{0:T(1024)S(1)} %copy-done.4), kind=kOutput, calls=%fused_computation.3 | convolution fusion | flops 403243008 | bytes 5574656 | tf_op jit(solution)/shard_map/dot_general | solution.py:68
  41.5 1.7 %collective-permute-done.3 = f32[4,2,128,96]{2,3,1,0:T(8,128)S(1)} collective-permute-done((f32[4,2,128,96]{2,3,1,0:T(8,128)S(1)}, f32[4,2,128,96]{2,3,1,0:T(8,128)S(1)}, u32[]{:S(2)}, u32[]{:S(2)}) %collective-permute-start.3) | collective-permute-done | bytes 393248 | tf_op jit(solution)/shard_map/ppermute | solution.py:12
  43.3 1.1 collective-permute-start.4
  44.4 3.8 %collective-permute-done.4 = bf16[4,128,96]{1,2,0:T(8,128)(2,1)S(1)} collective-permute-done((bf16[4,128,96]{1,2,0:T(8,128)(2,1)S(1)}, bf16[4,128,96]{1,2,0:T(8,128)(2,1)S(1)}, u32[]{:S(2)}, u32[]{:S(2)}) %collective-permute-start.4) | collective-permute-done | bytes 98336 | tf_op jit(solution)/shard_map/ppermute | solution.py:12
  48.9 1.0 collective-permute-start.6
  49.9 2.8 %collective-permute-start.5 = (bf16[4,128,96]{1,2,0:T(8,128)(2,1)S(1)}, bf16[4,128,96]{1,2,0:T(8,128)(2,1)S(1)}, u32[]{:S(2)}, u32[]{:S(2)}) collective-permute-start(bf16[4,128,96]{1,2,0:T(8,128)(2,1)S(1)} %fusion.17), channel_id=1, source_target_pairs={{0,4},{1,5},{2,6},{3,7},{4,0},{5,1},{6,2},{7,3},{8,12},{9,13},{10,... | collective-permute-start | bytes 294920 | tf_op jit(solution)/shard_map/ppermute | solution.py:12
  52.7 5.1 %collective-permute-done.7 = bf16[4,128,96]{1,2,0:T(8,128)(2,1)S(1)} collective-permute-done((bf16[4,128,96]{1,2,0:T(8,128)(2,1)S(1)}, bf16[4,128,96]{1,2,0:T(8,128)(2,1)S(1)}, u32[]{:S(2)}, u32[]{:S(2)}) %collective-permute-start.7) | collective-permute-done | bytes 98336 | tf_op jit(solution)/shard_map/ppermute | solution.py:12
  57.8 11.6 %collective-permute-done.6 = bf16[4,128,96]{1,2,0:T(8,128)(2,1)S(1)} collective-permute-done((bf16[4,128,96]{1,2,0:T(8,128)(2,1)S(1)}, bf16[4,128,96]{1,2,0:T(8,128)(2,1)S(1)}, u32[]{:S(2)}, u32[]{:S(2)}) %collective-permute-start.6) | collective-permute-done | bytes 98336 | tf_op jit(solution)/shard_map/ppermute | solution.py:12
  69.5 4.6 %all-gather.2.cloned.1.call-done = bf16[512,2048]{1,0:T(8,128)(2,1)} async-done(((bf16[128,2048]{1,0:T(8,128)(2,1)}), bf16[512,2048]{1,0:T(8,128)(2,1)}) %all-gather.2.cloned.1.call-update) | async-done | bytes 2097168 | tf_op jit(solution)/shard_map/all_gather | solution.py:44
  74.0 2.2 %convolution_bitcast_fusion.1 = f32[2048,192]{0,1:T(8,128)S(1)} fusion(bf16[512,2048]{1,0:T(8,128)(2,1)} %all-gather.2.cloned.1.call-done, bf16[512,96]{0,1:T(8,128)(2,1)S(1)} %get-tuple-element.30, bf16[512,96]{0,1:T(8,128)(2,1)S(1)} %get-tuple-element.29), kind=kOutput, calls=%fused_computation.1 | convolution fusion | flops 403046400 | bytes 3866624 | tf_op jit(solution)/shard_map/dot_general | solution.py:79
  77.8 1.7 %collective-permute-done.8 = f32[4,2,128,96]{2,3,1,0:T(8,128)S(1)} collective-permute-done((f32[4,2,128,96]{2,3,1,0:T(8,128)S(1)}, f32[4,2,128,96]{2,3,1,0:T(8,128)S(1)}, u32[]{:S(2)}, u32[]{:S(2)}) %collective-permute-start.8) | collective-permute-done | bytes 393248 | tf_op jit(solution)/shard_map/ppermute | solution.py:12
  79.6 1.5 collective-permute-start.9
  81.2 5.5 %collective-permute-done.9 = bf16[4,2,128,96]{2,3,1,0:T(8,128)(2,1)S(1)} collective-permute-done((bf16[4,2,128,96]{2,3,1,0:T(8,128)(2,1)S(1)}, bf16[4,2,128,96]{2,3,1,0:T(8,128)(2,1)S(1)}, u32[]{:S(2)}, u32[]{:S(2)}) %collective-permute-start.9) | collective-permute-done | bytes 196640 | tf_op jit(solution)/shard_map/ppermute | solution.py:12
  86.6 0.8 fusion.24
  87.5 1.5 collective-permute-start.2
  89.8 5.0 %collective-permute-done.2 = bf16[1024,96]{0,1:T(8,128)(2,1)S(1)} collective-permute-done((bf16[1024,96]{0,1:T(8,128)(2,1)S(1)}, bf16[1024,96]{0,1:T(8,128)(2,1)S(1)}, u32[]{:S(2)}, u32[]{:S(2)}) %collective-permute-start.2) | collective-permute-done | bytes 196640 | tf_op jit(solution)/shard_map/ppermute | solution.py:12
  94.8 4.3 %fusion.1 = (bf16[1024,96]{0,1:T(8,128)(2,1)}, f32[1024,96]{0,1:T(8,128)S(1)}) fusion(bf16[1024,96]{0,1:T(8,128)(2,1)S(1)} %collective-permute-done.2, bf16[1024,96]{0,1:T(8,128)(2,1)S(1)} %collective-permute-done.1, f32[1024,96]{0,1:T(8,128)S(1)} %get-tuple-element.31, s32[1024]{0:T(1024)S(1)} %copy-done.4, bf16[2048,96]{0,1:T(8,128)(2,1)S(1)} %reshape.56, ...), kind=kOutput, calls=%fused_computation.14 | convolution fusion | flops 403734528 | bytes 5967872 | tf_op jit(solution)/shard_map/dot_general | solution.py:88
  99.1 1.5 collective-permute-start.11
  100.7 5.1 %collective-permute-done.11 = bf16[1024,96]{0,1:T(8,128)(2,1)S(1)} collective-permute-done((bf16[1024,96]{0,1:T(8,128)(2,1)S(1)}, bf16[1024,96]{0,1:T(8,128)(2,1)S(1)}, u32[]{:S(2)}, u32[]{:S(2)}) %collective-permute-start.11) | collective-permute-done | bytes 196640 | tf_op jit(solution)/shard_map/ppermute | solution.py:95
  105.7 0.8 convolution_bitcast_fusion.2
  106.6 1.6 reshape.57
  108.1 2.2 %constant_dynamic-slice_fusion.3 = (f32[4,2,1,128,96]{3,2,1,0,4:T(1,128)S(1)}, f32[4,2,1,128,96]{3,2,1,0,4:T(1,128)S(1)}) fusion(f32[4,2,2,128,96]{3,2,1,0,4:T(2,128)} %reshape.57, s32[]{:T(128)S(6)} %select_n.114, s32[]{:T(128)S(6)} %select_n.115), kind=kLoop, calls=%fused_computation.71 | loop fusion | bytes 1572872 | tf_op jit(solution)/shard_map/jit(dynamic_index_in_dim)/dynamic_slice | solution.py:40
  110.5 1.7 %collective-permute-done.12 = f32[4,2,128,96]{2,3,1,0:T(8,128)S(1)} collective-permute-done((f32[4,2,128,96]{2,3,1,0:T(8,128)S(1)}, f32[4,2,128,96]{2,3,1,0:T(8,128)S(1)}, u32[]{:S(2)}, u32[]{:S(2)}) %collective-permute-start.12) | collective-permute-done | bytes 393248 | tf_op jit(solution)/shard_map/ppermute | solution.py:12
  112.3 1.5 collective-permute-start.13
  113.8 3.4 %collective-permute-done.13 = bf16[4,128,96]{1,2,0:T(8,128)(2,1)S(1)} collective-permute-done((bf16[4,128,96]{1,2,0:T(8,128)(2,1)S(1)}, bf16[4,128,96]{1,2,0:T(8,128)(2,1)S(1)}, u32[]{:S(2)}, u32[]{:S(2)}) %collective-permute-start.13) | collective-permute-done | bytes 98336 | tf_op jit(solution)/shard_map/ppermute | solution.py:12
  117.2 1.1 collective-permute-start.16
  118.3 3.3 %collective-permute-start.14 = (bf16[4,128,96]{1,2,0:T(8,128)(2,1)S(1)}, bf16[4,128,96]{1,2,0:T(8,128)(2,1)S(1)}, u32[]{:S(2)}, u32[]{:S(2)}) collective-permute-start(bf16[4,128,96]{1,2,0:T(8,128)(2,1)S(1)} %fusion.18), channel_id=1, source_target_pairs={{0,4},{1,5},{2,6},{3,7},{4,0},{5,1},{6,2},{7,3},{8,12},{9,13},{10,... | collective-permute-start | bytes 294920 | tf_op jit(solution)/shard_map/ppermute | solution.py:12
  121.7 3.2 %collective-permute-done.16 = bf16[4,128,96]{1,2,0:T(8,128)(2,1)S(1)} collective-permute-done((bf16[4,128,96]{1,2,0:T(8,128)(2,1)S(1)}, bf16[4,128,96]{1,2,0:T(8,128)(2,1)S(1)}, u32[]{:S(2)}, u32[]{:S(2)}) %collective-permute-start.16) | collective-permute-done | bytes 98336 | tf_op jit(solution)/shard_map/ppermute | solution.py:12
  124.9 2.3 %collective-permute-done.15 = bf16[4,128,96]{1,2,0:T(8,128)(2,1)S(1)} collective-permute-done((bf16[4,128,96]{1,2,0:T(8,128)(2,1)S(1)}, bf16[4,128,96]{1,2,0:T(8,128)(2,1)S(1)}, u32[]{:S(2)}, u32[]{:S(2)}) %collective-permute-start.15) | collective-permute-done | bytes 98336 | tf_op jit(solution)/shard_map/ppermute | solution.py:12
  129.5 1.7 %collective-permute-done.17 = f32[4,2,128,96]{2,3,1,0:T(8,128)S(1)} collective-permute-done((f32[4,2,128,96]{2,3,1,0:T(8,128)S(1)}, f32[4,2,128,96]{2,3,1,0:T(8,128)S(1)}, u32[]{:S(2)}, u32[]{:S(2)}) %collective-permute-start.17) | collective-permute-done | bytes 393248 | tf_op jit(solution)/shard_map/ppermute | solution.py:12
  131.3 1.6 collective-permute-start.18
  133.0 5.4 %collective-permute-done.18 = bf16[4,2,128,96]{2,3,1,0:T(8,128)(2,1)S(1)} collective-permute-done((bf16[4,2,128,96]{2,3,1,0:T(8,128)(2,1)S(1)}, bf16[4,2,128,96]{2,3,1,0:T(8,128)(2,1)S(1)}, u32[]{:S(2)}, u32[]{:S(2)}) %collective-permute-start.18) | collective-permute-done | bytes 196640 | tf_op jit(solution)/shard_map/ppermute | solution.py:12
  138.6 1.6 collective-permute-start.19
  141.0 3.6 %convolution_bitcast_fusion.4 = f32[1024,96]{0,1:T(8,128)S(1)} fusion(bf16[2048,96]{0,1:T(8,128)(2,1)S(1)} %reshape.62, bf16[1024,2048]{1,0:T(8,128)(2,1)} %param.4), kind=kOutput, calls=%fused_computation.4 | convolution fusion | flops 402653184 | bytes 4980736 | tf_op jit(solution)/shard_map/dot_general | solution.py:88
  144.6 1.3 collective-permute-done.19
  145.9 1.0 multiply_reduce_fusion
  147.5 3.5 %all-to-all-start.1 = ((f32[16,1,96]{2,1,0:T(1,128)}), f32[16,1,96]{2,1,0:T(1,128)S(1)}, u32[]{:S(2)}, u32[]{:S(2)}) async-start(f32[16,1,96]{2,1,0:T(1,128)} %broadcast_in_dim.26), calls=%async_computation.1 | async-start | bytes 16384 | tf_op jit(solution)/shard_map/all_to_all | solution.py:99
  151.0 1.4 bitcast_add_fusion.4
  152.4 5.0 %all-to-all-done.1 = f32[16,1,96]{2,1,0:T(1,128)S(1)} async-done(((f32[16,1,96]{2,1,0:T(1,128)}), f32[16,1,96]{2,1,0:T(1,128)S(1)}, u32[]{:S(2)}, u32[]{:S(2)}) %all-to-all-start.1) | async-done | bytes 6176 | tf_op jit(solution)/shard_map/all_to_all | solution.py:99
  (64 shorter events, 10.3 us)
Async XLA Ops:
  8.7 15.2 %all-to-all-start = ((bf16[8,128,96]{1,2,0:T(8,128)(2,1)}), bf16[8,128,96]{1,2,0:T(8,128)(2,1)S(1)}, u32[]{:S(2)}, u32[]{:S(2)}) async-start(bf16[8,128,96]{1,2,0:T(8,128)(2,1)} %broadcast_in_dim.10), calls=%async_computation | async-start | bytes 393216 | tf_op jit(solution)/shard_map/all_to_all | solution.py:49
  16.0 58.1 %all-gather.2.cloned.1.call-start = ((), (), s32[]{:S(2)}) async-start(), calls=%async_computation.2 | async-start | bytes 2621440 | tf_op jit(solution)/shard_map/all_gather | solution.py:44
  23.9 1.4 collective-permute-start
  23.9 13.0 %copy-start.4 = (s32[1024]{0:T(1024)S(1)}, s32[1024]{0:T(1024)}, u32[]{:S(2)}) copy-start(s32[1024]{0:T(1024)} %param.7) | copy-start | bytes 12292
  29.9 7.0 %collective-permute-start.1 = (bf16[1024,96]{0,1:T(8,128)(2,1)S(1)}, bf16[1024,96]{0,1:T(8,128)(2,1)S(1)}, u32[]{:S(2)}, u32[]{:S(2)}) collective-permute-start(bf16[1024,96]{0,1:T(8,128)(2,1)S(1)} %get-tuple-element.22), channel_id=1, source_target_pairs={{0,16},{16,0},{1,17},{17,1},{2,18},{18,2},{3,19},{19,3},{4,20},{20... | collective-permute-start | bytes 589832 | tf_op jit(solution)/shard_map/ppermute | solution.py:12
  41.4 1.8 %collective-permute-start.3 = (f32[4,2,128,96]{2,3,1,0:T(8,128)S(1)}, f32[4,2,128,96]{2,3,1,0:T(8,128)S(1)}, u32[]{:S(2)}, u32[]{:S(2)}) collective-permute-start(f32[4,2,128,96]{2,3,1,0:T(8,128)S(1)} %bitcast.124), channel_id=1, source_target_pairs={{0,1},{1,0},{2,3},{3,2},{4,5},{5,4},{6,7},{7,6},{8,9},{9,8},{10,11... | collective-permute-start | bytes 1179656 | tf_op jit(solution)/shard_map/ppermute | solution.py:12
  43.3 4.9 %collective-permute-start.4 = (bf16[4,128,96]{1,2,0:T(8,128)(2,1)S(1)}, bf16[4,128,96]{1,2,0:T(8,128)(2,1)S(1)}, u32[]{:S(2)}, u32[]{:S(2)}) collective-permute-start(bf16[4,128,96]{1,2,0:T(8,128)(2,1)S(1)} %fusion.19), channel_id=1, source_target_pairs={{0,2},{1,3},{2,0},{3,1},{4,6},{5,7},{6,4},{7,5},{8,10},{9,11},{10,... | collective-permute-start | bytes 294920 | tf_op jit(solution)/shard_map/ppermute | solution.py:12
  48.2 9.6 %collective-permute-start.7 = (bf16[4,128,96]{1,2,0:T(8,128)(2,1)S(1)}, bf16[4,128,96]{1,2,0:T(8,128)(2,1)S(1)}, u32[]{:S(2)}, u32[]{:S(2)}) collective-permute-start(bf16[4,128,96]{1,2,0:T(8,128)(2,1)S(1)} %fusion.17), channel_id=1, source_target_pairs={{0,12},{1,13},{2,14},{3,15},{4,8},{5,9},{6,10},{7,11},{8,4},{9,5},... | collective-permute-start | bytes 294920 | tf_op jit(solution)/shard_map/ppermute | solution.py:12
  48.9 20.5 %collective-permute-start.6 = (bf16[4,128,96]{1,2,0:T(8,128)(2,1)S(1)}, bf16[4,128,96]{1,2,0:T(8,128)(2,1)S(1)}, u32[]{:S(2)}, u32[]{:S(2)}) collective-permute-start(bf16[4,128,96]{1,2,0:T(8,128)(2,1)S(1)} %fusion.17), channel_id=1, source_target_pairs={{0,8},{1,9},{2,10},{3,11},{4,12},{5,13},{6,14},{7,15},{8,0},{9,1},... | collective-permute-start | bytes 294920 | tf_op jit(solution)/shard_map/ppermute | solution.py:12
  49.9 19.5 %collective-permute-start.5 = (bf16[4,128,96]{1,2,0:T(8,128)(2,1)S(1)}, bf16[4,128,96]{1,2,0:T(8,128)(2,1)S(1)}, u32[]{:S(2)}, u32[]{:S(2)}) collective-permute-start(bf16[4,128,96]{1,2,0:T(8,128)(2,1)S(1)} %fusion.17), channel_id=1, source_target_pairs={{0,4},{1,5},{2,6},{3,7},{4,0},{5,1},{6,2},{7,3},{8,12},{9,13},{10,... | collective-permute-start | bytes 294920 | tf_op jit(solution)/shard_map/ppermute | solution.py:12
  77.7 1.8 %collective-permute-start.8 = (f32[4,2,128,96]{2,3,1,0:T(8,128)S(1)}, f32[4,2,128,96]{2,3,1,0:T(8,128)S(1)}, u32[]{:S(2)}, u32[]{:S(2)}) collective-permute-start(f32[4,2,128,96]{2,3,1,0:T(8,128)S(1)} %bitcast.125), channel_id=1, source_target_pairs={{0,1},{1,0},{2,3},{3,2},{4,5},{5,4},{6,7},{7,6},{8,9},{9,8},{10,11... | collective-permute-start | bytes 1179656 | tf_op jit(solution)/shard_map/ppermute | solution.py:12
  79.6 7.0 %collective-permute-start.9 = (bf16[4,2,128,96]{2,3,1,0:T(8,128)(2,1)S(1)}, bf16[4,2,128,96]{2,3,1,0:T(8,128)(2,1)S(1)}, u32[]{:S(2)}, u32[]{:S(2)}) collective-permute-start(bf16[4,2,128,96]{2,3,1,0:T(8,128)(2,1)S(1)} %fusion.15), channel_id=1, source_target_pairs={{0,2},{1,3},{2,0},{3,1},{4,6},{5,7},{6,4},{7,5},{8,10},{9,11},{10,... | collective-permute-start | bytes 589832 | tf_op jit(solution)/shard_map/ppermute | solution.py:12
  87.5 1.5 collective-permute-start.10
  87.5 7.3 %collective-permute-start.2 = (bf16[1024,96]{0,1:T(8,128)(2,1)S(1)}, bf16[1024,96]{0,1:T(8,128)(2,1)S(1)}, u32[]{:S(2)}, u32[]{:S(2)}) collective-permute-start(bf16[1024,96]{0,1:T(8,128)(2,1)S(1)} %get-tuple-element.21), channel_id=1, source_target_pairs={{0,16},{16,0},{1,17},{17,1},{2,18},{18,2},{3,19},{19,3},{4,20},{20... | collective-permute-start | bytes 589832 | tf_op jit(solution)/shard_map/ppermute | solution.py:12
  89.7 16.0 %copy-start = (bf16[1024,2048]{1,0:T(8,128)(2,1)S(1)}, bf16[1024,2048]{1,0:T(8,128)(2,1)}, u32[]{:S(2)}) copy-start(bf16[1024,2048]{1,0:T(8,128)(2,1)} %param.4) | copy-start | bytes 12582916
  99.1 6.6 %collective-permute-start.11 = (bf16[1024,96]{0,1:T(8,128)(2,1)S(1)}, bf16[1024,96]{0,1:T(8,128)(2,1)S(1)}, u32[]{:S(2)}, u32[]{:S(2)}) collective-permute-start(bf16[1024,96]{0,1:T(8,128)(2,1)S(1)} %reduce-precision_convert_fusion), channel_id=1, source_target_pairs={{0,16},{16,0},{1,17},{17,1},{2,18},{18,2},{3,19},{19,3},{4,20},{20... | collective-permute-start | bytes 589832 | tf_op jit(solution)/shard_map/ppermute | solution.py:95
  106.5 20.8 %copy-start.1 = (bf16[512,2048]{1,0:T(8,128)(2,1)S(1)}, bf16[512,2048]{1,0:T(8,128)(2,1)}, u32[]{:S(2)}) copy-start(bf16[512,2048]{1,0:T(8,128)(2,1)} %all-gather.2.cloned.1.call-done) | copy-start | bytes 6291460
  110.4 1.8 %collective-permute-start.12 = (f32[4,2,128,96]{2,3,1,0:T(8,128)S(1)}, f32[4,2,128,96]{2,3,1,0:T(8,128)S(1)}, u32[]{:S(2)}, u32[]{:S(2)}) collective-permute-start(f32[4,2,128,96]{2,3,1,0:T(8,128)S(1)} %bitcast.126), channel_id=1, source_target_pairs={{0,1},{1,0},{2,3},{3,2},{4,5},{5,4},{6,7},{7,6},{8,9},{9,8},{10,11... | collective-permute-start | bytes 1179656 | tf_op jit(solution)/shard_map/ppermute | solution.py:12
  112.3 4.9 %collective-permute-start.13 = (bf16[4,128,96]{1,2,0:T(8,128)(2,1)S(1)}, bf16[4,128,96]{1,2,0:T(8,128)(2,1)S(1)}, u32[]{:S(2)}, u32[]{:S(2)}) collective-permute-start(bf16[4,128,96]{1,2,0:T(8,128)(2,1)S(1)} %fusion.20), channel_id=1, source_target_pairs={{0,2},{1,3},{2,0},{3,1},{4,6},{5,7},{6,4},{7,5},{8,10},{9,11},{10,... | collective-permute-start | bytes 294920 | tf_op jit(solution)/shard_map/ppermute | solution.py:12
  117.2 7.7 %collective-permute-start.16 = (bf16[4,128,96]{1,2,0:T(8,128)(2,1)S(1)}, bf16[4,128,96]{1,2,0:T(8,128)(2,1)S(1)}, u32[]{:S(2)}, u32[]{:S(2)}) collective-permute-start(bf16[4,128,96]{1,2,0:T(8,128)(2,1)S(1)} %fusion.18), channel_id=1, source_target_pairs={{0,12},{1,13},{2,14},{3,15},{4,8},{5,9},{6,10},{7,11},{8,4},{9,5},... | collective-permute-start | bytes 294920 | tf_op jit(solution)/shard_map/ppermute | solution.py:12
  118.3 8.9 %collective-permute-start.15 = (bf16[4,128,96]{1,2,0:T(8,128)(2,1)S(1)}, bf16[4,128,96]{1,2,0:T(8,128)(2,1)S(1)}, u32[]{:S(2)}, u32[]{:S(2)}) collective-permute-start(bf16[4,128,96]{1,2,0:T(8,128)(2,1)S(1)} %fusion.18), channel_id=1, source_target_pairs={{0,8},{1,9},{2,10},{3,11},{4,12},{5,13},{6,14},{7,15},{8,0},{9,1},... | collective-permute-start | bytes 294920 | tf_op jit(solution)/shard_map/ppermute | solution.py:12
  118.3 8.9 %collective-permute-start.14 = (bf16[4,128,96]{1,2,0:T(8,128)(2,1)S(1)}, bf16[4,128,96]{1,2,0:T(8,128)(2,1)S(1)}, u32[]{:S(2)}, u32[]{:S(2)}) collective-permute-start(bf16[4,128,96]{1,2,0:T(8,128)(2,1)S(1)} %fusion.18), channel_id=1, source_target_pairs={{0,4},{1,5},{2,6},{3,7},{4,0},{5,1},{6,2},{7,3},{8,12},{9,13},{10,... | collective-permute-start | bytes 294920 | tf_op jit(solution)/shard_map/ppermute | solution.py:12
  127.9 10.7 %copy-start.2 = (bf16[1024,96]{0,1:T(8,128)(2,1)S(1)}, bf16[1024,96]{0,1:T(8,128)(2,1)}, u32[]{:S(2)}) copy-start(bf16[1024,96]{0,1:T(8,128)(2,1)} %get-tuple-element.5) | copy-start | bytes 589828
  129.5 1.8 %collective-permute-start.17 = (f32[4,2,128,96]{2,3,1,0:T(8,128)S(1)}, f32[4,2,128,96]{2,3,1,0:T(8,128)S(1)}, u32[]{:S(2)}, u32[]{:S(2)}) collective-permute-start(f32[4,2,128,96]{2,3,1,0:T(8,128)S(1)} %bitcast.127), channel_id=1, source_target_pairs={{0,1},{1,0},{2,3},{3,2},{4,5},{5,4},{6,7},{7,6},{8,9},{9,8},{10,11... | collective-permute-start | bytes 1179656 | tf_op jit(solution)/shard_map/ppermute | solution.py:12
  131.3 7.0 %collective-permute-start.18 = (bf16[4,2,128,96]{2,3,1,0:T(8,128)(2,1)S(1)}, bf16[4,2,128,96]{2,3,1,0:T(8,128)(2,1)S(1)}, u32[]{:S(2)}, u32[]{:S(2)}) collective-permute-start(bf16[4,2,128,96]{2,3,1,0:T(8,128)(2,1)S(1)} %fusion.16), channel_id=1, source_target_pairs={{0,2},{1,3},{2,0},{3,1},{4,6},{5,7},{6,4},{7,5},{8,10},{9,11},{10,... | collective-permute-start | bytes 589832 | tf_op jit(solution)/shard_map/ppermute | solution.py:12
  138.5 1.7 %collective-permute-start.20 = (bf16[4,2,128,96]{2,3,1,0:T(8,128)(2,1)S(1)}, bf16[4,2,128,96]{2,3,1,0:T(8,128)(2,1)S(1)}, u32[]{:S(2)}, u32[]{:S(2)}) collective-permute-start(bf16[4,2,128,96]{2,3,1,0:T(8,128)(2,1)S(1)} %get-tuple-element.7), channel_id=1, source_target_pairs={{0,1},{1,0},{2,3},{3,2},{4,5},{5,4},{6,7},{7,6},{8,9},{9,8},{10,11... | collective-permute-start | bytes 589832 | tf_op jit(solution)/shard_map/ppermute | solution.py:12
  138.6 7.3 %collective-permute-start.19 = (bf16[1024,96]{0,1:T(8,128)(2,1)S(1)}, bf16[1024,96]{0,1:T(8,128)(2,1)S(1)}, u32[]{:S(2)}, u32[]{:S(2)}) collective-permute-start(bf16[1024,96]{0,1:T(8,128)(2,1)S(1)} %copy-done.2), channel_id=1, source_target_pairs={{0,16},{16,0},{1,17},{17,1},{2,18},{18,2},{3,19},{19,3},{4,20},{20... | collective-permute-start | bytes 589832 | tf_op jit(solution)/shard_map/ppermute | solution.py:96
  140.3 10.7 %copy-start.3 = (f32[128,96]{0,1:T(8,128)S(1)}, f32[128,96]{0,1:T(8,128)}, u32[]{:S(2)}) copy-start(f32[128,96]{0,1:T(8,128)} %param.5) | copy-start | bytes 147460
  147.5 10.0 %all-to-all-start.1 = ((f32[16,1,96]{2,1,0:T(1,128)}), f32[16,1,96]{2,1,0:T(1,128)S(1)}, u32[]{:S(2)}, u32[]{:S(2)}) async-start(f32[16,1,96]{2,1,0:T(1,128)} %broadcast_in_dim.26), calls=%async_computation.1 | async-start | bytes 16384 | tf_op jit(solution)/shard_map/all_to_all | solution.py:99
Sparse Core Ops, SparseCore 0:
  18.4 55.6 all-gather.1

commit v2 on v1

v2 whole, which is shorter than its diff:
```python
import functools

import jax
import jax.numpy as jnp
from jax import lax
from jax.experimental import pallas as pl
from jax.experimental.pallas import tpu as pltpu
from jax.sharding import PartitionSpec as P

LOW = jnp.bfloat16
WIDE = jnp.float32
INNER = 4


def swapped(shard, axis, bit):
    peers = lax.axis_size(axis)
    return lax.ppermute(shard, axis, [(i, i ^ bit) for i in range(peers)])


def split(wide):
    high = lax.reduce_precision(wide, 8, 7)
    return high.astype(LOW), (wide - high).astype(LOW)


def tied(*arrays):
    return lax.optimization_barrier(arrays)


def halved(whole):
    half = whole.shape[0] // 2
    return whole[:half], whole[half:]


def reorder_kernel(order, own, me_ref, given, taken, sems):
    me = me_ref[0]
    copies = []
    for slot, code in enumerate(order):
        start = pl.multiple_of((me ^ code) * own, own)
        copies.append(
            pltpu.make_async_copy(
                given.at[:, pl.ds(start, own)], taken.at[:, pl.ds(slot * own, own)], sems.at[slot]
            )
        )
    for copy in copies:
        copy.start()
    for copy in copies:
        copy.wait()


def reordered(features, me, order, own):
    if own % 128:
        parts = [lax.dynamic_slice_in_dim(features, (me ^ code) * own, own, 1) for code in order]
        return jnp.concatenate(parts, axis=1)
    return pl.pallas_call(
        functools.partial(reorder_kernel, order, own),
        out_shape=jax.ShapeDtypeStruct(features.shape, features.dtype),
        in_specs=[pl.BlockSpec(memory_space=pltpu.SMEM), pl.BlockSpec(memory_space=pl.ANY)],
        out_specs=pl.BlockSpec(memory_space=pl.ANY),
        scratch_shapes=[pltpu.SemaphoreType.DMA((len(order),))],
        compiler_params=pltpu.CompilerParams(vmem_limit_bytes=1 << 20),
        cost_estimate=pl.CostEstimate(flops=0, bytes_accessed=2 * features.size * 2, transcendentals=0),
    )(me.astype(jnp.int32)[None], features)


def on_device(features, coeffs, inverse, labels):
    nfeat = lax.axis_size("feat")
    nrows = lax.axis_size("rows")
    block = lax.axis_index("feat")
    me = lax.axis_index("rows")
    own, classes = coeffs.shape
    outer = nrows // INNER
    near = [z * INNER for z in range(outer)]
    quad = [0, 2, 1, 3]
    order = [q + z for q in quad for z in near]

    def picked(array, codes, axis):
        parts = [lax.dynamic_slice_in_dim(array, (me ^ code) * own, own, axis) for code in codes]
        return jnp.concatenate(parts, axis=axis)

    def over_outer(mine):
        return jnp.concatenate([mine] + [swapped(mine, "rows", z) for z in near[1:]], axis=0)

    def over_bit(mine, bit):
        return jnp.concatenate([mine, swapped(mine, "rows", bit)], axis=0)

    coeffs_low = coeffs.astype(LOW)
    blocks = [picked(inverse, [z + q for q in quad], 1).astype(LOW) for z in near]
    inverse_low = jnp.concatenate(
        [blocks[0]] + [swapped(sent, "rows", z) for sent, z in zip(blocks[1:], near[1:])], axis=0
    )
    all_coeffs = over_bit(over_bit(over_outer(coeffs_low), 2), 1)
    features = reordered(features, me, order, own)
    all_coeffs, inverse_low = tied(all_coeffs, inverse_low)

    fitted = jnp.dot(features, all_coeffs, preferred_element_type=WIDE)
    bits = [1 << k for k in range((nfeat - 1).bit_length())]
    for bit in bits[:-1]:
        fitted = fitted + swapped(fitted, "feat", bit)
    fit_high, rest = split(fitted)
    targets = (labels[:, None] == jnp.arange(classes, dtype=jnp.int32)[None, :]).astype(WIDE)
    incoming = (targets - fitted) - swapped(fit_high, "feat", bits[-1]).astype(WIDE)
    incoming_low = incoming.astype(LOW)
    sign = -1.0

    def moved(rest):
        return swapped(rest, "feat", bits[-1])

    contract = (((0,), (0,)), ((), ()))
    kept = jnp.zeros_like(incoming)
    delta_kept = jnp.zeros_like(coeffs)
    for turn in range(nfeat):
        grad = lax.dot_general(features, incoming_low, contract, preferred_element_type=WIDE)
        keep, send = halved(grad)
        grad = keep + swapped(send, "rows", 1)
        keep, send = halved(grad)
        grad = keep + swapped(send.astype(LOW), "rows", 2).astype(WIDE)
        grad_low, rest = tied(grad.astype(LOW), rest)
        parts = [swapped(grad_low, "rows", z) for z in near[1:]]
        *parts, rest = tied(*parts, moved(rest))
        incoming = incoming + sign * rest.astype(WIDE)
        for step, got in enumerate(parts, 1):
            got = got.astype(WIDE)
            grad = grad + jnp.concatenate(
                [got[(slot ^ step) * own:((slot ^ step) + 1) * own] for slot in range(outer)], axis=0
            )
        pair = jnp.concatenate(split(grad), axis=1)
        part = lax.dot_general(inverse_low, pair, contract, preferred_element_type=WIDE)
        part = part[:, :classes] + part[:, classes:]
        keep, send = halved(part)
        part = keep + swapped(send, "rows", 1)
        top, bottom = halved(part)
        delta = part + swapped(jnp.concatenate([bottom, top]).astype(LOW), "rows", 2).astype(WIDE)
        delta_low = delta.astype(LOW)
        slots = [delta_low] + [swapped(delta_low, "rows", z) for z in near[1:]]
        delta_low = jnp.concatenate([s[:own] for s in slots] + [s[own:] for s in slots], axis=0)
        delta_low = over_bit(delta_low, 1)
        outgoing = incoming - jnp.dot(features, delta_low, preferred_element_type=WIDE)
        active = block == turn
        kept = jnp.where(active, outgoing, kept)
        delta_kept = jnp.where(active, delta[:own], delta_kept)
        if turn < nfeat - 1:
            along = [(i, (i + 1) % nfeat) for i in range(nfeat)]
            high, rest = split(outgoing)
            incoming_low = lax.ppermute(high, "feat", along)
            incoming, sign = incoming_low.astype(WIDE), 1.0

            def moved(rest):
                return lax.ppermute(rest, "feat", along)

    squares = jnp.sum(kept * kept, axis=0, keepdims=True)
    squares = lax.all_to_all(
        jnp.broadcast_to(squares[None], (nrows, 1, classes)), "rows", 0, 0, tiled=True
    )
    return (coeffs + delta_kept, kept[None], jnp.sum(squares, axis=0))


def solution(mesh):
    placed = (P("rows", "feat"), P(("feat", "rows"), None), P(("feat", "rows"), None), P("rows"))
    return jax.shard_map(
        on_device,
        mesh=mesh,
        in_specs=placed,
        out_specs=(P(("feat", "rows"), None), P("feat", "rows", None), P("feat", None)),
        check_vma=False,
    )
```

time: 165 us -> 127 us (0.77)
  waiting for transfers between devices: 80.6 us -> 61.8 us
  starting transfers between devices: 32.2 us -> 45.6 us
  between operations: 14.5 us -> 1.19 us
  matrix products: 18.3 us -> 9.51 us
  local copies, waits for them, and re-layouts: 11.4 us -> 4.78 us
  other arithmetic: 7.75 us -> 2.58 us
    ppermute x19 -> x32, starting transfers between devices: 18.2 us -> 40 us  [swapped(): return lax.ppermute(shard, axis, [(i, i ^ bit) for i in range(peers)])]
    ppermute x19 -> x32, waiting for transfers between devices: 59 us -> 49.6 us  [swapped(): return lax.ppermute(shard, axis, [(i, i ^ bit) for i in range(peers)])]
    all_to_all x1 -> x0, starting transfers between devices: 7.28 us -> none  [on_device(): lax.all_to_all(jnp.broadcast_to(coeffs_low[None], (nrows // 2, own, class...]
    all_to_all x1 -> x0, waiting for transfers between devices: 5.79 us -> none  [on_device(): lax.all_to_all(jnp.broadcast_to(coeffs_low[None], (nrows // 2, own, class...]
    all_gather x1 -> x0, waiting for transfers between devices: 4.56 us -> none  [on_device(): lax.all_gather(inverse.astype(LOW), 'rows', axis=0, axis_index_groups=sam...]
    reshape x7 -> x0, local copies, waits for them, and re-layouts: 4.41 us -> none  [the longest x2 2.23 us: on_device(): grad = lax.dot_general(features, incoming_low, contract, preferred_elemen...]
    dynamic_slice x6 -> x0, local copies, waits for them, and re-layouts: 4.38 us -> none  [the longest x4 4.22 us: halves(): keep = lax.dynamic_index_in_dim(whole, bit, axis_at, keepdims=False)]
    convert_element_type x8 -> x4, other arithmetic: 4.1 us -> 0.08 us  [the longest x2 0.05 us: on_device(): grad_low, rest = tied(grad.astype(LOW), rest)]
  transfers between devices with their start and end apart: 24 -> 35, of which waited for: 20 -> 24; matrix products, arithmetic and copies ran while one was open for 11% -> 2% of each run, Pallas kernels for 0% -> 1%
where the time goes in v2:
time: 127 us
  waiting for transfers between devices  61.8 us (49%)
  starting transfers between devices  45.6 us (36%)
  matrix products  9.51 us (7%)
  local copies, waits for them, and re-layouts  4.78 us (4%)
  other arithmetic  2.58 us (2%)
  Pallas kernels  1.33 us (1%)
    ppermute x32, waiting for transfers between devices, swapped(): return lax.ppermute(shard, axis, [(i, i ^ bit) for i in range(peers)])  49.6 us
    ppermute x32, starting transfers between devices, swapped(): return lax.ppermute(shard, axis, [(i, i ^ bit) for i in range(peers)])  40 us
    ppermute x1, waiting for transfers between devices, on_device(): incoming_low = lax.ppermute(high, 'feat', along)  6.42 us
    dot_general x2, matrix products, on_device(): jnp.dot(features, delta_low, preferred_element_type=WIDE)  5.95 us
    all_to_all x1, waiting for transfers between devices, on_device(): lax.all_to_all(jnp.broadcast_to(squares[None], (nrows, 1, classes)), 'row...  5.76 us
    all_to_all x1, starting transfers between devices, on_device(): lax.all_to_all(jnp.broadcast_to(squares[None], (nrows, 1, classes)), 'row...  4.36 us
  transfers between devices with their start and end apart: 35, of which 24 were waited for; matrix products, arithmetic and copies ran while one was open for 2% of the time, Pallas kernels for 1%

profile of v2, /device:TPU:0, one launch (start us, length us, event | category | flops | bytes accessed | tf_op | source)
XLA Modules:
  0.0 126.8 jit_solution(15845903191847594684)
XLA Ops:
  1.4 3.0 %collective-permute-start = (bf16[128,96]{0,1:T(8,128)(2,1)S(1)}, bf16[128,96]{0,1:T(8,128)(2,1)S(1)}, u32[]{:S(2)}, u32[]{:S(2)}) collective-permute-start(bf16[128,96]{0,1:T(8,128)(2,1)S(1)} %get-tuple-element.44), channel_id=1, source_target_pairs={{0,4},{1,5},{2,6},{3,7},{4,0},{5,1},{6,2},{7,3},{8,12},{9,13},{10,... | collective-permute-start | bytes 73736 | tf_op jit(solution)/shard_map/ppermute | solution.py:17
  4.5 2.6 %collective-permute-start.1 = (bf16[128,96]{0,1:T(8,128)(2,1)S(1)}, bf16[128,96]{0,1:T(8,128)(2,1)S(1)}, u32[]{:S(2)}, u32[]{:S(2)}) collective-permute-start(bf16[128,96]{0,1:T(8,128)(2,1)S(1)} %get-tuple-element.44), channel_id=1, source_target_pairs={{0,8},{1,9},{2,10},{3,11},{4,12},{5,13},{6,14},{7,15},{8,0},{9,1},... | collective-permute-start | bytes 73736 | tf_op jit(solution)/shard_map/ppermute | solution.py:17
  7.1 1.3 %dynamic-slice_convert_fusion.15 = (bf16[128,128]{1,0:T(8,128)(2,1)S(1)}, bf16[128,128]{1,0:T(8,128)(2,1)S(1)}, bf16[128,128]{1,0:T(8,128)(2,1)S(1)}, bf16[128,1...) fusion(f32[128,2048]{1,0:T(8,128)} %param.6, ...), kind=kLoop, calls=%fused_computation.113 | loop fusion | bytes 1048640 | tf_op jit(solution)/shard_map/convert.22
  8.4 3.9 %collective-permute-start.7 = (bf16[128,512]{1,0:T(8,128)(2,1)S(1)}, bf16[128,512]{1,0:T(8,128)(2,1)S(1)}, u32[]{:S(2)}, u32[]{:S(2)}) collective-permute-start(bf16[128,512]{1,0:T(8,128)(2,1)S(1)} %pad_maximum_fusion.3), channel_id=1, source_target_pairs={{0,12},{1,13},{2,14},{3,15},{4,8},{5,9},{6,10},{7,11},{8,4},{9,5},... | collective-permute-start | bytes 393224 | tf_op jit(solution)/shard_map/ppermute | solution.py:17
  13.1 1.8 %collective-permute-start.3 = (bf16[512,96]{0,1:T(8,128)(2,1)S(1)}, bf16[512,96]{0,1:T(8,128)(2,1)S(1)}, u32[]{:S(2)}, u32[]{:S(2)}) collective-permute-start(bf16[512,96]{0,1:T(8,128)(2,1)S(1)} %pad_maximum_fusion.4), channel_id=1, source_target_pairs={{0,2},{1,3},{2,0},{3,1},{4,6},{5,7},{6,4},{7,5},{8,10},{9,11},{10,... | collective-permute-start | bytes 294920 | tf_op jit(solution)/shard_map/ppermute | solution.py:17
  15.0 2.8 %collective-permute-done.3 = bf16[512,96]{0,1:T(8,128)(2,1)S(1)} collective-permute-done((bf16[512,96]{0,1:T(8,128)(2,1)S(1)}, bf16[512,96]{0,1:T(8,128)(2,1)S(1)}, u32[]{:S(2)}, u32[]{:S(2)}) %collective-permute-start.3) | collective-permute-done | bytes 98336 | tf_op jit(solution)/shard_map/ppermute | solution.py:17
  17.9 2.2 %copy-done.1 = bf16[1024,2048]{1,0:T(8,128)(2,1)S(1)} copy-done((bf16[1024,2048]{1,0:T(8,128)(2,1)S(1)}, bf16[1024,2048]{1,0:T(8,128)(2,1)}, u32[]{:S(2)}) %copy-start.1) | copy-done | bytes 4194328
  20.1 1.3 %shard_map.67 = bf16[1024,2048]{1,0:T(8,128)(2,1)S(1)} custom-call(s32[1]{0:T(128)} %bitcast.me_ref, bf16[1024,2048]{1,0:T(8,128)(2,1)S(1)} %copy-done.1), custom_call_target="tpu_custom_call" | custom-call | bytes 8388608 | tf_op jit(solution)/shard_map/pallas_call | solution.py:54
  21.5 1.0 collective-permute-done.6
  22.5 1.4 %fusion = (bf16[1024,96]{0,1:T(8,128)(2,1)S(1)}, bf16[1024,96]{0,1:T(8,128)(2,1)S(1)}, f32[1024,96]{0,1:T(8,128)S(1)}) fusion(bf16[1024,2048]{1,0:T(8,128)(2,1)S(1)} %shard_map.67, bf16[2048,96]{0,1:T(8,128)(2,1)S(1)} %constant_dynamic-update-slice_fusion.5), kind=kOutput, calls=%fused_computation.5 | convolution fusion | flops 403046400 | bytes 5373952 | tf_op jit(solution)/shard_map/dot_general | solution.py:95
  24.0 1.6 %collective-permute-start.8 = (bf16[1024,96]{0,1:T(8,128)(2,1)S(1)}, bf16[1024,96]{0,1:T(8,128)(2,1)S(1)}, u32[]{:S(2)}, u32[]{:S(2)}) collective-permute-start(bf16[1024,96]{0,1:T(8,128)(2,1)S(1)} %get-tuple-element.62), channel_id=1, source_target_pairs={{0,16},{16,0},{1,17},{17,1},{2,18},{18,2},{3,19},{19,3},{4,20},{20... | collective-permute-start | bytes 589832 | tf_op jit(solution)/shard_map/ppermute | solution.py:17
  25.5 4.9 %collective-permute-done.8 = bf16[1024,96]{0,1:T(8,128)(2,1)S(1)} collective-permute-done((bf16[1024,96]{0,1:T(8,128)(2,1)S(1)}, bf16[1024,96]{0,1:T(8,128)(2,1)S(1)}, u32[]{:S(2)}, u32[]{:S(2)}) %collective-permute-start.8) | collective-permute-done | bytes 196640 | tf_op jit(solution)/shard_map/ppermute | solution.py:17
  31.3 1.7 %collective-permute-done.9 = f32[1024,96]{0,1:T(8,128)S(1)} collective-permute-done((f32[1024,96]{0,1:T(8,128)S(1)}, f32[1024,96]{0,1:T(8,128)S(1)}, u32[]{:S(2)}, u32[]{:S(2)}) %collective-permute-start.9) | collective-permute-done | bytes 393248 | tf_op jit(solution)/shard_map/ppermute | solution.py:17
  33.1 1.8 %collective-permute-start.10 = (bf16[512,96]{0,1:T(8,128)(2,1)S(1)}, bf16[512,96]{0,1:T(8,128)(2,1)S(1)}, u32[]{:S(2)}, u32[]{:S(2)}) collective-permute-start(bf16[512,96]{0,1:T(8,128)(2,1)S(1)} %slice.371), channel_id=1, source_target_pairs={{0,2},{1,3},{2,0},{3,1},{4,6},{5,7},{6,4},{7,5},{8,10},{9,11},{10,... | collective-permute-start | bytes 294920 | tf_op jit(solution)/shard_map/ppermute | solution.py:17
  34.9 3.1 %collective-permute-done.10 = bf16[512,96]{0,1:T(8,128)(2,1)S(1)} collective-permute-done((bf16[512,96]{0,1:T(8,128)(2,1)S(1)}, bf16[512,96]{0,1:T(8,128)(2,1)S(1)}, u32[]{:S(2)}, u32[]{:S(2)}) %collective-permute-start.10) | collective-permute-done | bytes 98336 | tf_op jit(solution)/shard_map/ppermute | solution.py:17
  38.0 1.8 %collective-permute-start.14 = (bf16[1024,96]{0,1:T(8,128)(2,1)S(1)}, bf16[1024,96]{0,1:T(8,128)(2,1)S(1)}, u32[]{:S(2)}, u32[]{:S(2)}) collective-permute-start(bf16[1024,96]{0,1:T(8,128)(2,1)S(1)} %get-tuple-element.20), channel_id=1, source_target_pairs={{0,16},{16,0},{1,17},{17,1},{2,18},{18,2},{3,19},{19,3},{4,20},{20... | collective-permute-start | bytes 589832 | tf_op jit(solution)/shard_map/ppermute | solution.py:17
  39.8 1.3 collective-permute-start.11
  41.0 2.9 %collective-permute-start.12 = (bf16[512,96]{0,1:T(8,128)(2,1)S(1)}, bf16[512,96]{0,1:T(8,128)(2,1)S(1)}, u32[]{:S(2)}, u32[]{:S(2)}) collective-permute-start(bf16[512,96]{0,1:T(8,128)(2,1)S(1)} %fusion.20), channel_id=1, source_target_pairs={{0,8},{1,9},{2,10},{3,11},{4,12},{5,13},{6,14},{7,15},{8,0},{9,1},... | collective-permute-start | bytes 294920 | tf_op jit(solution)/shard_map/ppermute | solution.py:17
  44.2 1.1 collective-permute-done.11
  45.3 5.6 %collective-permute-done.12 = bf16[512,96]{0,1:T(8,128)(2,1)S(1)} collective-permute-done((bf16[512,96]{0,1:T(8,128)(2,1)S(1)}, bf16[512,96]{0,1:T(8,128)(2,1)S(1)}, u32[]{:S(2)}, u32[]{:S(2)}) %collective-permute-start.12) | collective-permute-done | bytes 98336 | tf_op jit(solution)/shard_map/ppermute | solution.py:17
  51.5 1.3 %collective-permute-done.15 = f32[256,96]{0,1:T(8,128)S(1)} collective-permute-done((f32[256,96]{0,1:T(8,128)S(1)}, f32[256,96]{0,1:T(8,128)S(1)}, u32[]{:S(2)}, u32[]{:S(2)}) %collective-permute-start.15) | collective-permute-done | bytes 98336 | tf_op jit(solution)/shard_map/ppermute | solution.py:17
  52.8 1.6 %collective-permute-start.16 = (bf16[256,96]{0,1:T(8,128)(2,1)S(1)}, bf16[256,96]{0,1:T(8,128)(2,1)S(1)}, u32[]{:S(2)}, u32[]{:S(2)}) collective-permute-start(bf16[256,96]{0,1:T(8,128)(2,1)S(1)} %pad_maximum_fusion.5), channel_id=1, source_target_pairs={{0,2},{1,3},{2,0},{3,1},{4,6},{5,7},{6,4},{7,5},{8,10},{9,11},{10,... | collective-permute-start | bytes 147464 | tf_op jit(solution)/shard_map/ppermute | solution.py:17
  54.4 2.6 %collective-permute-done.16 = bf16[256,96]{0,1:T(8,128)(2,1)S(1)} collective-permute-done((bf16[256,96]{0,1:T(8,128)(2,1)S(1)}, bf16[256,96]{0,1:T(8,128)(2,1)S(1)}, u32[]{:S(2)}, u32[]{:S(2)}) %collective-permute-start.16) | collective-permute-done | bytes 49184 | tf_op jit(solution)/shard_map/ppermute | solution.py:17
  57.0 1.7 %collective-permute-start.17 = (bf16[256,96]{0,1:T(8,128)(2,1)S(1)}, bf16[256,96]{0,1:T(8,128)(2,1)S(1)}, u32[]{:S(2)}, u32[]{:S(2)}) collective-permute-start(bf16[256,96]{0,1:T(8,128)(2,1)S(1)} %get-tuple-element.39), channel_id=1, source_target_pairs={{0,4},{1,5},{2,6},{3,7},{4,0},{5,1},{6,2},{7,3},{8,12},{9,13},{10,... | collective-permute-start | bytes 147464 | tf_op jit(solution)/shard_map/ppermute | solution.py:17
  58.7 1.4 %collective-permute-start.18 = (bf16[256,96]{0,1:T(8,128)(2,1)S(1)}, bf16[256,96]{0,1:T(8,128)(2,1)S(1)}, u32[]{:S(2)}, u32[]{:S(2)}) collective-permute-start(bf16[256,96]{0,1:T(8,128)(2,1)S(1)} %get-tuple-element.39), channel_id=1, source_target_pairs={{0,8},{1,9},{2,10},{3,11},{4,12},{5,13},{6,14},{7,15},{8,0},{9,1},... | collective-permute-start | bytes 147464 | tf_op jit(solution)/shard_map/ppermute | solution.py:17
  60.0 1.4 %collective-permute-start.19 = (bf16[256,96]{0,1:T(8,128)(2,1)S(1)}, bf16[256,96]{0,1:T(8,128)(2,1)S(1)}, u32[]{:S(2)}, u32[]{:S(2)}) collective-permute-start(bf16[256,96]{0,1:T(8,128)(2,1)S(1)} %get-tuple-element.39), channel_id=1, source_target_pairs={{0,12},{1,13},{2,14},{3,15},{4,8},{5,9},{6,10},{7,11},{8,4},{9,5},... | collective-permute-start | bytes 147464 | tf_op jit(solution)/shard_map/ppermute | solution.py:17
  61.5 3.0 %collective-permute-done.18 = bf16[256,96]{0,1:T(8,128)(2,1)S(1)} collective-permute-done((bf16[256,96]{0,1:T(8,128)(2,1)S(1)}, bf16[256,96]{0,1:T(8,128)(2,1)S(1)}, u32[]{:S(2)}, u32[]{:S(2)}) %collective-permute-start.18) | collective-permute-done | bytes 49184 | tf_op jit(solution)/shard_map/ppermute | solution.py:17
  64.6 1.3 %collective-permute-done.19 = bf16[256,96]{0,1:T(8,128)(2,1)S(1)} collective-permute-done((bf16[256,96]{0,1:T(8,128)(2,1)S(1)}, bf16[256,96]{0,1:T(8,128)(2,1)S(1)}, u32[]{:S(2)}, u32[]{:S(2)}) %collective-permute-start.19) | collective-permute-done | bytes 49184 | tf_op jit(solution)/shard_map/ppermute | solution.py:17
  66.2 1.4 %collective-permute-done.20 = bf16[1024,96]{0,1:T(8,128)(2,1)S(1)} collective-permute-done((bf16[1024,96]{0,1:T(8,128)(2,1)S(1)}, bf16[1024,96]{0,1:T(8,128)(2,1)S(1)}, u32[]{:S(2)}, u32[]{:S(2)}) %collective-permute-start.20) | collective-permute-done | bytes 196640 | tf_op jit(solution)/shard_map/ppermute | solution.py:17
  67.6 1.5 %fusion.1 = (bf16[1024,96]{0,1:T(8,128)(2,1)S(1)}, f32[1024,96]{0,1:T(8,128)S(1)}) fusion(bf16[1024,96]{0,1:T(8,128)(2,1)S(1)} %collective-permute-done.14, bf16[1024,96]{0,1:T(8,128)(2,1)S(1)} %collective-permute-done.8, f32[1024,96]{0,1:T(8,128)S(1)} %get-tuple-element.111, s32[1024]{0:T(1024)S(1)} %copy-done.3, bf16[1024,2048]{1,0:T(8,128)(2,1)S(1)} %shard_map.67, ...), kind=kOutput, calls=%fused_computation.6 | convolution fusion | flops 403832832 | bytes 5967872 | tf_op jit(solution)/shard_map/dot_general | solution.py:137
  69.7 6.4 %collective-permute-done.21 = bf16[1024,96]{0,1:T(8,128)(2,1)S(1)} collective-permute-done((bf16[1024,96]{0,1:T(8,128)(2,1)S(1)}, bf16[1024,96]{0,1:T(8,128)(2,1)S(1)}, u32[]{:S(2)}, u32[]{:S(2)}) %collective-permute-start.21) | collective-permute-done | bytes 196640 | tf_op jit(solution)/shard_map/ppermute | solution.py:144
  77.0 1.7 %collective-permute-done.22 = f32[1024,96]{0,1:T(8,128)S(1)} collective-permute-done((f32[1024,96]{0,1:T(8,128)S(1)}, f32[1024,96]{0,1:T(8,128)S(1)}, u32[]{:S(2)}, u32[]{:S(2)}) %collective-permute-start.22) | collective-permute-done | bytes 393248 | tf_op jit(solution)/shard_map/ppermute | solution.py:17
  78.8 1.6 %collective-permute-start.23 = (bf16[512,96]{0,1:T(8,128)(2,1)S(1)}, bf16[512,96]{0,1:T(8,128)(2,1)S(1)}, u32[]{:S(2)}, u32[]{:S(2)}) collective-permute-start(bf16[512,96]{0,1:T(8,128)(2,1)S(1)} %slice.370), channel_id=1, source_target_pairs={{0,2},{1,3},{2,0},{3,1},{4,6},{5,7},{6,4},{7,5},{8,10},{9,11},{10,... | collective-permute-start | bytes 294920 | tf_op jit(solution)/shard_map/ppermute | solution.py:17
  80.4 3.3 %collective-permute-done.23 = bf16[512,96]{0,1:T(8,128)(2,1)S(1)} collective-permute-done((bf16[512,96]{0,1:T(8,128)(2,1)S(1)}, bf16[512,96]{0,1:T(8,128)(2,1)S(1)}, u32[]{:S(2)}, u32[]{:S(2)}) %collective-permute-start.23) | collective-permute-done | bytes 98336 | tf_op jit(solution)/shard_map/ppermute | solution.py:17
  84.3 2.1 %collective-permute-start.25 = (bf16[512,96]{0,1:T(8,128)(2,1)S(1)}, bf16[512,96]{0,1:T(8,128)(2,1)S(1)}, u32[]{:S(2)}, u32[]{:S(2)}) collective-permute-start(bf16[512,96]{0,1:T(8,128)(2,1)S(1)} %fusion.21), channel_id=1, source_target_pairs={{0,8},{1,9},{2,10},{3,11},{4,12},{5,13},{6,14},{7,15},{8,0},{9,1},... | collective-permute-start | bytes 294920 | tf_op jit(solution)/shard_map/ppermute | solution.py:17
  86.4 2.3 %collective-permute-start.26 = (bf16[512,96]{0,1:T(8,128)(2,1)S(1)}, bf16[512,96]{0,1:T(8,128)(2,1)S(1)}, u32[]{:S(2)}, u32[]{:S(2)}) collective-permute-start(bf16[512,96]{0,1:T(8,128)(2,1)S(1)} %fusion.21), channel_id=1, source_target_pairs={{0,12},{1,13},{2,14},{3,15},{4,8},{5,9},{6,10},{7,11},{8,4},{9,5},... | collective-permute-start | bytes 294920 | tf_op jit(solution)/shard_map/ppermute | solution.py:17
  89.2 5.1 %collective-permute-done.25 = bf16[512,96]{0,1:T(8,128)(2,1)S(1)} collective-permute-done((bf16[512,96]{0,1:T(8,128)(2,1)S(1)}, bf16[512,96]{0,1:T(8,128)(2,1)S(1)}, u32[]{:S(2)}, u32[]{:S(2)}) %collective-permute-start.25) | collective-permute-done | bytes 98336 | tf_op jit(solution)/shard_map/ppermute | solution.py:17
  94.8 1.3 %collective-permute-done.28 = f32[256,96]{0,1:T(8,128)S(1)} collective-permute-done((f32[256,96]{0,1:T(8,128)S(1)}, f32[256,96]{0,1:T(8,128)S(1)}, u32[]{:S(2)}, u32[]{:S(2)}) %collective-permute-start.28) | collective-permute-done | bytes 98336 | tf_op jit(solution)/shard_map/ppermute | solution.py:17
  96.2 1.6 %collective-permute-start.29 = (bf16[256,96]{0,1:T(8,128)(2,1)S(1)}, bf16[256,96]{0,1:T(8,128)(2,1)S(1)}, u32[]{:S(2)}, u32[]{:S(2)}) collective-permute-start(bf16[256,96]{0,1:T(8,128)(2,1)S(1)} %pad_maximum_fusion.6), channel_id=1, source_target_pairs={{0,2},{1,3},{2,0},{3,1},{4,6},{5,7},{6,4},{7,5},{8,10},{9,11},{10,... | collective-permute-start | bytes 147464 | tf_op jit(solution)/shard_map/ppermute | solution.py:17
  97.8 2.6 %collective-permute-done.29 = bf16[256,96]{0,1:T(8,128)(2,1)S(1)} collective-permute-done((bf16[256,96]{0,1:T(8,128)(2,1)S(1)}, bf16[256,96]{0,1:T(8,128)(2,1)S(1)}, u32[]{:S(2)}, u32[]{:S(2)}) %collective-permute-start.29) | collective-permute-done | bytes 49184 | tf_op jit(solution)/shard_map/ppermute | solution.py:17
  100.4 1.7 %collective-permute-start.30 = (bf16[256,96]{0,1:T(8,128)(2,1)S(1)}, bf16[256,96]{0,1:T(8,128)(2,1)S(1)}, u32[]{:S(2)}, u32[]{:S(2)}) collective-permute-start(bf16[256,96]{0,1:T(8,128)(2,1)S(1)} %get-tuple-element.33), channel_id=1, source_target_pairs={{0,4},{1,5},{2,6},{3,7},{4,0},{5,1},{6,2},{7,3},{8,12},{9,13},{10,... | collective-permute-start | bytes 147464 | tf_op jit(solution)/shard_map/ppermute | solution.py:17
  102.8 2.0 %collective-permute-start.32 = (bf16[256,96]{0,1:T(8,128)(2,1)S(1)}, bf16[256,96]{0,1:T(8,128)(2,1)S(1)}, u32[]{:S(2)}, u32[]{:S(2)}) collective-permute-start(bf16[256,96]{0,1:T(8,128)(2,1)S(1)} %get-tuple-element.33), channel_id=1, source_target_pairs={{0,12},{1,13},{2,14},{3,15},{4,8},{5,9},{6,10},{7,11},{8,4},{9,5},... | collective-permute-start | bytes 147464 | tf_op jit(solution)/shard_map/ppermute | solution.py:17
  104.8 2.7 %collective-permute-done.31 = bf16[256,96]{0,1:T(8,128)(2,1)S(1)} collective-permute-done((bf16[256,96]{0,1:T(8,128)(2,1)S(1)}, bf16[256,96]{0,1:T(8,128)(2,1)S(1)}, u32[]{:S(2)}, u32[]{:S(2)}) %collective-permute-start.31) | collective-permute-done | bytes 49184 | tf_op jit(solution)/shard_map/ppermute | solution.py:17
  107.5 1.2 collective-permute-done.32
  109.0 1.4 %collective-permute-done.33 = bf16[1024,96]{0,1:T(8,128)(2,1)S(1)} collective-permute-done((bf16[1024,96]{0,1:T(8,128)(2,1)S(1)}, bf16[1024,96]{0,1:T(8,128)(2,1)S(1)}, u32[]{:S(2)}, u32[]{:S(2)}) %collective-permute-start.33) | collective-permute-done | bytes 196640 | tf_op jit(solution)/shard_map/ppermute | solution.py:17
  110.3 4.5 %multiply_reduce_fusion = (f32[96]{0:T(128)S(1)}, f32[1024,96]{0,1:T(8,128)}) fusion(f32[1024,96]{0,1:T(8,128)S(1)} %get-tuple-element.38, pred[]{:T(512)S(6)} %eq.23, bf16[1024,96]{0,1:T(8,128)(2,1)S(1)} %collective-permute-done.27, bf16[1024,96]{0,1:T(8,128)(2,1)S(1)} %collective-permute-done.21, pred[]{:T(512)S(6)} %eq.19, ...), kind=kOutput, calls=%fused_computation.9 | convolution fusion | flops 403439520 | bytes 5767554 | tf_op jit(solution)/shard_map/dot_general | solution.py:137
  115.5 4.4 %all-to-all-start = ((f32[16,1,96]{2,1,0:T(1,128)}), f32[16,1,96]{2,1,0:T(1,128)S(1)}, u32[]{:S(2)}, u32[]{:S(2)}) async-start(f32[16,1,96]{2,1,0:T(1,128)} %broadcast_in_dim.23), calls=%async_computation | async-start | bytes 16384 | tf_op jit(solution)/shard_map/all_to_all | solution.py:151
  120.5 5.8 %all-to-all-done = f32[16,1,96]{2,1,0:T(1,128)S(1)} async-done(((f32[16,1,96]{2,1,0:T(1,128)}), f32[16,1,96]{2,1,0:T(1,128)S(1)}, u32[]{:S(2)}, u32[]{:S(2)}) %all-to-all-start) | async-done | bytes 6176 | tf_op jit(solution)/shard_map/all_to_all | solution.py:151
  (110 shorter events, 9.9 us)
Async XLA Ops:
  1.4 11.0 %collective-permute-start = (bf16[128,96]{0,1:T(8,128)(2,1)S(1)}, bf16[128,96]{0,1:T(8,128)(2,1)S(1)}, u32[]{:S(2)}, u32[]{:S(2)}) collective-permute-start(bf16[128,96]{0,1:T(8,128)(2,1)S(1)} %get-tuple-element.44), channel_id=1, source_target_pairs={{0,4},{1,5},{2,6},{3,7},{4,0},{5,1},{6,2},{7,3},{8,12},{9,13},{10,... | collective-permute-start | bytes 73736 | tf_op jit(solution)/shard_map/ppermute | solution.py:17
  4.5 8.6 %collective-permute-start.1 = (bf16[128,96]{0,1:T(8,128)(2,1)S(1)}, bf16[128,96]{0,1:T(8,128)(2,1)S(1)}, u32[]{:S(2)}, u32[]{:S(2)}) collective-permute-start(bf16[128,96]{0,1:T(8,128)(2,1)S(1)} %get-tuple-element.44), channel_id=1, source_target_pairs={{0,8},{1,9},{2,10},{3,11},{4,12},{5,13},{6,14},{7,15},{8,0},{9,1},... | collective-permute-start | bytes 73736 | tf_op jit(solution)/shard_map/ppermute | solution.py:17
  7.1 6.0 %collective-permute-start.2 = (bf16[128,96]{0,1:T(8,128)(2,1)S(1)}, bf16[128,96]{0,1:T(8,128)(2,1)S(1)}, u32[]{:S(2)}, u32[]{:S(2)}) collective-permute-start(bf16[128,96]{0,1:T(8,128)(2,1)S(1)} %get-tuple-element.44), channel_id=1, source_target_pairs={{0,12},{1,13},{2,14},{3,15},{4,8},{5,9},{6,10},{7,11},{8,4},{9,5},... | collective-permute-start | bytes 73736 | tf_op jit(solution)/shard_map/ppermute | solution.py:17
  8.4 13.0 %collective-permute-start.7 = (bf16[128,512]{1,0:T(8,128)(2,1)S(1)}, bf16[128,512]{1,0:T(8,128)(2,1)S(1)}, u32[]{:S(2)}, u32[]{:S(2)}) collective-permute-start(bf16[128,512]{1,0:T(8,128)(2,1)S(1)} %pad_maximum_fusion.3), channel_id=1, source_target_pairs={{0,12},{1,13},{2,14},{3,15},{4,8},{5,9},{6,10},{7,11},{8,4},{9,5},... | collective-permute-start | bytes 393224 | tf_op jit(solution)/shard_map/ppermute | solution.py:17
  12.3 10.1 %collective-permute-start.6 = (bf16[128,512]{1,0:T(8,128)(2,1)S(1)}, bf16[128,512]{1,0:T(8,128)(2,1)S(1)}, u32[]{:S(2)}, u32[]{:S(2)}) collective-permute-start(bf16[128,512]{1,0:T(8,128)(2,1)S(1)} %pad_maximum_fusion.2), channel_id=1, source_target_pairs={{0,8},{1,9},{2,10},{3,11},{4,12},{5,13},{6,14},{7,15},{8,0},{9,1},... | collective-permute-start | bytes 393224 | tf_op jit(solution)/shard_map/ppermute | solution.py:17
  12.5 10.0 %collective-permute-start.5 = (bf16[128,512]{1,0:T(8,128)(2,1)S(1)}, bf16[128,512]{1,0:T(8,128)(2,1)S(1)}, u32[]{:S(2)}, u32[]{:S(2)}) collective-permute-start(bf16[128,512]{1,0:T(8,128)(2,1)S(1)} %pad_maximum_fusion.1), channel_id=1, source_target_pairs={{0,4},{1,5},{2,6},{3,7},{4,0},{5,1},{6,2},{7,3},{8,12},{9,13},{10,... | collective-permute-start | bytes 393224 | tf_op jit(solution)/shard_map/ppermute | solution.py:17
  13.1 4.7 %collective-permute-start.3 = (bf16[512,96]{0,1:T(8,128)(2,1)S(1)}, bf16[512,96]{0,1:T(8,128)(2,1)S(1)}, u32[]{:S(2)}, u32[]{:S(2)}) collective-permute-start(bf16[512,96]{0,1:T(8,128)(2,1)S(1)} %pad_maximum_fusion.4), channel_id=1, source_target_pairs={{0,2},{1,3},{2,0},{3,1},{4,6},{5,7},{6,4},{7,5},{8,10},{9,11},{10,... | collective-permute-start | bytes 294920 | tf_op jit(solution)/shard_map/ppermute | solution.py:17
  17.8 4.7 %collective-permute-start.4 = (bf16[1024,96]{0,1:T(8,128)(2,1)S(1)}, bf16[1024,96]{0,1:T(8,128)(2,1)S(1)}, u32[]{:S(2)}, u32[]{:S(2)}) collective-permute-start(bf16[1024,96]{0,1:T(8,128)(2,1)S(1)} %get-tuple-element.83), channel_id=1, source_target_pairs={{0,1},{1,0},{2,3},{3,2},{4,5},{5,4},{6,7},{7,6},{8,9},{9,8},{10,11... | collective-permute-start | bytes 589832 | tf_op jit(solution)/shard_map/ppermute | solution.py:17
  17.9 2.2 %copy-start.1 = (bf16[1024,2048]{1,0:T(8,128)(2,1)S(1)}, bf16[1024,2048]{1,0:T(8,128)(2,1)}, u32[]{:S(2)}) copy-start(bf16[1024,2048]{1,0:T(8,128)(2,1)} %given.1) | copy-start | bytes 12582916
  21.4 54.7 %copy-start = (bf16[1024,2048]{1,0:T(8,128)(2,1)}, bf16[1024,2048]{1,0:T(8,128)(2,1)S(1)}, u32[]{:S(2)}) copy-start(bf16[1024,2048]{1,0:T(8,128)(2,1)S(1)} %shard_map.67) | copy-start | bytes 12582916
  21.4 8.9 %copy-start.3 = (s32[1024]{0:T(1024)S(1)}, s32[1024]{0:T(1024)}, u32[]{:S(2)}) copy-start(s32[1024]{0:T(1024)} %param.7) | copy-start | bytes 12292
  24.0 6.4 %collective-permute-start.8 = (bf16[1024,96]{0,1:T(8,128)(2,1)S(1)}, bf16[1024,96]{0,1:T(8,128)(2,1)S(1)}, u32[]{:S(2)}, u32[]{:S(2)}) collective-permute-start(bf16[1024,96]{0,1:T(8,128)(2,1)S(1)} %get-tuple-element.62), channel_id=1, source_target_pairs={{0,16},{16,0},{1,17},{17,1},{2,18},{18,2},{3,19},{19,3},{4,20},{20... | collective-permute-start | bytes 589832 | tf_op jit(solution)/shard_map/ppermute | solution.py:17
  31.2 1.8 %collective-permute-start.9 = (f32[1024,96]{0,1:T(8,128)S(1)}, f32[1024,96]{0,1:T(8,128)S(1)}, u32[]{:S(2)}, u32[]{:S(2)}) collective-permute-start(f32[1024,96]{0,1:T(8,128)S(1)} %slice.247), channel_id=1, source_target_pairs={{0,1},{1,0},{2,3},{3,2},{4,5},{5,4},{6,7},{7,6},{8,9},{9,8},{10,11... | collective-permute-start | bytes 1179656 | tf_op jit(solution)/shard_map/ppermute | solution.py:17
  33.1 4.9 %collective-permute-start.10 = (bf16[512,96]{0,1:T(8,128)(2,1)S(1)}, bf16[512,96]{0,1:T(8,128)(2,1)S(1)}, u32[]{:S(2)}, u32[]{:S(2)}) collective-permute-start(bf16[512,96]{0,1:T(8,128)(2,1)S(1)} %slice.371), channel_id=1, source_target_pairs={{0,2},{1,3},{2,0},{3,1},{4,6},{5,7},{6,4},{7,5},{8,10},{9,11},{10,... | collective-permute-start | bytes 294920 | tf_op jit(solution)/shard_map/ppermute | solution.py:17
  38.0 12.9 %collective-permute-start.14 = (bf16[1024,96]{0,1:T(8,128)(2,1)S(1)}, bf16[1024,96]{0,1:T(8,128)(2,1)S(1)}, u32[]{:S(2)}, u32[]{:S(2)}) collective-permute-start(bf16[1024,96]{0,1:T(8,128)(2,1)S(1)} %get-tuple-element.20), channel_id=1, source_target_pairs={{0,16},{16,0},{1,17},{17,1},{2,18},{18,2},{3,19},{19,3},{4,20},{20... | collective-permute-start | bytes 589832 | tf_op jit(solution)/shard_map/ppermute | solution.py:17
  39.8 5.5 %collective-permute-start.11 = (bf16[512,96]{0,1:T(8,128)(2,1)S(1)}, bf16[512,96]{0,1:T(8,128)(2,1)S(1)}, u32[]{:S(2)}, u32[]{:S(2)}) collective-permute-start(bf16[512,96]{0,1:T(8,128)(2,1)S(1)} %fusion.20), channel_id=1, source_target_pairs={{0,4},{1,5},{2,6},{3,7},{4,0},{5,1},{6,2},{7,3},{8,12},{9,13},{10,... | collective-permute-start | bytes 294920 | tf_op jit(solution)/shard_map/ppermute | solution.py:17
  41.0 9.9 %collective-permute-start.12 = (bf16[512,96]{0,1:T(8,128)(2,1)S(1)}, bf16[512,96]{0,1:T(8,128)(2,1)S(1)}, u32[]{:S(2)}, u32[]{:S(2)}) collective-permute-start(bf16[512,96]{0,1:T(8,128)(2,1)S(1)} %fusion.20), channel_id=1, source_target_pairs={{0,8},{1,9},{2,10},{3,11},{4,12},{5,13},{6,14},{7,15},{8,0},{9,1},... | collective-permute-start | bytes 294920 | tf_op jit(solution)/shard_map/ppermute | solution.py:17
  43.9 7.0 %collective-permute-start.13 = (bf16[512,96]{0,1:T(8,128)(2,1)S(1)}, bf16[512,96]{0,1:T(8,128)(2,1)S(1)}, u32[]{:S(2)}, u32[]{:S(2)}) collective-permute-start(bf16[512,96]{0,1:T(8,128)(2,1)S(1)} %fusion.20), channel_id=1, source_target_pairs={{0,12},{1,13},{2,14},{3,15},{4,8},{5,9},{6,10},{7,11},{8,4},{9,5},... | collective-permute-start | bytes 294920 | tf_op jit(solution)/shard_map/ppermute | solution.py:17
  51.4 1.4 %collective-permute-start.15 = (f32[256,96]{0,1:T(8,128)S(1)}, f32[256,96]{0,1:T(8,128)S(1)}, u32[]{:S(2)}, u32[]{:S(2)}) collective-permute-start(f32[256,96]{0,1:T(8,128)S(1)} %slice.263), channel_id=1, source_target_pairs={{0,1},{1,0},{2,3},{3,2},{4,5},{5,4},{6,7},{7,6},{8,9},{9,8},{10,11... | collective-permute-start | bytes 294920 | tf_op jit(solution)/shard_map/ppermute | solution.py:17
  52.8 4.2 %collective-permute-start.16 = (bf16[256,96]{0,1:T(8,128)(2,1)S(1)}, bf16[256,96]{0,1:T(8,128)(2,1)S(1)}, u32[]{:S(2)}, u32[]{:S(2)}) collective-permute-start(bf16[256,96]{0,1:T(8,128)(2,1)S(1)} %pad_maximum_fusion.5), channel_id=1, source_target_pairs={{0,2},{1,3},{2,0},{3,1},{4,6},{5,7},{6,4},{7,5},{8,10},{9,11},{10,... | collective-permute-start | bytes 147464 | tf_op jit(solution)/shard_map/ppermute | solution.py:17
  57.0 4.5 %collective-permute-start.17 = (bf16[256,96]{0,1:T(8,128)(2,1)S(1)}, bf16[256,96]{0,1:T(8,128)(2,1)S(1)}, u32[]{:S(2)}, u32[]{:S(2)}) collective-permute-start(bf16[256,96]{0,1:T(8,128)(2,1)S(1)} %get-tuple-element.39), channel_id=1, source_target_pairs={{0,4},{1,5},{2,6},{3,7},{4,0},{5,1},{6,2},{7,3},{8,12},{9,13},{10,... | collective-permute-start | bytes 147464 | tf_op jit(solution)/shard_map/ppermute | solution.py:17
  58.7 5.9 %collective-permute-start.18 = (bf16[256,96]{0,1:T(8,128)(2,1)S(1)}, bf16[256,96]{0,1:T(8,128)(2,1)S(1)}, u32[]{:S(2)}, u32[]{:S(2)}) collective-permute-start(bf16[256,96]{0,1:T(8,128)(2,1)S(1)} %get-tuple-element.39), channel_id=1, source_target_pairs={{0,8},{1,9},{2,10},{3,11},{4,12},{5,13},{6,14},{7,15},{8,0},{9,1},... | collective-permute-start | bytes 147464 | tf_op jit(solution)/shard_map/ppermute | solution.py:17
  60.0 5.9 %collective-permute-start.19 = (bf16[256,96]{0,1:T(8,128)(2,1)S(1)}, bf16[256,96]{0,1:T(8,128)(2,1)S(1)}, u32[]{:S(2)}, u32[]{:S(2)}) collective-permute-start(bf16[256,96]{0,1:T(8,128)(2,1)S(1)} %get-tuple-element.39), channel_id=1, source_target_pairs={{0,12},{1,13},{2,14},{3,15},{4,8},{5,9},{6,10},{7,11},{8,4},{9,5},... | collective-permute-start | bytes 147464 | tf_op jit(solution)/shard_map/ppermute | solution.py:17
  66.0 1.5 %collective-permute-start.20 = (bf16[1024,96]{0,1:T(8,128)(2,1)S(1)}, bf16[1024,96]{0,1:T(8,128)(2,1)S(1)}, u32[]{:S(2)}, u32[]{:S(2)}) collective-permute-start(bf16[1024,96]{0,1:T(8,128)(2,1)S(1)} %get-tuple-element.95), channel_id=1, source_target_pairs={{0,1},{1,0},{2,3},{3,2},{4,5},{5,4},{6,7},{7,6},{8,9},{9,8},{10,11... | collective-permute-start | bytes 589832 | tf_op jit(solution)/shard_map/ppermute | solution.py:17
  69.1 7.0 %collective-permute-start.21 = (bf16[1024,96]{0,1:T(8,128)(2,1)S(1)}, bf16[1024,96]{0,1:T(8,128)(2,1)S(1)}, u32[]{:S(2)}, u32[]{:S(2)}) collective-permute-start(bf16[1024,96]{0,1:T(8,128)(2,1)S(1)} %reduce-precision_convert_fusion), channel_id=1, source_target_pairs={{0,16},{16,0},{1,17},{17,1},{2,18},{18,2},{3,19},{19,3},{4,20},{20... | collective-permute-start | bytes 589832 | tf_op jit(solution)/shard_map/ppermute | solution.py:144
  76.9 1.8 %collective-permute-start.22 = (f32[1024,96]{0,1:T(8,128)S(1)}, f32[1024,96]{0,1:T(8,128)S(1)}, u32[]{:S(2)}, u32[]{:S(2)}) collective-permute-start(f32[1024,96]{0,1:T(8,128)S(1)} %slice.275), channel_id=1, source_target_pairs={{0,1},{1,0},{2,3},{3,2},{4,5},{5,4},{6,7},{7,6},{8,9},{9,8},{10,11... | collective-permute-start | bytes 1179656 | tf_op jit(solution)/shard_map/ppermute | solution.py:17
  78.8 4.9 %collective-permute-start.23 = (bf16[512,96]{0,1:T(8,128)(2,1)S(1)}, bf16[512,96]{0,1:T(8,128)(2,1)S(1)}, u32[]{:S(2)}, u32[]{:S(2)}) collective-permute-start(bf16[512,96]{0,1:T(8,128)(2,1)S(1)} %slice.370), channel_id=1, source_target_pairs={{0,2},{1,3},{2,0},{3,1},{4,6},{5,7},{6,4},{7,5},{8,10},{9,11},{10,... | collective-permute-start | bytes 294920 | tf_op jit(solution)/shard_map/ppermute | solution.py:17
  83.7 10.5 %collective-permute-start.27 = (bf16[1024,96]{0,1:T(8,128)(2,1)S(1)}, bf16[1024,96]{0,1:T(8,128)(2,1)S(1)}, u32[]{:S(2)}, u32[]{:S(2)}) collective-permute-start(bf16[1024,96]{0,1:T(8,128)(2,1)S(1)} %get-tuple-element.26), channel_id=1, source_target_pairs={{0,16},{16,0},{1,17},{17,1},{2,18},{18,2},{3,19},{19,3},{4,20},{20... | collective-permute-start | bytes 589832 | tf_op jit(solution)/shard_map/ppermute | solution.py:148
  84.3 4.8 %collective-permute-start.24 = (bf16[512,96]{0,1:T(8,128)(2,1)S(1)}, bf16[512,96]{0,1:T(8,128)(2,1)S(1)}, u32[]{:S(2)}, u32[]{:S(2)}) collective-permute-start(bf16[512,96]{0,1:T(8,128)(2,1)S(1)} %fusion.21), channel_id=1, source_target_pairs={{0,4},{1,5},{2,6},{3,7},{4,0},{5,1},{6,2},{7,3},{8,12},{9,13},{10,... | collective-permute-start | bytes 294920 | tf_op jit(solution)/shard_map/ppermute | solution.py:17
  84.3 9.9 %collective-permute-start.25 = (bf16[512,96]{0,1:T(8,128)(2,1)S(1)}, bf16[512,96]{0,1:T(8,128)(2,1)S(1)}, u32[]{:S(2)}, u32[]{:S(2)}) collective-permute-start(bf16[512,96]{0,1:T(8,128)(2,1)S(1)} %fusion.21), channel_id=1, source_target_pairs={{0,8},{1,9},{2,10},{3,11},{4,12},{5,13},{6,14},{7,15},{8,0},{9,1},... | collective-permute-start | bytes 294920 | tf_op jit(solution)/shard_map/ppermute | solution.py:17
  86.4 7.9 %collective-permute-start.26 = (bf16[512,96]{0,1:T(8,128)(2,1)S(1)}, bf16[512,96]{0,1:T(8,128)(2,1)S(1)}, u32[]{:S(2)}, u32[]{:S(2)}) collective-permute-start(bf16[512,96]{0,1:T(8,128)(2,1)S(1)} %fusion.21), channel_id=1, source_target_pairs={{0,12},{1,13},{2,14},{3,15},{4,8},{5,9},{6,10},{7,11},{8,4},{9,5},... | collective-permute-start | bytes 294920 | tf_op jit(solution)/shard_map/ppermute | solution.py:17
  94.8 1.4 %collective-permute-start.28 = (f32[256,96]{0,1:T(8,128)S(1)}, f32[256,96]{0,1:T(8,128)S(1)}, u32[]{:S(2)}, u32[]{:S(2)}) collective-permute-start(f32[256,96]{0,1:T(8,128)S(1)} %slice.291), channel_id=1, source_target_pairs={{0,1},{1,0},{2,3},{3,2},{4,5},{5,4},{6,7},{7,6},{8,9},{9,8},{10,11... | collective-permute-start | bytes 294920 | tf_op jit(solution)/shard_map/ppermute | solution.py:17
  96.2 4.2 %collective-permute-start.29 = (bf16[256,96]{0,1:T(8,128)(2,1)S(1)}, bf16[256,96]{0,1:T(8,128)(2,1)S(1)}, u32[]{:S(2)}, u32[]{:S(2)}) collective-permute-start(bf16[256,96]{0,1:T(8,128)(2,1)S(1)} %pad_maximum_fusion.6), channel_id=1, source_target_pairs={{0,2},{1,3},{2,0},{3,1},{4,6},{5,7},{6,4},{7,5},{8,10},{9,11},{10,... | collective-permute-start | bytes 147464 | tf_op jit(solution)/shard_map/ppermute | solution.py:17
  100.4 19.5 %copy-start.2 = (f32[128,96]{0,1:T(8,128)S(1)}, f32[128,96]{0,1:T(8,128)}, u32[]{:S(2)}) copy-start(f32[128,96]{0,1:T(8,128)} %param.5) | copy-start | bytes 147460
  100.4 4.5 %collective-permute-start.30 = (bf16[256,96]{0,1:T(8,128)(2,1)S(1)}, bf16[256,96]{0,1:T(8,128)(2,1)S(1)}, u32[]{:S(2)}, u32[]{:S(2)}) collective-permute-start(bf16[256,96]{0,1:T(8,128)(2,1)S(1)} %get-tuple-element.33), channel_id=1, source_target_pairs={{0,4},{1,5},{2,6},{3,7},{4,0},{5,1},{6,2},{7,3},{8,12},{9,13},{10,... | collective-permute-start | bytes 147464 | tf_op jit(solution)/shard_map/ppermute | solution.py:17
  102.1 5.4 %collective-permute-start.31 = (bf16[256,96]{0,1:T(8,128)(2,1)S(1)}, bf16[256,96]{0,1:T(8,128)(2,1)S(1)}, u32[]{:S(2)}, u32[]{:S(2)}) collective-permute-start(bf16[256,96]{0,1:T(8,128)(2,1)S(1)} %get-tuple-element.33), channel_id=1, source_target_pairs={{0,8},{1,9},{2,10},{3,11},{4,12},{5,13},{6,14},{7,15},{8,0},{9,1},... | collective-permute-start | bytes 147464 | tf_op jit(solution)/shard_map/ppermute | solution.py:17
  102.8 5.9 %collective-permute-start.32 = (bf16[256,96]{0,1:T(8,128)(2,1)S(1)}, bf16[256,96]{0,1:T(8,128)(2,1)S(1)}, u32[]{:S(2)}, u32[]{:S(2)}) collective-permute-start(bf16[256,96]{0,1:T(8,128)(2,1)S(1)} %get-tuple-element.33), channel_id=1, source_target_pairs={{0,12},{1,13},{2,14},{3,15},{4,8},{5,9},{6,10},{7,11},{8,4},{9,5},... | collective-permute-start | bytes 147464 | tf_op jit(solution)/shard_map/ppermute | solution.py:17
  108.8 1.5 %collective-permute-start.33 = (bf16[1024,96]{0,1:T(8,128)(2,1)S(1)}, bf16[1024,96]{0,1:T(8,128)(2,1)S(1)}, u32[]{:S(2)}, u32[]{:S(2)}) collective-permute-start(bf16[1024,96]{0,1:T(8,128)(2,1)S(1)} %get-tuple-element.85), channel_id=1, source_target_pairs={{0,1},{1,0},{2,3},{3,2},{4,5},{5,4},{6,7},{7,6},{8,9},{9,8},{10,11... | collective-permute-start | bytes 589832 | tf_op jit(solution)/shard_map/ppermute | solution.py:17
  115.5 10.8 %all-to-all-start = ((f32[16,1,96]{2,1,0:T(1,128)}), f32[16,1,96]{2,1,0:T(1,128)S(1)}, u32[]{:S(2)}, u32[]{:S(2)}) async-start(f32[16,1,96]{2,1,0:T(1,128)} %broadcast_in_dim.23), calls=%async_computation | async-start | bytes 16384 | tf_op jit(solution)/shard_map/all_to_all | solution.py:151

commit v3 on v2

--- a/solution.py
+++ b/solution.py
@@ -83,29 +83,29 @@
     def over_bit(mine, bit):
         return jnp.concatenate([mine, swapped(mine, "rows", bit)], axis=0)
 
-    coeffs_low = coeffs.astype(LOW)
+    coeffs_low, *actives = tied(coeffs.astype(LOW), *[block == turn for turn in range(nfeat)])
     blocks = [picked(inverse, [z + q for q in quad], 1).astype(LOW) for z in near]
+    near_coeffs, features = tied(over_outer(coeffs_low), reordered(features, me, order, own))
+    all_coeffs = over_bit(over_bit(near_coeffs, 2), 1)
+
     inverse_low = jnp.concatenate(
         [blocks[0]] + [swapped(sent, "rows", z) for sent, z in zip(blocks[1:], near[1:])], axis=0
     )
-    all_coeffs = over_bit(over_bit(over_outer(coeffs_low), 2), 1)
-    features = reordered(features, me, order, own)
-    all_coeffs, inverse_low = tied(all_coeffs, inverse_low)
-
     fitted = jnp.dot(features, all_coeffs, preferred_element_type=WIDE)
-    bits = [1 << k for k in range((nfeat - 1).bit_length())]
-    for bit in bits[:-1]:
-        fitted = fitted + swapped(fitted, "feat", bit)
-    fit_high, rest = split(fitted)
     targets = (labels[:, None] == jnp.arange(classes, dtype=jnp.int32)[None, :]).astype(WIDE)
-    incoming = (targets - fitted) - swapped(fit_high, "feat", bits[-1]).astype(WIDE)
+    if nfeat == 2:
+        fit_high, fit_rest = split(fitted)
+        fit_high, inverse_low = tied(swapped(fit_high, "feat", 1), inverse_low)
+        incoming = (targets - fitted) - fit_high.astype(WIDE)
+    else:
+        for bit in [1 << k for k in range((nfeat - 1).bit_length())]:
+            fitted = fitted + swapped(fitted, "feat", bit)
+        incoming = targets - fitted
     incoming_low = incoming.astype(LOW)
-    sign = -1.0
-
-    def moved(rest):
-        return swapped(rest, "feat", bits[-1])
 
     contract = (((0,), (0,)), ((), ()))
+    along = [(i, (i + 1) % nfeat) for i in range(nfeat)]
+    rest = None
     kept = jnp.zeros_like(incoming)
     delta_kept = jnp.zeros_like(coeffs)
     for turn in range(nfeat):
@@ -113,11 +113,15 @@
         keep, send = halved(grad)
         grad = keep + swapped(send, "rows", 1)
         keep, send = halved(grad)
-        grad = keep + swapped(send.astype(LOW), "rows", 2).astype(WIDE)
-        grad_low, rest = tied(grad.astype(LOW), rest)
+        got = swapped(send.astype(LOW), "rows", 2)
+        grad = keep + got.astype(WIDE)
+        grad_low = grad.astype(LOW)
+        if turn > 0:
+            grad_low, rest = tied(grad_low, rest)
         parts = [swapped(grad_low, "rows", z) for z in near[1:]]
-        *parts, rest = tied(*parts, moved(rest))
-        incoming = incoming + sign * rest.astype(WIDE)
+        if turn > 0:
+            *parts, rest = tied(*parts, lax.ppermute(rest, "feat", along))
+            incoming = incoming + rest.astype(WIDE)
         for step, got in enumerate(parts, 1):
             got = got.astype(WIDE)
             grad = grad + jnp.concatenate(
@@ -135,17 +139,20 @@
         delta_low = jnp.concatenate([s[:own] for s in slots] + [s[own:] for s in slots], axis=0)
         delta_low = over_bit(delta_low, 1)
         outgoing = incoming - jnp.dot(features, delta_low, preferred_element_type=WIDE)
-        active = block == turn
-        kept = jnp.where(active, outgoing, kept)
+        active = actives[turn]
         delta_kept = jnp.where(active, delta[:own], delta_kept)
         if turn < nfeat - 1:
-            along = [(i, (i + 1) % nfeat) for i in range(nfeat)]
             high, rest = split(outgoing)
+            if nfeat == 2:
+                high = jnp.where(actives[0], high, fit_rest)
             incoming_low = lax.ppermute(high, "feat", along)
-            incoming, sign = incoming_low.astype(WIDE), 1.0
-
-            def moved(rest):
-                return lax.ppermute(rest, "feat", along)
+            incoming = incoming_low.astype(WIDE)
+            if nfeat == 2:
+                outgoing = outgoing - incoming
+                incoming = incoming - fit_rest.astype(WIDE)
+        else:
+            outgoing = lax.optimization_barrier(outgoing)
+        kept = jnp.where(active, outgoing, kept)
 
     squares = jnp.sum(kept * kept, axis=0, keepdims=True)
     squares = lax.all_to_all(

time: 127 us -> 122 us (0.961)
  waiting for transfers between devices: 61.8 us -> 56.8 us
  matrix products: 9.51 us -> 6.43 us
  starting transfers between devices: 45.6 us -> 47.3 us
    ppermute x32 -> x31, waiting for transfers between devices: 49.6 us -> 45.5 us  [swapped(): return lax.ppermute(shard, axis, [(i, i ^ bit) for i in range(peers)])]
    dot_general x2, matrix products: 5.95 us -> 2.91 us  [on_device(): jnp.dot(features, delta_low, preferred_element_type=WIDE)]
    ppermute x32 -> x31, starting transfers between devices: 40 us -> 40 us  [swapped(): return lax.ppermute(shard, axis, [(i, i ^ bit) for i in range(peers)])]
  transfers between devices with their start and end apart: 35 -> 34, of which waited for: 24 -> 23; matrix products, arithmetic and copies ran while one was open for 2% -> 3% of each run, Pallas kernels for 1% -> 1%
where the time goes in v3:
time: 122 us; the launch traced here: 121 us
  waiting for transfers between devices  56.8 us (47%)
  starting transfers between devices  47.3 us (39%)
  matrix products  6.43 us (5%)
  local copies, waits for them, and re-layouts  4.69 us (4%)
  other arithmetic  3.53 us (3%)
  Pallas kernels  1.33 us (1%)
    ppermute x31, waiting for transfers between devices, swapped(): return lax.ppermute(shard, axis, [(i, i ^ bit) for i in range(peers)])  45.5 us
    ppermute x31, starting transfers between devices, swapped(): return lax.ppermute(shard, axis, [(i, i ^ bit) for i in range(peers)])  40 us
    all_to_all x1, waiting for transfers between devices, on_device(): lax.all_to_all(jnp.broadcast_to(squares[None], (nrows, 1, classes)), 'row...  5.76 us
    ppermute x1, waiting for transfers between devices, on_device(): incoming_low = lax.ppermute(high, 'feat', along)  5.46 us
    all_to_all x1, starting transfers between devices, on_device(): lax.all_to_all(jnp.broadcast_to(squares[None], (nrows, 1, classes)), 'row...  4.15 us
    dot_general x2, matrix products, on_device(): jnp.dot(features, delta_low, preferred_element_type=WIDE)  2.91 us
    unnamed x28, local copies, waits for them, and re-layouts  2.47 us
  transfers between devices with their start and end apart: 34, of which 23 were waited for; matrix products, arithmetic and copies ran while one was open for 3% of the time, Pallas kernels for 1%

profile of v3, /device:TPU:0, one launch (start us, length us, event | category | flops | bytes accessed | tf_op | source)
XLA Modules:
  0.0 121.2 jit_solution(11960707528283168799)
XLA Ops:
  1.4 5.0 %collective-permute-start.2 = (bf16[128,96]{0,1:T(8,128)(2,1)S(1)}, bf16[128,96]{0,1:T(8,128)(2,1)S(1)}, u32[]{:S(2)}, u32[]{:S(2)}) collective-permute-start(bf16[128,96]{0,1:T(8,128)(2,1)S(1)} %convert_element_type.95), channel_id=1, source_target_pairs={{0,12},{1,13},{2,14},{3,15},{4,8},{5,9},{6,10},{7,11},{8,4},{9,5},... | collective-permute-start | bytes 73736 | tf_op jit(solution)/shard_map/ppermute | solution.py:17
  7.1 1.3 %dynamic-slice_convert_fusion.15 = (bf16[128,128]{1,0:T(8,128)(2,1)S(1)}, bf16[128,128]{1,0:T(8,128)(2,1)S(1)}, bf16[128,128]{1,0:T(8,128)(2,1)S(1)}, bf16[128,1...) fusion(f32[128,2048]{1,0:T(8,128)} %param.6, ...), kind=kLoop, calls=%fused_computation.115 | loop fusion | bytes 1048640 | tf_op jit(solution)/shard_map/convert.22
  8.4 2.2 %copy-done = bf16[1024,2048]{1,0:T(8,128)(2,1)S(1)} copy-done((bf16[1024,2048]{1,0:T(8,128)(2,1)S(1)}, bf16[1024,2048]{1,0:T(8,128)(2,1)}, u32[]{:S(2)}) %copy-start) | copy-done | bytes 4194328
  10.6 1.3 %shard_map.67 = bf16[1024,2048]{1,0:T(8,128)(2,1)S(1)} custom-call(s32[1]{0:T(128)} %bitcast.me_ref, bf16[1024,2048]{1,0:T(8,128)(2,1)S(1)} %copy-done), custom_call_target="tpu_custom_call" | custom-call | bytes 8388608 | tf_op jit(solution)/shard_map/pallas_call | solution.py:54
  12.0 1.8 %collective-permute-start.3 = (bf16[512,96]{0,1:T(8,128)(2,1)S(1)}, bf16[512,96]{0,1:T(8,128)(2,1)S(1)}, u32[]{:S(2)}, u32[]{:S(2)}) collective-permute-start(bf16[512,96]{0,1:T(8,128)(2,1)S(1)} %pad_maximum_fusion.5), channel_id=1, source_target_pairs={{0,2},{1,3},{2,0},{3,1},{4,6},{5,7},{6,4},{7,5},{8,10},{9,11},{10,... | collective-permute-start | bytes 294920 | tf_op jit(solution)/shard_map/ppermute | solution.py:17
  13.8 3.7 %collective-permute-start.8 = (bf16[128,512]{1,0:T(8,128)(2,1)S(1)}, bf16[128,512]{1,0:T(8,128)(2,1)S(1)}, u32[]{:S(2)}, u32[]{:S(2)}) collective-permute-start(bf16[128,512]{1,0:T(8,128)(2,1)S(1)} %pad_maximum_fusion.4), channel_id=1, source_target_pairs={{0,12},{1,13},{2,14},{3,15},{4,8},{5,9},{6,10},{7,11},{8,4},{9,5},... | collective-permute-start | bytes 393224 | tf_op jit(solution)/shard_map/ppermute | solution.py:17
  17.6 1.6 %collective-permute-start.7 = (bf16[128,512]{1,0:T(8,128)(2,1)S(1)}, bf16[128,512]{1,0:T(8,128)(2,1)S(1)}, u32[]{:S(2)}, u32[]{:S(2)}) collective-permute-start(bf16[128,512]{1,0:T(8,128)(2,1)S(1)} %pad_maximum_fusion.3), channel_id=1, source_target_pairs={{0,8},{1,9},{2,10},{3,11},{4,12},{5,13},{6,14},{7,15},{8,0},{9,1},... | collective-permute-start | bytes 393224 | tf_op jit(solution)/shard_map/ppermute | solution.py:17
  19.3 2.1 %collective-permute-start.6 = (bf16[128,512]{1,0:T(8,128)(2,1)S(1)}, bf16[128,512]{1,0:T(8,128)(2,1)S(1)}, u32[]{:S(2)}, u32[]{:S(2)}) collective-permute-start(bf16[128,512]{1,0:T(8,128)(2,1)S(1)} %pad_maximum_fusion.2), channel_id=1, source_target_pairs={{0,4},{1,5},{2,6},{3,7},{4,0},{5,1},{6,2},{7,3},{8,12},{9,13},{10,... | collective-permute-start | bytes 393224 | tf_op jit(solution)/shard_map/ppermute | solution.py:17
  21.4 1.4 %reduce-precision_convert_fusion.1 = (bf16[1024,96]{0,1:T(8,128)(2,1)S(1)}, f32[1024,96]{0,1:T(8,128)S(1)}) fusion(bf16[1024,2048]{1,0:T(8,128)(2,1)S(1)} %shard_map.67, bf16[1024,96]{0,1:T(8,128)(2,1)S(1)} %collective-permute-done.4, bf16[512,96]{0,1:T(8,128)(2,1)S(1)} %collective-permute-done.3, bf16[512,96]{0,1:T(8,128)(2,1)S(1)} %pad_maximum_fusion.5), kind=kOutput, calls=%fused_computation.4 | convolution fusion | flops 404029440 | bytes 5177344 | tf_op jit(solution)/shard_map/dot_general | solution.py:94
  22.8 1.6 %collective-permute-start.5 = (bf16[1024,96]{0,1:T(8,128)(2,1)S(1)}, bf16[1024,96]{0,1:T(8,128)(2,1)S(1)}, u32[]{:S(2)}, u32[]{:S(2)}) collective-permute-start(bf16[1024,96]{0,1:T(8,128)(2,1)S(1)} %get-tuple-element.95), channel_id=1, source_target_pairs={{0,16},{16,0},{1,17},{17,1},{2,18},{18,2},{3,19},{19,3},{4,20},{20... | collective-permute-start | bytes 589832 | tf_op jit(solution)/shard_map/ppermute | solution.py:17
  24.3 3.2 %collective-permute-done.7 = bf16[128,512]{1,0:T(8,128)(2,1)S(1)} collective-permute-done((bf16[128,512]{1,0:T(8,128)(2,1)S(1)}, bf16[128,512]{1,0:T(8,128)(2,1)S(1)}, u32[]{:S(2)}, u32[]{:S(2)}) %collective-permute-start.7) | collective-permute-done | bytes 131104 | tf_op jit(solution)/shard_map/ppermute | solution.py:17
  27.7 1.9 %collective-permute-done.5 = bf16[1024,96]{0,1:T(8,128)(2,1)S(1)} collective-permute-done((bf16[1024,96]{0,1:T(8,128)(2,1)S(1)}, bf16[1024,96]{0,1:T(8,128)(2,1)S(1)}, u32[]{:S(2)}, u32[]{:S(2)}) %collective-permute-start.5) | collective-permute-done | bytes 196640 | tf_op jit(solution)/shard_map/ppermute | solution.py:17
  30.5 1.7 %collective-permute-done.9 = f32[1024,96]{0,1:T(8,128)S(1)} collective-permute-done((f32[1024,96]{0,1:T(8,128)S(1)}, f32[1024,96]{0,1:T(8,128)S(1)}, u32[]{:S(2)}, u32[]{:S(2)}) %collective-permute-start.9) | collective-permute-done | bytes 393248 | tf_op jit(solution)/shard_map/ppermute | solution.py:17
  32.3 1.6 %collective-permute-start.10 = (bf16[512,96]{0,1:T(8,128)(2,1)S(1)}, bf16[512,96]{0,1:T(8,128)(2,1)S(1)}, u32[]{:S(2)}, u32[]{:S(2)}) collective-permute-start(bf16[512,96]{0,1:T(8,128)(2,1)S(1)} %slice.371), channel_id=1, source_target_pairs={{0,2},{1,3},{2,0},{3,1},{4,6},{5,7},{6,4},{7,5},{8,10},{9,11},{10,... | collective-permute-start | bytes 294920 | tf_op jit(solution)/shard_map/ppermute | solution.py:17
  33.9 3.3 %collective-permute-done.10 = bf16[512,96]{0,1:T(8,128)(2,1)S(1)} collective-permute-done((bf16[512,96]{0,1:T(8,128)(2,1)S(1)}, bf16[512,96]{0,1:T(8,128)(2,1)S(1)}, u32[]{:S(2)}, u32[]{:S(2)}) %collective-permute-start.10) | collective-permute-done | bytes 98336 | tf_op jit(solution)/shard_map/ppermute | solution.py:17
  37.6 2.4 %collective-permute-start.13 = (bf16[512,96]{0,1:T(8,128)(2,1)S(1)}, bf16[512,96]{0,1:T(8,128)(2,1)S(1)}, u32[]{:S(2)}, u32[]{:S(2)}) collective-permute-start(bf16[512,96]{0,1:T(8,128)(2,1)S(1)} %fusion.31), channel_id=1, source_target_pairs={{0,12},{1,13},{2,14},{3,15},{4,8},{5,9},{6,10},{7,11},{8,4},{9,5},... | collective-permute-start | bytes 294920 | tf_op jit(solution)/shard_map/ppermute | solution.py:17
  40.8 5.6 %collective-permute-done.12 = bf16[512,96]{0,1:T(8,128)(2,1)S(1)} collective-permute-done((bf16[512,96]{0,1:T(8,128)(2,1)S(1)}, bf16[512,96]{0,1:T(8,128)(2,1)S(1)}, u32[]{:S(2)}, u32[]{:S(2)}) %collective-permute-start.12) | collective-permute-done | bytes 98336 | tf_op jit(solution)/shard_map/ppermute | solution.py:17
  47.7 1.3 %collective-permute-done.14 = f32[256,96]{0,1:T(8,128)S(1)} collective-permute-done((f32[256,96]{0,1:T(8,128)S(1)}, f32[256,96]{0,1:T(8,128)S(1)}, u32[]{:S(2)}, u32[]{:S(2)}) %collective-permute-start.14) | collective-permute-done | bytes 98336 | tf_op jit(solution)/shard_map/ppermute | solution.py:17
  49.1 1.6 %collective-permute-start.15 = (bf16[256,96]{0,1:T(8,128)(2,1)S(1)}, bf16[256,96]{0,1:T(8,128)(2,1)S(1)}, u32[]{:S(2)}, u32[]{:S(2)}) collective-permute-start(bf16[256,96]{0,1:T(8,128)(2,1)S(1)} %pad_maximum_fusion.6), channel_id=1, source_target_pairs={{0,2},{1,3},{2,0},{3,1},{4,6},{5,7},{6,4},{7,5},{8,10},{9,11},{10,... | collective-permute-start | bytes 147464 | tf_op jit(solution)/shard_map/ppermute | solution.py:17
  50.6 2.6 %collective-permute-done.15 = bf16[256,96]{0,1:T(8,128)(2,1)S(1)} collective-permute-done((bf16[256,96]{0,1:T(8,128)(2,1)S(1)}, bf16[256,96]{0,1:T(8,128)(2,1)S(1)}, u32[]{:S(2)}, u32[]{:S(2)}) %collective-permute-start.15) | collective-permute-done | bytes 49184 | tf_op jit(solution)/shard_map/ppermute | solution.py:17
  53.2 1.7 %collective-permute-start.16 = (bf16[256,96]{0,1:T(8,128)(2,1)S(1)}, bf16[256,96]{0,1:T(8,128)(2,1)S(1)}, u32[]{:S(2)}, u32[]{:S(2)}) collective-permute-start(bf16[256,96]{0,1:T(8,128)(2,1)S(1)} %get-tuple-element.33), channel_id=1, source_target_pairs={{0,4},{1,5},{2,6},{3,7},{4,0},{5,1},{6,2},{7,3},{8,12},{9,13},{10,... | collective-permute-start | bytes 147464 | tf_op jit(solution)/shard_map/ppermute | solution.py:17
  55.0 2.7 %collective-permute-start.18 = (bf16[256,96]{0,1:T(8,128)(2,1)S(1)}, bf16[256,96]{0,1:T(8,128)(2,1)S(1)}, u32[]{:S(2)}, u32[]{:S(2)}) collective-permute-start(bf16[256,96]{0,1:T(8,128)(2,1)S(1)} %get-tuple-element.33), channel_id=1, source_target_pairs={{0,12},{1,13},{2,14},{3,15},{4,8},{5,9},{6,10},{7,11},{8,4},{9,5},... | collective-permute-start | bytes 147464 | tf_op jit(solution)/shard_map/ppermute | solution.py:17
  57.7 2.6 %collective-permute-done.17 = bf16[256,96]{0,1:T(8,128)(2,1)S(1)} collective-permute-done((bf16[256,96]{0,1:T(8,128)(2,1)S(1)}, bf16[256,96]{0,1:T(8,128)(2,1)S(1)}, u32[]{:S(2)}, u32[]{:S(2)}) %collective-permute-start.17) | collective-permute-done | bytes 49184 | tf_op jit(solution)/shard_map/ppermute | solution.py:17
  61.3 1.4 %collective-permute-done.19 = bf16[1024,96]{0,1:T(8,128)(2,1)S(1)} collective-permute-done((bf16[1024,96]{0,1:T(8,128)(2,1)S(1)}, bf16[1024,96]{0,1:T(8,128)(2,1)S(1)}, u32[]{:S(2)}, u32[]{:S(2)}) %collective-permute-start.19) | collective-permute-done | bytes 196640 | tf_op jit(solution)/shard_map/ppermute | solution.py:17
  62.7 1.5 %fusion.17 = (bf16[1024,96]{0,1:T(8,128)(2,1)S(1)}, f32[1024,96]{0,1:T(8,128)S(1)}) fusion(pred[]{:T(512)S(6)} %eq.19, f32[1024,96]{0,1:T(8,128)S(1)} %get-tuple-element.96, bf16[1024,2048]{1,0:T(8,128)(2,1)S(1)} %shard_map.67, bf16[2048,96]{0,1:T(8,128)(2,1)S(1)} %constant_dynamic-update-slice_fusion.8, bf16[1024,96]{0,1:T(8,128)(2,1)S(1)} %collective-permute-done.5, ...), kind=kOutput, calls=%fused_computation.33 | convolution fusion | flops 403832832 | bytes 5771265 | tf_op jit(solution)/shard_map/dot_general | solution.py:141
  64.1 1.6 %collective-permute-start.20 = (bf16[1024,96]{0,1:T(8,128)(2,1)S(1)}, bf16[1024,96]{0,1:T(8,128)(2,1)S(1)}, u32[]{:S(2)}, u32[]{:S(2)}) collective-permute-start(bf16[1024,96]{0,1:T(8,128)(2,1)S(1)} %get-tuple-element.97), channel_id=1, source_target_pairs={{0,16},{16,0},{1,17},{17,1},{2,18},{18,2},{3,19},{19,3},{4,20},{20... | collective-permute-start | bytes 589832 | tf_op jit(solution)/shard_map/ppermute | solution.py:148
  65.7 5.5 %collective-permute-done.20 = bf16[1024,96]{0,1:T(8,128)(2,1)S(1)} collective-permute-done((bf16[1024,96]{0,1:T(8,128)(2,1)S(1)}, bf16[1024,96]{0,1:T(8,128)(2,1)S(1)}, u32[]{:S(2)}, u32[]{:S(2)}) %collective-permute-start.20) | collective-permute-done | bytes 196640 | tf_op jit(solution)/shard_map/ppermute | solution.py:148
  72.1 1.7 %collective-permute-done.21 = f32[1024,96]{0,1:T(8,128)S(1)} collective-permute-done((f32[1024,96]{0,1:T(8,128)S(1)}, f32[1024,96]{0,1:T(8,128)S(1)}, u32[]{:S(2)}, u32[]{:S(2)}) %collective-permute-start.21) | collective-permute-done | bytes 393248 | tf_op jit(solution)/shard_map/ppermute | solution.py:17
  73.8 1.6 %collective-permute-start.22 = (bf16[512,96]{0,1:T(8,128)(2,1)S(1)}, bf16[512,96]{0,1:T(8,128)(2,1)S(1)}, u32[]{:S(2)}, u32[]{:S(2)}) collective-permute-start(bf16[512,96]{0,1:T(8,128)(2,1)S(1)} %slice.370), channel_id=1, source_target_pairs={{0,2},{1,3},{2,0},{3,1},{4,6},{5,7},{6,4},{7,5},{8,10},{9,11},{10,... | collective-permute-start | bytes 294920 | tf_op jit(solution)/shard_map/ppermute | solution.py:17
  75.5 3.3 %collective-permute-done.22 = bf16[512,96]{0,1:T(8,128)(2,1)S(1)} collective-permute-done((bf16[512,96]{0,1:T(8,128)(2,1)S(1)}, bf16[512,96]{0,1:T(8,128)(2,1)S(1)}, u32[]{:S(2)}, u32[]{:S(2)}) %collective-permute-start.22) | collective-permute-done | bytes 98336 | tf_op jit(solution)/shard_map/ppermute | solution.py:17
  78.8 1.6 %collective-permute-start.26 = (bf16[1024,96]{0,1:T(8,128)(2,1)S(1)}, bf16[1024,96]{0,1:T(8,128)(2,1)S(1)}, u32[]{:S(2)}, u32[]{:S(2)}) collective-permute-start(bf16[1024,96]{0,1:T(8,128)(2,1)S(1)} %fusion.5), channel_id=1, source_target_pairs={{0,16},{16,0},{1,17},{17,1},{2,18},{18,2},{3,19},{19,3},{4,20},{20... | collective-permute-start | bytes 589832 | tf_op jit(solution)/shard_map/ppermute | solution.py:123
  80.3 0.9 collective-permute-start.23
  81.2 2.2 %collective-permute-start.24 = (bf16[512,96]{0,1:T(8,128)(2,1)S(1)}, bf16[512,96]{0,1:T(8,128)(2,1)S(1)}, u32[]{:S(2)}, u32[]{:S(2)}) collective-permute-start(bf16[512,96]{0,1:T(8,128)(2,1)S(1)} %fusion.32), channel_id=1, source_target_pairs={{0,8},{1,9},{2,10},{3,11},{4,12},{5,13},{6,14},{7,15},{8,0},{9,1},... | collective-permute-start | bytes 294920 | tf_op jit(solution)/shard_map/ppermute | solution.py:17
  83.5 1.3 %collective-permute-start.25 = (bf16[512,96]{0,1:T(8,128)(2,1)S(1)}, bf16[512,96]{0,1:T(8,128)(2,1)S(1)}, u32[]{:S(2)}, u32[]{:S(2)}) collective-permute-start(bf16[512,96]{0,1:T(8,128)(2,1)S(1)} %fusion.32), channel_id=1, source_target_pairs={{0,12},{1,13},{2,14},{3,15},{4,8},{5,9},{6,10},{7,11},{8,4},{9,5},... | collective-permute-start | bytes 294920 | tf_op jit(solution)/shard_map/ppermute | solution.py:17
  85.6 5.3 %collective-permute-done.24 = bf16[512,96]{0,1:T(8,128)(2,1)S(1)} collective-permute-done((bf16[512,96]{0,1:T(8,128)(2,1)S(1)}, bf16[512,96]{0,1:T(8,128)(2,1)S(1)}, u32[]{:S(2)}, u32[]{:S(2)}) %collective-permute-start.24) | collective-permute-done | bytes 98336 | tf_op jit(solution)/shard_map/ppermute | solution.py:17
  91.4 1.3 %collective-permute-done.27 = f32[256,96]{0,1:T(8,128)S(1)} collective-permute-done((f32[256,96]{0,1:T(8,128)S(1)}, f32[256,96]{0,1:T(8,128)S(1)}, u32[]{:S(2)}, u32[]{:S(2)}) %collective-permute-start.27) | collective-permute-done | bytes 98336 | tf_op jit(solution)/shard_map/ppermute | solution.py:17
  92.7 1.6 %collective-permute-start.28 = (bf16[256,96]{0,1:T(8,128)(2,1)S(1)}, bf16[256,96]{0,1:T(8,128)(2,1)S(1)}, u32[]{:S(2)}, u32[]{:S(2)}) collective-permute-start(bf16[256,96]{0,1:T(8,128)(2,1)S(1)} %pad_maximum_fusion.7), channel_id=1, source_target_pairs={{0,2},{1,3},{2,0},{3,1},{4,6},{5,7},{6,4},{7,5},{8,10},{9,11},{10,... | collective-permute-start | bytes 147464 | tf_op jit(solution)/shard_map/ppermute | solution.py:17
  94.3 2.6 %collective-permute-done.28 = bf16[256,96]{0,1:T(8,128)(2,1)S(1)} collective-permute-done((bf16[256,96]{0,1:T(8,128)(2,1)S(1)}, bf16[256,96]{0,1:T(8,128)(2,1)S(1)}, u32[]{:S(2)}, u32[]{:S(2)}) %collective-permute-start.28) | collective-permute-done | bytes 49184 | tf_op jit(solution)/shard_map/ppermute | solution.py:17
  96.9 1.7 %collective-permute-start.29 = (bf16[256,96]{0,1:T(8,128)(2,1)S(1)}, bf16[256,96]{0,1:T(8,128)(2,1)S(1)}, u32[]{:S(2)}, u32[]{:S(2)}) collective-permute-start(bf16[256,96]{0,1:T(8,128)(2,1)S(1)} %get-tuple-element.29), channel_id=1, source_target_pairs={{0,4},{1,5},{2,6},{3,7},{4,0},{5,1},{6,2},{7,3},{8,12},{9,13},{10,... | collective-permute-start | bytes 147464 | tf_op jit(solution)/shard_map/ppermute | solution.py:17
  98.6 1.0 collective-permute-start.30
  99.6 1.8 %collective-permute-start.31 = (bf16[256,96]{0,1:T(8,128)(2,1)S(1)}, bf16[256,96]{0,1:T(8,128)(2,1)S(1)}, u32[]{:S(2)}, u32[]{:S(2)}) collective-permute-start(bf16[256,96]{0,1:T(8,128)(2,1)S(1)} %get-tuple-element.29), channel_id=1, source_target_pairs={{0,12},{1,13},{2,14},{3,15},{4,8},{5,9},{6,10},{7,11},{8,4},{9,5},... | collective-permute-start | bytes 147464 | tf_op jit(solution)/shard_map/ppermute | solution.py:17
  101.4 2.9 %collective-permute-done.30 = bf16[256,96]{0,1:T(8,128)(2,1)S(1)} collective-permute-done((bf16[256,96]{0,1:T(8,128)(2,1)S(1)}, bf16[256,96]{0,1:T(8,128)(2,1)S(1)}, u32[]{:S(2)}, u32[]{:S(2)}) %collective-permute-start.30) | collective-permute-done | bytes 49184 | tf_op jit(solution)/shard_map/ppermute | solution.py:17
  104.2 1.2 collective-permute-done.31
  105.7 1.4 %collective-permute-done.32 = bf16[1024,96]{0,1:T(8,128)(2,1)S(1)} collective-permute-done((bf16[1024,96]{0,1:T(8,128)(2,1)S(1)}, bf16[1024,96]{0,1:T(8,128)(2,1)S(1)}, u32[]{:S(2)}, u32[]{:S(2)}) %collective-permute-start.32) | collective-permute-done | bytes 196640 | tf_op jit(solution)/shard_map/ppermute | solution.py:17
  107.1 1.4 %fusion.1 = f32[1024,96]{0,1:T(8,128)S(1)} fusion(bf16[1024,96]{0,1:T(8,128)(2,1)S(1)} %collective-permute-done.20, bf16[1024,96]{0,1:T(8,128)(2,1)S(1)} %collective-permute-done.26, f32[1024,96]{0,1:T(8,128)S(1)} %get-tuple-element.96, bf16[1024,2048]{1,0:T(8,128)(2,1)S(1)} %shard_map.67, bf16[2048,96]{0,1:T(8,128)(2,1)S(1)} %constant_dynamic-update-slice_fusion.25), kind=kOutput, calls=%fused_computation.9 | convolution fusion | flops 403537920 | bytes 5767168 | tf_op jit(solution)/shard_map/dot_general | solution.py:141
  108.6 0.9 multiply_reduce_fusion
  110.1 4.1 %all-to-all-start = ((f32[16,1,96]{2,1,0:T(1,128)}), f32[16,1,96]{2,1,0:T(1,128)S(1)}, u32[]{:S(2)}, u32[]{:S(2)}) async-start(f32[16,1,96]{2,1,0:T(1,128)} %broadcast_in_dim.23), calls=%async_computation | async-start | bytes 16384 | tf_op jit(solution)/shard_map/all_to_all | solution.py:158
  114.9 5.8 %all-to-all-done = f32[16,1,96]{2,1,0:T(1,128)S(1)} async-done(((f32[16,1,96]{2,1,0:T(1,128)}), f32[16,1,96]{2,1,0:T(1,128)S(1)}, u32[]{:S(2)}, u32[]{:S(2)}) %all-to-all-start) | async-done | bytes 6176 | tf_op jit(solution)/shard_map/all_to_all | solution.py:158
  (102 shorter events, 10.8 us)
Async XLA Ops:
  1.4 10.5 %collective-permute-start.2 = (bf16[128,96]{0,1:T(8,128)(2,1)S(1)}, bf16[128,96]{0,1:T(8,128)(2,1)S(1)}, u32[]{:S(2)}, u32[]{:S(2)}) collective-permute-start(bf16[128,96]{0,1:T(8,128)(2,1)S(1)} %convert_element_type.95), channel_id=1, source_target_pairs={{0,12},{1,13},{2,14},{3,15},{4,8},{5,9},{6,10},{7,11},{8,4},{9,5},... | collective-permute-start | bytes 73736 | tf_op jit(solution)/shard_map/ppermute | solution.py:17
  6.5 5.5 %collective-permute-start.1 = (bf16[128,96]{0,1:T(8,128)(2,1)S(1)}, bf16[128,96]{0,1:T(8,128)(2,1)S(1)}, u32[]{:S(2)}, u32[]{:S(2)}) collective-permute-start(bf16[128,96]{0,1:T(8,128)(2,1)S(1)} %convert_element_type.95), channel_id=1, source_target_pairs={{0,8},{1,9},{2,10},{3,11},{4,12},{5,13},{6,14},{7,15},{8,0},{9,1},... | collective-permute-start | bytes 73736 | tf_op jit(solution)/shard_map/ppermute | solution.py:17
  6.5 5.5 %collective-permute-start = (bf16[128,96]{0,1:T(8,128)(2,1)S(1)}, bf16[128,96]{0,1:T(8,128)(2,1)S(1)}, u32[]{:S(2)}, u32[]{:S(2)}) collective-permute-start(bf16[128,96]{0,1:T(8,128)(2,1)S(1)} %convert_element_type.95), channel_id=1, source_target_pairs={{0,4},{1,5},{2,6},{3,7},{4,0},{5,1},{6,2},{7,3},{8,12},{9,13},{10,... | collective-permute-start | bytes 73736 | tf_op jit(solution)/shard_map/ppermute | solution.py:17
  8.4 2.2 %copy-start = (bf16[1024,2048]{1,0:T(8,128)(2,1)S(1)}, bf16[1024,2048]{1,0:T(8,128)(2,1)}, u32[]{:S(2)}) copy-start(bf16[1024,2048]{1,0:T(8,128)(2,1)} %given.1) | copy-start | bytes 12582916
  11.9 17.6 %copy-start.2 = (s32[1024]{0:T(1024)S(1)}, s32[1024]{0:T(1024)}, u32[]{:S(2)}) copy-start(s32[1024]{0:T(1024)} %param.7) | copy-start | bytes 12292
  12.0 5.5 %collective-permute-start.3 = (bf16[512,96]{0,1:T(8,128)(2,1)S(1)}, bf16[512,96]{0,1:T(8,128)(2,1)S(1)}, u32[]{:S(2)}, u32[]{:S(2)}) collective-permute-start(bf16[512,96]{0,1:T(8,128)(2,1)S(1)} %pad_maximum_fusion.5), channel_id=1, source_target_pairs={{0,2},{1,3},{2,0},{3,1},{4,6},{5,7},{6,4},{7,5},{8,10},{9,11},{10,... | collective-permute-start | bytes 294920 | tf_op jit(solution)/shard_map/ppermute | solution.py:17
  13.8 10.5 %collective-permute-start.8 = (bf16[128,512]{1,0:T(8,128)(2,1)S(1)}, bf16[128,512]{1,0:T(8,128)(2,1)S(1)}, u32[]{:S(2)}, u32[]{:S(2)}) collective-permute-start(bf16[128,512]{1,0:T(8,128)(2,1)S(1)} %pad_maximum_fusion.4), channel_id=1, source_target_pairs={{0,12},{1,13},{2,14},{3,15},{4,8},{5,9},{6,10},{7,11},{8,4},{9,5},... | collective-permute-start | bytes 393224 | tf_op jit(solution)/shard_map/ppermute | solution.py:17
  17.5 3.8 %collective-permute-start.4 = (bf16[1024,96]{0,1:T(8,128)(2,1)S(1)}, bf16[1024,96]{0,1:T(8,128)(2,1)S(1)}, u32[]{:S(2)}, u32[]{:S(2)}) collective-permute-start(bf16[1024,96]{0,1:T(8,128)(2,1)S(1)} %pad_maximum_fusion.1), channel_id=1, source_target_pairs={{0,1},{1,0},{2,3},{3,2},{4,5},{5,4},{6,7},{7,6},{8,9},{9,8},{10,11... | collective-permute-start | bytes 589832 | tf_op jit(solution)/shard_map/ppermute | solution.py:17
  17.6 9.9 %collective-permute-start.7 = (bf16[128,512]{1,0:T(8,128)(2,1)S(1)}, bf16[128,512]{1,0:T(8,128)(2,1)S(1)}, u32[]{:S(2)}, u32[]{:S(2)}) collective-permute-start(bf16[128,512]{1,0:T(8,128)(2,1)S(1)} %pad_maximum_fusion.3), channel_id=1, source_target_pairs={{0,8},{1,9},{2,10},{3,11},{4,12},{5,13},{6,14},{7,15},{8,0},{9,1},... | collective-permute-start | bytes 393224 | tf_op jit(solution)/shard_map/ppermute | solution.py:17
  19.3 8.4 %collective-permute-start.6 = (bf16[128,512]{1,0:T(8,128)(2,1)S(1)}, bf16[128,512]{1,0:T(8,128)(2,1)S(1)}, u32[]{:S(2)}, u32[]{:S(2)}) collective-permute-start(bf16[128,512]{1,0:T(8,128)(2,1)S(1)} %pad_maximum_fusion.2), channel_id=1, source_target_pairs={{0,4},{1,5},{2,6},{3,7},{4,0},{5,1},{6,2},{7,3},{8,12},{9,13},{10,... | collective-permute-start | bytes 393224 | tf_op jit(solution)/shard_map/ppermute | solution.py:17
  22.8 6.8 %collective-permute-start.5 = (bf16[1024,96]{0,1:T(8,128)(2,1)S(1)}, bf16[1024,96]{0,1:T(8,128)(2,1)S(1)}, u32[]{:S(2)}, u32[]{:S(2)}) collective-permute-start(bf16[1024,96]{0,1:T(8,128)(2,1)S(1)} %get-tuple-element.95), channel_id=1, source_target_pairs={{0,16},{16,0},{1,17},{17,1},{2,18},{18,2},{3,19},{19,3},{4,20},{20... | collective-permute-start | bytes 589832 | tf_op jit(solution)/shard_map/ppermute | solution.py:17
  30.4 1.8 %collective-permute-start.9 = (f32[1024,96]{0,1:T(8,128)S(1)}, f32[1024,96]{0,1:T(8,128)S(1)}, u32[]{:S(2)}, u32[]{:S(2)}) collective-permute-start(f32[1024,96]{0,1:T(8,128)S(1)} %slice.247), channel_id=1, source_target_pairs={{0,1},{1,0},{2,3},{3,2},{4,5},{5,4},{6,7},{7,6},{8,9},{9,8},{10,11... | collective-permute-start | bytes 1179656 | tf_op jit(solution)/shard_map/ppermute | solution.py:17
  32.3 4.9 %collective-permute-start.10 = (bf16[512,96]{0,1:T(8,128)(2,1)S(1)}, bf16[512,96]{0,1:T(8,128)(2,1)S(1)}, u32[]{:S(2)}, u32[]{:S(2)}) collective-permute-start(bf16[512,96]{0,1:T(8,128)(2,1)S(1)} %slice.371), channel_id=1, source_target_pairs={{0,2},{1,3},{2,0},{3,1},{4,6},{5,7},{6,4},{7,5},{8,10},{9,11},{10,... | collective-permute-start | bytes 294920 | tf_op jit(solution)/shard_map/ppermute | solution.py:17
  37.2 9.1 %collective-permute-start.12 = (bf16[512,96]{0,1:T(8,128)(2,1)S(1)}, bf16[512,96]{0,1:T(8,128)(2,1)S(1)}, u32[]{:S(2)}, u32[]{:S(2)}) collective-permute-start(bf16[512,96]{0,1:T(8,128)(2,1)S(1)} %fusion.31), channel_id=1, source_target_pairs={{0,8},{1,9},{2,10},{3,11},{4,12},{5,13},{6,14},{7,15},{8,0},{9,1},... | collective-permute-start | bytes 294920 | tf_op jit(solution)/shard_map/ppermute | solution.py:17
  37.6 8.8 %collective-permute-start.13 = (bf16[512,96]{0,1:T(8,128)(2,1)S(1)}, bf16[512,96]{0,1:T(8,128)(2,1)S(1)}, u32[]{:S(2)}, u32[]{:S(2)}) collective-permute-start(bf16[512,96]{0,1:T(8,128)(2,1)S(1)} %fusion.31), channel_id=1, source_target_pairs={{0,12},{1,13},{2,14},{3,15},{4,8},{5,9},{6,10},{7,11},{8,4},{9,5},... | collective-permute-start | bytes 294920 | tf_op jit(solution)/shard_map/ppermute | solution.py:17
  39.9 7.2 %collective-permute-start.11 = (bf16[512,96]{0,1:T(8,128)(2,1)S(1)}, bf16[512,96]{0,1:T(8,128)(2,1)S(1)}, u32[]{:S(2)}, u32[]{:S(2)}) collective-permute-start(bf16[512,96]{0,1:T(8,128)(2,1)S(1)} %fusion.31), channel_id=1, source_target_pairs={{0,4},{1,5},{2,6},{3,7},{4,0},{5,1},{6,2},{7,3},{8,12},{9,13},{10,... | collective-permute-start | bytes 294920 | tf_op jit(solution)/shard_map/ppermute | solution.py:17
  47.6 1.4 %collective-permute-start.14 = (f32[256,96]{0,1:T(8,128)S(1)}, f32[256,96]{0,1:T(8,128)S(1)}, u32[]{:S(2)}, u32[]{:S(2)}) collective-permute-start(f32[256,96]{0,1:T(8,128)S(1)} %slice.263), channel_id=1, source_target_pairs={{0,1},{1,0},{2,3},{3,2},{4,5},{5,4},{6,7},{7,6},{8,9},{9,8},{10,11... | collective-permute-start | bytes 294920 | tf_op jit(solution)/shard_map/ppermute | solution.py:17
  49.1 4.2 %collective-permute-start.15 = (bf16[256,96]{0,1:T(8,128)(2,1)S(1)}, bf16[256,96]{0,1:T(8,128)(2,1)S(1)}, u32[]{:S(2)}, u32[]{:S(2)}) collective-permute-start(bf16[256,96]{0,1:T(8,128)(2,1)S(1)} %pad_maximum_fusion.6), channel_id=1, source_target_pairs={{0,2},{1,3},{2,0},{3,1},{4,6},{5,7},{6,4},{7,5},{8,10},{9,11},{10,... | collective-permute-start | bytes 147464 | tf_op jit(solution)/shard_map/ppermute | solution.py:17
  53.2 4.5 %collective-permute-start.16 = (bf16[256,96]{0,1:T(8,128)(2,1)S(1)}, bf16[256,96]{0,1:T(8,128)(2,1)S(1)}, u32[]{:S(2)}, u32[]{:S(2)}) collective-permute-start(bf16[256,96]{0,1:T(8,128)(2,1)S(1)} %get-tuple-element.33), channel_id=1, source_target_pairs={{0,4},{1,5},{2,6},{3,7},{4,0},{5,1},{6,2},{7,3},{8,12},{9,13},{10,... | collective-permute-start | bytes 147464 | tf_op jit(solution)/shard_map/ppermute | solution.py:17
  55.0 5.3 %collective-permute-start.17 = (bf16[256,96]{0,1:T(8,128)(2,1)S(1)}, bf16[256,96]{0,1:T(8,128)(2,1)S(1)}, u32[]{:S(2)}, u32[]{:S(2)}) collective-permute-start(bf16[256,96]{0,1:T(8,128)(2,1)S(1)} %get-tuple-element.33), channel_id=1, source_target_pairs={{0,8},{1,9},{2,10},{3,11},{4,12},{5,13},{6,14},{7,15},{8,0},{9,1},... | collective-permute-start | bytes 147464 | tf_op jit(solution)/shard_map/ppermute | solution.py:17
  55.0 6.0 %collective-permute-start.18 = (bf16[256,96]{0,1:T(8,128)(2,1)S(1)}, bf16[256,96]{0,1:T(8,128)(2,1)S(1)}, u32[]{:S(2)}, u32[]{:S(2)}) collective-permute-start(bf16[256,96]{0,1:T(8,128)(2,1)S(1)} %get-tuple-element.33), channel_id=1, source_target_pairs={{0,12},{1,13},{2,14},{3,15},{4,8},{5,9},{6,10},{7,11},{8,4},{9,5},... | collective-permute-start | bytes 147464 | tf_op jit(solution)/shard_map/ppermute | solution.py:17
  61.1 1.5 %collective-permute-start.19 = (bf16[1024,96]{0,1:T(8,128)(2,1)S(1)}, bf16[1024,96]{0,1:T(8,128)(2,1)S(1)}, u32[]{:S(2)}, u32[]{:S(2)}) collective-permute-start(bf16[1024,96]{0,1:T(8,128)(2,1)S(1)} %get-tuple-element.85), channel_id=1, source_target_pairs={{0,1},{1,0},{2,3},{3,2},{4,5},{5,4},{6,7},{7,6},{8,9},{9,8},{10,11... | collective-permute-start | bytes 589832 | tf_op jit(solution)/shard_map/ppermute | solution.py:17
  64.1 7.0 %collective-permute-start.20 = (bf16[1024,96]{0,1:T(8,128)(2,1)S(1)}, bf16[1024,96]{0,1:T(8,128)(2,1)S(1)}, u32[]{:S(2)}, u32[]{:S(2)}) collective-permute-start(bf16[1024,96]{0,1:T(8,128)(2,1)S(1)} %get-tuple-element.97), channel_id=1, source_target_pairs={{0,16},{16,0},{1,17},{17,1},{2,18},{18,2},{3,19},{19,3},{4,20},{20... | collective-permute-start | bytes 589832 | tf_op jit(solution)/shard_map/ppermute | solution.py:148
  72.0 1.8 %collective-permute-start.21 = (f32[1024,96]{0,1:T(8,128)S(1)}, f32[1024,96]{0,1:T(8,128)S(1)}, u32[]{:S(2)}, u32[]{:S(2)}) collective-permute-start(f32[1024,96]{0,1:T(8,128)S(1)} %slice.275), channel_id=1, source_target_pairs={{0,1},{1,0},{2,3},{3,2},{4,5},{5,4},{6,7},{7,6},{8,9},{9,8},{10,11... | collective-permute-start | bytes 1179656 | tf_op jit(solution)/shard_map/ppermute | solution.py:17
  73.8 4.9 %collective-permute-start.22 = (bf16[512,96]{0,1:T(8,128)(2,1)S(1)}, bf16[512,96]{0,1:T(8,128)(2,1)S(1)}, u32[]{:S(2)}, u32[]{:S(2)}) collective-permute-start(bf16[512,96]{0,1:T(8,128)(2,1)S(1)} %slice.370), channel_id=1, source_target_pairs={{0,2},{1,3},{2,0},{3,1},{4,6},{5,7},{6,4},{7,5},{8,10},{9,11},{10,... | collective-permute-start | bytes 294920 | tf_op jit(solution)/shard_map/ppermute | solution.py:17
  78.8 12.1 %collective-permute-start.26 = (bf16[1024,96]{0,1:T(8,128)(2,1)S(1)}, bf16[1024,96]{0,1:T(8,128)(2,1)S(1)}, u32[]{:S(2)}, u32[]{:S(2)}) collective-permute-start(bf16[1024,96]{0,1:T(8,128)(2,1)S(1)} %fusion.5), channel_id=1, source_target_pairs={{0,16},{16,0},{1,17},{17,1},{2,18},{18,2},{3,19},{19,3},{4,20},{20... | collective-permute-start | bytes 589832 | tf_op jit(solution)/shard_map/ppermute | solution.py:123
  80.3 5.2 %collective-permute-start.23 = (bf16[512,96]{0,1:T(8,128)(2,1)S(1)}, bf16[512,96]{0,1:T(8,128)(2,1)S(1)}, u32[]{:S(2)}, u32[]{:S(2)}) collective-permute-start(bf16[512,96]{0,1:T(8,128)(2,1)S(1)} %fusion.32), channel_id=1, source_target_pairs={{0,4},{1,5},{2,6},{3,7},{4,0},{5,1},{6,2},{7,3},{8,12},{9,13},{10,... | collective-permute-start | bytes 294920 | tf_op jit(solution)/shard_map/ppermute | solution.py:17
  81.2 9.6 %collective-permute-start.24 = (bf16[512,96]{0,1:T(8,128)(2,1)S(1)}, bf16[512,96]{0,1:T(8,128)(2,1)S(1)}, u32[]{:S(2)}, u32[]{:S(2)}) collective-permute-start(bf16[512,96]{0,1:T(8,128)(2,1)S(1)} %fusion.32), channel_id=1, source_target_pairs={{0,8},{1,9},{2,10},{3,11},{4,12},{5,13},{6,14},{7,15},{8,0},{9,1},... | collective-permute-start | bytes 294920 | tf_op jit(solution)/shard_map/ppermute | solution.py:17
  83.5 7.4 %collective-permute-start.25 = (bf16[512,96]{0,1:T(8,128)(2,1)S(1)}, bf16[512,96]{0,1:T(8,128)(2,1)S(1)}, u32[]{:S(2)}, u32[]{:S(2)}) collective-permute-start(bf16[512,96]{0,1:T(8,128)(2,1)S(1)} %fusion.32), channel_id=1, source_target_pairs={{0,12},{1,13},{2,14},{3,15},{4,8},{5,9},{6,10},{7,11},{8,4},{9,5},... | collective-permute-start | bytes 294920 | tf_op jit(solution)/shard_map/ppermute | solution.py:17
  91.3 1.4 %collective-permute-start.27 = (f32[256,96]{0,1:T(8,128)S(1)}, f32[256,96]{0,1:T(8,128)S(1)}, u32[]{:S(2)}, u32[]{:S(2)}) collective-permute-start(f32[256,96]{0,1:T(8,128)S(1)} %slice.291), channel_id=1, source_target_pairs={{0,1},{1,0},{2,3},{3,2},{4,5},{5,4},{6,7},{7,6},{8,9},{9,8},{10,11... | collective-permute-start | bytes 294920 | tf_op jit(solution)/shard_map/ppermute | solution.py:17
  92.7 4.2 %collective-permute-start.28 = (bf16[256,96]{0,1:T(8,128)(2,1)S(1)}, bf16[256,96]{0,1:T(8,128)(2,1)S(1)}, u32[]{:S(2)}, u32[]{:S(2)}) collective-permute-start(bf16[256,96]{0,1:T(8,128)(2,1)S(1)} %pad_maximum_fusion.7), channel_id=1, source_target_pairs={{0,2},{1,3},{2,0},{3,1},{4,6},{5,7},{6,4},{7,5},{8,10},{9,11},{10,... | collective-permute-start | bytes 147464 | tf_op jit(solution)/shard_map/ppermute | solution.py:17
  96.9 4.5 %collective-permute-start.29 = (bf16[256,96]{0,1:T(8,128)(2,1)S(1)}, bf16[256,96]{0,1:T(8,128)(2,1)S(1)}, u32[]{:S(2)}, u32[]{:S(2)}) collective-permute-start(bf16[256,96]{0,1:T(8,128)(2,1)S(1)} %get-tuple-element.29), channel_id=1, source_target_pairs={{0,4},{1,5},{2,6},{3,7},{4,0},{5,1},{6,2},{7,3},{8,12},{9,13},{10,... | collective-permute-start | bytes 147464 | tf_op jit(solution)/shard_map/ppermute | solution.py:17
  98.6 5.6 %collective-permute-start.30 = (bf16[256,96]{0,1:T(8,128)(2,1)S(1)}, bf16[256,96]{0,1:T(8,128)(2,1)S(1)}, u32[]{:S(2)}, u32[]{:S(2)}) collective-permute-start(bf16[256,96]{0,1:T(8,128)(2,1)S(1)} %get-tuple-element.29), channel_id=1, source_target_pairs={{0,8},{1,9},{2,10},{3,11},{4,12},{5,13},{6,14},{7,15},{8,0},{9,1},... | collective-permute-start | bytes 147464 | tf_op jit(solution)/shard_map/ppermute | solution.py:17
  99.6 5.9 %collective-permute-start.31 = (bf16[256,96]{0,1:T(8,128)(2,1)S(1)}, bf16[256,96]{0,1:T(8,128)(2,1)S(1)}, u32[]{:S(2)}, u32[]{:S(2)}) collective-permute-start(bf16[256,96]{0,1:T(8,128)(2,1)S(1)} %get-tuple-element.29), channel_id=1, source_target_pairs={{0,12},{1,13},{2,14},{3,15},{4,8},{5,9},{6,10},{7,11},{8,4},{9,5},... | collective-permute-start | bytes 147464 | tf_op jit(solution)/shard_map/ppermute | solution.py:17
  105.6 1.5 %collective-permute-start.32 = (bf16[1024,96]{0,1:T(8,128)(2,1)S(1)}, bf16[1024,96]{0,1:T(8,128)(2,1)S(1)}, u32[]{:S(2)}, u32[]{:S(2)}) collective-permute-start(bf16[1024,96]{0,1:T(8,128)(2,1)S(1)} %get-tuple-element.75), channel_id=1, source_target_pairs={{0,1},{1,0},{2,3},{3,2},{4,5},{5,4},{6,7},{7,6},{8,9},{9,8},{10,11... | collective-permute-start | bytes 589832 | tf_op jit(solution)/shard_map/ppermute | solution.py:17
  107.1 7.2 %copy-start.1 = (f32[128,96]{0,1:T(8,128)S(1)}, f32[128,96]{0,1:T(8,128)}, u32[]{:S(2)}) copy-start(f32[128,96]{0,1:T(8,128)} %param.5) | copy-start | bytes 147460
  110.1 10.6 %all-to-all-start = ((f32[16,1,96]{2,1,0:T(1,128)}), f32[16,1,96]{2,1,0:T(1,128)S(1)}, u32[]{:S(2)}, u32[]{:S(2)}) async-start(f32[16,1,96]{2,1,0:T(1,128)} %broadcast_in_dim.23), calls=%async_computation | async-start | bytes 16384 | tf_op jit(solution)/shard_map/all_to_all | solution.py:158

commit v4 on v3

--- a/solution.py
+++ b/solution.py
@@ -31,16 +31,15 @@
     return whole[:half], whole[half:]
 
 
-def reorder_kernel(order, own, me_ref, given, taken, sems):
+def reorder_kernel(order, own, me_ref, given, near, far, sems):
     me = me_ref[0]
+    half = len(order) // 2
     copies = []
     for slot, code in enumerate(order):
         start = pl.multiple_of((me ^ code) * own, own)
-        copies.append(
-            pltpu.make_async_copy(
-                given.at[:, pl.ds(start, own)], taken.at[:, pl.ds(slot * own, own)], sems.at[slot]
-            )
-        )
+        place = pl.ds(slot % half * own, own)
+        taken = (near if slot < half else far).at[:, place]
+        copies.append(pltpu.make_async_copy(given.at[:, pl.ds(start, own)], taken, sems.at[slot]))
     for copy in copies:
         copy.start()
     for copy in copies:
@@ -48,14 +47,19 @@
 
 
 def reordered(features, me, order, own):
+    samples, width = features.shape
+    half = width // 2
     if own % 128:
-        parts = [lax.dynamic_slice_in_dim(features, (me ^ code) * own, own, 1) for code in order]
-        return jnp.concatenate(parts, axis=1)
+        column = jnp.arange(width)
+        source = (me ^ jnp.repeat(jnp.array(order), own)) * own + column % own
+        pick = (column[:, None] == source[None, :]).astype(LOW)
+        taken = jnp.dot(features, pick, preferred_element_type=WIDE).astype(LOW)
+        return taken[:, :half], taken[:, half:]
     return pl.pallas_call(
         functools.partial(reorder_kernel, order, own),
-        out_shape=jax.ShapeDtypeStruct(features.shape, features.dtype),
+        out_shape=[jax.ShapeDtypeStruct((samples, half), features.dtype)] * 2,
         in_specs=[pl.BlockSpec(memory_space=pltpu.SMEM), pl.BlockSpec(memory_space=pl.ANY)],
-        out_specs=pl.BlockSpec(memory_space=pl.ANY),
+        out_specs=[pl.BlockSpec(memory_space=pl.ANY)] * 2,
         scratch_shapes=[pltpu.SemaphoreType.DMA((len(order),))],
         compiler_params=pltpu.CompilerParams(vmem_limit_bytes=1 << 20),
         cost_estimate=pl.CostEstimate(flops=0, bytes_accessed=2 * features.size * 2, transcendentals=0),
@@ -85,13 +89,29 @@
 
     coeffs_low, *actives = tied(coeffs.astype(LOW), *[block == turn for turn in range(nfeat)])
     blocks = [picked(inverse, [z + q for q in quad], 1).astype(LOW) for z in near]
-    near_coeffs, features = tied(over_outer(coeffs_low), reordered(features, me, order, own))
-    all_coeffs = over_bit(over_bit(near_coeffs, 2), 1)
+    near_coeffs, keeping, sending = tied(over_outer(coeffs_low), *reordered(features, me, order, own))
+    near_coeffs = over_bit(near_coeffs, 2)
+
+    def product(rows):
+        far = swapped(rows, "rows", 1)
+        first, far = tied(jnp.dot(keeping, rows, preferred_element_type=WIDE), far)
+        return first + jnp.dot(sending, far, preferred_element_type=WIDE)
+
+
+    keeping, sending = reordered(features, me, order, own)
+    near_coeffs, keeping, *blocks = tied(over_outer(coeffs_low), keeping, *blocks)
+    near_coeffs = over_bit(near_coeffs, 2)
+
+    def product(rows):
+        far = swapped(rows, "rows", 1)
+        first, far = tied(jnp.dot(keeping, rows, preferred_element_type=WIDE), far)
+        return first + jnp.dot(sending, far, preferred_element_type=WIDE)
+
 
     inverse_low = jnp.concatenate(
         [blocks[0]] + [swapped(sent, "rows", z) for sent, z in zip(blocks[1:], near[1:])], axis=0
     )
-    fitted = jnp.dot(features, all_coeffs, preferred_element_type=WIDE)
+    fitted = product(near_coeffs)
     targets = (labels[:, None] == jnp.arange(classes, dtype=jnp.int32)[None, :]).astype(WIDE)
     if nfeat == 2:
         fit_high, fit_rest = split(fitted)
@@ -109,9 +129,10 @@
     kept = jnp.zeros_like(incoming)
     delta_kept = jnp.zeros_like(coeffs)
     for turn in range(nfeat):
-        grad = lax.dot_general(features, incoming_low, contract, preferred_element_type=WIDE)
-        keep, send = halved(grad)
-        grad = keep + swapped(send, "rows", 1)
+        send = lax.dot_general(sending, incoming_low, contract, preferred_element_type=WIDE)
+        grad = lax.dot_general(keeping, incoming_low, contract, preferred_element_type=WIDE)
+        grad, got = tied(grad, swapped(send, "rows", 1))
+        grad = grad + got
         keep, send = halved(grad)
         got = swapped(send.astype(LOW), "rows", 2)
         grad = keep + got.astype(WIDE)
@@ -137,8 +158,7 @@
         delta_low = delta.astype(LOW)
         slots = [delta_low] + [swapped(delta_low, "rows", z) for z in near[1:]]
         delta_low = jnp.concatenate([s[:own] for s in slots] + [s[own:] for s in slots], axis=0)
-        delta_low = over_bit(delta_low, 1)
-        outgoing = incoming - jnp.dot(features, delta_low, preferred_element_type=WIDE)
+        outgoing = incoming - product(delta_low)
         active = actives[turn]
         delta_kept = jnp.where(active, delta[:own], delta_kept)
         if turn < nfeat - 1:
@@ -150,10 +170,9 @@
             if nfeat == 2:
                 outgoing = outgoing - incoming
                 incoming = incoming - fit_rest.astype(WIDE)
-        else:
-            outgoing = lax.optimization_barrier(outgoing)
         kept = jnp.where(active, outgoing, kept)
 
+    kept = lax.optimization_barrier(kept)
     squares = jnp.sum(kept * kept, axis=0, keepdims=True)
     squares = lax.all_to_all(
         jnp.broadcast_to(squares[None], (nrows, 1, classes)), "rows", 0, 0, tiled=True

time: 122 us -> 117 us (0.959)
  starting transfers between devices: 47.3 us -> 40 us
  waiting for transfers between devices: 56.8 us -> 59.4 us
    ppermute x31, starting transfers between devices: 40 us -> 33.4 us  [swapped(): return lax.ppermute(shard, axis, [(i, i ^ bit) for i in range(peers)])]
    ppermute x31, waiting for transfers between devices: 45.5 us -> 48.3 us  [swapped(): return lax.ppermute(shard, axis, [(i, i ^ bit) for i in range(peers)])]
    dot_general x5 -> x10, matrix products: 5.91 us -> 6.53 us  [the longest x3 2.33 us: product(): first, far = tied(jnp.dot(keeping, rows, preferred_element_type=WIDE), far)]
    unnamed x28 -> x23, local copies, waits for them, and re-layouts: 2.47 us -> 2.36 us
  transfers between devices with their start and end apart: 34 -> 34, of which waited for: 23 -> 23; matrix products, arithmetic and copies ran while one was open for 3% -> 5% of each run, Pallas kernels for 1% -> 1%
where the time goes in v4:
time: 117 us
  waiting for transfers between devices  59.4 us (51%)
  starting transfers between devices  40 us (34%)
  matrix products  7.05 us (6%)
  local copies, waits for them, and re-layouts  4.51 us (4%)
  other arithmetic  3.13 us (3%)
  Pallas kernels  1.34 us (1%)
  between operations  1.18 us (1%)
    ppermute x31, waiting for transfers between devices, swapped(): return lax.ppermute(shard, axis, [(i, i ^ bit) for i in range(peers)])  48.3 us
    ppermute x31, starting transfers between devices, swapped(): return lax.ppermute(shard, axis, [(i, i ^ bit) for i in range(peers)])  33.4 us
    all_to_all x1, waiting for transfers between devices, on_device(): lax.all_to_all(jnp.broadcast_to(squares[None], (nrows, 1, classes)), 'row...  5.72 us
    ppermute x1, waiting for transfers between devices, on_device(): incoming_low = lax.ppermute(high, 'feat', along)  5.45 us
    all_to_all x1, starting transfers between devices, on_device(): lax.all_to_all(jnp.broadcast_to(squares[None], (nrows, 1, classes)), 'row...  3.43 us
    unnamed x23, local copies, waits for them, and re-layouts  2.36 us
  transfers between devices with their start and end apart: 34, of which 23 were waited for; matrix products, arithmetic and copies ran while one was open for 5% of the time, Pallas kernels for 1%

profile of v4, /device:TPU:0, one launch (start us, length us, event | category | flops | bytes accessed | tf_op | source)
XLA Modules:
  0.0 116.6 jit_solution(9394040417156538644)
XLA Ops:
  0.6 0.8 convert_element_type.95
  1.4 5.0 %collective-permute-start.2 = (bf16[128,96]{0,1:T(8,128)(2,1)S(1)}, bf16[128,96]{0,1:T(8,128)(2,1)S(1)}, u32[]{:S(2)}, u32[]{:S(2)}) collective-permute-start(bf16[128,96]{0,1:T(8,128)(2,1)S(1)} %convert_element_type.95), channel_id=1, source_target_pairs={{0,12},{1,13},{2,14},{3,15},{4,8},{5,9},{6,10},{7,11},{8,4},{9,5},... | collective-permute-start | bytes 73736 | tf_op jit(solution)/shard_map/ppermute | solution.py:17
  7.1 1.3 %dynamic-slice_convert_fusion.3 = (bf16[128,128]{1,0:T(8,128)(2,1)S(1)}, bf16[128,128]{1,0:T(8,128)(2,1)S(1)}, bf16[128,128]{1,0:T(8,128)(2,1)S(1)}, bf16[128,12...) fusion(f32[128,2048]{1,0:T(8,128)} %param.6, ...), kind=kLoop, calls=%fused_computation.59 | loop fusion | bytes 1048640 | tf_op jit(solution)/shard_map/convert.10
  8.5 2.2 %copy-done = bf16[1024,2048]{1,0:T(8,128)(2,1)S(1)} copy-done((bf16[1024,2048]{1,0:T(8,128)(2,1)S(1)}, bf16[1024,2048]{1,0:T(8,128)(2,1)}, u32[]{:S(2)}) %copy-start) | copy-done | bytes 4194328
  10.7 1.3 %shard_map.67 = (bf16[1024,1024]{1,0:T(8,128)(2,1)S(1)}, bf16[1024,1024]{1,0:T(8,128)(2,1)S(1)}) custom-call(s32[1]{0:T(128)} %bitcast.me_ref, bf16[1024,2048]{1,0:T(8,128)(2,1)S(1)} %copy-done), custom_call_target="tpu_custom_call" | custom-call | bytes 8388608 | tf_op jit(solution)/shard_map/pallas_call | solution.py:58
  12.1 1.8 %collective-permute-start.3 = (bf16[512,96]{0,1:T(8,128)(2,1)S(1)}, bf16[512,96]{0,1:T(8,128)(2,1)S(1)}, u32[]{:S(2)}, u32[]{:S(2)}) collective-permute-start(bf16[512,96]{0,1:T(8,128)(2,1)S(1)} %pad_maximum_fusion.5), channel_id=1, source_target_pairs={{0,2},{1,3},{2,0},{3,1},{4,6},{5,7},{6,4},{7,5},{8,10},{9,11},{10,... | collective-permute-start | bytes 294920 | tf_op jit(solution)/shard_map/ppermute | solution.py:17
  13.9 1.2 %collective-permute-start.6 = (bf16[128,512]{1,0:T(8,128)(2,1)S(1)}, bf16[128,512]{1,0:T(8,128)(2,1)S(1)}, u32[]{:S(2)}, u32[]{:S(2)}) collective-permute-start(bf16[128,512]{1,0:T(8,128)(2,1)S(1)} %get-tuple-element.41), channel_id=1, source_target_pairs={{0,4},{1,5},{2,6},{3,7},{4,0},{5,1},{6,2},{7,3},{8,12},{9,13},{10,... | collective-permute-start | bytes 393224 | tf_op jit(solution)/shard_map/ppermute | solution.py:17
  15.1 2.9 %collective-permute-start.7 = (bf16[128,512]{1,0:T(8,128)(2,1)S(1)}, bf16[128,512]{1,0:T(8,128)(2,1)S(1)}, u32[]{:S(2)}, u32[]{:S(2)}) collective-permute-start(bf16[128,512]{1,0:T(8,128)(2,1)S(1)} %get-tuple-element.42), channel_id=1, source_target_pairs={{0,8},{1,9},{2,10},{3,11},{4,12},{5,13},{6,14},{7,15},{8,0},{9,1},... | collective-permute-start | bytes 393224 | tf_op jit(solution)/shard_map/ppermute | solution.py:17
  18.4 0.8 fusion.42
  19.2 0.6 collective-permute-done.4
  19.8 0.8 fusion.43
  20.7 1.6 %collective-permute-start.5 = (bf16[1024,96]{0,1:T(8,128)(2,1)S(1)}, bf16[1024,96]{0,1:T(8,128)(2,1)S(1)}, u32[]{:S(2)}, u32[]{:S(2)}) collective-permute-start(bf16[1024,96]{0,1:T(8,128)(2,1)S(1)} %get-tuple-element.71), channel_id=1, source_target_pairs={{0,16},{16,0},{1,17},{17,1},{2,18},{18,2},{3,19},{19,3},{4,20},{20... | collective-permute-start | bytes 589832 | tf_op jit(solution)/shard_map/ppermute | solution.py:17
  22.2 5.0 %collective-permute-done.7 = bf16[128,512]{1,0:T(8,128)(2,1)S(1)} collective-permute-done((bf16[128,512]{1,0:T(8,128)(2,1)S(1)}, bf16[128,512]{1,0:T(8,128)(2,1)S(1)}, u32[]{:S(2)}, u32[]{:S(2)}) %collective-permute-start.7) | collective-permute-done | bytes 131104 | tf_op jit(solution)/shard_map/ppermute | solution.py:17
  28.8 1.2 %collective-permute-done.9 = f32[1024,96]{0,1:T(8,128)S(1)} collective-permute-done((f32[1024,96]{0,1:T(8,128)S(1)}, f32[1024,96]{0,1:T(8,128)S(1)}, u32[]{:S(2)}, u32[]{:S(2)}) %collective-permute-start.9) | collective-permute-done | bytes 393248 | tf_op jit(solution)/shard_map/ppermute | solution.py:17
  30.4 4.5 %collective-permute-done.10 = bf16[512,96]{0,1:T(8,128)(2,1)S(1)} collective-permute-done((bf16[512,96]{0,1:T(8,128)(2,1)S(1)}, bf16[512,96]{0,1:T(8,128)(2,1)S(1)}, u32[]{:S(2)}, u32[]{:S(2)}) %collective-permute-start.10) | collective-permute-done | bytes 98336 | tf_op jit(solution)/shard_map/ppermute | solution.py:17
  35.0 2.5 %collective-permute-start.12 = (bf16[512,96]{0,1:T(8,128)(2,1)S(1)}, bf16[512,96]{0,1:T(8,128)(2,1)S(1)}, u32[]{:S(2)}, u32[]{:S(2)}) collective-permute-start(bf16[512,96]{0,1:T(8,128)(2,1)S(1)} %fusion.22), channel_id=1, source_target_pairs={{0,8},{1,9},{2,10},{3,11},{4,12},{5,13},{6,14},{7,15},{8,0},{9,1},... | collective-permute-start | bytes 294920 | tf_op jit(solution)/shard_map/ppermute | solution.py:17
  37.6 1.4 %collective-permute-start.13 = (bf16[512,96]{0,1:T(8,128)(2,1)S(1)}, bf16[512,96]{0,1:T(8,128)(2,1)S(1)}, u32[]{:S(2)}, u32[]{:S(2)}) collective-permute-start(bf16[512,96]{0,1:T(8,128)(2,1)S(1)} %fusion.22), channel_id=1, source_target_pairs={{0,12},{1,13},{2,14},{3,15},{4,8},{5,9},{6,10},{7,11},{8,4},{9,5},... | collective-permute-start | bytes 294920 | tf_op jit(solution)/shard_map/ppermute | solution.py:17
  39.2 5.7 %collective-permute-done.12 = bf16[512,96]{0,1:T(8,128)(2,1)S(1)} collective-permute-done((bf16[512,96]{0,1:T(8,128)(2,1)S(1)}, bf16[512,96]{0,1:T(8,128)(2,1)S(1)}, u32[]{:S(2)}, u32[]{:S(2)}) %collective-permute-start.12) | collective-permute-done | bytes 98336 | tf_op jit(solution)/shard_map/ppermute | solution.py:17
  45.9 1.3 %collective-permute-done.14 = f32[256,96]{0,1:T(8,128)S(1)} collective-permute-done((f32[256,96]{0,1:T(8,128)S(1)}, f32[256,96]{0,1:T(8,128)S(1)}, u32[]{:S(2)}, u32[]{:S(2)}) %collective-permute-start.14) | collective-permute-done | bytes 98336 | tf_op jit(solution)/shard_map/ppermute | solution.py:17
  47.8 3.6 %collective-permute-done.15 = bf16[256,96]{0,1:T(8,128)(2,1)S(1)} collective-permute-done((bf16[256,96]{0,1:T(8,128)(2,1)S(1)}, bf16[256,96]{0,1:T(8,128)(2,1)S(1)}, u32[]{:S(2)}, u32[]{:S(2)}) %collective-permute-start.15) | collective-permute-done | bytes 49184 | tf_op jit(solution)/shard_map/ppermute | solution.py:17
  51.4 3.3 %collective-permute-start.18 = (bf16[256,96]{0,1:T(8,128)(2,1)S(1)}, bf16[256,96]{0,1:T(8,128)(2,1)S(1)}, u32[]{:S(2)}, u32[]{:S(2)}) collective-permute-start(bf16[256,96]{0,1:T(8,128)(2,1)S(1)} %get-tuple-element.67), channel_id=1, source_target_pairs={{0,12},{1,13},{2,14},{3,15},{4,8},{5,9},{6,10},{7,11},{8,4},{9,5},... | collective-permute-start | bytes 147464 | tf_op jit(solution)/shard_map/ppermute | solution.py:17
  55.0 0.9 collective-permute-start.16
  55.9 3.2 %collective-permute-done.16 = bf16[256,96]{0,1:T(8,128)(2,1)S(1)} collective-permute-done((bf16[256,96]{0,1:T(8,128)(2,1)S(1)}, bf16[256,96]{0,1:T(8,128)(2,1)S(1)}, u32[]{:S(2)}, u32[]{:S(2)}) %collective-permute-start.16) | collective-permute-done | bytes 49184 | tf_op jit(solution)/shard_map/ppermute | solution.py:17
  59.1 1.1 collective-permute-done.17
  60.4 0.8 fusion.44
  61.2 0.6 collective-permute-done.19
  61.8 0.8 fusion.45
  62.8 1.6 %collective-permute-start.20 = (bf16[1024,96]{0,1:T(8,128)(2,1)S(1)}, bf16[1024,96]{0,1:T(8,128)(2,1)S(1)}, u32[]{:S(2)}, u32[]{:S(2)}) collective-permute-start(bf16[1024,96]{0,1:T(8,128)(2,1)S(1)} %fusion.9), channel_id=1, source_target_pairs={{0,16},{16,0},{1,17},{17,1},{2,18},{18,2},{3,19},{19,3},{4,20},{20... | collective-permute-start | bytes 589832 | tf_op jit(solution)/shard_map/ppermute | solution.py:168
  64.4 5.5 %collective-permute-done.20 = bf16[1024,96]{0,1:T(8,128)(2,1)S(1)} collective-permute-done((bf16[1024,96]{0,1:T(8,128)(2,1)S(1)}, bf16[1024,96]{0,1:T(8,128)(2,1)S(1)}, u32[]{:S(2)}, u32[]{:S(2)}) %collective-permute-start.20) | collective-permute-done | bytes 196640 | tf_op jit(solution)/shard_map/ppermute | solution.py:168
  70.9 1.2 %collective-permute-done.21 = f32[1024,96]{0,1:T(8,128)S(1)} collective-permute-done((f32[1024,96]{0,1:T(8,128)S(1)}, f32[1024,96]{0,1:T(8,128)S(1)}, u32[]{:S(2)}, u32[]{:S(2)}) %collective-permute-start.21) | collective-permute-done | bytes 393248 | tf_op jit(solution)/shard_map/ppermute | solution.py:17
  72.7 4.3 %collective-permute-done.22 = bf16[512,96]{0,1:T(8,128)(2,1)S(1)} collective-permute-done((bf16[512,96]{0,1:T(8,128)(2,1)S(1)}, bf16[512,96]{0,1:T(8,128)(2,1)S(1)}, u32[]{:S(2)}, u32[]{:S(2)}) %collective-permute-start.22) | collective-permute-done | bytes 98336 | tf_op jit(solution)/shard_map/ppermute | solution.py:17
  77.1 1.6 %collective-permute-start.26 = (bf16[1024,96]{0,1:T(8,128)(2,1)S(1)}, bf16[1024,96]{0,1:T(8,128)(2,1)S(1)}, u32[]{:S(2)}, u32[]{:S(2)}) collective-permute-start(bf16[1024,96]{0,1:T(8,128)(2,1)S(1)} %get-tuple-element.54), channel_id=1, source_target_pairs={{0,16},{16,0},{1,17},{17,1},{2,18},{18,2},{3,19},{19,3},{4,20},{20... | collective-permute-start | bytes 589832 | tf_op jit(solution)/shard_map/ppermute | solution.py:144
  78.7 1.9 %collective-permute-start.25 = (bf16[512,96]{0,1:T(8,128)(2,1)S(1)}, bf16[512,96]{0,1:T(8,128)(2,1)S(1)}, u32[]{:S(2)}, u32[]{:S(2)}) collective-permute-start(bf16[512,96]{0,1:T(8,128)(2,1)S(1)} %fusion.23), channel_id=1, source_target_pairs={{0,12},{1,13},{2,14},{3,15},{4,8},{5,9},{6,10},{7,11},{8,4},{9,5},... | collective-permute-start | bytes 294920 | tf_op jit(solution)/shard_map/ppermute | solution.py:17
  80.6 2.4 %collective-permute-start.23 = (bf16[512,96]{0,1:T(8,128)(2,1)S(1)}, bf16[512,96]{0,1:T(8,128)(2,1)S(1)}, u32[]{:S(2)}, u32[]{:S(2)}) collective-permute-start(bf16[512,96]{0,1:T(8,128)(2,1)S(1)} %fusion.23), channel_id=1, source_target_pairs={{0,4},{1,5},{2,6},{3,7},{4,0},{5,1},{6,2},{7,3},{8,12},{9,13},{10,... | collective-permute-start | bytes 294920 | tf_op jit(solution)/shard_map/ppermute | solution.py:17
  83.0 3.1 %collective-permute-done.25 = bf16[512,96]{0,1:T(8,128)(2,1)S(1)} collective-permute-done((bf16[512,96]{0,1:T(8,128)(2,1)S(1)}, bf16[512,96]{0,1:T(8,128)(2,1)S(1)}, u32[]{:S(2)}, u32[]{:S(2)}) %collective-permute-start.25) | collective-permute-done | bytes 98336 | tf_op jit(solution)/shard_map/ppermute | solution.py:17
  86.2 3.2 %collective-permute-done.24 = bf16[512,96]{0,1:T(8,128)(2,1)S(1)} collective-permute-done((bf16[512,96]{0,1:T(8,128)(2,1)S(1)}, bf16[512,96]{0,1:T(8,128)(2,1)S(1)}, u32[]{:S(2)}, u32[]{:S(2)}) %collective-permute-start.24) | collective-permute-done | bytes 98336 | tf_op jit(solution)/shard_map/ppermute | solution.py:17
  89.9 1.3 %collective-permute-done.27 = f32[256,96]{0,1:T(8,128)S(1)} collective-permute-done((f32[256,96]{0,1:T(8,128)S(1)}, f32[256,96]{0,1:T(8,128)S(1)}, u32[]{:S(2)}, u32[]{:S(2)}) %collective-permute-start.27) | collective-permute-done | bytes 98336 | tf_op jit(solution)/shard_map/ppermute | solution.py:17
  91.8 3.6 %collective-permute-done.28 = bf16[256,96]{0,1:T(8,128)(2,1)S(1)} collective-permute-done((bf16[256,96]{0,1:T(8,128)(2,1)S(1)}, bf16[256,96]{0,1:T(8,128)(2,1)S(1)}, u32[]{:S(2)}, u32[]{:S(2)}) %collective-permute-start.28) | collective-permute-done | bytes 49184 | tf_op jit(solution)/shard_map/ppermute | solution.py:17
  95.4 2.1 %collective-permute-start.31 = (bf16[256,96]{0,1:T(8,128)(2,1)S(1)}, bf16[256,96]{0,1:T(8,128)(2,1)S(1)}, u32[]{:S(2)}, u32[]{:S(2)}) collective-permute-start(bf16[256,96]{0,1:T(8,128)(2,1)S(1)} %get-tuple-element.61), channel_id=1, source_target_pairs={{0,12},{1,13},{2,14},{3,15},{4,8},{5,9},{6,10},{7,11},{8,4},{9,5},... | collective-permute-start | bytes 147464 | tf_op jit(solution)/shard_map/ppermute | solution.py:17
  97.5 2.4 %collective-permute-start.29 = (bf16[256,96]{0,1:T(8,128)(2,1)S(1)}, bf16[256,96]{0,1:T(8,128)(2,1)S(1)}, u32[]{:S(2)}, u32[]{:S(2)}) collective-permute-start(bf16[256,96]{0,1:T(8,128)(2,1)S(1)} %get-tuple-element.61), channel_id=1, source_target_pairs={{0,4},{1,5},{2,6},{3,7},{4,0},{5,1},{6,2},{7,3},{8,12},{9,13},{10,... | collective-permute-start | bytes 147464 | tf_op jit(solution)/shard_map/ppermute | solution.py:17
  99.9 2.3 %collective-permute-done.29 = bf16[256,96]{0,1:T(8,128)(2,1)S(1)} collective-permute-done((bf16[256,96]{0,1:T(8,128)(2,1)S(1)}, bf16[256,96]{0,1:T(8,128)(2,1)S(1)}, u32[]{:S(2)}, u32[]{:S(2)}) %collective-permute-start.29) | collective-permute-done | bytes 49184 | tf_op jit(solution)/shard_map/ppermute | solution.py:17
  102.2 0.8 collective-permute-done.30
  103.2 0.8 fusion.46
  104.0 0.6 collective-permute-done.32
  104.6 0.8 fusion.47
  106.3 3.4 %all-to-all-start = ((f32[16,1,96]{2,1,0:T(1,128)}), f32[16,1,96]{2,1,0:T(1,128)S(1)}, u32[]{:S(2)}, u32[]{:S(2)}) async-start(f32[16,1,96]{2,1,0:T(1,128)} %broadcast_in_dim.23), calls=%async_computation | async-start | bytes 16384 | tf_op jit(solution)/shard_map/all_to_all | solution.py:177
  109.8 0.6 fusion.25
  110.4 5.7 %all-to-all-done = f32[16,1,96]{2,1,0:T(1,128)S(1)} async-done(((f32[16,1,96]{2,1,0:T(1,128)}), f32[16,1,96]{2,1,0:T(1,128)S(1)}, u32[]{:S(2)}, u32[]{:S(2)}) %all-to-all-start) | async-done | bytes 6176 | tf_op jit(solution)/shard_map/all_to_all | solution.py:177
  (102 shorter events, 9.9 us)
Async XLA Ops:
  1.4 10.6 %collective-permute-start.2 = (bf16[128,96]{0,1:T(8,128)(2,1)S(1)}, bf16[128,96]{0,1:T(8,128)(2,1)S(1)}, u32[]{:S(2)}, u32[]{:S(2)}) collective-permute-start(bf16[128,96]{0,1:T(8,128)(2,1)S(1)} %convert_element_type.95), channel_id=1, source_target_pairs={{0,12},{1,13},{2,14},{3,15},{4,8},{5,9},{6,10},{7,11},{8,4},{9,5},... | collective-permute-start | bytes 73736 | tf_op jit(solution)/shard_map/ppermute | solution.py:17
  6.5 5.6 %collective-permute-start.1 = (bf16[128,96]{0,1:T(8,128)(2,1)S(1)}, bf16[128,96]{0,1:T(8,128)(2,1)S(1)}, u32[]{:S(2)}, u32[]{:S(2)}) collective-permute-start(bf16[128,96]{0,1:T(8,128)(2,1)S(1)} %convert_element_type.95), channel_id=1, source_target_pairs={{0,8},{1,9},{2,10},{3,11},{4,12},{5,13},{6,14},{7,15},{8,0},{9,1},... | collective-permute-start | bytes 73736 | tf_op jit(solution)/shard_map/ppermute | solution.py:17
  6.5 5.6 %collective-permute-start = (bf16[128,96]{0,1:T(8,128)(2,1)S(1)}, bf16[128,96]{0,1:T(8,128)(2,1)S(1)}, u32[]{:S(2)}, u32[]{:S(2)}) collective-permute-start(bf16[128,96]{0,1:T(8,128)(2,1)S(1)} %convert_element_type.95), channel_id=1, source_target_pairs={{0,4},{1,5},{2,6},{3,7},{4,0},{5,1},{6,2},{7,3},{8,12},{9,13},{10,... | collective-permute-start | bytes 73736 | tf_op jit(solution)/shard_map/ppermute | solution.py:17
  8.5 2.2 %copy-start = (bf16[1024,2048]{1,0:T(8,128)(2,1)S(1)}, bf16[1024,2048]{1,0:T(8,128)(2,1)}, u32[]{:S(2)}) copy-start(bf16[1024,2048]{1,0:T(8,128)(2,1)} %given.1) | copy-start | bytes 12582916
  12.1 6.2 %collective-permute-start.3 = (bf16[512,96]{0,1:T(8,128)(2,1)S(1)}, bf16[512,96]{0,1:T(8,128)(2,1)S(1)}, u32[]{:S(2)}, u32[]{:S(2)}) collective-permute-start(bf16[512,96]{0,1:T(8,128)(2,1)S(1)} %pad_maximum_fusion.5), channel_id=1, source_target_pairs={{0,2},{1,3},{2,0},{3,1},{4,6},{5,7},{6,4},{7,5},{8,10},{9,11},{10,... | collective-permute-start | bytes 294920 | tf_op jit(solution)/shard_map/ppermute | solution.py:17
  13.9 8.3 %collective-permute-start.6 = (bf16[128,512]{1,0:T(8,128)(2,1)S(1)}, bf16[128,512]{1,0:T(8,128)(2,1)S(1)}, u32[]{:S(2)}, u32[]{:S(2)}) collective-permute-start(bf16[128,512]{1,0:T(8,128)(2,1)S(1)} %get-tuple-element.41), channel_id=1, source_target_pairs={{0,4},{1,5},{2,6},{3,7},{4,0},{5,1},{6,2},{7,3},{8,12},{9,13},{10,... | collective-permute-start | bytes 393224 | tf_op jit(solution)/shard_map/ppermute | solution.py:17
  15.1 12.0 %collective-permute-start.7 = (bf16[128,512]{1,0:T(8,128)(2,1)S(1)}, bf16[128,512]{1,0:T(8,128)(2,1)S(1)}, u32[]{:S(2)}, u32[]{:S(2)}) collective-permute-start(bf16[128,512]{1,0:T(8,128)(2,1)S(1)} %get-tuple-element.42), channel_id=1, source_target_pairs={{0,8},{1,9},{2,10},{3,11},{4,12},{5,13},{6,14},{7,15},{8,0},{9,1},... | collective-permute-start | bytes 393224 | tf_op jit(solution)/shard_map/ppermute | solution.py:17
  18.1 9.1 %collective-permute-start.8 = (bf16[128,512]{1,0:T(8,128)(2,1)S(1)}, bf16[128,512]{1,0:T(8,128)(2,1)S(1)}, u32[]{:S(2)}, u32[]{:S(2)}) collective-permute-start(bf16[128,512]{1,0:T(8,128)(2,1)S(1)} %get-tuple-element.43), channel_id=1, source_target_pairs={{0,12},{1,13},{2,14},{3,15},{4,8},{5,9},{6,10},{7,11},{8,4},{9,5},... | collective-permute-start | bytes 393224 | tf_op jit(solution)/shard_map/ppermute | solution.py:17
  18.3 1.5 %collective-permute-start.4 = (bf16[1024,96]{0,1:T(8,128)(2,1)S(1)}, bf16[1024,96]{0,1:T(8,128)(2,1)S(1)}, u32[]{:S(2)}, u32[]{:S(2)}) collective-permute-start(bf16[1024,96]{0,1:T(8,128)(2,1)S(1)} %constant_dynamic-update-slice_fusion), channel_id=1, source_target_pairs={{0,1},{1,0},{2,3},{3,2},{4,5},{5,4},{6,7},{7,6},{8,9},{9,8},{10,11... | collective-permute-start | bytes 589832 | tf_op jit(solution)/shard_map/ppermute | solution.py:17
  19.8 7.9 %copy-start.3 = (s32[1024]{0:T(1024)S(1)}, s32[1024]{0:T(1024)}, u32[]{:S(2)}) copy-start(s32[1024]{0:T(1024)} %param.7) | copy-start | bytes 12292
  20.7 7.0 %collective-permute-start.5 = (bf16[1024,96]{0,1:T(8,128)(2,1)S(1)}, bf16[1024,96]{0,1:T(8,128)(2,1)S(1)}, u32[]{:S(2)}, u32[]{:S(2)}) collective-permute-start(bf16[1024,96]{0,1:T(8,128)(2,1)S(1)} %get-tuple-element.71), channel_id=1, source_target_pairs={{0,16},{16,0},{1,17},{17,1},{2,18},{18,2},{3,19},{19,3},{4,20},{20... | collective-permute-start | bytes 589832 | tf_op jit(solution)/shard_map/ppermute | solution.py:17
  28.2 1.8 %collective-permute-start.9 = (f32[1024,96]{0,1:T(8,128)S(1)}, f32[1024,96]{0,1:T(8,128)S(1)}, u32[]{:S(2)}, u32[]{:S(2)}) collective-permute-start(f32[1024,96]{0,1:T(8,128)S(1)} %fusion.49), channel_id=1, source_target_pairs={{0,1},{1,0},{2,3},{3,2},{4,5},{5,4},{6,7},{7,6},{8,9},{9,8},{10,11... | collective-permute-start | bytes 1179656 | tf_op jit(solution)/shard_map/ppermute | solution.py:17
  30.1 4.9 %collective-permute-start.10 = (bf16[512,96]{0,1:T(8,128)(2,1)S(1)}, bf16[512,96]{0,1:T(8,128)(2,1)S(1)}, u32[]{:S(2)}, u32[]{:S(2)}) collective-permute-start(bf16[512,96]{0,1:T(8,128)(2,1)S(1)} %slice.333), channel_id=1, source_target_pairs={{0,2},{1,3},{2,0},{3,1},{4,6},{5,7},{6,4},{7,5},{8,10},{9,11},{10,... | collective-permute-start | bytes 294920 | tf_op jit(solution)/shard_map/ppermute | solution.py:17
  35.0 9.9 %collective-permute-start.12 = (bf16[512,96]{0,1:T(8,128)(2,1)S(1)}, bf16[512,96]{0,1:T(8,128)(2,1)S(1)}, u32[]{:S(2)}, u32[]{:S(2)}) collective-permute-start(bf16[512,96]{0,1:T(8,128)(2,1)S(1)} %fusion.22), channel_id=1, source_target_pairs={{0,8},{1,9},{2,10},{3,11},{4,12},{5,13},{6,14},{7,15},{8,0},{9,1},... | collective-permute-start | bytes 294920 | tf_op jit(solution)/shard_map/ppermute | solution.py:17
  37.6 7.4 %collective-permute-start.13 = (bf16[512,96]{0,1:T(8,128)(2,1)S(1)}, bf16[512,96]{0,1:T(8,128)(2,1)S(1)}, u32[]{:S(2)}, u32[]{:S(2)}) collective-permute-start(bf16[512,96]{0,1:T(8,128)(2,1)S(1)} %fusion.22), channel_id=1, source_target_pairs={{0,12},{1,13},{2,14},{3,15},{4,8},{5,9},{6,10},{7,11},{8,4},{9,5},... | collective-permute-start | bytes 294920 | tf_op jit(solution)/shard_map/ppermute | solution.py:17
  39.0 6.4 %collective-permute-start.11 = (bf16[512,96]{0,1:T(8,128)(2,1)S(1)}, bf16[512,96]{0,1:T(8,128)(2,1)S(1)}, u32[]{:S(2)}, u32[]{:S(2)}) collective-permute-start(bf16[512,96]{0,1:T(8,128)(2,1)S(1)} %fusion.22), channel_id=1, source_target_pairs={{0,4},{1,5},{2,6},{3,7},{4,0},{5,1},{6,2},{7,3},{8,12},{9,13},{10,... | collective-permute-start | bytes 294920 | tf_op jit(solution)/shard_map/ppermute | solution.py:17
  45.8 1.4 %collective-permute-start.14 = (f32[256,96]{0,1:T(8,128)S(1)}, f32[256,96]{0,1:T(8,128)S(1)}, u32[]{:S(2)}, u32[]{:S(2)}) collective-permute-start(f32[256,96]{0,1:T(8,128)S(1)} %slice.245), channel_id=1, source_target_pairs={{0,1},{1,0},{2,3},{3,2},{4,5},{5,4},{6,7},{7,6},{8,9},{9,8},{10,11... | collective-permute-start | bytes 294920 | tf_op jit(solution)/shard_map/ppermute | solution.py:17
  47.2 4.2 %collective-permute-start.15 = (bf16[256,96]{0,1:T(8,128)(2,1)S(1)}, bf16[256,96]{0,1:T(8,128)(2,1)S(1)}, u32[]{:S(2)}, u32[]{:S(2)}) collective-permute-start(bf16[256,96]{0,1:T(8,128)(2,1)S(1)} %pad_maximum_fusion.6), channel_id=1, source_target_pairs={{0,2},{1,3},{2,0},{3,1},{4,6},{5,7},{6,4},{7,5},{8,10},{9,11},{10,... | collective-permute-start | bytes 147464 | tf_op jit(solution)/shard_map/ppermute | solution.py:17
  51.4 8.8 %collective-permute-start.18 = (bf16[256,96]{0,1:T(8,128)(2,1)S(1)}, bf16[256,96]{0,1:T(8,128)(2,1)S(1)}, u32[]{:S(2)}, u32[]{:S(2)}) collective-permute-start(bf16[256,96]{0,1:T(8,128)(2,1)S(1)} %get-tuple-element.67), channel_id=1, source_target_pairs={{0,12},{1,13},{2,14},{3,15},{4,8},{5,9},{6,10},{7,11},{8,4},{9,5},... | collective-permute-start | bytes 147464 | tf_op jit(solution)/shard_map/ppermute | solution.py:17
  54.7 5.5 %collective-permute-start.17 = (bf16[256,96]{0,1:T(8,128)(2,1)S(1)}, bf16[256,96]{0,1:T(8,128)(2,1)S(1)}, u32[]{:S(2)}, u32[]{:S(2)}) collective-permute-start(bf16[256,96]{0,1:T(8,128)(2,1)S(1)} %get-tuple-element.67), channel_id=1, source_target_pairs={{0,8},{1,9},{2,10},{3,11},{4,12},{5,13},{6,14},{7,15},{8,0},{9,1},... | collective-permute-start | bytes 147464 | tf_op jit(solution)/shard_map/ppermute | solution.py:17
  55.0 4.1 %collective-permute-start.16 = (bf16[256,96]{0,1:T(8,128)(2,1)S(1)}, bf16[256,96]{0,1:T(8,128)(2,1)S(1)}, u32[]{:S(2)}, u32[]{:S(2)}) collective-permute-start(bf16[256,96]{0,1:T(8,128)(2,1)S(1)} %get-tuple-element.67), channel_id=1, source_target_pairs={{0,4},{1,5},{2,6},{3,7},{4,0},{5,1},{6,2},{7,3},{8,12},{9,13},{10,... | collective-permute-start | bytes 147464 | tf_op jit(solution)/shard_map/ppermute | solution.py:17
  60.3 1.5 %collective-permute-start.19 = (bf16[1024,96]{0,1:T(8,128)(2,1)S(1)}, bf16[1024,96]{0,1:T(8,128)(2,1)S(1)}, u32[]{:S(2)}, u32[]{:S(2)}) collective-permute-start(bf16[1024,96]{0,1:T(8,128)(2,1)S(1)} %constant_dynamic-update-slice_fusion.2), channel_id=1, source_target_pairs={{0,1},{1,0},{2,3},{3,2},{4,5},{5,4},{6,7},{7,6},{8,9},{9,8},{10,11... | collective-permute-start | bytes 589832 | tf_op jit(solution)/shard_map/ppermute | solution.py:17
  62.8 7.0 %collective-permute-start.20 = (bf16[1024,96]{0,1:T(8,128)(2,1)S(1)}, bf16[1024,96]{0,1:T(8,128)(2,1)S(1)}, u32[]{:S(2)}, u32[]{:S(2)}) collective-permute-start(bf16[1024,96]{0,1:T(8,128)(2,1)S(1)} %fusion.9), channel_id=1, source_target_pairs={{0,16},{16,0},{1,17},{17,1},{2,18},{18,2},{3,19},{19,3},{4,20},{20... | collective-permute-start | bytes 589832 | tf_op jit(solution)/shard_map/ppermute | solution.py:168
  70.3 1.8 %collective-permute-start.21 = (f32[1024,96]{0,1:T(8,128)S(1)}, f32[1024,96]{0,1:T(8,128)S(1)}, u32[]{:S(2)}, u32[]{:S(2)}) collective-permute-start(f32[1024,96]{0,1:T(8,128)S(1)} %fusion.51), channel_id=1, source_target_pairs={{0,1},{1,0},{2,3},{3,2},{4,5},{5,4},{6,7},{7,6},{8,9},{9,8},{10,11... | collective-permute-start | bytes 1179656 | tf_op jit(solution)/shard_map/ppermute | solution.py:17
  72.2 4.9 %collective-permute-start.22 = (bf16[512,96]{0,1:T(8,128)(2,1)S(1)}, bf16[512,96]{0,1:T(8,128)(2,1)S(1)}, u32[]{:S(2)}, u32[]{:S(2)}) collective-permute-start(bf16[512,96]{0,1:T(8,128)(2,1)S(1)} %slice.332), channel_id=1, source_target_pairs={{0,2},{1,3},{2,0},{3,1},{4,6},{5,7},{6,4},{7,5},{8,10},{9,11},{10,... | collective-permute-start | bytes 294920 | tf_op jit(solution)/shard_map/ppermute | solution.py:17
  77.1 12.3 %collective-permute-start.26 = (bf16[1024,96]{0,1:T(8,128)(2,1)S(1)}, bf16[1024,96]{0,1:T(8,128)(2,1)S(1)}, u32[]{:S(2)}, u32[]{:S(2)}) collective-permute-start(bf16[1024,96]{0,1:T(8,128)(2,1)S(1)} %get-tuple-element.54), channel_id=1, source_target_pairs={{0,16},{16,0},{1,17},{17,1},{2,18},{18,2},{3,19},{19,3},{4,20},{20... | collective-permute-start | bytes 589832 | tf_op jit(solution)/shard_map/ppermute | solution.py:144
  78.7 7.5 %collective-permute-start.25 = (bf16[512,96]{0,1:T(8,128)(2,1)S(1)}, bf16[512,96]{0,1:T(8,128)(2,1)S(1)}, u32[]{:S(2)}, u32[]{:S(2)}) collective-permute-start(bf16[512,96]{0,1:T(8,128)(2,1)S(1)} %fusion.23), channel_id=1, source_target_pairs={{0,12},{1,13},{2,14},{3,15},{4,8},{5,9},{6,10},{7,11},{8,4},{9,5},... | collective-permute-start | bytes 294920 | tf_op jit(solution)/shard_map/ppermute | solution.py:17
  80.6 8.8 %collective-permute-start.24 = (bf16[512,96]{0,1:T(8,128)(2,1)S(1)}, bf16[512,96]{0,1:T(8,128)(2,1)S(1)}, u32[]{:S(2)}, u32[]{:S(2)}) collective-permute-start(bf16[512,96]{0,1:T(8,128)(2,1)S(1)} %fusion.23), channel_id=1, source_target_pairs={{0,8},{1,9},{2,10},{3,11},{4,12},{5,13},{6,14},{7,15},{8,0},{9,1},... | collective-permute-start | bytes 294920 | tf_op jit(solution)/shard_map/ppermute | solution.py:17
  80.6 8.8 %collective-permute-start.23 = (bf16[512,96]{0,1:T(8,128)(2,1)S(1)}, bf16[512,96]{0,1:T(8,128)(2,1)S(1)}, u32[]{:S(2)}, u32[]{:S(2)}) collective-permute-start(bf16[512,96]{0,1:T(8,128)(2,1)S(1)} %fusion.23), channel_id=1, source_target_pairs={{0,4},{1,5},{2,6},{3,7},{4,0},{5,1},{6,2},{7,3},{8,12},{9,13},{10,... | collective-permute-start | bytes 294920 | tf_op jit(solution)/shard_map/ppermute | solution.py:17
  89.8 1.4 %collective-permute-start.27 = (f32[256,96]{0,1:T(8,128)S(1)}, f32[256,96]{0,1:T(8,128)S(1)}, u32[]{:S(2)}, u32[]{:S(2)}) collective-permute-start(f32[256,96]{0,1:T(8,128)S(1)} %slice.271), channel_id=1, source_target_pairs={{0,1},{1,0},{2,3},{3,2},{4,5},{5,4},{6,7},{7,6},{8,9},{9,8},{10,11... | collective-permute-start | bytes 294920 | tf_op jit(solution)/shard_map/ppermute | solution.py:17
  91.3 4.2 %collective-permute-start.28 = (bf16[256,96]{0,1:T(8,128)(2,1)S(1)}, bf16[256,96]{0,1:T(8,128)(2,1)S(1)}, u32[]{:S(2)}, u32[]{:S(2)}) collective-permute-start(bf16[256,96]{0,1:T(8,128)(2,1)S(1)} %pad_maximum_fusion.7), channel_id=1, source_target_pairs={{0,2},{1,3},{2,0},{3,1},{4,6},{5,7},{6,4},{7,5},{8,10},{9,11},{10,... | collective-permute-start | bytes 147464 | tf_op jit(solution)/shard_map/ppermute | solution.py:17
  95.4 7.5 %collective-permute-start.31 = (bf16[256,96]{0,1:T(8,128)(2,1)S(1)}, bf16[256,96]{0,1:T(8,128)(2,1)S(1)}, u32[]{:S(2)}, u32[]{:S(2)}) collective-permute-start(bf16[256,96]{0,1:T(8,128)(2,1)S(1)} %get-tuple-element.61), channel_id=1, source_target_pairs={{0,12},{1,13},{2,14},{3,15},{4,8},{5,9},{6,10},{7,11},{8,4},{9,5},... | collective-permute-start | bytes 147464 | tf_op jit(solution)/shard_map/ppermute | solution.py:17
  97.5 5.4 %collective-permute-start.30 = (bf16[256,96]{0,1:T(8,128)(2,1)S(1)}, bf16[256,96]{0,1:T(8,128)(2,1)S(1)}, u32[]{:S(2)}, u32[]{:S(2)}) collective-permute-start(bf16[256,96]{0,1:T(8,128)(2,1)S(1)} %get-tuple-element.61), channel_id=1, source_target_pairs={{0,8},{1,9},{2,10},{3,11},{4,12},{5,13},{6,14},{7,15},{8,0},{9,1},... | collective-permute-start | bytes 147464 | tf_op jit(solution)/shard_map/ppermute | solution.py:17
  97.5 4.6 %collective-permute-start.29 = (bf16[256,96]{0,1:T(8,128)(2,1)S(1)}, bf16[256,96]{0,1:T(8,128)(2,1)S(1)}, u32[]{:S(2)}, u32[]{:S(2)}) collective-permute-start(bf16[256,96]{0,1:T(8,128)(2,1)S(1)} %get-tuple-element.61), channel_id=1, source_target_pairs={{0,4},{1,5},{2,6},{3,7},{4,0},{5,1},{6,2},{7,3},{8,12},{9,13},{10,... | collective-permute-start | bytes 147464 | tf_op jit(solution)/shard_map/ppermute | solution.py:17
  103.1 1.5 %collective-permute-start.32 = (bf16[1024,96]{0,1:T(8,128)(2,1)S(1)}, bf16[1024,96]{0,1:T(8,128)(2,1)S(1)}, u32[]{:S(2)}, u32[]{:S(2)}) collective-permute-start(bf16[1024,96]{0,1:T(8,128)(2,1)S(1)} %constant_dynamic-update-slice_fusion.10), channel_id=1, source_target_pairs={{0,1},{1,0},{2,3},{3,2},{4,5},{5,4},{6,7},{7,6},{8,9},{9,8},{10,11... | collective-permute-start | bytes 589832 | tf_op jit(solution)/shard_map/ppermute | solution.py:17
  103.9 5.8 %copy-start.2 = (f32[128,96]{0,1:T(8,128)S(1)}, f32[128,96]{0,1:T(8,128)}, u32[]{:S(2)}) copy-start(f32[128,96]{0,1:T(8,128)} %param.5) | copy-start | bytes 147460
  105.6 11.1 %copy-start.1 = (f32[1024,96]{0,1:T(8,128)}, f32[1024,96]{0,1:T(8,128)S(1)}, u32[]{:S(2)}) copy-start(f32[1024,96]{0,1:T(8,128)S(1)} %fusion.2) | copy-start | bytes 1179652
  106.3 9.8 %all-to-all-start = ((f32[16,1,96]{2,1,0:T(1,128)}), f32[16,1,96]{2,1,0:T(1,128)S(1)}, u32[]{:S(2)}, u32[]{:S(2)}) async-start(f32[16,1,96]{2,1,0:T(1,128)} %broadcast_in_dim.23), calls=%async_computation | async-start | bytes 16384 | tf_op jit(solution)/shard_map/all_to_all | solution.py:177

commit v5 on v4

--- a/solution.py
+++ b/solution.py
@@ -137,10 +137,10 @@
         got = swapped(send.astype(LOW), "rows", 2)
         grad = keep + got.astype(WIDE)
         grad_low = grad.astype(LOW)
-        if turn > 0:
+        if turn > 0 and nfeat > 2:
             grad_low, rest = tied(grad_low, rest)
         parts = [swapped(grad_low, "rows", z) for z in near[1:]]
-        if turn > 0:
+        if turn > 0 and nfeat > 2:
             *parts, rest = tied(*parts, lax.ppermute(rest, "feat", along))
             incoming = incoming + rest.astype(WIDE)
         for step, got in enumerate(parts, 1):
@@ -158,18 +158,20 @@
         delta_low = delta.astype(LOW)
         slots = [delta_low] + [swapped(delta_low, "rows", z) for z in near[1:]]
         delta_low = jnp.concatenate([s[:own] for s in slots] + [s[own:] for s in slots], axis=0)
-        outgoing = incoming - product(delta_low)
+        change = product(delta_low)
+        outgoing = incoming - change
         active = actives[turn]
         delta_kept = jnp.where(active, delta[:own], delta_kept)
-        if turn < nfeat - 1:
+        if turn < nfeat - 1 and nfeat == 2:
+            sent = jnp.where(actives[0], change + fit_rest.astype(WIDE), fit_rest.astype(WIDE))
+            got = lax.ppermute(sent.astype(LOW), "feat", along).astype(WIDE)
+            outgoing = outgoing - got
+            incoming = incoming - got
+            incoming_low = incoming.astype(LOW)
+        elif turn < nfeat - 1:
             high, rest = split(outgoing)
-            if nfeat == 2:
-                high = jnp.where(actives[0], high, fit_rest)
             incoming_low = lax.ppermute(high, "feat", along)
             incoming = incoming_low.astype(WIDE)
-            if nfeat == 2:
-                outgoing = outgoing - incoming
-                incoming = incoming - fit_rest.astype(WIDE)
         kept = jnp.where(active, outgoing, kept)
 
     kept = lax.optimization_barrier(kept)

time: 117 us -> 115 us (0.983)
  starting transfers between devices: 40 us -> 37.7 us
    ppermute x2 -> x1, starting transfers between devices: 3.11 us -> 1.55 us  [on_device(): got = lax.ppermute(sent.astype(LOW), 'feat', along).astype(WIDE)]
    ppermute x2 -> x1, waiting for transfers between devices: 5.46 us -> 5.45 us  [on_device(): got = lax.ppermute(sent.astype(LOW), 'feat', along).astype(WIDE)]
  transfers between devices with their start and end apart: 34 -> 33, of which waited for: 23 -> 23; matrix products, arithmetic and copies ran while one was open for 5% -> 5% of each run, Pallas kernels for 1% -> 1%
where the time goes in v5:
time: 115 us; the launch traced here: 114 us
  waiting for transfers between devices  59.8 us (52%)
  starting transfers between devices  37.7 us (33%)
  matrix products  7.07 us (6%)
  local copies, waits for them, and re-layouts  4.5 us (4%)
  other arithmetic  2.92 us (3%)
  Pallas kernels  1.34 us (1%)
    ppermute x31, waiting for transfers between devices, swapped(): return lax.ppermute(shard, axis, [(i, i ^ bit) for i in range(peers)])  48.6 us
    ppermute x31, starting transfers between devices, swapped(): return lax.ppermute(shard, axis, [(i, i ^ bit) for i in range(peers)])  32.7 us
    all_to_all x1, waiting for transfers between devices, on_device(): lax.all_to_all(jnp.broadcast_to(squares[None], (nrows, 1, classes)), 'row...  5.73 us
    ppermute x1, waiting for transfers between devices, on_device(): got = lax.ppermute(sent.astype(LOW), 'feat', along).astype(WIDE)  5.45 us
    all_to_all x1, starting transfers between devices, on_device(): lax.all_to_all(jnp.broadcast_to(squares[None], (nrows, 1, classes)), 'row...  3.48 us
    unnamed x23, local copies, waits for them, and re-layouts  2.36 us
    dot_general x3, matrix products, product(): return first + jnp.dot(sending, far, preferred_element_type=WIDE)  2.34 us
    dot_general x3, matrix products, product(): first, far = tied(jnp.dot(keeping, rows, preferred_element_type=WIDE), far)  2.33 us
  transfers between devices with their start and end apart: 33, of which 23 were waited for; matrix products, arithmetic and copies ran while one was open for 5% of the time, Pallas kernels for 1%

profile of v5, /device:TPU:0, one launch (start us, length us, event | category | flops | bytes accessed | tf_op | source)
XLA Modules:
  0.0 114.4 jit_solution(7951402813633964088)
XLA Ops:
  0.6 0.8 convert_element_type.93
  1.4 5.0 %collective-permute-start.2 = (bf16[128,96]{0,1:T(8,128)(2,1)S(1)}, bf16[128,96]{0,1:T(8,128)(2,1)S(1)}, u32[]{:S(2)}, u32[]{:S(2)}) collective-permute-start(bf16[128,96]{0,1:T(8,128)(2,1)S(1)} %convert_element_type.93), channel_id=1, source_target_pairs={{0,12},{1,13},{2,14},{3,15},{4,8},{5,9},{6,10},{7,11},{8,4},{9,5},... | collective-permute-start | bytes 73736 | tf_op jit(solution)/shard_map/ppermute | solution.py:17
  7.1 1.3 %dynamic-slice_convert_fusion.3 = (bf16[128,128]{1,0:T(8,128)(2,1)S(1)}, bf16[128,128]{1,0:T(8,128)(2,1)S(1)}, bf16[128,128]{1,0:T(8,128)(2,1)S(1)}, bf16[128,12...) fusion(f32[128,2048]{1,0:T(8,128)} %param.6, ...), kind=kLoop, calls=%fused_computation.58 | loop fusion | bytes 1048640 | tf_op jit(solution)/shard_map/convert.10
  8.5 2.2 %copy-done = bf16[1024,2048]{1,0:T(8,128)(2,1)S(1)} copy-done((bf16[1024,2048]{1,0:T(8,128)(2,1)S(1)}, bf16[1024,2048]{1,0:T(8,128)(2,1)}, u32[]{:S(2)}) %copy-start) | copy-done | bytes 4194328
  10.7 1.3 %shard_map.67 = (bf16[1024,1024]{1,0:T(8,128)(2,1)S(1)}, bf16[1024,1024]{1,0:T(8,128)(2,1)S(1)}) custom-call(s32[1]{0:T(128)} %bitcast.me_ref, bf16[1024,2048]{1,0:T(8,128)(2,1)S(1)} %copy-done), custom_call_target="tpu_custom_call" | custom-call | bytes 8388608 | tf_op jit(solution)/shard_map/pallas_call | solution.py:58
  12.1 1.8 %collective-permute-start.3 = (bf16[512,96]{0,1:T(8,128)(2,1)S(1)}, bf16[512,96]{0,1:T(8,128)(2,1)S(1)}, u32[]{:S(2)}, u32[]{:S(2)}) collective-permute-start(bf16[512,96]{0,1:T(8,128)(2,1)S(1)} %pad_maximum_fusion.5), channel_id=1, source_target_pairs={{0,2},{1,3},{2,0},{3,1},{4,6},{5,7},{6,4},{7,5},{8,10},{9,11},{10,... | collective-permute-start | bytes 294920 | tf_op jit(solution)/shard_map/ppermute | solution.py:17
  13.9 1.2 %collective-permute-start.6 = (bf16[128,512]{1,0:T(8,128)(2,1)S(1)}, bf16[128,512]{1,0:T(8,128)(2,1)S(1)}, u32[]{:S(2)}, u32[]{:S(2)}) collective-permute-start(bf16[128,512]{1,0:T(8,128)(2,1)S(1)} %get-tuple-element.35), channel_id=1, source_target_pairs={{0,4},{1,5},{2,6},{3,7},{4,0},{5,1},{6,2},{7,3},{8,12},{9,13},{10,... | collective-permute-start | bytes 393224 | tf_op jit(solution)/shard_map/ppermute | solution.py:17
  15.1 2.9 %collective-permute-start.7 = (bf16[128,512]{1,0:T(8,128)(2,1)S(1)}, bf16[128,512]{1,0:T(8,128)(2,1)S(1)}, u32[]{:S(2)}, u32[]{:S(2)}) collective-permute-start(bf16[128,512]{1,0:T(8,128)(2,1)S(1)} %get-tuple-element.36), channel_id=1, source_target_pairs={{0,8},{1,9},{2,10},{3,11},{4,12},{5,13},{6,14},{7,15},{8,0},{9,1},... | collective-permute-start | bytes 393224 | tf_op jit(solution)/shard_map/ppermute | solution.py:17
  18.4 0.8 fusion.47
  19.2 0.6 collective-permute-done.4
  19.8 0.8 reduce-precision_convert_fusion
  20.6 1.6 %collective-permute-start.5 = (bf16[1024,96]{0,1:T(8,128)(2,1)S(1)}, bf16[1024,96]{0,1:T(8,128)(2,1)S(1)}, u32[]{:S(2)}, u32[]{:S(2)}) collective-permute-start(bf16[1024,96]{0,1:T(8,128)(2,1)S(1)} %get-tuple-element.97), channel_id=1, source_target_pairs={{0,16},{16,0},{1,17},{17,1},{2,18},{18,2},{3,19},{19,3},{4,20},{20... | collective-permute-start | bytes 589832 | tf_op jit(solution)/shard_map/ppermute | solution.py:17
  22.2 5.0 %collective-permute-done.7 = bf16[128,512]{1,0:T(8,128)(2,1)S(1)} collective-permute-done((bf16[128,512]{1,0:T(8,128)(2,1)S(1)}, bf16[128,512]{1,0:T(8,128)(2,1)S(1)}, u32[]{:S(2)}, u32[]{:S(2)}) %collective-permute-start.7) | collective-permute-done | bytes 131104 | tf_op jit(solution)/shard_map/ppermute | solution.py:17
  28.7 1.2 %collective-permute-done.9 = f32[1024,96]{0,1:T(8,128)S(1)} collective-permute-done((f32[1024,96]{0,1:T(8,128)S(1)}, f32[1024,96]{0,1:T(8,128)S(1)}, u32[]{:S(2)}, u32[]{:S(2)}) %collective-permute-start.9) | collective-permute-done | bytes 393248 | tf_op jit(solution)/shard_map/ppermute | solution.py:17
  30.4 4.5 %collective-permute-done.10 = bf16[512,96]{0,1:T(8,128)(2,1)S(1)} collective-permute-done((bf16[512,96]{0,1:T(8,128)(2,1)S(1)}, bf16[512,96]{0,1:T(8,128)(2,1)S(1)}, u32[]{:S(2)}, u32[]{:S(2)}) %collective-permute-start.10) | collective-permute-done | bytes 98336 | tf_op jit(solution)/shard_map/ppermute | solution.py:17
  35.0 2.6 %collective-permute-start.12 = (bf16[512,96]{0,1:T(8,128)(2,1)S(1)}, bf16[512,96]{0,1:T(8,128)(2,1)S(1)}, u32[]{:S(2)}, u32[]{:S(2)}) collective-permute-start(bf16[512,96]{0,1:T(8,128)(2,1)S(1)} %fusion.19), channel_id=1, source_target_pairs={{0,8},{1,9},{2,10},{3,11},{4,12},{5,13},{6,14},{7,15},{8,0},{9,1},... | collective-permute-start | bytes 294920 | tf_op jit(solution)/shard_map/ppermute | solution.py:17
  37.6 1.4 %collective-permute-start.13 = (bf16[512,96]{0,1:T(8,128)(2,1)S(1)}, bf16[512,96]{0,1:T(8,128)(2,1)S(1)}, u32[]{:S(2)}, u32[]{:S(2)}) collective-permute-start(bf16[512,96]{0,1:T(8,128)(2,1)S(1)} %fusion.19), channel_id=1, source_target_pairs={{0,12},{1,13},{2,14},{3,15},{4,8},{5,9},{6,10},{7,11},{8,4},{9,5},... | collective-permute-start | bytes 294920 | tf_op jit(solution)/shard_map/ppermute | solution.py:17
  39.2 5.7 %collective-permute-done.12 = bf16[512,96]{0,1:T(8,128)(2,1)S(1)} collective-permute-done((bf16[512,96]{0,1:T(8,128)(2,1)S(1)}, bf16[512,96]{0,1:T(8,128)(2,1)S(1)}, u32[]{:S(2)}, u32[]{:S(2)}) %collective-permute-start.12) | collective-permute-done | bytes 98336 | tf_op jit(solution)/shard_map/ppermute | solution.py:17
  45.9 1.3 %collective-permute-done.14 = f32[256,96]{0,1:T(8,128)S(1)} collective-permute-done((f32[256,96]{0,1:T(8,128)S(1)}, f32[256,96]{0,1:T(8,128)S(1)}, u32[]{:S(2)}, u32[]{:S(2)}) %collective-permute-start.14) | collective-permute-done | bytes 98336 | tf_op jit(solution)/shard_map/ppermute | solution.py:17
  47.2 0.6 collective-permute-start.15
  47.8 3.5 %collective-permute-done.15 = bf16[256,96]{0,1:T(8,128)(2,1)S(1)} collective-permute-done((bf16[256,96]{0,1:T(8,128)(2,1)S(1)}, bf16[256,96]{0,1:T(8,128)(2,1)S(1)}, u32[]{:S(2)}, u32[]{:S(2)}) %collective-permute-start.15) | collective-permute-done | bytes 49184 | tf_op jit(solution)/shard_map/ppermute | solution.py:17
  51.4 3.3 %collective-permute-start.18 = (bf16[256,96]{0,1:T(8,128)(2,1)S(1)}, bf16[256,96]{0,1:T(8,128)(2,1)S(1)}, u32[]{:S(2)}, u32[]{:S(2)}) collective-permute-start(bf16[256,96]{0,1:T(8,128)(2,1)S(1)} %get-tuple-element.53), channel_id=1, source_target_pairs={{0,12},{1,13},{2,14},{3,15},{4,8},{5,9},{6,10},{7,11},{8,4},{9,5},... | collective-permute-start | bytes 147464 | tf_op jit(solution)/shard_map/ppermute | solution.py:17
  55.0 0.9 collective-permute-start.16
  55.9 3.2 %collective-permute-done.16 = bf16[256,96]{0,1:T(8,128)(2,1)S(1)} collective-permute-done((bf16[256,96]{0,1:T(8,128)(2,1)S(1)}, bf16[256,96]{0,1:T(8,128)(2,1)S(1)}, u32[]{:S(2)}, u32[]{:S(2)}) %collective-permute-start.16) | collective-permute-done | bytes 49184 | tf_op jit(solution)/shard_map/ppermute | solution.py:17
  59.1 1.1 collective-permute-done.17
  60.4 0.8 fusion.48
  61.2 0.6 collective-permute-done.19
  61.9 0.8 fusion.3
  62.7 1.6 %collective-permute-start.20 = (bf16[1024,96]{0,1:T(8,128)(2,1)S(1)}, bf16[1024,96]{0,1:T(8,128)(2,1)S(1)}, u32[]{:S(2)}, u32[]{:S(2)}) collective-permute-start(bf16[1024,96]{0,1:T(8,128)(2,1)S(1)} %get-tuple-element.99), channel_id=1, source_target_pairs={{0,16},{16,0},{1,17},{17,1},{2,18},{18,2},{3,19},{19,3},{4,20},{20... | collective-permute-start | bytes 589832 | tf_op jit(solution)/shard_map/ppermute | solution.py:167
  64.2 5.5 %collective-permute-done.20 = bf16[1024,96]{0,1:T(8,128)(2,1)S(1)} collective-permute-done((bf16[1024,96]{0,1:T(8,128)(2,1)S(1)}, bf16[1024,96]{0,1:T(8,128)(2,1)S(1)}, u32[]{:S(2)}, u32[]{:S(2)}) %collective-permute-start.20) | collective-permute-done | bytes 196640 | tf_op jit(solution)/shard_map/ppermute | solution.py:167
  70.7 1.2 %collective-permute-done.21 = f32[1024,96]{0,1:T(8,128)S(1)} collective-permute-done((f32[1024,96]{0,1:T(8,128)S(1)}, f32[1024,96]{0,1:T(8,128)S(1)}, u32[]{:S(2)}, u32[]{:S(2)}) %collective-permute-start.21) | collective-permute-done | bytes 393248 | tf_op jit(solution)/shard_map/ppermute | solution.py:17
  72.6 4.3 %collective-permute-done.22 = bf16[512,96]{0,1:T(8,128)(2,1)S(1)} collective-permute-done((bf16[512,96]{0,1:T(8,128)(2,1)S(1)}, bf16[512,96]{0,1:T(8,128)(2,1)S(1)}, u32[]{:S(2)}, u32[]{:S(2)}) %collective-permute-start.22) | collective-permute-done | bytes 98336 | tf_op jit(solution)/shard_map/ppermute | solution.py:17
  76.9 1.6 %collective-permute-start.24 = (bf16[512,96]{0,1:T(8,128)(2,1)S(1)}, bf16[512,96]{0,1:T(8,128)(2,1)S(1)}, u32[]{:S(2)}, u32[]{:S(2)}) collective-permute-start(bf16[512,96]{0,1:T(8,128)(2,1)S(1)} %fusion.20), channel_id=1, source_target_pairs={{0,8},{1,9},{2,10},{3,11},{4,12},{5,13},{6,14},{7,15},{8,0},{9,1},... | collective-permute-start | bytes 294920 | tf_op jit(solution)/shard_map/ppermute | solution.py:17
  78.5 1.2 %collective-permute-start.25 = (bf16[512,96]{0,1:T(8,128)(2,1)S(1)}, bf16[512,96]{0,1:T(8,128)(2,1)S(1)}, u32[]{:S(2)}, u32[]{:S(2)}) collective-permute-start(bf16[512,96]{0,1:T(8,128)(2,1)S(1)} %fusion.20), channel_id=1, source_target_pairs={{0,12},{1,13},{2,14},{3,15},{4,8},{5,9},{6,10},{7,11},{8,4},{9,5},... | collective-permute-start | bytes 294920 | tf_op jit(solution)/shard_map/ppermute | solution.py:17
  79.7 0.8 collective-permute-start.23
  80.5 6.2 %collective-permute-done.24 = bf16[512,96]{0,1:T(8,128)(2,1)S(1)} collective-permute-done((bf16[512,96]{0,1:T(8,128)(2,1)S(1)}, bf16[512,96]{0,1:T(8,128)(2,1)S(1)}, u32[]{:S(2)}, u32[]{:S(2)}) %collective-permute-start.24) | collective-permute-done | bytes 98336 | tf_op jit(solution)/shard_map/ppermute | solution.py:17
  87.5 1.3 %collective-permute-done.26 = f32[256,96]{0,1:T(8,128)S(1)} collective-permute-done((f32[256,96]{0,1:T(8,128)S(1)}, f32[256,96]{0,1:T(8,128)S(1)}, u32[]{:S(2)}, u32[]{:S(2)}) %collective-permute-start.26) | collective-permute-done | bytes 98336 | tf_op jit(solution)/shard_map/ppermute | solution.py:17
  89.4 3.6 %collective-permute-done.27 = bf16[256,96]{0,1:T(8,128)(2,1)S(1)} collective-permute-done((bf16[256,96]{0,1:T(8,128)(2,1)S(1)}, bf16[256,96]{0,1:T(8,128)(2,1)S(1)}, u32[]{:S(2)}, u32[]{:S(2)}) %collective-permute-start.27) | collective-permute-done | bytes 49184 | tf_op jit(solution)/shard_map/ppermute | solution.py:17
  93.0 2.2 %collective-permute-start.30 = (bf16[256,96]{0,1:T(8,128)(2,1)S(1)}, bf16[256,96]{0,1:T(8,128)(2,1)S(1)}, u32[]{:S(2)}, u32[]{:S(2)}) collective-permute-start(bf16[256,96]{0,1:T(8,128)(2,1)S(1)} %get-tuple-element.49), channel_id=1, source_target_pairs={{0,12},{1,13},{2,14},{3,15},{4,8},{5,9},{6,10},{7,11},{8,4},{9,5},... | collective-permute-start | bytes 147464 | tf_op jit(solution)/shard_map/ppermute | solution.py:17
  95.2 0.9 collective-permute-start.29
  96.1 1.3 %collective-permute-start.28 = (bf16[256,96]{0,1:T(8,128)(2,1)S(1)}, bf16[256,96]{0,1:T(8,128)(2,1)S(1)}, u32[]{:S(2)}, u32[]{:S(2)}) collective-permute-start(bf16[256,96]{0,1:T(8,128)(2,1)S(1)} %get-tuple-element.49), channel_id=1, source_target_pairs={{0,4},{1,5},{2,6},{3,7},{4,0},{5,1},{6,2},{7,3},{8,12},{9,13},{10,... | collective-permute-start | bytes 147464 | tf_op jit(solution)/shard_map/ppermute | solution.py:17
  97.4 3.1 %collective-permute-done.28 = bf16[256,96]{0,1:T(8,128)(2,1)S(1)} collective-permute-done((bf16[256,96]{0,1:T(8,128)(2,1)S(1)}, bf16[256,96]{0,1:T(8,128)(2,1)S(1)}, u32[]{:S(2)}, u32[]{:S(2)}) %collective-permute-start.28) | collective-permute-done | bytes 49184 | tf_op jit(solution)/shard_map/ppermute | solution.py:17
  100.9 0.8 fusion.49
  101.7 0.6 collective-permute-done.31
  102.3 0.8 fusion.50
  104.1 3.5 %all-to-all-start = ((f32[16,1,96]{2,1,0:T(1,128)}), f32[16,1,96]{2,1,0:T(1,128)S(1)}, u32[]{:S(2)}, u32[]{:S(2)}) async-start(f32[16,1,96]{2,1,0:T(1,128)} %broadcast_in_dim.23), calls=%async_computation | async-start | bytes 16384 | tf_op jit(solution)/shard_map/all_to_all | solution.py:179
  107.6 0.6 fusion.26
  108.2 5.7 %all-to-all-done = f32[16,1,96]{2,1,0:T(1,128)S(1)} async-done(((f32[16,1,96]{2,1,0:T(1,128)}), f32[16,1,96]{2,1,0:T(1,128)S(1)}, u32[]{:S(2)}, u32[]{:S(2)}) %all-to-all-start) | async-done | bytes 6176 | tf_op jit(solution)/shard_map/all_to_all | solution.py:179
  (97 shorter events, 9.5 us)
Async XLA Ops:
  1.4 10.6 %collective-permute-start.2 = (bf16[128,96]{0,1:T(8,128)(2,1)S(1)}, bf16[128,96]{0,1:T(8,128)(2,1)S(1)}, u32[]{:S(2)}, u32[]{:S(2)}) collective-permute-start(bf16[128,96]{0,1:T(8,128)(2,1)S(1)} %convert_element_type.93), channel_id=1, source_target_pairs={{0,12},{1,13},{2,14},{3,15},{4,8},{5,9},{6,10},{7,11},{8,4},{9,5},... | collective-permute-start | bytes 73736 | tf_op jit(solution)/shard_map/ppermute | solution.py:17
  6.5 5.6 %collective-permute-start.1 = (bf16[128,96]{0,1:T(8,128)(2,1)S(1)}, bf16[128,96]{0,1:T(8,128)(2,1)S(1)}, u32[]{:S(2)}, u32[]{:S(2)}) collective-permute-start(bf16[128,96]{0,1:T(8,128)(2,1)S(1)} %convert_element_type.93), channel_id=1, source_target_pairs={{0,8},{1,9},{2,10},{3,11},{4,12},{5,13},{6,14},{7,15},{8,0},{9,1},... | collective-permute-start | bytes 73736 | tf_op jit(solution)/shard_map/ppermute | solution.py:17
  6.5 5.6 %collective-permute-start = (bf16[128,96]{0,1:T(8,128)(2,1)S(1)}, bf16[128,96]{0,1:T(8,128)(2,1)S(1)}, u32[]{:S(2)}, u32[]{:S(2)}) collective-permute-start(bf16[128,96]{0,1:T(8,128)(2,1)S(1)} %convert_element_type.93), channel_id=1, source_target_pairs={{0,4},{1,5},{2,6},{3,7},{4,0},{5,1},{6,2},{7,3},{8,12},{9,13},{10,... | collective-permute-start | bytes 73736 | tf_op jit(solution)/shard_map/ppermute | solution.py:17
  8.5 2.2 %copy-start = (bf16[1024,2048]{1,0:T(8,128)(2,1)S(1)}, bf16[1024,2048]{1,0:T(8,128)(2,1)}, u32[]{:S(2)}) copy-start(bf16[1024,2048]{1,0:T(8,128)(2,1)} %given.1) | copy-start | bytes 12582916
  12.1 6.2 %collective-permute-start.3 = (bf16[512,96]{0,1:T(8,128)(2,1)S(1)}, bf16[512,96]{0,1:T(8,128)(2,1)S(1)}, u32[]{:S(2)}, u32[]{:S(2)}) collective-permute-start(bf16[512,96]{0,1:T(8,128)(2,1)S(1)} %pad_maximum_fusion.5), channel_id=1, source_target_pairs={{0,2},{1,3},{2,0},{3,1},{4,6},{5,7},{6,4},{7,5},{8,10},{9,11},{10,... | collective-permute-start | bytes 294920 | tf_op jit(solution)/shard_map/ppermute | solution.py:17
  13.9 8.3 %collective-permute-start.6 = (bf16[128,512]{1,0:T(8,128)(2,1)S(1)}, bf16[128,512]{1,0:T(8,128)(2,1)S(1)}, u32[]{:S(2)}, u32[]{:S(2)}) collective-permute-start(bf16[128,512]{1,0:T(8,128)(2,1)S(1)} %get-tuple-element.35), channel_id=1, source_target_pairs={{0,4},{1,5},{2,6},{3,7},{4,0},{5,1},{6,2},{7,3},{8,12},{9,13},{10,... | collective-permute-start | bytes 393224 | tf_op jit(solution)/shard_map/ppermute | solution.py:17
  15.1 12.0 %collective-permute-start.7 = (bf16[128,512]{1,0:T(8,128)(2,1)S(1)}, bf16[128,512]{1,0:T(8,128)(2,1)S(1)}, u32[]{:S(2)}, u32[]{:S(2)}) collective-permute-start(bf16[128,512]{1,0:T(8,128)(2,1)S(1)} %get-tuple-element.36), channel_id=1, source_target_pairs={{0,8},{1,9},{2,10},{3,11},{4,12},{5,13},{6,14},{7,15},{8,0},{9,1},... | collective-permute-start | bytes 393224 | tf_op jit(solution)/shard_map/ppermute | solution.py:17
  18.1 9.1 %collective-permute-start.8 = (bf16[128,512]{1,0:T(8,128)(2,1)S(1)}, bf16[128,512]{1,0:T(8,128)(2,1)S(1)}, u32[]{:S(2)}, u32[]{:S(2)}) collective-permute-start(bf16[128,512]{1,0:T(8,128)(2,1)S(1)} %get-tuple-element.37), channel_id=1, source_target_pairs={{0,12},{1,13},{2,14},{3,15},{4,8},{5,9},{6,10},{7,11},{8,4},{9,5},... | collective-permute-start | bytes 393224 | tf_op jit(solution)/shard_map/ppermute | solution.py:17
  18.3 1.5 %collective-permute-start.4 = (bf16[1024,96]{0,1:T(8,128)(2,1)S(1)}, bf16[1024,96]{0,1:T(8,128)(2,1)S(1)}, u32[]{:S(2)}, u32[]{:S(2)}) collective-permute-start(bf16[1024,96]{0,1:T(8,128)(2,1)S(1)} %constant_dynamic-update-slice_fusion), channel_id=1, source_target_pairs={{0,1},{1,0},{2,3},{3,2},{4,5},{5,4},{6,7},{7,6},{8,9},{9,8},{10,11... | collective-permute-start | bytes 589832 | tf_op jit(solution)/shard_map/ppermute | solution.py:17
  19.8 7.8 %copy-start.3 = (s32[1024]{0:T(1024)S(1)}, s32[1024]{0:T(1024)}, u32[]{:S(2)}) copy-start(s32[1024]{0:T(1024)} %param.7) | copy-start | bytes 12292
  20.6 7.0 %collective-permute-start.5 = (bf16[1024,96]{0,1:T(8,128)(2,1)S(1)}, bf16[1024,96]{0,1:T(8,128)(2,1)S(1)}, u32[]{:S(2)}, u32[]{:S(2)}) collective-permute-start(bf16[1024,96]{0,1:T(8,128)(2,1)S(1)} %get-tuple-element.97), channel_id=1, source_target_pairs={{0,16},{16,0},{1,17},{17,1},{2,18},{18,2},{3,19},{19,3},{4,20},{20... | collective-permute-start | bytes 589832 | tf_op jit(solution)/shard_map/ppermute | solution.py:17
  28.2 1.8 %collective-permute-start.9 = (f32[1024,96]{0,1:T(8,128)S(1)}, f32[1024,96]{0,1:T(8,128)S(1)}, u32[]{:S(2)}, u32[]{:S(2)}) collective-permute-start(f32[1024,96]{0,1:T(8,128)S(1)} %fusion.23), channel_id=1, source_target_pairs={{0,1},{1,0},{2,3},{3,2},{4,5},{5,4},{6,7},{7,6},{8,9},{9,8},{10,11... | collective-permute-start | bytes 1179656 | tf_op jit(solution)/shard_map/ppermute | solution.py:17
  30.0 4.9 %collective-permute-start.10 = (bf16[512,96]{0,1:T(8,128)(2,1)S(1)}, bf16[512,96]{0,1:T(8,128)(2,1)S(1)}, u32[]{:S(2)}, u32[]{:S(2)}) collective-permute-start(bf16[512,96]{0,1:T(8,128)(2,1)S(1)} %slice.333), channel_id=1, source_target_pairs={{0,2},{1,3},{2,0},{3,1},{4,6},{5,7},{6,4},{7,5},{8,10},{9,11},{10,... | collective-permute-start | bytes 294920 | tf_op jit(solution)/shard_map/ppermute | solution.py:17
  35.0 9.9 %collective-permute-start.12 = (bf16[512,96]{0,1:T(8,128)(2,1)S(1)}, bf16[512,96]{0,1:T(8,128)(2,1)S(1)}, u32[]{:S(2)}, u32[]{:S(2)}) collective-permute-start(bf16[512,96]{0,1:T(8,128)(2,1)S(1)} %fusion.19), channel_id=1, source_target_pairs={{0,8},{1,9},{2,10},{3,11},{4,12},{5,13},{6,14},{7,15},{8,0},{9,1},... | collective-permute-start | bytes 294920 | tf_op jit(solution)/shard_map/ppermute | solution.py:17
  37.6 7.3 %collective-permute-start.13 = (bf16[512,96]{0,1:T(8,128)(2,1)S(1)}, bf16[512,96]{0,1:T(8,128)(2,1)S(1)}, u32[]{:S(2)}, u32[]{:S(2)}) collective-permute-start(bf16[512,96]{0,1:T(8,128)(2,1)S(1)} %fusion.19), channel_id=1, source_target_pairs={{0,12},{1,13},{2,14},{3,15},{4,8},{5,9},{6,10},{7,11},{8,4},{9,5},... | collective-permute-start | bytes 294920 | tf_op jit(solution)/shard_map/ppermute | solution.py:17
  39.0 6.4 %collective-permute-start.11 = (bf16[512,96]{0,1:T(8,128)(2,1)S(1)}, bf16[512,96]{0,1:T(8,128)(2,1)S(1)}, u32[]{:S(2)}, u32[]{:S(2)}) collective-permute-start(bf16[512,96]{0,1:T(8,128)(2,1)S(1)} %fusion.19), channel_id=1, source_target_pairs={{0,4},{1,5},{2,6},{3,7},{4,0},{5,1},{6,2},{7,3},{8,12},{9,13},{10,... | collective-permute-start | bytes 294920 | tf_op jit(solution)/shard_map/ppermute | solution.py:17
  45.8 1.4 %collective-permute-start.14 = (f32[256,96]{0,1:T(8,128)S(1)}, f32[256,96]{0,1:T(8,128)S(1)}, u32[]{:S(2)}, u32[]{:S(2)}) collective-permute-start(f32[256,96]{0,1:T(8,128)S(1)} %slice.245), channel_id=1, source_target_pairs={{0,1},{1,0},{2,3},{3,2},{4,5},{5,4},{6,7},{7,6},{8,9},{9,8},{10,11... | collective-permute-start | bytes 294920 | tf_op jit(solution)/shard_map/ppermute | solution.py:17
  47.2 4.2 %collective-permute-start.15 = (bf16[256,96]{0,1:T(8,128)(2,1)S(1)}, bf16[256,96]{0,1:T(8,128)(2,1)S(1)}, u32[]{:S(2)}, u32[]{:S(2)}) collective-permute-start(bf16[256,96]{0,1:T(8,128)(2,1)S(1)} %pad_maximum_fusion.6), channel_id=1, source_target_pairs={{0,2},{1,3},{2,0},{3,1},{4,6},{5,7},{6,4},{7,5},{8,10},{9,11},{10,... | collective-permute-start | bytes 147464 | tf_op jit(solution)/shard_map/ppermute | solution.py:17
  51.4 8.8 %collective-permute-start.18 = (bf16[256,96]{0,1:T(8,128)(2,1)S(1)}, bf16[256,96]{0,1:T(8,128)(2,1)S(1)}, u32[]{:S(2)}, u32[]{:S(2)}) collective-permute-start(bf16[256,96]{0,1:T(8,128)(2,1)S(1)} %get-tuple-element.53), channel_id=1, source_target_pairs={{0,12},{1,13},{2,14},{3,15},{4,8},{5,9},{6,10},{7,11},{8,4},{9,5},... | collective-permute-start | bytes 147464 | tf_op jit(solution)/shard_map/ppermute | solution.py:17
  54.7 5.5 %collective-permute-start.17 = (bf16[256,96]{0,1:T(8,128)(2,1)S(1)}, bf16[256,96]{0,1:T(8,128)(2,1)S(1)}, u32[]{:S(2)}, u32[]{:S(2)}) collective-permute-start(bf16[256,96]{0,1:T(8,128)(2,1)S(1)} %get-tuple-element.53), channel_id=1, source_target_pairs={{0,8},{1,9},{2,10},{3,11},{4,12},{5,13},{6,14},{7,15},{8,0},{9,1},... | collective-permute-start | bytes 147464 | tf_op jit(solution)/shard_map/ppermute | solution.py:17
  55.0 4.1 %collective-permute-start.16 = (bf16[256,96]{0,1:T(8,128)(2,1)S(1)}, bf16[256,96]{0,1:T(8,128)(2,1)S(1)}, u32[]{:S(2)}, u32[]{:S(2)}) collective-permute-start(bf16[256,96]{0,1:T(8,128)(2,1)S(1)} %get-tuple-element.53), channel_id=1, source_target_pairs={{0,4},{1,5},{2,6},{3,7},{4,0},{5,1},{6,2},{7,3},{8,12},{9,13},{10,... | collective-permute-start | bytes 147464 | tf_op jit(solution)/shard_map/ppermute | solution.py:17
  60.3 1.5 %collective-permute-start.19 = (bf16[1024,96]{0,1:T(8,128)(2,1)S(1)}, bf16[1024,96]{0,1:T(8,128)(2,1)S(1)}, u32[]{:S(2)}, u32[]{:S(2)}) collective-permute-start(bf16[1024,96]{0,1:T(8,128)(2,1)S(1)} %constant_dynamic-update-slice_fusion.2), channel_id=1, source_target_pairs={{0,1},{1,0},{2,3},{3,2},{4,5},{5,4},{6,7},{7,6},{8,9},{9,8},{10,11... | collective-permute-start | bytes 589832 | tf_op jit(solution)/shard_map/ppermute | solution.py:17
  62.7 7.0 %collective-permute-start.20 = (bf16[1024,96]{0,1:T(8,128)(2,1)S(1)}, bf16[1024,96]{0,1:T(8,128)(2,1)S(1)}, u32[]{:S(2)}, u32[]{:S(2)}) collective-permute-start(bf16[1024,96]{0,1:T(8,128)(2,1)S(1)} %get-tuple-element.99), channel_id=1, source_target_pairs={{0,16},{16,0},{1,17},{17,1},{2,18},{18,2},{3,19},{19,3},{4,20},{20... | collective-permute-start | bytes 589832 | tf_op jit(solution)/shard_map/ppermute | solution.py:167
  70.1 1.8 %collective-permute-start.21 = (f32[1024,96]{0,1:T(8,128)S(1)}, f32[1024,96]{0,1:T(8,128)S(1)}, u32[]{:S(2)}, u32[]{:S(2)}) collective-permute-start(f32[1024,96]{0,1:T(8,128)S(1)} %fusion.33), channel_id=1, source_target_pairs={{0,1},{1,0},{2,3},{3,2},{4,5},{5,4},{6,7},{7,6},{8,9},{9,8},{10,11... | collective-permute-start | bytes 1179656 | tf_op jit(solution)/shard_map/ppermute | solution.py:17
  72.0 4.9 %collective-permute-start.22 = (bf16[512,96]{0,1:T(8,128)(2,1)S(1)}, bf16[512,96]{0,1:T(8,128)(2,1)S(1)}, u32[]{:S(2)}, u32[]{:S(2)}) collective-permute-start(bf16[512,96]{0,1:T(8,128)(2,1)S(1)} %slice.332), channel_id=1, source_target_pairs={{0,2},{1,3},{2,0},{3,1},{4,6},{5,7},{6,4},{7,5},{8,10},{9,11},{10,... | collective-permute-start | bytes 294920 | tf_op jit(solution)/shard_map/ppermute | solution.py:17
  76.9 9.7 %collective-permute-start.24 = (bf16[512,96]{0,1:T(8,128)(2,1)S(1)}, bf16[512,96]{0,1:T(8,128)(2,1)S(1)}, u32[]{:S(2)}, u32[]{:S(2)}) collective-permute-start(bf16[512,96]{0,1:T(8,128)(2,1)S(1)} %fusion.20), channel_id=1, source_target_pairs={{0,8},{1,9},{2,10},{3,11},{4,12},{5,13},{6,14},{7,15},{8,0},{9,1},... | collective-permute-start | bytes 294920 | tf_op jit(solution)/shard_map/ppermute | solution.py:17
  78.5 8.1 %collective-permute-start.25 = (bf16[512,96]{0,1:T(8,128)(2,1)S(1)}, bf16[512,96]{0,1:T(8,128)(2,1)S(1)}, u32[]{:S(2)}, u32[]{:S(2)}) collective-permute-start(bf16[512,96]{0,1:T(8,128)(2,1)S(1)} %fusion.20), channel_id=1, source_target_pairs={{0,12},{1,13},{2,14},{3,15},{4,8},{5,9},{6,10},{7,11},{8,4},{9,5},... | collective-permute-start | bytes 294920 | tf_op jit(solution)/shard_map/ppermute | solution.py:17
  79.7 7.2 %collective-permute-start.23 = (bf16[512,96]{0,1:T(8,128)(2,1)S(1)}, bf16[512,96]{0,1:T(8,128)(2,1)S(1)}, u32[]{:S(2)}, u32[]{:S(2)}) collective-permute-start(bf16[512,96]{0,1:T(8,128)(2,1)S(1)} %fusion.20), channel_id=1, source_target_pairs={{0,4},{1,5},{2,6},{3,7},{4,0},{5,1},{6,2},{7,3},{8,12},{9,13},{10,... | collective-permute-start | bytes 294920 | tf_op jit(solution)/shard_map/ppermute | solution.py:17
  87.4 1.4 %collective-permute-start.26 = (f32[256,96]{0,1:T(8,128)S(1)}, f32[256,96]{0,1:T(8,128)S(1)}, u32[]{:S(2)}, u32[]{:S(2)}) collective-permute-start(f32[256,96]{0,1:T(8,128)S(1)} %slice.271), channel_id=1, source_target_pairs={{0,1},{1,0},{2,3},{3,2},{4,5},{5,4},{6,7},{7,6},{8,9},{9,8},{10,11... | collective-permute-start | bytes 294920 | tf_op jit(solution)/shard_map/ppermute | solution.py:17
  88.8 4.2 %collective-permute-start.27 = (bf16[256,96]{0,1:T(8,128)(2,1)S(1)}, bf16[256,96]{0,1:T(8,128)(2,1)S(1)}, u32[]{:S(2)}, u32[]{:S(2)}) collective-permute-start(bf16[256,96]{0,1:T(8,128)(2,1)S(1)} %pad_maximum_fusion.7), channel_id=1, source_target_pairs={{0,2},{1,3},{2,0},{3,1},{4,6},{5,7},{6,4},{7,5},{8,10},{9,11},{10,... | collective-permute-start | bytes 147464 | tf_op jit(solution)/shard_map/ppermute | solution.py:17
  93.0 7.8 %collective-permute-start.30 = (bf16[256,96]{0,1:T(8,128)(2,1)S(1)}, bf16[256,96]{0,1:T(8,128)(2,1)S(1)}, u32[]{:S(2)}, u32[]{:S(2)}) collective-permute-start(bf16[256,96]{0,1:T(8,128)(2,1)S(1)} %get-tuple-element.49), channel_id=1, source_target_pairs={{0,12},{1,13},{2,14},{3,15},{4,8},{5,9},{6,10},{7,11},{8,4},{9,5},... | collective-permute-start | bytes 147464 | tf_op jit(solution)/shard_map/ppermute | solution.py:17
  95.2 5.5 %collective-permute-start.29 = (bf16[256,96]{0,1:T(8,128)(2,1)S(1)}, bf16[256,96]{0,1:T(8,128)(2,1)S(1)}, u32[]{:S(2)}, u32[]{:S(2)}) collective-permute-start(bf16[256,96]{0,1:T(8,128)(2,1)S(1)} %get-tuple-element.49), channel_id=1, source_target_pairs={{0,8},{1,9},{2,10},{3,11},{4,12},{5,13},{6,14},{7,15},{8,0},{9,1},... | collective-permute-start | bytes 147464 | tf_op jit(solution)/shard_map/ppermute | solution.py:17
  96.1 4.3 %collective-permute-start.28 = (bf16[256,96]{0,1:T(8,128)(2,1)S(1)}, bf16[256,96]{0,1:T(8,128)(2,1)S(1)}, u32[]{:S(2)}, u32[]{:S(2)}) collective-permute-start(bf16[256,96]{0,1:T(8,128)(2,1)S(1)} %get-tuple-element.49), channel_id=1, source_target_pairs={{0,4},{1,5},{2,6},{3,7},{4,0},{5,1},{6,2},{7,3},{8,12},{9,13},{10,... | collective-permute-start | bytes 147464 | tf_op jit(solution)/shard_map/ppermute | solution.py:17
  100.8 1.5 %collective-permute-start.31 = (bf16[1024,96]{0,1:T(8,128)(2,1)S(1)}, bf16[1024,96]{0,1:T(8,128)(2,1)S(1)}, u32[]{:S(2)}, u32[]{:S(2)}) collective-permute-start(bf16[1024,96]{0,1:T(8,128)(2,1)S(1)} %constant_dynamic-update-slice_fusion.10), channel_id=1, source_target_pairs={{0,1},{1,0},{2,3},{3,2},{4,5},{5,4},{6,7},{7,6},{8,9},{9,8},{10,11... | collective-permute-start | bytes 589832 | tf_op jit(solution)/shard_map/ppermute | solution.py:17
  103.1 4.4 %copy-start.2 = (f32[128,96]{0,1:T(8,128)S(1)}, f32[128,96]{0,1:T(8,128)}, u32[]{:S(2)}) copy-start(f32[128,96]{0,1:T(8,128)} %param.5) | copy-start | bytes 147460
  103.3 11.1 %copy-start.1 = (f32[1024,96]{0,1:T(8,128)}, f32[1024,96]{0,1:T(8,128)S(1)}, u32[]{:S(2)}) copy-start(f32[1024,96]{0,1:T(8,128)S(1)} %fusion.1) | copy-start | bytes 1179652
  104.1 9.9 %all-to-all-start = ((f32[16,1,96]{2,1,0:T(1,128)}), f32[16,1,96]{2,1,0:T(1,128)S(1)}, u32[]{:S(2)}, u32[]{:S(2)}) async-start(f32[16,1,96]{2,1,0:T(1,128)} %broadcast_in_dim.23), calls=%async_computation | async-start | bytes 16384 | tf_op jit(solution)/shard_map/all_to_all | solution.py:179

commit v6 on v5

--- a/solution.py
+++ b/solution.py
@@ -61,7 +61,7 @@
         in_specs=[pl.BlockSpec(memory_space=pltpu.SMEM), pl.BlockSpec(memory_space=pl.ANY)],
         out_specs=[pl.BlockSpec(memory_space=pl.ANY)] * 2,
         scratch_shapes=[pltpu.SemaphoreType.DMA((len(order),))],
-        compiler_params=pltpu.CompilerParams(vmem_limit_bytes=1 << 20),
+        compiler_params=pltpu.CompilerParams(vmem_limit_bytes=48 << 20),
         cost_estimate=pl.CostEstimate(flops=0, bytes_accessed=2 * features.size * 2, transcendentals=0),
     )(me.astype(jnp.int32)[None], features)
 

time: 115 us -> 114 us (level)
  local copies, waits for them, and re-layouts: 4.5 us -> 2.35 us
    unnamed x23 -> x21, local copies, waits for them, and re-layouts: 2.36 us -> 0.18 us
  transfers between devices with their start and end apart: 33 -> 33, of which waited for: 23 -> 24; matrix products, arithmetic and copies ran while one was open for 5% -> 6% of each run, Pallas kernels for 1% -> 2%
where the time goes in v6:
time: 114 us; the launch traced here: 113 us
  waiting for transfers between devices  59.8 us (52%)
  starting transfers between devices  37.6 us (33%)
  matrix products  7.18 us (6%)
  other arithmetic  2.97 us (3%)
  Pallas kernels  2.41 us (2%)
  local copies, waits for them, and re-layouts  2.35 us (2%)
    ppermute x31, waiting for transfers between devices, swapped(): return lax.ppermute(shard, axis, [(i, i ^ bit) for i in range(peers)])  48.7 us
    ppermute x31, starting transfers between devices, swapped(): return lax.ppermute(shard, axis, [(i, i ^ bit) for i in range(peers)])  32.6 us
    all_to_all x1, waiting for transfers between devices, on_device(): lax.all_to_all(jnp.broadcast_to(squares[None], (nrows, 1, classes)), 'row...  5.72 us
    ppermute x1, waiting for transfers between devices, on_device(): got = lax.ppermute(sent.astype(LOW), 'feat', along).astype(WIDE)  5.46 us
    all_to_all x1, starting transfers between devices, on_device(): lax.all_to_all(jnp.broadcast_to(squares[None], (nrows, 1, classes)), 'row...  3.43 us
    pallas_call x1, Pallas kernels, reordered(): pl.pallas_call(functools.partial(reorder_kernel, order, own), out_shape=[...  2.41 us
    dot_general x3, matrix products, product(): return first + jnp.dot(sending, far, preferred_element_type=WIDE)  2.37 us
    dot_general x3, matrix products, product(): first, far = tied(jnp.dot(keeping, rows, preferred_element_type=WIDE), far)  2.33 us
  transfers between devices with their start and end apart: 33, of which 24 were waited for; matrix products, arithmetic and copies ran while one was open for 6% of the time, Pallas kernels for 2%

profile of v6, /device:TPU:0, one launch (start us, length us, event | category | flops | bytes accessed | tf_op | source)
XLA Modules:
  0.0 113.4 jit_solution(2387041821517311066)
XLA Ops:
  0.6 0.8 convert_element_type.93
  1.4 5.0 %collective-permute-start.2 = (bf16[128,96]{0,1:T(8,128)(2,1)S(1)}, bf16[128,96]{0,1:T(8,128)(2,1)S(1)}, u32[]{:S(2)}, u32[]{:S(2)}) collective-permute-start(bf16[128,96]{0,1:T(8,128)(2,1)S(1)} %convert_element_type.93), channel_id=1, source_target_pairs={{0,12},{1,13},{2,14},{3,15},{4,8},{5,9},{6,10},{7,11},{8,4},{9,5},... | collective-permute-start | bytes 73736 | tf_op jit(solution)/shard_map/ppermute | solution.py:17
  7.1 1.3 %dynamic-slice_convert_fusion.3 = (bf16[128,128]{1,0:T(8,128)(2,1)S(1)}, bf16[128,128]{1,0:T(8,128)(2,1)S(1)}, bf16[128,128]{1,0:T(8,128)(2,1)S(1)}, bf16[128,12...) fusion(f32[128,2048]{1,0:T(8,128)} %param.6, ...), kind=kLoop, calls=%fused_computation.58 | loop fusion | bytes 1048640 | tf_op jit(solution)/shard_map/convert.10
  8.5 2.4 %shard_map.67 = (bf16[1024,1024]{1,0:T(8,128)(2,1)S(1)}, bf16[1024,1024]{1,0:T(8,128)(2,1)S(1)}) custom-call(s32[1]{0:T(128)} %bitcast.me_ref, bf16[1024,2048]{1,0:T(8,128)(2,1)} %given.1), custom_call_target="tpu_custom_call" | custom-call | bytes 8388608 | tf_op jit(solution)/shard_map/pallas_call | solution.py:58
  11.2 1.6 %collective-permute-start.3 = (bf16[512,96]{0,1:T(8,128)(2,1)S(1)}, bf16[512,96]{0,1:T(8,128)(2,1)S(1)}, u32[]{:S(2)}, u32[]{:S(2)}) collective-permute-start(bf16[512,96]{0,1:T(8,128)(2,1)S(1)} %pad_maximum_fusion.5), channel_id=1, source_target_pairs={{0,2},{1,3},{2,0},{3,1},{4,6},{5,7},{6,4},{7,5},{8,10},{9,11},{10,... | collective-permute-start | bytes 294920 | tf_op jit(solution)/shard_map/ppermute | solution.py:17
  12.8 1.2 %collective-permute-start.6 = (bf16[128,512]{1,0:T(8,128)(2,1)S(1)}, bf16[128,512]{1,0:T(8,128)(2,1)S(1)}, u32[]{:S(2)}, u32[]{:S(2)}) collective-permute-start(bf16[128,512]{1,0:T(8,128)(2,1)S(1)} %get-tuple-element.35), channel_id=1, source_target_pairs={{0,4},{1,5},{2,6},{3,7},{4,0},{5,1},{6,2},{7,3},{8,12},{9,13},{10,... | collective-permute-start | bytes 393224 | tf_op jit(solution)/shard_map/ppermute | solution.py:17
  14.0 2.9 %collective-permute-start.7 = (bf16[128,512]{1,0:T(8,128)(2,1)S(1)}, bf16[128,512]{1,0:T(8,128)(2,1)S(1)}, u32[]{:S(2)}, u32[]{:S(2)}) collective-permute-start(bf16[128,512]{1,0:T(8,128)(2,1)S(1)} %get-tuple-element.36), channel_id=1, source_target_pairs={{0,8},{1,9},{2,10},{3,11},{4,12},{5,13},{6,14},{7,15},{8,0},{9,1},... | collective-permute-start | bytes 393224 | tf_op jit(solution)/shard_map/ppermute | solution.py:17
  17.3 0.8 fusion.47
  18.1 0.6 collective-permute-done.4
  18.8 0.8 reduce-precision_convert_fusion
  19.5 1.6 %collective-permute-start.5 = (bf16[1024,96]{0,1:T(8,128)(2,1)S(1)}, bf16[1024,96]{0,1:T(8,128)(2,1)S(1)}, u32[]{:S(2)}, u32[]{:S(2)}) collective-permute-start(bf16[1024,96]{0,1:T(8,128)(2,1)S(1)} %get-tuple-element.97), channel_id=1, source_target_pairs={{0,16},{16,0},{1,17},{17,1},{2,18},{18,2},{3,19},{19,3},{4,20},{20... | collective-permute-start | bytes 589832 | tf_op jit(solution)/shard_map/ppermute | solution.py:17
  21.1 4.9 %collective-permute-done.7 = bf16[128,512]{1,0:T(8,128)(2,1)S(1)} collective-permute-done((bf16[128,512]{1,0:T(8,128)(2,1)S(1)}, bf16[128,512]{1,0:T(8,128)(2,1)S(1)}, u32[]{:S(2)}, u32[]{:S(2)}) %collective-permute-start.7) | collective-permute-done | bytes 131104 | tf_op jit(solution)/shard_map/ppermute | solution.py:17
  27.7 1.2 %collective-permute-done.9 = f32[1024,96]{0,1:T(8,128)S(1)} collective-permute-done((f32[1024,96]{0,1:T(8,128)S(1)}, f32[1024,96]{0,1:T(8,128)S(1)}, u32[]{:S(2)}, u32[]{:S(2)}) %collective-permute-start.9) | collective-permute-done | bytes 393248 | tf_op jit(solution)/shard_map/ppermute | solution.py:17
  29.6 4.3 %collective-permute-done.10 = bf16[512,96]{0,1:T(8,128)(2,1)S(1)} collective-permute-done((bf16[512,96]{0,1:T(8,128)(2,1)S(1)}, bf16[512,96]{0,1:T(8,128)(2,1)S(1)}, u32[]{:S(2)}, u32[]{:S(2)}) %collective-permute-start.10) | collective-permute-done | bytes 98336 | tf_op jit(solution)/shard_map/ppermute | solution.py:17
  33.9 2.5 %collective-permute-start.12 = (bf16[512,96]{0,1:T(8,128)(2,1)S(1)}, bf16[512,96]{0,1:T(8,128)(2,1)S(1)}, u32[]{:S(2)}, u32[]{:S(2)}) collective-permute-start(bf16[512,96]{0,1:T(8,128)(2,1)S(1)} %fusion.19), channel_id=1, source_target_pairs={{0,8},{1,9},{2,10},{3,11},{4,12},{5,13},{6,14},{7,15},{8,0},{9,1},... | collective-permute-start | bytes 294920 | tf_op jit(solution)/shard_map/ppermute | solution.py:17
  36.5 1.4 %collective-permute-start.13 = (bf16[512,96]{0,1:T(8,128)(2,1)S(1)}, bf16[512,96]{0,1:T(8,128)(2,1)S(1)}, u32[]{:S(2)}, u32[]{:S(2)}) collective-permute-start(bf16[512,96]{0,1:T(8,128)(2,1)S(1)} %fusion.19), channel_id=1, source_target_pairs={{0,12},{1,13},{2,14},{3,15},{4,8},{5,9},{6,10},{7,11},{8,4},{9,5},... | collective-permute-start | bytes 294920 | tf_op jit(solution)/shard_map/ppermute | solution.py:17
  38.1 5.8 %collective-permute-done.12 = bf16[512,96]{0,1:T(8,128)(2,1)S(1)} collective-permute-done((bf16[512,96]{0,1:T(8,128)(2,1)S(1)}, bf16[512,96]{0,1:T(8,128)(2,1)S(1)}, u32[]{:S(2)}, u32[]{:S(2)}) %collective-permute-start.12) | collective-permute-done | bytes 98336 | tf_op jit(solution)/shard_map/ppermute | solution.py:17
  44.9 1.3 %collective-permute-done.14 = f32[256,96]{0,1:T(8,128)S(1)} collective-permute-done((f32[256,96]{0,1:T(8,128)S(1)}, f32[256,96]{0,1:T(8,128)S(1)}, u32[]{:S(2)}, u32[]{:S(2)}) %collective-permute-start.14) | collective-permute-done | bytes 98336 | tf_op jit(solution)/shard_map/ppermute | solution.py:17
  46.8 3.6 %collective-permute-done.15 = bf16[256,96]{0,1:T(8,128)(2,1)S(1)} collective-permute-done((bf16[256,96]{0,1:T(8,128)(2,1)S(1)}, bf16[256,96]{0,1:T(8,128)(2,1)S(1)}, u32[]{:S(2)}, u32[]{:S(2)}) %collective-permute-start.15) | collective-permute-done | bytes 49184 | tf_op jit(solution)/shard_map/ppermute | solution.py:17
  50.4 3.3 %collective-permute-start.18 = (bf16[256,96]{0,1:T(8,128)(2,1)S(1)}, bf16[256,96]{0,1:T(8,128)(2,1)S(1)}, u32[]{:S(2)}, u32[]{:S(2)}) collective-permute-start(bf16[256,96]{0,1:T(8,128)(2,1)S(1)} %get-tuple-element.53), channel_id=1, source_target_pairs={{0,12},{1,13},{2,14},{3,15},{4,8},{5,9},{6,10},{7,11},{8,4},{9,5},... | collective-permute-start | bytes 147464 | tf_op jit(solution)/shard_map/ppermute | solution.py:17
  53.9 0.9 collective-permute-start.16
  54.8 3.2 %collective-permute-done.16 = bf16[256,96]{0,1:T(8,128)(2,1)S(1)} collective-permute-done((bf16[256,96]{0,1:T(8,128)(2,1)S(1)}, bf16[256,96]{0,1:T(8,128)(2,1)S(1)}, u32[]{:S(2)}, u32[]{:S(2)}) %collective-permute-start.16) | collective-permute-done | bytes 49184 | tf_op jit(solution)/shard_map/ppermute | solution.py:17
  58.0 1.1 %collective-permute-done.17 = bf16[256,96]{0,1:T(8,128)(2,1)S(1)} collective-permute-done((bf16[256,96]{0,1:T(8,128)(2,1)S(1)}, bf16[256,96]{0,1:T(8,128)(2,1)S(1)}, u32[]{:S(2)}, u32[]{:S(2)}) %collective-permute-start.17) | collective-permute-done | bytes 49184 | tf_op jit(solution)/shard_map/ppermute | solution.py:17
  59.3 0.8 fusion.48
  60.1 0.6 collective-permute-done.19
  60.8 0.8 fusion.3
  61.6 1.6 %collective-permute-start.20 = (bf16[1024,96]{0,1:T(8,128)(2,1)S(1)}, bf16[1024,96]{0,1:T(8,128)(2,1)S(1)}, u32[]{:S(2)}, u32[]{:S(2)}) collective-permute-start(bf16[1024,96]{0,1:T(8,128)(2,1)S(1)} %get-tuple-element.99), channel_id=1, source_target_pairs={{0,16},{16,0},{1,17},{17,1},{2,18},{18,2},{3,19},{19,3},{4,20},{20... | collective-permute-start | bytes 589832 | tf_op jit(solution)/shard_map/ppermute | solution.py:167
  63.1 5.5 %collective-permute-done.20 = bf16[1024,96]{0,1:T(8,128)(2,1)S(1)} collective-permute-done((bf16[1024,96]{0,1:T(8,128)(2,1)S(1)}, bf16[1024,96]{0,1:T(8,128)(2,1)S(1)}, u32[]{:S(2)}, u32[]{:S(2)}) %collective-permute-start.20) | collective-permute-done | bytes 196640 | tf_op jit(solution)/shard_map/ppermute | solution.py:167
  69.7 1.2 %collective-permute-done.21 = f32[1024,96]{0,1:T(8,128)S(1)} collective-permute-done((f32[1024,96]{0,1:T(8,128)S(1)}, f32[1024,96]{0,1:T(8,128)S(1)}, u32[]{:S(2)}, u32[]{:S(2)}) %collective-permute-start.21) | collective-permute-done | bytes 393248 | tf_op jit(solution)/shard_map/ppermute | solution.py:17
  70.9 0.6 collective-permute-start.22
  71.5 4.3 %collective-permute-done.22 = bf16[512,96]{0,1:T(8,128)(2,1)S(1)} collective-permute-done((bf16[512,96]{0,1:T(8,128)(2,1)S(1)}, bf16[512,96]{0,1:T(8,128)(2,1)S(1)}, u32[]{:S(2)}, u32[]{:S(2)}) %collective-permute-start.22) | collective-permute-done | bytes 98336 | tf_op jit(solution)/shard_map/ppermute | solution.py:17
  75.9 1.6 %collective-permute-start.24 = (bf16[512,96]{0,1:T(8,128)(2,1)S(1)}, bf16[512,96]{0,1:T(8,128)(2,1)S(1)}, u32[]{:S(2)}, u32[]{:S(2)}) collective-permute-start(bf16[512,96]{0,1:T(8,128)(2,1)S(1)} %fusion.20), channel_id=1, source_target_pairs={{0,8},{1,9},{2,10},{3,11},{4,12},{5,13},{6,14},{7,15},{8,0},{9,1},... | collective-permute-start | bytes 294920 | tf_op jit(solution)/shard_map/ppermute | solution.py:17
  77.5 1.2 %collective-permute-start.25 = (bf16[512,96]{0,1:T(8,128)(2,1)S(1)}, bf16[512,96]{0,1:T(8,128)(2,1)S(1)}, u32[]{:S(2)}, u32[]{:S(2)}) collective-permute-start(bf16[512,96]{0,1:T(8,128)(2,1)S(1)} %fusion.20), channel_id=1, source_target_pairs={{0,12},{1,13},{2,14},{3,15},{4,8},{5,9},{6,10},{7,11},{8,4},{9,5},... | collective-permute-start | bytes 294920 | tf_op jit(solution)/shard_map/ppermute | solution.py:17
  78.6 0.8 collective-permute-start.23
  79.4 6.2 %collective-permute-done.24 = bf16[512,96]{0,1:T(8,128)(2,1)S(1)} collective-permute-done((bf16[512,96]{0,1:T(8,128)(2,1)S(1)}, bf16[512,96]{0,1:T(8,128)(2,1)S(1)}, u32[]{:S(2)}, u32[]{:S(2)}) %collective-permute-start.24) | collective-permute-done | bytes 98336 | tf_op jit(solution)/shard_map/ppermute | solution.py:17
  86.4 1.3 %collective-permute-done.26 = f32[256,96]{0,1:T(8,128)S(1)} collective-permute-done((f32[256,96]{0,1:T(8,128)S(1)}, f32[256,96]{0,1:T(8,128)S(1)}, u32[]{:S(2)}, u32[]{:S(2)}) %collective-permute-start.26) | collective-permute-done | bytes 98336 | tf_op jit(solution)/shard_map/ppermute | solution.py:17
  88.3 3.6 %collective-permute-done.27 = bf16[256,96]{0,1:T(8,128)(2,1)S(1)} collective-permute-done((bf16[256,96]{0,1:T(8,128)(2,1)S(1)}, bf16[256,96]{0,1:T(8,128)(2,1)S(1)}, u32[]{:S(2)}, u32[]{:S(2)}) %collective-permute-start.27) | collective-permute-done | bytes 49184 | tf_op jit(solution)/shard_map/ppermute | solution.py:17
  91.9 2.2 %collective-permute-start.30 = (bf16[256,96]{0,1:T(8,128)(2,1)S(1)}, bf16[256,96]{0,1:T(8,128)(2,1)S(1)}, u32[]{:S(2)}, u32[]{:S(2)}) collective-permute-start(bf16[256,96]{0,1:T(8,128)(2,1)S(1)} %get-tuple-element.49), channel_id=1, source_target_pairs={{0,12},{1,13},{2,14},{3,15},{4,8},{5,9},{6,10},{7,11},{8,4},{9,5},... | collective-permute-start | bytes 147464 | tf_op jit(solution)/shard_map/ppermute | solution.py:17
  94.2 0.9 collective-permute-start.29
  95.1 1.3 %collective-permute-start.28 = (bf16[256,96]{0,1:T(8,128)(2,1)S(1)}, bf16[256,96]{0,1:T(8,128)(2,1)S(1)}, u32[]{:S(2)}, u32[]{:S(2)}) collective-permute-start(bf16[256,96]{0,1:T(8,128)(2,1)S(1)} %get-tuple-element.49), channel_id=1, source_target_pairs={{0,4},{1,5},{2,6},{3,7},{4,0},{5,1},{6,2},{7,3},{8,12},{9,13},{10,... | collective-permute-start | bytes 147464 | tf_op jit(solution)/shard_map/ppermute | solution.py:17
  96.4 3.1 %collective-permute-done.28 = bf16[256,96]{0,1:T(8,128)(2,1)S(1)} collective-permute-done((bf16[256,96]{0,1:T(8,128)(2,1)S(1)}, bf16[256,96]{0,1:T(8,128)(2,1)S(1)}, u32[]{:S(2)}, u32[]{:S(2)}) %collective-permute-start.28) | collective-permute-done | bytes 49184 | tf_op jit(solution)/shard_map/ppermute | solution.py:17
  99.9 0.8 fusion.49
  100.6 0.6 collective-permute-done.31
  101.3 0.8 fusion.50
  102.4 0.6 broadcast_in_dim.23
  103.1 3.4 %all-to-all-start = ((f32[16,1,96]{2,1,0:T(1,128)}), f32[16,1,96]{2,1,0:T(1,128)S(1)}, u32[]{:S(2)}, u32[]{:S(2)}) async-start(f32[16,1,96]{2,1,0:T(1,128)} %broadcast_in_dim.23), calls=%async_computation | async-start | bytes 16384 | tf_op jit(solution)/shard_map/all_to_all | solution.py:179
  106.5 0.6 fusion.26
  107.2 5.7 %all-to-all-done = f32[16,1,96]{2,1,0:T(1,128)S(1)} async-done(((f32[16,1,96]{2,1,0:T(1,128)}), f32[16,1,96]{2,1,0:T(1,128)S(1)}, u32[]{:S(2)}, u32[]{:S(2)}) %all-to-all-start) | async-done | bytes 6176 | tf_op jit(solution)/shard_map/all_to_all | solution.py:179
  (95 shorter events, 9.6 us)
Async XLA Ops:
  1.4 9.5 %collective-permute-start.2 = (bf16[128,96]{0,1:T(8,128)(2,1)S(1)}, bf16[128,96]{0,1:T(8,128)(2,1)S(1)}, u32[]{:S(2)}, u32[]{:S(2)}) collective-permute-start(bf16[128,96]{0,1:T(8,128)(2,1)S(1)} %convert_element_type.93), channel_id=1, source_target_pairs={{0,12},{1,13},{2,14},{3,15},{4,8},{5,9},{6,10},{7,11},{8,4},{9,5},... | collective-permute-start | bytes 73736 | tf_op jit(solution)/shard_map/ppermute | solution.py:17
  6.5 4.7 %collective-permute-start.1 = (bf16[128,96]{0,1:T(8,128)(2,1)S(1)}, bf16[128,96]{0,1:T(8,128)(2,1)S(1)}, u32[]{:S(2)}, u32[]{:S(2)}) collective-permute-start(bf16[128,96]{0,1:T(8,128)(2,1)S(1)} %convert_element_type.93), channel_id=1, source_target_pairs={{0,8},{1,9},{2,10},{3,11},{4,12},{5,13},{6,14},{7,15},{8,0},{9,1},... | collective-permute-start | bytes 73736 | tf_op jit(solution)/shard_map/ppermute | solution.py:17
  6.5 4.7 %collective-permute-start = (bf16[128,96]{0,1:T(8,128)(2,1)S(1)}, bf16[128,96]{0,1:T(8,128)(2,1)S(1)}, u32[]{:S(2)}, u32[]{:S(2)}) collective-permute-start(bf16[128,96]{0,1:T(8,128)(2,1)S(1)} %convert_element_type.93), channel_id=1, source_target_pairs={{0,4},{1,5},{2,6},{3,7},{4,0},{5,1},{6,2},{7,3},{8,12},{9,13},{10,... | collective-permute-start | bytes 73736 | tf_op jit(solution)/shard_map/ppermute | solution.py:17
  11.2 6.0 %collective-permute-start.3 = (bf16[512,96]{0,1:T(8,128)(2,1)S(1)}, bf16[512,96]{0,1:T(8,128)(2,1)S(1)}, u32[]{:S(2)}, u32[]{:S(2)}) collective-permute-start(bf16[512,96]{0,1:T(8,128)(2,1)S(1)} %pad_maximum_fusion.5), channel_id=1, source_target_pairs={{0,2},{1,3},{2,0},{3,1},{4,6},{5,7},{6,4},{7,5},{8,10},{9,11},{10,... | collective-permute-start | bytes 294920 | tf_op jit(solution)/shard_map/ppermute | solution.py:17
  12.8 8.3 %collective-permute-start.6 = (bf16[128,512]{1,0:T(8,128)(2,1)S(1)}, bf16[128,512]{1,0:T(8,128)(2,1)S(1)}, u32[]{:S(2)}, u32[]{:S(2)}) collective-permute-start(bf16[128,512]{1,0:T(8,128)(2,1)S(1)} %get-tuple-element.35), channel_id=1, source_target_pairs={{0,4},{1,5},{2,6},{3,7},{4,0},{5,1},{6,2},{7,3},{8,12},{9,13},{10,... | collective-permute-start | bytes 393224 | tf_op jit(solution)/shard_map/ppermute | solution.py:17
  14.0 12.0 %collective-permute-start.7 = (bf16[128,512]{1,0:T(8,128)(2,1)S(1)}, bf16[128,512]{1,0:T(8,128)(2,1)S(1)}, u32[]{:S(2)}, u32[]{:S(2)}) collective-permute-start(bf16[128,512]{1,0:T(8,128)(2,1)S(1)} %get-tuple-element.36), channel_id=1, source_target_pairs={{0,8},{1,9},{2,10},{3,11},{4,12},{5,13},{6,14},{7,15},{8,0},{9,1},... | collective-permute-start | bytes 393224 | tf_op jit(solution)/shard_map/ppermute | solution.py:17
  16.9 9.1 %collective-permute-start.8 = (bf16[128,512]{1,0:T(8,128)(2,1)S(1)}, bf16[128,512]{1,0:T(8,128)(2,1)S(1)}, u32[]{:S(2)}, u32[]{:S(2)}) collective-permute-start(bf16[128,512]{1,0:T(8,128)(2,1)S(1)} %get-tuple-element.37), channel_id=1, source_target_pairs={{0,12},{1,13},{2,14},{3,15},{4,8},{5,9},{6,10},{7,11},{8,4},{9,5},... | collective-permute-start | bytes 393224 | tf_op jit(solution)/shard_map/ppermute | solution.py:17
  17.2 1.5 %collective-permute-start.4 = (bf16[1024,96]{0,1:T(8,128)(2,1)S(1)}, bf16[1024,96]{0,1:T(8,128)(2,1)S(1)}, u32[]{:S(2)}, u32[]{:S(2)}) collective-permute-start(bf16[1024,96]{0,1:T(8,128)(2,1)S(1)} %constant_dynamic-update-slice_fusion), channel_id=1, source_target_pairs={{0,1},{1,0},{2,3},{3,2},{4,5},{5,4},{6,7},{7,6},{8,9},{9,8},{10,11... | collective-permute-start | bytes 589832 | tf_op jit(solution)/shard_map/ppermute | solution.py:17
  18.8 7.8 %copy-start.2 = (s32[1024]{0:T(1024)S(1)}, s32[1024]{0:T(1024)}, u32[]{:S(2)}) copy-start(s32[1024]{0:T(1024)} %param.7) | copy-start | bytes 12292
  19.5 7.0 %collective-permute-start.5 = (bf16[1024,96]{0,1:T(8,128)(2,1)S(1)}, bf16[1024,96]{0,1:T(8,128)(2,1)S(1)}, u32[]{:S(2)}, u32[]{:S(2)}) collective-permute-start(bf16[1024,96]{0,1:T(8,128)(2,1)S(1)} %get-tuple-element.97), channel_id=1, source_target_pairs={{0,16},{16,0},{1,17},{17,1},{2,18},{18,2},{3,19},{19,3},{4,20},{20... | collective-permute-start | bytes 589832 | tf_op jit(solution)/shard_map/ppermute | solution.py:17
  27.1 1.8 %collective-permute-start.9 = (f32[1024,96]{0,1:T(8,128)S(1)}, f32[1024,96]{0,1:T(8,128)S(1)}, u32[]{:S(2)}, u32[]{:S(2)}) collective-permute-start(f32[1024,96]{0,1:T(8,128)S(1)} %fusion.23), channel_id=1, source_target_pairs={{0,1},{1,0},{2,3},{3,2},{4,5},{5,4},{6,7},{7,6},{8,9},{9,8},{10,11... | collective-permute-start | bytes 1179656 | tf_op jit(solution)/shard_map/ppermute | solution.py:17
  29.0 4.9 %collective-permute-start.10 = (bf16[512,96]{0,1:T(8,128)(2,1)S(1)}, bf16[512,96]{0,1:T(8,128)(2,1)S(1)}, u32[]{:S(2)}, u32[]{:S(2)}) collective-permute-start(bf16[512,96]{0,1:T(8,128)(2,1)S(1)} %slice.333), channel_id=1, source_target_pairs={{0,2},{1,3},{2,0},{3,1},{4,6},{5,7},{6,4},{7,5},{8,10},{9,11},{10,... | collective-permute-start | bytes 294920 | tf_op jit(solution)/shard_map/ppermute | solution.py:17
  33.9 10.0 %collective-permute-start.12 = (bf16[512,96]{0,1:T(8,128)(2,1)S(1)}, bf16[512,96]{0,1:T(8,128)(2,1)S(1)}, u32[]{:S(2)}, u32[]{:S(2)}) collective-permute-start(bf16[512,96]{0,1:T(8,128)(2,1)S(1)} %fusion.19), channel_id=1, source_target_pairs={{0,8},{1,9},{2,10},{3,11},{4,12},{5,13},{6,14},{7,15},{8,0},{9,1},... | collective-permute-start | bytes 294920 | tf_op jit(solution)/shard_map/ppermute | solution.py:17
  36.5 7.5 %collective-permute-start.13 = (bf16[512,96]{0,1:T(8,128)(2,1)S(1)}, bf16[512,96]{0,1:T(8,128)(2,1)S(1)}, u32[]{:S(2)}, u32[]{:S(2)}) collective-permute-start(bf16[512,96]{0,1:T(8,128)(2,1)S(1)} %fusion.19), channel_id=1, source_target_pairs={{0,12},{1,13},{2,14},{3,15},{4,8},{5,9},{6,10},{7,11},{8,4},{9,5},... | collective-permute-start | bytes 294920 | tf_op jit(solution)/shard_map/ppermute | solution.py:17
  37.9 6.5 %collective-permute-start.11 = (bf16[512,96]{0,1:T(8,128)(2,1)S(1)}, bf16[512,96]{0,1:T(8,128)(2,1)S(1)}, u32[]{:S(2)}, u32[]{:S(2)}) collective-permute-start(bf16[512,96]{0,1:T(8,128)(2,1)S(1)} %fusion.19), channel_id=1, source_target_pairs={{0,4},{1,5},{2,6},{3,7},{4,0},{5,1},{6,2},{7,3},{8,12},{9,13},{10,... | collective-permute-start | bytes 294920 | tf_op jit(solution)/shard_map/ppermute | solution.py:17
  44.8 1.4 %collective-permute-start.14 = (f32[256,96]{0,1:T(8,128)S(1)}, f32[256,96]{0,1:T(8,128)S(1)}, u32[]{:S(2)}, u32[]{:S(2)}) collective-permute-start(f32[256,96]{0,1:T(8,128)S(1)} %slice.245), channel_id=1, source_target_pairs={{0,1},{1,0},{2,3},{3,2},{4,5},{5,4},{6,7},{7,6},{8,9},{9,8},{10,11... | collective-permute-start | bytes 294920 | tf_op jit(solution)/shard_map/ppermute | solution.py:17
  46.2 4.2 %collective-permute-start.15 = (bf16[256,96]{0,1:T(8,128)(2,1)S(1)}, bf16[256,96]{0,1:T(8,128)(2,1)S(1)}, u32[]{:S(2)}, u32[]{:S(2)}) collective-permute-start(bf16[256,96]{0,1:T(8,128)(2,1)S(1)} %pad_maximum_fusion.6), channel_id=1, source_target_pairs={{0,2},{1,3},{2,0},{3,1},{4,6},{5,7},{6,4},{7,5},{8,10},{9,11},{10,... | collective-permute-start | bytes 147464 | tf_op jit(solution)/shard_map/ppermute | solution.py:17
  50.4 8.8 %collective-permute-start.18 = (bf16[256,96]{0,1:T(8,128)(2,1)S(1)}, bf16[256,96]{0,1:T(8,128)(2,1)S(1)}, u32[]{:S(2)}, u32[]{:S(2)}) collective-permute-start(bf16[256,96]{0,1:T(8,128)(2,1)S(1)} %get-tuple-element.53), channel_id=1, source_target_pairs={{0,12},{1,13},{2,14},{3,15},{4,8},{5,9},{6,10},{7,11},{8,4},{9,5},... | collective-permute-start | bytes 147464 | tf_op jit(solution)/shard_map/ppermute | solution.py:17
  53.6 5.5 %collective-permute-start.17 = (bf16[256,96]{0,1:T(8,128)(2,1)S(1)}, bf16[256,96]{0,1:T(8,128)(2,1)S(1)}, u32[]{:S(2)}, u32[]{:S(2)}) collective-permute-start(bf16[256,96]{0,1:T(8,128)(2,1)S(1)} %get-tuple-element.53), channel_id=1, source_target_pairs={{0,8},{1,9},{2,10},{3,11},{4,12},{5,13},{6,14},{7,15},{8,0},{9,1},... | collective-permute-start | bytes 147464 | tf_op jit(solution)/shard_map/ppermute | solution.py:17
  53.9 4.1 %collective-permute-start.16 = (bf16[256,96]{0,1:T(8,128)(2,1)S(1)}, bf16[256,96]{0,1:T(8,128)(2,1)S(1)}, u32[]{:S(2)}, u32[]{:S(2)}) collective-permute-start(bf16[256,96]{0,1:T(8,128)(2,1)S(1)} %get-tuple-element.53), channel_id=1, source_target_pairs={{0,4},{1,5},{2,6},{3,7},{4,0},{5,1},{6,2},{7,3},{8,12},{9,13},{10,... | collective-permute-start | bytes 147464 | tf_op jit(solution)/shard_map/ppermute | solution.py:17
  59.3 1.5 %collective-permute-start.19 = (bf16[1024,96]{0,1:T(8,128)(2,1)S(1)}, bf16[1024,96]{0,1:T(8,128)(2,1)S(1)}, u32[]{:S(2)}, u32[]{:S(2)}) collective-permute-start(bf16[1024,96]{0,1:T(8,128)(2,1)S(1)} %constant_dynamic-update-slice_fusion.2), channel_id=1, source_target_pairs={{0,1},{1,0},{2,3},{3,2},{4,5},{5,4},{6,7},{7,6},{8,9},{9,8},{10,11... | collective-permute-start | bytes 589832 | tf_op jit(solution)/shard_map/ppermute | solution.py:17
  61.6 7.0 %collective-permute-start.20 = (bf16[1024,96]{0,1:T(8,128)(2,1)S(1)}, bf16[1024,96]{0,1:T(8,128)(2,1)S(1)}, u32[]{:S(2)}, u32[]{:S(2)}) collective-permute-start(bf16[1024,96]{0,1:T(8,128)(2,1)S(1)} %get-tuple-element.99), channel_id=1, source_target_pairs={{0,16},{16,0},{1,17},{17,1},{2,18},{18,2},{3,19},{19,3},{4,20},{20... | collective-permute-start | bytes 589832 | tf_op jit(solution)/shard_map/ppermute | solution.py:167
  69.1 1.8 %collective-permute-start.21 = (f32[1024,96]{0,1:T(8,128)S(1)}, f32[1024,96]{0,1:T(8,128)S(1)}, u32[]{:S(2)}, u32[]{:S(2)}) collective-permute-start(f32[1024,96]{0,1:T(8,128)S(1)} %fusion.33), channel_id=1, source_target_pairs={{0,1},{1,0},{2,3},{3,2},{4,5},{5,4},{6,7},{7,6},{8,9},{9,8},{10,11... | collective-permute-start | bytes 1179656 | tf_op jit(solution)/shard_map/ppermute | solution.py:17
  70.9 4.9 %collective-permute-start.22 = (bf16[512,96]{0,1:T(8,128)(2,1)S(1)}, bf16[512,96]{0,1:T(8,128)(2,1)S(1)}, u32[]{:S(2)}, u32[]{:S(2)}) collective-permute-start(bf16[512,96]{0,1:T(8,128)(2,1)S(1)} %slice.332), channel_id=1, source_target_pairs={{0,2},{1,3},{2,0},{3,1},{4,6},{5,7},{6,4},{7,5},{8,10},{9,11},{10,... | collective-permute-start | bytes 294920 | tf_op jit(solution)/shard_map/ppermute | solution.py:17
  75.9 9.7 %collective-permute-start.24 = (bf16[512,96]{0,1:T(8,128)(2,1)S(1)}, bf16[512,96]{0,1:T(8,128)(2,1)S(1)}, u32[]{:S(2)}, u32[]{:S(2)}) collective-permute-start(bf16[512,96]{0,1:T(8,128)(2,1)S(1)} %fusion.20), channel_id=1, source_target_pairs={{0,8},{1,9},{2,10},{3,11},{4,12},{5,13},{6,14},{7,15},{8,0},{9,1},... | collective-permute-start | bytes 294920 | tf_op jit(solution)/shard_map/ppermute | solution.py:17
  77.5 8.1 %collective-permute-start.25 = (bf16[512,96]{0,1:T(8,128)(2,1)S(1)}, bf16[512,96]{0,1:T(8,128)(2,1)S(1)}, u32[]{:S(2)}, u32[]{:S(2)}) collective-permute-start(bf16[512,96]{0,1:T(8,128)(2,1)S(1)} %fusion.20), channel_id=1, source_target_pairs={{0,12},{1,13},{2,14},{3,15},{4,8},{5,9},{6,10},{7,11},{8,4},{9,5},... | collective-permute-start | bytes 294920 | tf_op jit(solution)/shard_map/ppermute | solution.py:17
  78.6 7.2 %collective-permute-start.23 = (bf16[512,96]{0,1:T(8,128)(2,1)S(1)}, bf16[512,96]{0,1:T(8,128)(2,1)S(1)}, u32[]{:S(2)}, u32[]{:S(2)}) collective-permute-start(bf16[512,96]{0,1:T(8,128)(2,1)S(1)} %fusion.20), channel_id=1, source_target_pairs={{0,4},{1,5},{2,6},{3,7},{4,0},{5,1},{6,2},{7,3},{8,12},{9,13},{10,... | collective-permute-start | bytes 294920 | tf_op jit(solution)/shard_map/ppermute | solution.py:17
  86.3 1.4 %collective-permute-start.26 = (f32[256,96]{0,1:T(8,128)S(1)}, f32[256,96]{0,1:T(8,128)S(1)}, u32[]{:S(2)}, u32[]{:S(2)}) collective-permute-start(f32[256,96]{0,1:T(8,128)S(1)} %slice.271), channel_id=1, source_target_pairs={{0,1},{1,0},{2,3},{3,2},{4,5},{5,4},{6,7},{7,6},{8,9},{9,8},{10,11... | collective-permute-start | bytes 294920 | tf_op jit(solution)/shard_map/ppermute | solution.py:17
  87.7 4.2 %collective-permute-start.27 = (bf16[256,96]{0,1:T(8,128)(2,1)S(1)}, bf16[256,96]{0,1:T(8,128)(2,1)S(1)}, u32[]{:S(2)}, u32[]{:S(2)}) collective-permute-start(bf16[256,96]{0,1:T(8,128)(2,1)S(1)} %pad_maximum_fusion.7), channel_id=1, source_target_pairs={{0,2},{1,3},{2,0},{3,1},{4,6},{5,7},{6,4},{7,5},{8,10},{9,11},{10,... | collective-permute-start | bytes 147464 | tf_op jit(solution)/shard_map/ppermute | solution.py:17
  91.9 7.8 %collective-permute-start.30 = (bf16[256,96]{0,1:T(8,128)(2,1)S(1)}, bf16[256,96]{0,1:T(8,128)(2,1)S(1)}, u32[]{:S(2)}, u32[]{:S(2)}) collective-permute-start(bf16[256,96]{0,1:T(8,128)(2,1)S(1)} %get-tuple-element.49), channel_id=1, source_target_pairs={{0,12},{1,13},{2,14},{3,15},{4,8},{5,9},{6,10},{7,11},{8,4},{9,5},... | collective-permute-start | bytes 147464 | tf_op jit(solution)/shard_map/ppermute | solution.py:17
  94.2 5.5 %collective-permute-start.29 = (bf16[256,96]{0,1:T(8,128)(2,1)S(1)}, bf16[256,96]{0,1:T(8,128)(2,1)S(1)}, u32[]{:S(2)}, u32[]{:S(2)}) collective-permute-start(bf16[256,96]{0,1:T(8,128)(2,1)S(1)} %get-tuple-element.49), channel_id=1, source_target_pairs={{0,8},{1,9},{2,10},{3,11},{4,12},{5,13},{6,14},{7,15},{8,0},{9,1},... | collective-permute-start | bytes 147464 | tf_op jit(solution)/shard_map/ppermute | solution.py:17
  95.1 4.3 %collective-permute-start.28 = (bf16[256,96]{0,1:T(8,128)(2,1)S(1)}, bf16[256,96]{0,1:T(8,128)(2,1)S(1)}, u32[]{:S(2)}, u32[]{:S(2)}) collective-permute-start(bf16[256,96]{0,1:T(8,128)(2,1)S(1)} %get-tuple-element.49), channel_id=1, source_target_pairs={{0,4},{1,5},{2,6},{3,7},{4,0},{5,1},{6,2},{7,3},{8,12},{9,13},{10,... | collective-permute-start | bytes 147464 | tf_op jit(solution)/shard_map/ppermute | solution.py:17
  99.8 1.5 %collective-permute-start.31 = (bf16[1024,96]{0,1:T(8,128)(2,1)S(1)}, bf16[1024,96]{0,1:T(8,128)(2,1)S(1)}, u32[]{:S(2)}, u32[]{:S(2)}) collective-permute-start(bf16[1024,96]{0,1:T(8,128)(2,1)S(1)} %constant_dynamic-update-slice_fusion.10), channel_id=1, source_target_pairs={{0,1},{1,0},{2,3},{3,2},{4,5},{5,4},{6,7},{7,6},{8,9},{9,8},{10,11... | collective-permute-start | bytes 589832 | tf_op jit(solution)/shard_map/ppermute | solution.py:17
  102.1 4.4 %copy-start.1 = (f32[128,96]{0,1:T(8,128)S(1)}, f32[128,96]{0,1:T(8,128)}, u32[]{:S(2)}) copy-start(f32[128,96]{0,1:T(8,128)} %param.5) | copy-start | bytes 147460
  102.3 11.1 %copy-start = (f32[1024,96]{0,1:T(8,128)}, f32[1024,96]{0,1:T(8,128)S(1)}, u32[]{:S(2)}) copy-start(f32[1024,96]{0,1:T(8,128)S(1)} %fusion.1) | copy-start | bytes 1179652
  103.1 9.8 %all-to-all-start = ((f32[16,1,96]{2,1,0:T(1,128)}), f32[16,1,96]{2,1,0:T(1,128)S(1)}, u32[]{:S(2)}, u32[]{:S(2)}) async-start(f32[16,1,96]{2,1,0:T(1,128)} %broadcast_in_dim.23), calls=%async_computation | async-start | bytes 16384 | tf_op jit(solution)/shard_map/all_to_all | solution.py:179

commit v7 on v6

--- a/solution.py
+++ b/solution.py
@@ -115,6 +115,7 @@
     targets = (labels[:, None] == jnp.arange(classes, dtype=jnp.int32)[None, :]).astype(WIDE)
     if nfeat == 2:
         fit_high, fit_rest = split(fitted)
+        fit_high, inverse = tied(fit_high, inverse)
         fit_high, inverse_low = tied(swapped(fit_high, "feat", 1), inverse_low)
         incoming = (targets - fitted) - fit_high.astype(WIDE)
     else:
@@ -122,6 +123,9 @@
             fitted = fitted + swapped(fitted, "feat", bit)
         incoming = targets - fitted
     incoming_low = incoming.astype(LOW)
+
+    own_rest = split(picked(inverse, [z + q for q in quad for z in near[:1]], 1))[1]
+    inverse_low = jnp.concatenate([inverse_low, own_rest], axis=0)
 
     contract = (((0,), (0,)), ((), ()))
     along = [(i, (i + 1) % nfeat) for i in range(nfeat)]
@@ -131,8 +135,8 @@
     for turn in range(nfeat):
         send = lax.dot_general(sending, incoming_low, contract, preferred_element_type=WIDE)
         grad = lax.dot_general(keeping, incoming_low, contract, preferred_element_type=WIDE)
-        grad, got = tied(grad, swapped(send, "rows", 1))
-        grad = grad + got
+        grad, got = tied(grad, swapped(send.astype(LOW), "rows", 1))
+        grad = grad + got.astype(WIDE)
         keep, send = halved(grad)
         got = swapped(send.astype(LOW), "rows", 2)
         grad = keep + got.astype(WIDE)
@@ -148,7 +152,7 @@
             grad = grad + jnp.concatenate(
                 [got[(slot ^ step) * own:((slot ^ step) + 1) * own] for slot in range(outer)], axis=0
             )
-        pair = jnp.concatenate(split(grad), axis=1)
+        pair = jnp.concatenate(split(jnp.concatenate([grad, grad[:own]], axis=0)), axis=1)
         part = lax.dot_general(inverse_low, pair, contract, preferred_element_type=WIDE)
         part = part[:, :classes] + part[:, classes:]
         keep, send = halved(part)

time: 114 us -> 113 us (level)
  waiting for transfers between devices: 59.8 us -> 58.2 us
    ppermute x31, waiting for transfers between devices: 48.7 us -> 47 us  [swapped(): return lax.ppermute(shard, axis, [(i, i ^ bit) for i in range(peers)])]
where the time goes in v7:
time: 113 us
  waiting for transfers between devices  58.2 us (52%)
  starting transfers between devices  37.7 us (33%)
  matrix products  7.3 us (6%)
  local copies, waits for them, and re-layouts  3.29 us (3%)
  other arithmetic  2.95 us (3%)
  Pallas kernels  2.41 us (2%)
  between operations  1.16 us (1%)
    ppermute x31, waiting for transfers between devices, swapped(): return lax.ppermute(shard, axis, [(i, i ^ bit) for i in range(peers)])  47 us
    ppermute x31, starting transfers between devices, swapped(): return lax.ppermute(shard, axis, [(i, i ^ bit) for i in range(peers)])  32.7 us
    all_to_all x1, waiting for transfers between devices, on_device(): lax.all_to_all(jnp.broadcast_to(squares[None], (nrows, 1, classes)), 'row...  5.73 us
    ppermute x1, waiting for transfers between devices, on_device(): got = lax.ppermute(sent.astype(LOW), 'feat', along).astype(WIDE)  5.45 us
    all_to_all x1, starting transfers between devices, on_device(): lax.all_to_all(jnp.broadcast_to(squares[None], (nrows, 1, classes)), 'row...  3.48 us
    pallas_call x1, Pallas kernels, reordered(): pl.pallas_call(functools.partial(reorder_kernel, order, own), out_shape=[...  2.41 us
    dot_general x3, matrix products, product(): return first + jnp.dot(sending, far, preferred_element_type=WIDE)  2.36 us
    dot_general x3, matrix products, product(): first, far = tied(jnp.dot(keeping, rows, preferred_element_type=WIDE), far)  2.33 us
  transfers between devices with their start and end apart: 33, of which 24 were waited for; matrix products, arithmetic and copies ran while one was open for 6% of the time, Pallas kernels for 2%

profile of v7, /device:TPU:0, one launch (start us, length us, event | category | flops | bytes accessed | tf_op | source)
XLA Modules:
  0.0 113.0 jit_solution(17549218080037222478)
XLA Ops:
  0.6 0.8 convert_element_type.108
  1.4 5.0 %collective-permute-start.2 = (bf16[128,96]{0,1:T(8,128)(2,1)S(1)}, bf16[128,96]{0,1:T(8,128)(2,1)S(1)}, u32[]{:S(2)}, u32[]{:S(2)}) collective-permute-start(bf16[128,96]{0,1:T(8,128)(2,1)S(1)} %convert_element_type.108), channel_id=1, source_target_pairs={{0,12},{1,13},{2,14},{3,15},{4,8},{5,9},{6,10},{7,11},{8,4},{9,5},... | collective-permute-start | bytes 73736 | tf_op jit(solution)/shard_map/ppermute | solution.py:17
  7.1 1.3 %dynamic-slice_convert_fusion.3 = (bf16[128,128]{1,0:T(8,128)(2,1)S(1)}, bf16[128,128]{1,0:T(8,128)(2,1)S(1)}, bf16[128,128]{1,0:T(8,128)(2,1)S(1)}, bf16[128,12...) fusion(f32[128,2048]{1,0:T(8,128)} %param.6, ...), kind=kLoop, calls=%fused_computation.66 | loop fusion | bytes 1048640 | tf_op jit(solution)/shard_map/convert.10
  8.5 2.4 %shard_map.67 = (bf16[1024,1024]{1,0:T(8,128)(2,1)S(1)}, bf16[1024,1024]{1,0:T(8,128)(2,1)S(1)}) custom-call(s32[1]{0:T(128)} %bitcast.me_ref, bf16[1024,2048]{1,0:T(8,128)(2,1)} %given.1), custom_call_target="tpu_custom_call" | custom-call | bytes 8388608 | tf_op jit(solution)/shard_map/pallas_call | solution.py:58
  11.2 1.6 %collective-permute-start.3 = (bf16[512,96]{0,1:T(8,128)(2,1)S(1)}, bf16[512,96]{0,1:T(8,128)(2,1)S(1)}, u32[]{:S(2)}, u32[]{:S(2)}) collective-permute-start(bf16[512,96]{0,1:T(8,128)(2,1)S(1)} %pad_maximum_fusion.10), channel_id=1, source_target_pairs={{0,2},{1,3},{2,0},{3,1},{4,6},{5,7},{6,4},{7,5},{8,10},{9,11},{10,... | collective-permute-start | bytes 294920 | tf_op jit(solution)/shard_map/ppermute | solution.py:17
  12.8 1.2 %collective-permute-start.6 = (bf16[128,512]{1,0:T(8,128)(2,1)S(1)}, bf16[128,512]{1,0:T(8,128)(2,1)S(1)}, u32[]{:S(2)}, u32[]{:S(2)}) collective-permute-start(bf16[128,512]{1,0:T(8,128)(2,1)S(1)} %get-tuple-element.38), channel_id=1, source_target_pairs={{0,4},{1,5},{2,6},{3,7},{4,0},{5,1},{6,2},{7,3},{8,12},{9,13},{10,... | collective-permute-start | bytes 393224 | tf_op jit(solution)/shard_map/ppermute | solution.py:17
  14.0 2.9 %collective-permute-start.7 = (bf16[128,512]{1,0:T(8,128)(2,1)S(1)}, bf16[128,512]{1,0:T(8,128)(2,1)S(1)}, u32[]{:S(2)}, u32[]{:S(2)}) collective-permute-start(bf16[128,512]{1,0:T(8,128)(2,1)S(1)} %get-tuple-element.39), channel_id=1, source_target_pairs={{0,8},{1,9},{2,10},{3,11},{4,12},{5,13},{6,14},{7,15},{8,0},{9,1},... | collective-permute-start | bytes 393224 | tf_op jit(solution)/shard_map/ppermute | solution.py:17
  17.3 0.8 fusion.44
  18.1 0.6 collective-permute-done.4
  18.8 0.8 reduce-precision_convert_fusion
  19.5 1.6 %collective-permute-start.5 = (bf16[1024,96]{0,1:T(8,128)(2,1)S(1)}, bf16[1024,96]{0,1:T(8,128)(2,1)S(1)}, u32[]{:S(2)}, u32[]{:S(2)}) collective-permute-start(bf16[1024,96]{0,1:T(8,128)(2,1)S(1)} %get-tuple-element.36), channel_id=1, source_target_pairs={{0,16},{16,0},{1,17},{17,1},{2,18},{18,2},{3,19},{19,3},{4,20},{20... | collective-permute-start | bytes 589832 | tf_op jit(solution)/shard_map/ppermute | solution.py:17
  21.1 4.9 %collective-permute-done.7 = bf16[128,512]{1,0:T(8,128)(2,1)S(1)} collective-permute-done((bf16[128,512]{1,0:T(8,128)(2,1)S(1)}, bf16[128,512]{1,0:T(8,128)(2,1)S(1)}, u32[]{:S(2)}, u32[]{:S(2)}) %collective-permute-start.7) | collective-permute-done | bytes 131104 | tf_op jit(solution)/shard_map/ppermute | solution.py:17
  27.7 0.9 collective-permute-done.9
  29.3 1.0 constant_dynamic-slice_fusion.3
  30.2 3.4 %collective-permute-done.10 = bf16[512,96]{0,1:T(8,128)(2,1)S(1)} collective-permute-done((bf16[512,96]{0,1:T(8,128)(2,1)S(1)}, bf16[512,96]{0,1:T(8,128)(2,1)S(1)}, u32[]{:S(2)}, u32[]{:S(2)}) %collective-permute-start.10) | collective-permute-done | bytes 98336 | tf_op jit(solution)/shard_map/ppermute | solution.py:17
  33.6 2.5 %collective-permute-start.12 = (bf16[512,96]{0,1:T(8,128)(2,1)S(1)}, bf16[512,96]{0,1:T(8,128)(2,1)S(1)}, u32[]{:S(2)}, u32[]{:S(2)}) collective-permute-start(bf16[512,96]{0,1:T(8,128)(2,1)S(1)} %fusion.20), channel_id=1, source_target_pairs={{0,8},{1,9},{2,10},{3,11},{4,12},{5,13},{6,14},{7,15},{8,0},{9,1},... | collective-permute-start | bytes 294920 | tf_op jit(solution)/shard_map/ppermute | solution.py:17
  36.2 1.5 %collective-permute-start.13 = (bf16[512,96]{0,1:T(8,128)(2,1)S(1)}, bf16[512,96]{0,1:T(8,128)(2,1)S(1)}, u32[]{:S(2)}, u32[]{:S(2)}) collective-permute-start(bf16[512,96]{0,1:T(8,128)(2,1)S(1)} %fusion.20), channel_id=1, source_target_pairs={{0,12},{1,13},{2,14},{3,15},{4,8},{5,9},{6,10},{7,11},{8,4},{9,5},... | collective-permute-start | bytes 294920 | tf_op jit(solution)/shard_map/ppermute | solution.py:17
  38.0 5.6 %collective-permute-done.12 = bf16[512,96]{0,1:T(8,128)(2,1)S(1)} collective-permute-done((bf16[512,96]{0,1:T(8,128)(2,1)S(1)}, bf16[512,96]{0,1:T(8,128)(2,1)S(1)}, u32[]{:S(2)}, u32[]{:S(2)}) %collective-permute-start.12) | collective-permute-done | bytes 98336 | tf_op jit(solution)/shard_map/ppermute | solution.py:17
  44.6 1.3 %collective-permute-done.14 = f32[256,96]{0,1:T(8,128)S(1)} collective-permute-done((f32[256,96]{0,1:T(8,128)S(1)}, f32[256,96]{0,1:T(8,128)S(1)}, u32[]{:S(2)}, u32[]{:S(2)}) %collective-permute-start.14) | collective-permute-done | bytes 98336 | tf_op jit(solution)/shard_map/ppermute | solution.py:17
  46.5 3.6 %collective-permute-done.15 = bf16[256,96]{0,1:T(8,128)(2,1)S(1)} collective-permute-done((bf16[256,96]{0,1:T(8,128)(2,1)S(1)}, bf16[256,96]{0,1:T(8,128)(2,1)S(1)}, u32[]{:S(2)}, u32[]{:S(2)}) %collective-permute-start.15) | collective-permute-done | bytes 49184 | tf_op jit(solution)/shard_map/ppermute | solution.py:17
  50.1 3.3 %collective-permute-start.18 = (bf16[256,96]{0,1:T(8,128)(2,1)S(1)}, bf16[256,96]{0,1:T(8,128)(2,1)S(1)}, u32[]{:S(2)}, u32[]{:S(2)}) collective-permute-start(bf16[256,96]{0,1:T(8,128)(2,1)S(1)} %get-tuple-element.55), channel_id=1, source_target_pairs={{0,12},{1,13},{2,14},{3,15},{4,8},{5,9},{6,10},{7,11},{8,4},{9,5},... | collective-permute-start | bytes 147464 | tf_op jit(solution)/shard_map/ppermute | solution.py:17
  53.7 0.9 collective-permute-start.16
  54.6 3.2 %collective-permute-done.16 = bf16[256,96]{0,1:T(8,128)(2,1)S(1)} collective-permute-done((bf16[256,96]{0,1:T(8,128)(2,1)S(1)}, bf16[256,96]{0,1:T(8,128)(2,1)S(1)}, u32[]{:S(2)}, u32[]{:S(2)}) %collective-permute-start.16) | collective-permute-done | bytes 49184 | tf_op jit(solution)/shard_map/ppermute | solution.py:17
  57.8 1.1 %collective-permute-done.17 = bf16[256,96]{0,1:T(8,128)(2,1)S(1)} collective-permute-done((bf16[256,96]{0,1:T(8,128)(2,1)S(1)}, bf16[256,96]{0,1:T(8,128)(2,1)S(1)}, u32[]{:S(2)}, u32[]{:S(2)}) %collective-permute-start.17) | collective-permute-done | bytes 49184 | tf_op jit(solution)/shard_map/ppermute | solution.py:17
  59.1 0.8 fusion.45
  59.9 0.6 collective-permute-done.19
  60.5 0.8 fusion.5
  61.4 1.6 %collective-permute-start.20 = (bf16[1024,96]{0,1:T(8,128)(2,1)S(1)}, bf16[1024,96]{0,1:T(8,128)(2,1)S(1)}, u32[]{:S(2)}, u32[]{:S(2)}) collective-permute-start(bf16[1024,96]{0,1:T(8,128)(2,1)S(1)} %get-tuple-element.107), channel_id=1, source_target_pairs={{0,16},{16,0},{1,17},{17,1},{2,18},{18,2},{3,19},{19,3},{4,20},{20... | collective-permute-start | bytes 589832 | tf_op jit(solution)/shard_map/ppermute | solution.py:171
  62.9 5.4 %collective-permute-done.20 = bf16[1024,96]{0,1:T(8,128)(2,1)S(1)} collective-permute-done((bf16[1024,96]{0,1:T(8,128)(2,1)S(1)}, bf16[1024,96]{0,1:T(8,128)(2,1)S(1)}, u32[]{:S(2)}, u32[]{:S(2)}) %collective-permute-start.20) | collective-permute-done | bytes 196640 | tf_op jit(solution)/shard_map/ppermute | solution.py:171
  69.5 0.9 collective-permute-done.21
  71.0 4.3 %collective-permute-done.22 = bf16[512,96]{0,1:T(8,128)(2,1)S(1)} collective-permute-done((bf16[512,96]{0,1:T(8,128)(2,1)S(1)}, bf16[512,96]{0,1:T(8,128)(2,1)S(1)}, u32[]{:S(2)}, u32[]{:S(2)}) %collective-permute-start.22) | collective-permute-done | bytes 98336 | tf_op jit(solution)/shard_map/ppermute | solution.py:17
  75.4 1.6 %collective-permute-start.24 = (bf16[512,96]{0,1:T(8,128)(2,1)S(1)}, bf16[512,96]{0,1:T(8,128)(2,1)S(1)}, u32[]{:S(2)}, u32[]{:S(2)}) collective-permute-start(bf16[512,96]{0,1:T(8,128)(2,1)S(1)} %fusion.21), channel_id=1, source_target_pairs={{0,8},{1,9},{2,10},{3,11},{4,12},{5,13},{6,14},{7,15},{8,0},{9,1},... | collective-permute-start | bytes 294920 | tf_op jit(solution)/shard_map/ppermute | solution.py:17
  77.0 1.2 %collective-permute-start.25 = (bf16[512,96]{0,1:T(8,128)(2,1)S(1)}, bf16[512,96]{0,1:T(8,128)(2,1)S(1)}, u32[]{:S(2)}, u32[]{:S(2)}) collective-permute-start(bf16[512,96]{0,1:T(8,128)(2,1)S(1)} %fusion.21), channel_id=1, source_target_pairs={{0,12},{1,13},{2,14},{3,15},{4,8},{5,9},{6,10},{7,11},{8,4},{9,5},... | collective-permute-start | bytes 294920 | tf_op jit(solution)/shard_map/ppermute | solution.py:17
  78.1 0.8 collective-permute-start.23
  78.9 6.2 %collective-permute-done.24 = bf16[512,96]{0,1:T(8,128)(2,1)S(1)} collective-permute-done((bf16[512,96]{0,1:T(8,128)(2,1)S(1)}, bf16[512,96]{0,1:T(8,128)(2,1)S(1)}, u32[]{:S(2)}, u32[]{:S(2)}) %collective-permute-start.24) | collective-permute-done | bytes 98336 | tf_op jit(solution)/shard_map/ppermute | solution.py:17
  86.0 1.3 %collective-permute-done.26 = f32[256,96]{0,1:T(8,128)S(1)} collective-permute-done((f32[256,96]{0,1:T(8,128)S(1)}, f32[256,96]{0,1:T(8,128)S(1)}, u32[]{:S(2)}, u32[]{:S(2)}) %collective-permute-start.26) | collective-permute-done | bytes 98336 | tf_op jit(solution)/shard_map/ppermute | solution.py:17
  87.9 3.6 %collective-permute-done.27 = bf16[256,96]{0,1:T(8,128)(2,1)S(1)} collective-permute-done((bf16[256,96]{0,1:T(8,128)(2,1)S(1)}, bf16[256,96]{0,1:T(8,128)(2,1)S(1)}, u32[]{:S(2)}, u32[]{:S(2)}) %collective-permute-start.27) | collective-permute-done | bytes 49184 | tf_op jit(solution)/shard_map/ppermute | solution.py:17
  91.5 2.2 %collective-permute-start.30 = (bf16[256,96]{0,1:T(8,128)(2,1)S(1)}, bf16[256,96]{0,1:T(8,128)(2,1)S(1)}, u32[]{:S(2)}, u32[]{:S(2)}) collective-permute-start(bf16[256,96]{0,1:T(8,128)(2,1)S(1)} %get-tuple-element.53), channel_id=1, source_target_pairs={{0,12},{1,13},{2,14},{3,15},{4,8},{5,9},{6,10},{7,11},{8,4},{9,5},... | collective-permute-start | bytes 147464 | tf_op jit(solution)/shard_map/ppermute | solution.py:17
  93.7 0.9 collective-permute-start.29
  94.7 1.3 %collective-permute-start.28 = (bf16[256,96]{0,1:T(8,128)(2,1)S(1)}, bf16[256,96]{0,1:T(8,128)(2,1)S(1)}, u32[]{:S(2)}, u32[]{:S(2)}) collective-permute-start(bf16[256,96]{0,1:T(8,128)(2,1)S(1)} %get-tuple-element.53), channel_id=1, source_target_pairs={{0,4},{1,5},{2,6},{3,7},{4,0},{5,1},{6,2},{7,3},{8,12},{9,13},{10,... | collective-permute-start | bytes 147464 | tf_op jit(solution)/shard_map/ppermute | solution.py:17
  96.0 3.1 %collective-permute-done.28 = bf16[256,96]{0,1:T(8,128)(2,1)S(1)} collective-permute-done((bf16[256,96]{0,1:T(8,128)(2,1)S(1)}, bf16[256,96]{0,1:T(8,128)(2,1)S(1)}, u32[]{:S(2)}, u32[]{:S(2)}) %collective-permute-start.28) | collective-permute-done | bytes 49184 | tf_op jit(solution)/shard_map/ppermute | solution.py:17
  99.4 0.8 fusion.46
  100.2 0.6 collective-permute-done.31
  100.9 0.8 fusion.47
  102.0 0.6 broadcast_in_dim.23
  102.6 3.5 %all-to-all-start = ((f32[16,1,96]{2,1,0:T(1,128)}), f32[16,1,96]{2,1,0:T(1,128)S(1)}, u32[]{:S(2)}, u32[]{:S(2)}) async-start(f32[16,1,96]{2,1,0:T(1,128)} %broadcast_in_dim.23), calls=%async_computation | async-start | bytes 16384 | tf_op jit(solution)/shard_map/all_to_all | solution.py:183
  106.1 0.6 fusion.26
  106.7 5.7 %all-to-all-done = f32[16,1,96]{2,1,0:T(1,128)S(1)} async-done(((f32[16,1,96]{2,1,0:T(1,128)}), f32[16,1,96]{2,1,0:T(1,128)S(1)}, u32[]{:S(2)}, u32[]{:S(2)}) %all-to-all-start) | async-done | bytes 6176 | tf_op jit(solution)/shard_map/all_to_all | solution.py:183
  (99 shorter events, 10.4 us)
Async XLA Ops:
  1.4 9.5 %collective-permute-start.2 = (bf16[128,96]{0,1:T(8,128)(2,1)S(1)}, bf16[128,96]{0,1:T(8,128)(2,1)S(1)}, u32[]{:S(2)}, u32[]{:S(2)}) collective-permute-start(bf16[128,96]{0,1:T(8,128)(2,1)S(1)} %convert_element_type.108), channel_id=1, source_target_pairs={{0,12},{1,13},{2,14},{3,15},{4,8},{5,9},{6,10},{7,11},{8,4},{9,5},... | collective-permute-start | bytes 73736 | tf_op jit(solution)/shard_map/ppermute | solution.py:17
  6.5 4.7 %collective-permute-start.1 = (bf16[128,96]{0,1:T(8,128)(2,1)S(1)}, bf16[128,96]{0,1:T(8,128)(2,1)S(1)}, u32[]{:S(2)}, u32[]{:S(2)}) collective-permute-start(bf16[128,96]{0,1:T(8,128)(2,1)S(1)} %convert_element_type.108), channel_id=1, source_target_pairs={{0,8},{1,9},{2,10},{3,11},{4,12},{5,13},{6,14},{7,15},{8,0},{9,1},... | collective-permute-start | bytes 73736 | tf_op jit(solution)/shard_map/ppermute | solution.py:17
  6.5 4.7 %collective-permute-start = (bf16[128,96]{0,1:T(8,128)(2,1)S(1)}, bf16[128,96]{0,1:T(8,128)(2,1)S(1)}, u32[]{:S(2)}, u32[]{:S(2)}) collective-permute-start(bf16[128,96]{0,1:T(8,128)(2,1)S(1)} %convert_element_type.108), channel_id=1, source_target_pairs={{0,4},{1,5},{2,6},{3,7},{4,0},{5,1},{6,2},{7,3},{8,12},{9,13},{10,... | collective-permute-start | bytes 73736 | tf_op jit(solution)/shard_map/ppermute | solution.py:17
  11.2 6.0 %collective-permute-start.3 = (bf16[512,96]{0,1:T(8,128)(2,1)S(1)}, bf16[512,96]{0,1:T(8,128)(2,1)S(1)}, u32[]{:S(2)}, u32[]{:S(2)}) collective-permute-start(bf16[512,96]{0,1:T(8,128)(2,1)S(1)} %pad_maximum_fusion.10), channel_id=1, source_target_pairs={{0,2},{1,3},{2,0},{3,1},{4,6},{5,7},{6,4},{7,5},{8,10},{9,11},{10,... | collective-permute-start | bytes 294920 | tf_op jit(solution)/shard_map/ppermute | solution.py:17
  12.8 8.3 %collective-permute-start.6 = (bf16[128,512]{1,0:T(8,128)(2,1)S(1)}, bf16[128,512]{1,0:T(8,128)(2,1)S(1)}, u32[]{:S(2)}, u32[]{:S(2)}) collective-permute-start(bf16[128,512]{1,0:T(8,128)(2,1)S(1)} %get-tuple-element.38), channel_id=1, source_target_pairs={{0,4},{1,5},{2,6},{3,7},{4,0},{5,1},{6,2},{7,3},{8,12},{9,13},{10,... | collective-permute-start | bytes 393224 | tf_op jit(solution)/shard_map/ppermute | solution.py:17
  14.0 12.0 %collective-permute-start.7 = (bf16[128,512]{1,0:T(8,128)(2,1)S(1)}, bf16[128,512]{1,0:T(8,128)(2,1)S(1)}, u32[]{:S(2)}, u32[]{:S(2)}) collective-permute-start(bf16[128,512]{1,0:T(8,128)(2,1)S(1)} %get-tuple-element.39), channel_id=1, source_target_pairs={{0,8},{1,9},{2,10},{3,11},{4,12},{5,13},{6,14},{7,15},{8,0},{9,1},... | collective-permute-start | bytes 393224 | tf_op jit(solution)/shard_map/ppermute | solution.py:17
  16.9 9.1 %collective-permute-start.8 = (bf16[128,512]{1,0:T(8,128)(2,1)S(1)}, bf16[128,512]{1,0:T(8,128)(2,1)S(1)}, u32[]{:S(2)}, u32[]{:S(2)}) collective-permute-start(bf16[128,512]{1,0:T(8,128)(2,1)S(1)} %get-tuple-element.40), channel_id=1, source_target_pairs={{0,12},{1,13},{2,14},{3,15},{4,8},{5,9},{6,10},{7,11},{8,4},{9,5},... | collective-permute-start | bytes 393224 | tf_op jit(solution)/shard_map/ppermute | solution.py:17
  17.2 1.5 %collective-permute-start.4 = (bf16[1024,96]{0,1:T(8,128)(2,1)S(1)}, bf16[1024,96]{0,1:T(8,128)(2,1)S(1)}, u32[]{:S(2)}, u32[]{:S(2)}) collective-permute-start(bf16[1024,96]{0,1:T(8,128)(2,1)S(1)} %constant_dynamic-update-slice_fusion), channel_id=1, source_target_pairs={{0,1},{1,0},{2,3},{3,2},{4,5},{5,4},{6,7},{7,6},{8,9},{9,8},{10,11... | collective-permute-start | bytes 589832 | tf_op jit(solution)/shard_map/ppermute | solution.py:17
  18.8 7.8 %copy-start.2 = (s32[1024]{0:T(1024)S(1)}, s32[1024]{0:T(1024)}, u32[]{:S(2)}) copy-start(s32[1024]{0:T(1024)} %param.7) | copy-start | bytes 12292
  19.5 7.0 %collective-permute-start.5 = (bf16[1024,96]{0,1:T(8,128)(2,1)S(1)}, bf16[1024,96]{0,1:T(8,128)(2,1)S(1)}, u32[]{:S(2)}, u32[]{:S(2)}) collective-permute-start(bf16[1024,96]{0,1:T(8,128)(2,1)S(1)} %get-tuple-element.36), channel_id=1, source_target_pairs={{0,16},{16,0},{1,17},{17,1},{2,18},{18,2},{3,19},{19,3},{4,20},{20... | collective-permute-start | bytes 589832 | tf_op jit(solution)/shard_map/ppermute | solution.py:17
  27.1 1.5 %collective-permute-start.9 = (bf16[1024,96]{0,1:T(8,128)(2,1)S(1)}, bf16[1024,96]{0,1:T(8,128)(2,1)S(1)}, u32[]{:S(2)}, u32[]{:S(2)}) collective-permute-start(bf16[1024,96]{0,1:T(8,128)(2,1)S(1)} %convolution_convert_fusion.1), channel_id=1, source_target_pairs={{0,1},{1,0},{2,3},{3,2},{4,5},{5,4},{6,7},{7,6},{8,9},{9,8},{10,11... | collective-permute-start | bytes 589832 | tf_op jit(solution)/shard_map/ppermute | solution.py:17
  28.7 4.9 %collective-permute-start.10 = (bf16[512,96]{0,1:T(8,128)(2,1)S(1)}, bf16[512,96]{0,1:T(8,128)(2,1)S(1)}, u32[]{:S(2)}, u32[]{:S(2)}) collective-permute-start(bf16[512,96]{0,1:T(8,128)(2,1)S(1)} %slice.343), channel_id=1, source_target_pairs={{0,2},{1,3},{2,0},{3,1},{4,6},{5,7},{6,4},{7,5},{8,10},{9,11},{10,... | collective-permute-start | bytes 294920 | tf_op jit(solution)/shard_map/ppermute | solution.py:17
  33.6 9.9 %collective-permute-start.12 = (bf16[512,96]{0,1:T(8,128)(2,1)S(1)}, bf16[512,96]{0,1:T(8,128)(2,1)S(1)}, u32[]{:S(2)}, u32[]{:S(2)}) collective-permute-start(bf16[512,96]{0,1:T(8,128)(2,1)S(1)} %fusion.20), channel_id=1, source_target_pairs={{0,8},{1,9},{2,10},{3,11},{4,12},{5,13},{6,14},{7,15},{8,0},{9,1},... | collective-permute-start | bytes 294920 | tf_op jit(solution)/shard_map/ppermute | solution.py:17
  36.2 7.4 %collective-permute-start.13 = (bf16[512,96]{0,1:T(8,128)(2,1)S(1)}, bf16[512,96]{0,1:T(8,128)(2,1)S(1)}, u32[]{:S(2)}, u32[]{:S(2)}) collective-permute-start(bf16[512,96]{0,1:T(8,128)(2,1)S(1)} %fusion.20), channel_id=1, source_target_pairs={{0,12},{1,13},{2,14},{3,15},{4,8},{5,9},{6,10},{7,11},{8,4},{9,5},... | collective-permute-start | bytes 294920 | tf_op jit(solution)/shard_map/ppermute | solution.py:17
  37.7 6.3 %collective-permute-start.11 = (bf16[512,96]{0,1:T(8,128)(2,1)S(1)}, bf16[512,96]{0,1:T(8,128)(2,1)S(1)}, u32[]{:S(2)}, u32[]{:S(2)}) collective-permute-start(bf16[512,96]{0,1:T(8,128)(2,1)S(1)} %fusion.20), channel_id=1, source_target_pairs={{0,4},{1,5},{2,6},{3,7},{4,0},{5,1},{6,2},{7,3},{8,12},{9,13},{10,... | collective-permute-start | bytes 294920 | tf_op jit(solution)/shard_map/ppermute | solution.py:17
  44.5 1.4 %collective-permute-start.14 = (f32[256,96]{0,1:T(8,128)S(1)}, f32[256,96]{0,1:T(8,128)S(1)}, u32[]{:S(2)}, u32[]{:S(2)}) collective-permute-start(f32[256,96]{0,1:T(8,128)S(1)} %slice.254), channel_id=1, source_target_pairs={{0,1},{1,0},{2,3},{3,2},{4,5},{5,4},{6,7},{7,6},{8,9},{9,8},{10,11... | collective-permute-start | bytes 294920 | tf_op jit(solution)/shard_map/ppermute | solution.py:17
  46.0 4.2 %collective-permute-start.15 = (bf16[256,96]{0,1:T(8,128)(2,1)S(1)}, bf16[256,96]{0,1:T(8,128)(2,1)S(1)}, u32[]{:S(2)}, u32[]{:S(2)}) collective-permute-start(bf16[256,96]{0,1:T(8,128)(2,1)S(1)} %pad_maximum_fusion.11), channel_id=1, source_target_pairs={{0,2},{1,3},{2,0},{3,1},{4,6},{5,7},{6,4},{7,5},{8,10},{9,11},{10,... | collective-permute-start | bytes 147464 | tf_op jit(solution)/shard_map/ppermute | solution.py:17
  50.1 8.8 %collective-permute-start.18 = (bf16[256,96]{0,1:T(8,128)(2,1)S(1)}, bf16[256,96]{0,1:T(8,128)(2,1)S(1)}, u32[]{:S(2)}, u32[]{:S(2)}) collective-permute-start(bf16[256,96]{0,1:T(8,128)(2,1)S(1)} %get-tuple-element.55), channel_id=1, source_target_pairs={{0,12},{1,13},{2,14},{3,15},{4,8},{5,9},{6,10},{7,11},{8,4},{9,5},... | collective-permute-start | bytes 147464 | tf_op jit(solution)/shard_map/ppermute | solution.py:17
  53.4 5.5 %collective-permute-start.17 = (bf16[256,96]{0,1:T(8,128)(2,1)S(1)}, bf16[256,96]{0,1:T(8,128)(2,1)S(1)}, u32[]{:S(2)}, u32[]{:S(2)}) collective-permute-start(bf16[256,96]{0,1:T(8,128)(2,1)S(1)} %get-tuple-element.55), channel_id=1, source_target_pairs={{0,8},{1,9},{2,10},{3,11},{4,12},{5,13},{6,14},{7,15},{8,0},{9,1},... | collective-permute-start | bytes 147464 | tf_op jit(solution)/shard_map/ppermute | solution.py:17
  53.7 4.1 %collective-permute-start.16 = (bf16[256,96]{0,1:T(8,128)(2,1)S(1)}, bf16[256,96]{0,1:T(8,128)(2,1)S(1)}, u32[]{:S(2)}, u32[]{:S(2)}) collective-permute-start(bf16[256,96]{0,1:T(8,128)(2,1)S(1)} %get-tuple-element.55), channel_id=1, source_target_pairs={{0,4},{1,5},{2,6},{3,7},{4,0},{5,1},{6,2},{7,3},{8,12},{9,13},{10,... | collective-permute-start | bytes 147464 | tf_op jit(solution)/shard_map/ppermute | solution.py:17
  59.0 1.5 %collective-permute-start.19 = (bf16[1024,96]{0,1:T(8,128)(2,1)S(1)}, bf16[1024,96]{0,1:T(8,128)(2,1)S(1)}, u32[]{:S(2)}, u32[]{:S(2)}) collective-permute-start(bf16[1024,96]{0,1:T(8,128)(2,1)S(1)} %constant_dynamic-update-slice_fusion.2), channel_id=1, source_target_pairs={{0,1},{1,0},{2,3},{3,2},{4,5},{5,4},{6,7},{7,6},{8,9},{9,8},{10,11... | collective-permute-start | bytes 589832 | tf_op jit(solution)/shard_map/ppermute | solution.py:17
  61.4 7.0 %collective-permute-start.20 = (bf16[1024,96]{0,1:T(8,128)(2,1)S(1)}, bf16[1024,96]{0,1:T(8,128)(2,1)S(1)}, u32[]{:S(2)}, u32[]{:S(2)}) collective-permute-start(bf16[1024,96]{0,1:T(8,128)(2,1)S(1)} %get-tuple-element.107), channel_id=1, source_target_pairs={{0,16},{16,0},{1,17},{17,1},{2,18},{18,2},{3,19},{19,3},{4,20},{20... | collective-permute-start | bytes 589832 | tf_op jit(solution)/shard_map/ppermute | solution.py:171
  68.9 1.5 %collective-permute-start.21 = (bf16[1024,96]{0,1:T(8,128)(2,1)S(1)}, bf16[1024,96]{0,1:T(8,128)(2,1)S(1)}, u32[]{:S(2)}, u32[]{:S(2)}) collective-permute-start(bf16[1024,96]{0,1:T(8,128)(2,1)S(1)} %convolution_convert_fusion), channel_id=1, source_target_pairs={{0,1},{1,0},{2,3},{3,2},{4,5},{5,4},{6,7},{7,6},{8,9},{9,8},{10,11... | collective-permute-start | bytes 589832 | tf_op jit(solution)/shard_map/ppermute | solution.py:17
  70.5 4.9 %collective-permute-start.22 = (bf16[512,96]{0,1:T(8,128)(2,1)S(1)}, bf16[512,96]{0,1:T(8,128)(2,1)S(1)}, u32[]{:S(2)}, u32[]{:S(2)}) collective-permute-start(bf16[512,96]{0,1:T(8,128)(2,1)S(1)} %slice.342), channel_id=1, source_target_pairs={{0,2},{1,3},{2,0},{3,1},{4,6},{5,7},{6,4},{7,5},{8,10},{9,11},{10,... | collective-permute-start | bytes 294920 | tf_op jit(solution)/shard_map/ppermute | solution.py:17
  75.4 9.7 %collective-permute-start.24 = (bf16[512,96]{0,1:T(8,128)(2,1)S(1)}, bf16[512,96]{0,1:T(8,128)(2,1)S(1)}, u32[]{:S(2)}, u32[]{:S(2)}) collective-permute-start(bf16[512,96]{0,1:T(8,128)(2,1)S(1)} %fusion.21), channel_id=1, source_target_pairs={{0,8},{1,9},{2,10},{3,11},{4,12},{5,13},{6,14},{7,15},{8,0},{9,1},... | collective-permute-start | bytes 294920 | tf_op jit(solution)/shard_map/ppermute | solution.py:17
  77.0 8.1 %collective-permute-start.25 = (bf16[512,96]{0,1:T(8,128)(2,1)S(1)}, bf16[512,96]{0,1:T(8,128)(2,1)S(1)}, u32[]{:S(2)}, u32[]{:S(2)}) collective-permute-start(bf16[512,96]{0,1:T(8,128)(2,1)S(1)} %fusion.21), channel_id=1, source_target_pairs={{0,12},{1,13},{2,14},{3,15},{4,8},{5,9},{6,10},{7,11},{8,4},{9,5},... | collective-permute-start | bytes 294920 | tf_op jit(solution)/shard_map/ppermute | solution.py:17
  78.1 7.2 %collective-permute-start.23 = (bf16[512,96]{0,1:T(8,128)(2,1)S(1)}, bf16[512,96]{0,1:T(8,128)(2,1)S(1)}, u32[]{:S(2)}, u32[]{:S(2)}) collective-permute-start(bf16[512,96]{0,1:T(8,128)(2,1)S(1)} %fusion.21), channel_id=1, source_target_pairs={{0,4},{1,5},{2,6},{3,7},{4,0},{5,1},{6,2},{7,3},{8,12},{9,13},{10,... | collective-permute-start | bytes 294920 | tf_op jit(solution)/shard_map/ppermute | solution.py:17
  85.9 1.4 %collective-permute-start.26 = (f32[256,96]{0,1:T(8,128)S(1)}, f32[256,96]{0,1:T(8,128)S(1)}, u32[]{:S(2)}, u32[]{:S(2)}) collective-permute-start(f32[256,96]{0,1:T(8,128)S(1)} %slice.281), channel_id=1, source_target_pairs={{0,1},{1,0},{2,3},{3,2},{4,5},{5,4},{6,7},{7,6},{8,9},{9,8},{10,11... | collective-permute-start | bytes 294920 | tf_op jit(solution)/shard_map/ppermute | solution.py:17
  87.3 4.2 %collective-permute-start.27 = (bf16[256,96]{0,1:T(8,128)(2,1)S(1)}, bf16[256,96]{0,1:T(8,128)(2,1)S(1)}, u32[]{:S(2)}, u32[]{:S(2)}) collective-permute-start(bf16[256,96]{0,1:T(8,128)(2,1)S(1)} %pad_maximum_fusion.12), channel_id=1, source_target_pairs={{0,2},{1,3},{2,0},{3,1},{4,6},{5,7},{6,4},{7,5},{8,10},{9,11},{10,... | collective-permute-start | bytes 147464 | tf_op jit(solution)/shard_map/ppermute | solution.py:17
  91.5 7.8 %collective-permute-start.30 = (bf16[256,96]{0,1:T(8,128)(2,1)S(1)}, bf16[256,96]{0,1:T(8,128)(2,1)S(1)}, u32[]{:S(2)}, u32[]{:S(2)}) collective-permute-start(bf16[256,96]{0,1:T(8,128)(2,1)S(1)} %get-tuple-element.53), channel_id=1, source_target_pairs={{0,12},{1,13},{2,14},{3,15},{4,8},{5,9},{6,10},{7,11},{8,4},{9,5},... | collective-permute-start | bytes 147464 | tf_op jit(solution)/shard_map/ppermute | solution.py:17
  93.7 5.5 %collective-permute-start.29 = (bf16[256,96]{0,1:T(8,128)(2,1)S(1)}, bf16[256,96]{0,1:T(8,128)(2,1)S(1)}, u32[]{:S(2)}, u32[]{:S(2)}) collective-permute-start(bf16[256,96]{0,1:T(8,128)(2,1)S(1)} %get-tuple-element.53), channel_id=1, source_target_pairs={{0,8},{1,9},{2,10},{3,11},{4,12},{5,13},{6,14},{7,15},{8,0},{9,1},... | collective-permute-start | bytes 147464 | tf_op jit(solution)/shard_map/ppermute | solution.py:17
  94.7 4.3 %collective-permute-start.28 = (bf16[256,96]{0,1:T(8,128)(2,1)S(1)}, bf16[256,96]{0,1:T(8,128)(2,1)S(1)}, u32[]{:S(2)}, u32[]{:S(2)}) collective-permute-start(bf16[256,96]{0,1:T(8,128)(2,1)S(1)} %get-tuple-element.53), channel_id=1, source_target_pairs={{0,4},{1,5},{2,6},{3,7},{4,0},{5,1},{6,2},{7,3},{8,12},{9,13},{10,... | collective-permute-start | bytes 147464 | tf_op jit(solution)/shard_map/ppermute | solution.py:17
  99.4 1.5 %collective-permute-start.31 = (bf16[1024,96]{0,1:T(8,128)(2,1)S(1)}, bf16[1024,96]{0,1:T(8,128)(2,1)S(1)}, u32[]{:S(2)}, u32[]{:S(2)}) collective-permute-start(bf16[1024,96]{0,1:T(8,128)(2,1)S(1)} %constant_dynamic-update-slice_fusion.10), channel_id=1, source_target_pairs={{0,1},{1,0},{2,3},{3,2},{4,5},{5,4},{6,7},{7,6},{8,9},{9,8},{10,11... | collective-permute-start | bytes 589832 | tf_op jit(solution)/shard_map/ppermute | solution.py:17
  101.6 4.5 %copy-start.1 = (f32[128,96]{0,1:T(8,128)S(1)}, f32[128,96]{0,1:T(8,128)}, u32[]{:S(2)}) copy-start(f32[128,96]{0,1:T(8,128)} %param.5) | copy-start | bytes 147460
  101.9 11.1 %copy-start = (f32[1024,96]{0,1:T(8,128)}, f32[1024,96]{0,1:T(8,128)S(1)}, u32[]{:S(2)}) copy-start(f32[1024,96]{0,1:T(8,128)S(1)} %fusion.3) | copy-start | bytes 1179652
  102.6 9.9 %all-to-all-start = ((f32[16,1,96]{2,1,0:T(1,128)}), f32[16,1,96]{2,1,0:T(1,128)S(1)}, u32[]{:S(2)}, u32[]{:S(2)}) async-start(f32[16,1,96]{2,1,0:T(1,128)} %broadcast_in_dim.23), calls=%async_computation | async-start | bytes 16384 | tf_op jit(solution)/shard_map/all_to_all | solution.py:183

commit v8 on v7

--- a/solution.py
+++ b/solution.py
@@ -87,10 +87,8 @@
     def over_bit(mine, bit):
         return jnp.concatenate([mine, swapped(mine, "rows", bit)], axis=0)
 
-    coeffs_low, *actives = tied(coeffs.astype(LOW), *[block == turn for turn in range(nfeat)])
+    wide_coeffs, *actives = tied(coeffs, *[block == turn for turn in range(nfeat)])
     blocks = [picked(inverse, [z + q for q in quad], 1).astype(LOW) for z in near]
-    near_coeffs, keeping, sending = tied(over_outer(coeffs_low), *reordered(features, me, order, own))
-    near_coeffs = over_bit(near_coeffs, 2)
 
     def product(rows):
         far = swapped(rows, "rows", 1)
@@ -99,8 +97,8 @@
 
 
     keeping, sending = reordered(features, me, order, own)
-    near_coeffs, keeping, *blocks = tied(over_outer(coeffs_low), keeping, *blocks)
-    near_coeffs = over_bit(near_coeffs, 2)
+    near_coeffs, keeping, *blocks = tied(over_outer(wide_coeffs), keeping, *blocks)
+    near_coeffs = over_bit(near_coeffs.astype(LOW), 2)
 
     def product(rows):
         far = swapped(rows, "rows", 1)

time: 113 us -> 113 us (level)
  no operation moved by 1% of the time
where the time goes in v8:
time: 113 us
  waiting for transfers between devices  57.8 us (51%)
  starting transfers between devices  37.7 us (33%)
  matrix products  7.31 us (6%)
  local copies, waits for them, and re-layouts  3.27 us (3%)
  other arithmetic  2.97 us (3%)
  Pallas kernels  2.41 us (2%)
  between operations  1.14 us (1%)
    ppermute x31, waiting for transfers between devices, swapped(): return lax.ppermute(shard, axis, [(i, i ^ bit) for i in range(peers)])  46.6 us
    ppermute x31, starting transfers between devices, swapped(): return lax.ppermute(shard, axis, [(i, i ^ bit) for i in range(peers)])  32.7 us
    all_to_all x1, waiting for transfers between devices, on_device(): lax.all_to_all(jnp.broadcast_to(squares[None], (nrows, 1, classes)), 'row...  5.74 us
    ppermute x1, waiting for transfers between devices, on_device(): got = lax.ppermute(sent.astype(LOW), 'feat', along).astype(WIDE)  5.45 us
    all_to_all x1, starting transfers between devices, on_device(): lax.all_to_all(jnp.broadcast_to(squares[None], (nrows, 1, classes)), 'row...  3.48 us
    pallas_call x1, Pallas kernels, reordered(): pl.pallas_call(functools.partial(reorder_kernel, order, own), out_shape=[...  2.41 us
    dot_general x3, matrix products, product(): return first + jnp.dot(sending, far, preferred_element_type=WIDE)  2.36 us
    dot_general x3, matrix products, product(): first, far = tied(jnp.dot(keeping, rows, preferred_element_type=WIDE), far)  2.34 us
  transfers between devices with their start and end apart: 33, of which 24 were waited for; matrix products, arithmetic and copies ran while one was open for 6% of the time, Pallas kernels for 2%

profile of v8, /device:TPU:0, one launch (start us, length us, event | category | flops | bytes accessed | tf_op | source)
XLA Modules:
  0.0 112.6 jit_solution(17148675584563564698)
XLA Ops:
  0.6 0.8 convert.112
  1.4 4.0 %collective-permute-start.1 = (bf16[128,96]{0,1:T(8,128)(2,1)S(1)}, bf16[128,96]{0,1:T(8,128)(2,1)S(1)}, u32[]{:S(2)}, u32[]{:S(2)}) collective-permute-start(bf16[128,96]{0,1:T(8,128)(2,1)S(1)} %convert.112), channel_id=1, source_target_pairs={{0,8},{1,9},{2,10},{3,11},{4,12},{5,13},{6,14},{7,15},{8,0},{9,1},... | collective-permute-start | bytes 73736 | tf_op jit(solution)/shard_map/ppermute | solution.py:17
  5.5 1.3 %collective-permute-start.2 = (bf16[128,96]{0,1:T(8,128)(2,1)S(1)}, bf16[128,96]{0,1:T(8,128)(2,1)S(1)}, u32[]{:S(2)}, u32[]{:S(2)}) collective-permute-start(bf16[128,96]{0,1:T(8,128)(2,1)S(1)} %convert.112), channel_id=1, source_target_pairs={{0,12},{1,13},{2,14},{3,15},{4,8},{5,9},{6,10},{7,11},{8,4},{9,5},... | collective-permute-start | bytes 73736 | tf_op jit(solution)/shard_map/ppermute | solution.py:17
  7.1 1.3 %dynamic-slice_convert_fusion.3 = (bf16[128,128]{1,0:T(8,128)(2,1)S(1)}, bf16[128,128]{1,0:T(8,128)(2,1)S(1)}, bf16[128,128]{1,0:T(8,128)(2,1)S(1)}, bf16[128,12...) fusion(f32[128,2048]{1,0:T(8,128)} %param.6, ...), kind=kLoop, calls=%fused_computation.67 | loop fusion | bytes 1048640 | tf_op jit(solution)/shard_map/convert.10
  8.5 2.4 %shard_map.67 = (bf16[1024,1024]{1,0:T(8,128)(2,1)S(1)}, bf16[1024,1024]{1,0:T(8,128)(2,1)S(1)}) custom-call(s32[1]{0:T(128)} %bitcast.me_ref, bf16[1024,2048]{1,0:T(8,128)(2,1)} %given.1), custom_call_target="tpu_custom_call" | custom-call | bytes 8388608 | tf_op jit(solution)/shard_map/pallas_call | solution.py:58
  11.1 1.6 %collective-permute-start.3 = (bf16[512,96]{0,1:T(8,128)(2,1)S(1)}, bf16[512,96]{0,1:T(8,128)(2,1)S(1)}, u32[]{:S(2)}, u32[]{:S(2)}) collective-permute-start(bf16[512,96]{0,1:T(8,128)(2,1)S(1)} %pad_maximum_fusion.6), channel_id=1, source_target_pairs={{0,2},{1,3},{2,0},{3,1},{4,6},{5,7},{6,4},{7,5},{8,10},{9,11},{10,... | collective-permute-start | bytes 294920 | tf_op jit(solution)/shard_map/ppermute | solution.py:17
  12.7 1.7 %collective-permute-start.6 = (bf16[128,512]{1,0:T(8,128)(2,1)S(1)}, bf16[128,512]{1,0:T(8,128)(2,1)S(1)}, u32[]{:S(2)}, u32[]{:S(2)}) collective-permute-start(bf16[128,512]{1,0:T(8,128)(2,1)S(1)} %get-tuple-element.38), channel_id=1, source_target_pairs={{0,4},{1,5},{2,6},{3,7},{4,0},{5,1},{6,2},{7,3},{8,12},{9,13},{10,... | collective-permute-start | bytes 393224 | tf_op jit(solution)/shard_map/ppermute | solution.py:17
  14.4 1.7 %collective-permute-start.7 = (bf16[128,512]{1,0:T(8,128)(2,1)S(1)}, bf16[128,512]{1,0:T(8,128)(2,1)S(1)}, u32[]{:S(2)}, u32[]{:S(2)}) collective-permute-start(bf16[128,512]{1,0:T(8,128)(2,1)S(1)} %get-tuple-element.39), channel_id=1, source_target_pairs={{0,8},{1,9},{2,10},{3,11},{4,12},{5,13},{6,14},{7,15},{8,0},{9,1},... | collective-permute-start | bytes 393224 | tf_op jit(solution)/shard_map/ppermute | solution.py:17
  16.1 1.0 collective-permute-start.8
  17.2 0.8 fusion.34
  18.0 0.6 collective-permute-done.4
  18.6 0.8 reduce-precision_convert_fusion
  19.4 1.6 %collective-permute-start.5 = (bf16[1024,96]{0,1:T(8,128)(2,1)S(1)}, bf16[1024,96]{0,1:T(8,128)(2,1)S(1)}, u32[]{:S(2)}, u32[]{:S(2)}) collective-permute-start(bf16[1024,96]{0,1:T(8,128)(2,1)S(1)} %get-tuple-element.36), channel_id=1, source_target_pairs={{0,16},{16,0},{1,17},{17,1},{2,18},{18,2},{3,19},{19,3},{4,20},{20... | collective-permute-start | bytes 589832 | tf_op jit(solution)/shard_map/ppermute | solution.py:17
  21.0 5.2 %collective-permute-done.7 = bf16[128,512]{1,0:T(8,128)(2,1)S(1)} collective-permute-done((bf16[128,512]{1,0:T(8,128)(2,1)S(1)}, bf16[128,512]{1,0:T(8,128)(2,1)S(1)}, u32[]{:S(2)}, u32[]{:S(2)}) %collective-permute-start.7) | collective-permute-done | bytes 131104 | tf_op jit(solution)/shard_map/ppermute | solution.py:17
  27.6 0.9 collective-permute-done.9
  29.2 1.0 constant_dynamic-slice_fusion.3
  30.1 3.4 %collective-permute-done.10 = bf16[512,96]{0,1:T(8,128)(2,1)S(1)} collective-permute-done((bf16[512,96]{0,1:T(8,128)(2,1)S(1)}, bf16[512,96]{0,1:T(8,128)(2,1)S(1)}, u32[]{:S(2)}, u32[]{:S(2)}) %collective-permute-start.10) | collective-permute-done | bytes 98336 | tf_op jit(solution)/shard_map/ppermute | solution.py:17
  33.5 2.8 %collective-permute-start.12 = (bf16[512,96]{0,1:T(8,128)(2,1)S(1)}, bf16[512,96]{0,1:T(8,128)(2,1)S(1)}, u32[]{:S(2)}, u32[]{:S(2)}) collective-permute-start(bf16[512,96]{0,1:T(8,128)(2,1)S(1)} %fusion.20), channel_id=1, source_target_pairs={{0,8},{1,9},{2,10},{3,11},{4,12},{5,13},{6,14},{7,15},{8,0},{9,1},... | collective-permute-start | bytes 294920 | tf_op jit(solution)/shard_map/ppermute | solution.py:17
  36.4 1.4 %collective-permute-start.13 = (bf16[512,96]{0,1:T(8,128)(2,1)S(1)}, bf16[512,96]{0,1:T(8,128)(2,1)S(1)}, u32[]{:S(2)}, u32[]{:S(2)}) collective-permute-start(bf16[512,96]{0,1:T(8,128)(2,1)S(1)} %fusion.20), channel_id=1, source_target_pairs={{0,12},{1,13},{2,14},{3,15},{4,8},{5,9},{6,10},{7,11},{8,4},{9,5},... | collective-permute-start | bytes 294920 | tf_op jit(solution)/shard_map/ppermute | solution.py:17
  37.8 6.1 %collective-permute-done.12 = bf16[512,96]{0,1:T(8,128)(2,1)S(1)} collective-permute-done((bf16[512,96]{0,1:T(8,128)(2,1)S(1)}, bf16[512,96]{0,1:T(8,128)(2,1)S(1)}, u32[]{:S(2)}, u32[]{:S(2)}) %collective-permute-start.12) | collective-permute-done | bytes 98336 | tf_op jit(solution)/shard_map/ppermute | solution.py:17
  44.9 1.3 %collective-permute-done.14 = f32[256,96]{0,1:T(8,128)S(1)} collective-permute-done((f32[256,96]{0,1:T(8,128)S(1)}, f32[256,96]{0,1:T(8,128)S(1)}, u32[]{:S(2)}, u32[]{:S(2)}) %collective-permute-start.14) | collective-permute-done | bytes 98336 | tf_op jit(solution)/shard_map/ppermute | solution.py:17
  46.8 3.6 %collective-permute-done.15 = bf16[256,96]{0,1:T(8,128)(2,1)S(1)} collective-permute-done((bf16[256,96]{0,1:T(8,128)(2,1)S(1)}, bf16[256,96]{0,1:T(8,128)(2,1)S(1)}, u32[]{:S(2)}, u32[]{:S(2)}) %collective-permute-start.15) | collective-permute-done | bytes 49184 | tf_op jit(solution)/shard_map/ppermute | solution.py:17
  50.4 2.5 %collective-permute-start.18 = (bf16[256,96]{0,1:T(8,128)(2,1)S(1)}, bf16[256,96]{0,1:T(8,128)(2,1)S(1)}, u32[]{:S(2)}, u32[]{:S(2)}) collective-permute-start(bf16[256,96]{0,1:T(8,128)(2,1)S(1)} %get-tuple-element.55), channel_id=1, source_target_pairs={{0,12},{1,13},{2,14},{3,15},{4,8},{5,9},{6,10},{7,11},{8,4},{9,5},... | collective-permute-start | bytes 147464 | tf_op jit(solution)/shard_map/ppermute | solution.py:17
  53.2 1.6 %collective-permute-start.16 = (bf16[256,96]{0,1:T(8,128)(2,1)S(1)}, bf16[256,96]{0,1:T(8,128)(2,1)S(1)}, u32[]{:S(2)}, u32[]{:S(2)}) collective-permute-start(bf16[256,96]{0,1:T(8,128)(2,1)S(1)} %get-tuple-element.55), channel_id=1, source_target_pairs={{0,4},{1,5},{2,6},{3,7},{4,0},{5,1},{6,2},{7,3},{8,12},{9,13},{10,... | collective-permute-start | bytes 147464 | tf_op jit(solution)/shard_map/ppermute | solution.py:17
  54.8 2.5 %collective-permute-done.16 = bf16[256,96]{0,1:T(8,128)(2,1)S(1)} collective-permute-done((bf16[256,96]{0,1:T(8,128)(2,1)S(1)}, bf16[256,96]{0,1:T(8,128)(2,1)S(1)}, u32[]{:S(2)}, u32[]{:S(2)}) %collective-permute-start.16) | collective-permute-done | bytes 49184 | tf_op jit(solution)/shard_map/ppermute | solution.py:17
  57.4 1.0 collective-permute-done.17
  58.6 0.8 fusion.46
  59.4 0.6 collective-permute-done.19
  60.0 0.8 fusion.5
  60.8 1.6 %collective-permute-start.20 = (bf16[1024,96]{0,1:T(8,128)(2,1)S(1)}, bf16[1024,96]{0,1:T(8,128)(2,1)S(1)}, u32[]{:S(2)}, u32[]{:S(2)}) collective-permute-start(bf16[1024,96]{0,1:T(8,128)(2,1)S(1)} %get-tuple-element.110), channel_id=1, source_target_pairs={{0,16},{16,0},{1,17},{17,1},{2,18},{18,2},{3,19},{19,3},{4,20},{20... | collective-permute-start | bytes 589832 | tf_op jit(solution)/shard_map/ppermute | solution.py:169
  62.4 5.5 %collective-permute-done.20 = bf16[1024,96]{0,1:T(8,128)(2,1)S(1)} collective-permute-done((bf16[1024,96]{0,1:T(8,128)(2,1)S(1)}, bf16[1024,96]{0,1:T(8,128)(2,1)S(1)}, u32[]{:S(2)}, u32[]{:S(2)}) %collective-permute-start.20) | collective-permute-done | bytes 196640 | tf_op jit(solution)/shard_map/ppermute | solution.py:169
  68.9 0.9 collective-permute-done.21
  70.5 4.3 %collective-permute-done.22 = bf16[512,96]{0,1:T(8,128)(2,1)S(1)} collective-permute-done((bf16[512,96]{0,1:T(8,128)(2,1)S(1)}, bf16[512,96]{0,1:T(8,128)(2,1)S(1)}, u32[]{:S(2)}, u32[]{:S(2)}) %collective-permute-start.22) | collective-permute-done | bytes 98336 | tf_op jit(solution)/shard_map/ppermute | solution.py:17
  74.9 1.6 %collective-permute-start.24 = (bf16[512,96]{0,1:T(8,128)(2,1)S(1)}, bf16[512,96]{0,1:T(8,128)(2,1)S(1)}, u32[]{:S(2)}, u32[]{:S(2)}) collective-permute-start(bf16[512,96]{0,1:T(8,128)(2,1)S(1)} %fusion.21), channel_id=1, source_target_pairs={{0,8},{1,9},{2,10},{3,11},{4,12},{5,13},{6,14},{7,15},{8,0},{9,1},... | collective-permute-start | bytes 294920 | tf_op jit(solution)/shard_map/ppermute | solution.py:17
  76.5 1.4 %collective-permute-start.25 = (bf16[512,96]{0,1:T(8,128)(2,1)S(1)}, bf16[512,96]{0,1:T(8,128)(2,1)S(1)}, u32[]{:S(2)}, u32[]{:S(2)}) collective-permute-start(bf16[512,96]{0,1:T(8,128)(2,1)S(1)} %fusion.21), channel_id=1, source_target_pairs={{0,12},{1,13},{2,14},{3,15},{4,8},{5,9},{6,10},{7,11},{8,4},{9,5},... | collective-permute-start | bytes 294920 | tf_op jit(solution)/shard_map/ppermute | solution.py:17
  78.4 6.3 %collective-permute-done.24 = bf16[512,96]{0,1:T(8,128)(2,1)S(1)} collective-permute-done((bf16[512,96]{0,1:T(8,128)(2,1)S(1)}, bf16[512,96]{0,1:T(8,128)(2,1)S(1)}, u32[]{:S(2)}, u32[]{:S(2)}) %collective-permute-start.24) | collective-permute-done | bytes 98336 | tf_op jit(solution)/shard_map/ppermute | solution.py:17
  85.7 1.3 %collective-permute-done.26 = f32[256,96]{0,1:T(8,128)S(1)} collective-permute-done((f32[256,96]{0,1:T(8,128)S(1)}, f32[256,96]{0,1:T(8,128)S(1)}, u32[]{:S(2)}, u32[]{:S(2)}) %collective-permute-start.26) | collective-permute-done | bytes 98336 | tf_op jit(solution)/shard_map/ppermute | solution.py:17
  87.6 3.6 %collective-permute-done.27 = bf16[256,96]{0,1:T(8,128)(2,1)S(1)} collective-permute-done((bf16[256,96]{0,1:T(8,128)(2,1)S(1)}, bf16[256,96]{0,1:T(8,128)(2,1)S(1)}, u32[]{:S(2)}, u32[]{:S(2)}) %collective-permute-start.27) | collective-permute-done | bytes 49184 | tf_op jit(solution)/shard_map/ppermute | solution.py:17
  91.2 2.2 %collective-permute-start.30 = (bf16[256,96]{0,1:T(8,128)(2,1)S(1)}, bf16[256,96]{0,1:T(8,128)(2,1)S(1)}, u32[]{:S(2)}, u32[]{:S(2)}) collective-permute-start(bf16[256,96]{0,1:T(8,128)(2,1)S(1)} %get-tuple-element.53), channel_id=1, source_target_pairs={{0,12},{1,13},{2,14},{3,15},{4,8},{5,9},{6,10},{7,11},{8,4},{9,5},... | collective-permute-start | bytes 147464 | tf_op jit(solution)/shard_map/ppermute | solution.py:17
  93.3 1.0 collective-permute-start.29
  94.4 1.3 %collective-permute-start.28 = (bf16[256,96]{0,1:T(8,128)(2,1)S(1)}, bf16[256,96]{0,1:T(8,128)(2,1)S(1)}, u32[]{:S(2)}, u32[]{:S(2)}) collective-permute-start(bf16[256,96]{0,1:T(8,128)(2,1)S(1)} %get-tuple-element.53), channel_id=1, source_target_pairs={{0,4},{1,5},{2,6},{3,7},{4,0},{5,1},{6,2},{7,3},{8,12},{9,13},{10,... | collective-permute-start | bytes 147464 | tf_op jit(solution)/shard_map/ppermute | solution.py:17
  95.6 3.0 %collective-permute-done.28 = bf16[256,96]{0,1:T(8,128)(2,1)S(1)} collective-permute-done((bf16[256,96]{0,1:T(8,128)(2,1)S(1)}, bf16[256,96]{0,1:T(8,128)(2,1)S(1)}, u32[]{:S(2)}, u32[]{:S(2)}) %collective-permute-start.28) | collective-permute-done | bytes 49184 | tf_op jit(solution)/shard_map/ppermute | solution.py:17
  99.0 0.8 fusion.47
  99.8 0.6 collective-permute-done.31
  100.5 0.8 fusion.48
  102.2 3.5 %all-to-all-start = ((f32[16,1,96]{2,1,0:T(1,128)}), f32[16,1,96]{2,1,0:T(1,128)S(1)}, u32[]{:S(2)}, u32[]{:S(2)}) async-start(f32[16,1,96]{2,1,0:T(1,128)} %broadcast_in_dim.23), calls=%async_computation | async-start | bytes 16384 | tf_op jit(solution)/shard_map/all_to_all | solution.py:181
  105.7 0.6 fusion.26
  106.3 5.7 %all-to-all-done = f32[16,1,96]{2,1,0:T(1,128)S(1)} async-done(((f32[16,1,96]{2,1,0:T(1,128)}), f32[16,1,96]{2,1,0:T(1,128)S(1)}, u32[]{:S(2)}, u32[]{:S(2)}) %all-to-all-start) | async-done | bytes 6176 | tf_op jit(solution)/shard_map/all_to_all | solution.py:181
  (98 shorter events, 10.3 us)
Async XLA Ops:
  1.4 9.5 %collective-permute-start.1 = (bf16[128,96]{0,1:T(8,128)(2,1)S(1)}, bf16[128,96]{0,1:T(8,128)(2,1)S(1)}, u32[]{:S(2)}, u32[]{:S(2)}) collective-permute-start(bf16[128,96]{0,1:T(8,128)(2,1)S(1)} %convert.112), channel_id=1, source_target_pairs={{0,8},{1,9},{2,10},{3,11},{4,12},{5,13},{6,14},{7,15},{8,0},{9,1},... | collective-permute-start | bytes 73736 | tf_op jit(solution)/shard_map/ppermute | solution.py:17
  5.5 5.6 %collective-permute-start.2 = (bf16[128,96]{0,1:T(8,128)(2,1)S(1)}, bf16[128,96]{0,1:T(8,128)(2,1)S(1)}, u32[]{:S(2)}, u32[]{:S(2)}) collective-permute-start(bf16[128,96]{0,1:T(8,128)(2,1)S(1)} %convert.112), channel_id=1, source_target_pairs={{0,12},{1,13},{2,14},{3,15},{4,8},{5,9},{6,10},{7,11},{8,4},{9,5},... | collective-permute-start | bytes 73736 | tf_op jit(solution)/shard_map/ppermute | solution.py:17
  6.8 4.3 %collective-permute-start = (bf16[128,96]{0,1:T(8,128)(2,1)S(1)}, bf16[128,96]{0,1:T(8,128)(2,1)S(1)}, u32[]{:S(2)}, u32[]{:S(2)}) collective-permute-start(bf16[128,96]{0,1:T(8,128)(2,1)S(1)} %convert.112), channel_id=1, source_target_pairs={{0,4},{1,5},{2,6},{3,7},{4,0},{5,1},{6,2},{7,3},{8,12},{9,13},{10,... | collective-permute-start | bytes 73736 | tf_op jit(solution)/shard_map/ppermute | solution.py:17
  8.5 2.6 %copy-start.1 = (f32[128,96]{0,1:T(8,128)S(1)}, f32[128,96]{0,1:T(8,128)}, u32[]{:S(2)}) copy-start(f32[128,96]{0,1:T(8,128)} %param.5) | copy-start | bytes 147460
  11.1 6.0 %collective-permute-start.3 = (bf16[512,96]{0,1:T(8,128)(2,1)S(1)}, bf16[512,96]{0,1:T(8,128)(2,1)S(1)}, u32[]{:S(2)}, u32[]{:S(2)}) collective-permute-start(bf16[512,96]{0,1:T(8,128)(2,1)S(1)} %pad_maximum_fusion.6), channel_id=1, source_target_pairs={{0,2},{1,3},{2,0},{3,1},{4,6},{5,7},{6,4},{7,5},{8,10},{9,11},{10,... | collective-permute-start | bytes 294920 | tf_op jit(solution)/shard_map/ppermute | solution.py:17
  12.7 8.3 %collective-permute-start.6 = (bf16[128,512]{1,0:T(8,128)(2,1)S(1)}, bf16[128,512]{1,0:T(8,128)(2,1)S(1)}, u32[]{:S(2)}, u32[]{:S(2)}) collective-permute-start(bf16[128,512]{1,0:T(8,128)(2,1)S(1)} %get-tuple-element.38), channel_id=1, source_target_pairs={{0,4},{1,5},{2,6},{3,7},{4,0},{5,1},{6,2},{7,3},{8,12},{9,13},{10,... | collective-permute-start | bytes 393224 | tf_op jit(solution)/shard_map/ppermute | solution.py:17
  14.4 11.8 %collective-permute-start.7 = (bf16[128,512]{1,0:T(8,128)(2,1)S(1)}, bf16[128,512]{1,0:T(8,128)(2,1)S(1)}, u32[]{:S(2)}, u32[]{:S(2)}) collective-permute-start(bf16[128,512]{1,0:T(8,128)(2,1)S(1)} %get-tuple-element.39), channel_id=1, source_target_pairs={{0,8},{1,9},{2,10},{3,11},{4,12},{5,13},{6,14},{7,15},{8,0},{9,1},... | collective-permute-start | bytes 393224 | tf_op jit(solution)/shard_map/ppermute | solution.py:17
  16.1 10.1 %collective-permute-start.8 = (bf16[128,512]{1,0:T(8,128)(2,1)S(1)}, bf16[128,512]{1,0:T(8,128)(2,1)S(1)}, u32[]{:S(2)}, u32[]{:S(2)}) collective-permute-start(bf16[128,512]{1,0:T(8,128)(2,1)S(1)} %get-tuple-element.40), channel_id=1, source_target_pairs={{0,12},{1,13},{2,14},{3,15},{4,8},{5,9},{6,10},{7,11},{8,4},{9,5},... | collective-permute-start | bytes 393224 | tf_op jit(solution)/shard_map/ppermute | solution.py:17
  17.1 1.5 %collective-permute-start.4 = (bf16[1024,96]{0,1:T(8,128)(2,1)S(1)}, bf16[1024,96]{0,1:T(8,128)(2,1)S(1)}, u32[]{:S(2)}, u32[]{:S(2)}) collective-permute-start(bf16[1024,96]{0,1:T(8,128)(2,1)S(1)} %pad_maximum_fusion.7), channel_id=1, source_target_pairs={{0,1},{1,0},{2,3},{3,2},{4,5},{5,4},{6,7},{7,6},{8,9},{9,8},{10,11... | collective-permute-start | bytes 589832 | tf_op jit(solution)/shard_map/ppermute | solution.py:17
  18.6 7.8 %copy-start.2 = (s32[1024]{0:T(1024)S(1)}, s32[1024]{0:T(1024)}, u32[]{:S(2)}) copy-start(s32[1024]{0:T(1024)} %param.7) | copy-start | bytes 12292
  19.4 7.0 %collective-permute-start.5 = (bf16[1024,96]{0,1:T(8,128)(2,1)S(1)}, bf16[1024,96]{0,1:T(8,128)(2,1)S(1)}, u32[]{:S(2)}, u32[]{:S(2)}) collective-permute-start(bf16[1024,96]{0,1:T(8,128)(2,1)S(1)} %get-tuple-element.36), channel_id=1, source_target_pairs={{0,16},{16,0},{1,17},{17,1},{2,18},{18,2},{3,19},{19,3},{4,20},{20... | collective-permute-start | bytes 589832 | tf_op jit(solution)/shard_map/ppermute | solution.py:17
  27.0 1.5 %collective-permute-start.9 = (bf16[1024,96]{0,1:T(8,128)(2,1)S(1)}, bf16[1024,96]{0,1:T(8,128)(2,1)S(1)}, u32[]{:S(2)}, u32[]{:S(2)}) collective-permute-start(bf16[1024,96]{0,1:T(8,128)(2,1)S(1)} %convolution_convert_fusion.1), channel_id=1, source_target_pairs={{0,1},{1,0},{2,3},{3,2},{4,5},{5,4},{6,7},{7,6},{8,9},{9,8},{10,11... | collective-permute-start | bytes 589832 | tf_op jit(solution)/shard_map/ppermute | solution.py:17
  28.6 4.9 %collective-permute-start.10 = (bf16[512,96]{0,1:T(8,128)(2,1)S(1)}, bf16[512,96]{0,1:T(8,128)(2,1)S(1)}, u32[]{:S(2)}, u32[]{:S(2)}) collective-permute-start(bf16[512,96]{0,1:T(8,128)(2,1)S(1)} %slice.343), channel_id=1, source_target_pairs={{0,2},{1,3},{2,0},{3,1},{4,6},{5,7},{6,4},{7,5},{8,10},{9,11},{10,... | collective-permute-start | bytes 294920 | tf_op jit(solution)/shard_map/ppermute | solution.py:17
  33.5 10.4 %collective-permute-start.12 = (bf16[512,96]{0,1:T(8,128)(2,1)S(1)}, bf16[512,96]{0,1:T(8,128)(2,1)S(1)}, u32[]{:S(2)}, u32[]{:S(2)}) collective-permute-start(bf16[512,96]{0,1:T(8,128)(2,1)S(1)} %fusion.20), channel_id=1, source_target_pairs={{0,8},{1,9},{2,10},{3,11},{4,12},{5,13},{6,14},{7,15},{8,0},{9,1},... | collective-permute-start | bytes 294920 | tf_op jit(solution)/shard_map/ppermute | solution.py:17
  36.4 7.6 %collective-permute-start.13 = (bf16[512,96]{0,1:T(8,128)(2,1)S(1)}, bf16[512,96]{0,1:T(8,128)(2,1)S(1)}, u32[]{:S(2)}, u32[]{:S(2)}) collective-permute-start(bf16[512,96]{0,1:T(8,128)(2,1)S(1)} %fusion.20), channel_id=1, source_target_pairs={{0,12},{1,13},{2,14},{3,15},{4,8},{5,9},{6,10},{7,11},{8,4},{9,5},... | collective-permute-start | bytes 294920 | tf_op jit(solution)/shard_map/ppermute | solution.py:17
  37.8 6.5 %collective-permute-start.11 = (bf16[512,96]{0,1:T(8,128)(2,1)S(1)}, bf16[512,96]{0,1:T(8,128)(2,1)S(1)}, u32[]{:S(2)}, u32[]{:S(2)}) collective-permute-start(bf16[512,96]{0,1:T(8,128)(2,1)S(1)} %fusion.20), channel_id=1, source_target_pairs={{0,4},{1,5},{2,6},{3,7},{4,0},{5,1},{6,2},{7,3},{8,12},{9,13},{10,... | collective-permute-start | bytes 294920 | tf_op jit(solution)/shard_map/ppermute | solution.py:17
  44.8 1.4 %collective-permute-start.14 = (f32[256,96]{0,1:T(8,128)S(1)}, f32[256,96]{0,1:T(8,128)S(1)}, u32[]{:S(2)}, u32[]{:S(2)}) collective-permute-start(f32[256,96]{0,1:T(8,128)S(1)} %slice.254), channel_id=1, source_target_pairs={{0,1},{1,0},{2,3},{3,2},{4,5},{5,4},{6,7},{7,6},{8,9},{9,8},{10,11... | collective-permute-start | bytes 294920 | tf_op jit(solution)/shard_map/ppermute | solution.py:17
  46.2 4.2 %collective-permute-start.15 = (bf16[256,96]{0,1:T(8,128)(2,1)S(1)}, bf16[256,96]{0,1:T(8,128)(2,1)S(1)}, u32[]{:S(2)}, u32[]{:S(2)}) collective-permute-start(bf16[256,96]{0,1:T(8,128)(2,1)S(1)} %pad_maximum_fusion.12), channel_id=1, source_target_pairs={{0,2},{1,3},{2,0},{3,1},{4,6},{5,7},{6,4},{7,5},{8,10},{9,11},{10,... | collective-permute-start | bytes 147464 | tf_op jit(solution)/shard_map/ppermute | solution.py:17
  50.4 8.1 %collective-permute-start.18 = (bf16[256,96]{0,1:T(8,128)(2,1)S(1)}, bf16[256,96]{0,1:T(8,128)(2,1)S(1)}, u32[]{:S(2)}, u32[]{:S(2)}) collective-permute-start(bf16[256,96]{0,1:T(8,128)(2,1)S(1)} %get-tuple-element.55), channel_id=1, source_target_pairs={{0,12},{1,13},{2,14},{3,15},{4,8},{5,9},{6,10},{7,11},{8,4},{9,5},... | collective-permute-start | bytes 147464 | tf_op jit(solution)/shard_map/ppermute | solution.py:17
  52.9 5.5 %collective-permute-start.17 = (bf16[256,96]{0,1:T(8,128)(2,1)S(1)}, bf16[256,96]{0,1:T(8,128)(2,1)S(1)}, u32[]{:S(2)}, u32[]{:S(2)}) collective-permute-start(bf16[256,96]{0,1:T(8,128)(2,1)S(1)} %get-tuple-element.55), channel_id=1, source_target_pairs={{0,8},{1,9},{2,10},{3,11},{4,12},{5,13},{6,14},{7,15},{8,0},{9,1},... | collective-permute-start | bytes 147464 | tf_op jit(solution)/shard_map/ppermute | solution.py:17
  53.2 4.2 %collective-permute-start.16 = (bf16[256,96]{0,1:T(8,128)(2,1)S(1)}, bf16[256,96]{0,1:T(8,128)(2,1)S(1)}, u32[]{:S(2)}, u32[]{:S(2)}) collective-permute-start(bf16[256,96]{0,1:T(8,128)(2,1)S(1)} %get-tuple-element.55), channel_id=1, source_target_pairs={{0,4},{1,5},{2,6},{3,7},{4,0},{5,1},{6,2},{7,3},{8,12},{9,13},{10,... | collective-permute-start | bytes 147464 | tf_op jit(solution)/shard_map/ppermute | solution.py:17
  58.5 1.5 %collective-permute-start.19 = (bf16[1024,96]{0,1:T(8,128)(2,1)S(1)}, bf16[1024,96]{0,1:T(8,128)(2,1)S(1)}, u32[]{:S(2)}, u32[]{:S(2)}) collective-permute-start(bf16[1024,96]{0,1:T(8,128)(2,1)S(1)} %constant_dynamic-update-slice_fusion), channel_id=1, source_target_pairs={{0,1},{1,0},{2,3},{3,2},{4,5},{5,4},{6,7},{7,6},{8,9},{9,8},{10,11... | collective-permute-start | bytes 589832 | tf_op jit(solution)/shard_map/ppermute | solution.py:17
  60.8 7.0 %collective-permute-start.20 = (bf16[1024,96]{0,1:T(8,128)(2,1)S(1)}, bf16[1024,96]{0,1:T(8,128)(2,1)S(1)}, u32[]{:S(2)}, u32[]{:S(2)}) collective-permute-start(bf16[1024,96]{0,1:T(8,128)(2,1)S(1)} %get-tuple-element.110), channel_id=1, source_target_pairs={{0,16},{16,0},{1,17},{17,1},{2,18},{18,2},{3,19},{19,3},{4,20},{20... | collective-permute-start | bytes 589832 | tf_op jit(solution)/shard_map/ppermute | solution.py:169
  68.4 1.5 %collective-permute-start.21 = (bf16[1024,96]{0,1:T(8,128)(2,1)S(1)}, bf16[1024,96]{0,1:T(8,128)(2,1)S(1)}, u32[]{:S(2)}, u32[]{:S(2)}) collective-permute-start(bf16[1024,96]{0,1:T(8,128)(2,1)S(1)} %convolution_convert_fusion), channel_id=1, source_target_pairs={{0,1},{1,0},{2,3},{3,2},{4,5},{5,4},{6,7},{7,6},{8,9},{9,8},{10,11... | collective-permute-start | bytes 589832 | tf_op jit(solution)/shard_map/ppermute | solution.py:17
  69.9 4.9 %collective-permute-start.22 = (bf16[512,96]{0,1:T(8,128)(2,1)S(1)}, bf16[512,96]{0,1:T(8,128)(2,1)S(1)}, u32[]{:S(2)}, u32[]{:S(2)}) collective-permute-start(bf16[512,96]{0,1:T(8,128)(2,1)S(1)} %slice.342), channel_id=1, source_target_pairs={{0,2},{1,3},{2,0},{3,1},{4,6},{5,7},{6,4},{7,5},{8,10},{9,11},{10,... | collective-permute-start | bytes 294920 | tf_op jit(solution)/shard_map/ppermute | solution.py:17
  74.9 9.8 %collective-permute-start.24 = (bf16[512,96]{0,1:T(8,128)(2,1)S(1)}, bf16[512,96]{0,1:T(8,128)(2,1)S(1)}, u32[]{:S(2)}, u32[]{:S(2)}) collective-permute-start(bf16[512,96]{0,1:T(8,128)(2,1)S(1)} %fusion.21), channel_id=1, source_target_pairs={{0,8},{1,9},{2,10},{3,11},{4,12},{5,13},{6,14},{7,15},{8,0},{9,1},... | collective-permute-start | bytes 294920 | tf_op jit(solution)/shard_map/ppermute | solution.py:17
  76.5 8.3 %collective-permute-start.25 = (bf16[512,96]{0,1:T(8,128)(2,1)S(1)}, bf16[512,96]{0,1:T(8,128)(2,1)S(1)}, u32[]{:S(2)}, u32[]{:S(2)}) collective-permute-start(bf16[512,96]{0,1:T(8,128)(2,1)S(1)} %fusion.21), channel_id=1, source_target_pairs={{0,12},{1,13},{2,14},{3,15},{4,8},{5,9},{6,10},{7,11},{8,4},{9,5},... | collective-permute-start | bytes 294920 | tf_op jit(solution)/shard_map/ppermute | solution.py:17
  77.8 7.2 %collective-permute-start.23 = (bf16[512,96]{0,1:T(8,128)(2,1)S(1)}, bf16[512,96]{0,1:T(8,128)(2,1)S(1)}, u32[]{:S(2)}, u32[]{:S(2)}) collective-permute-start(bf16[512,96]{0,1:T(8,128)(2,1)S(1)} %fusion.21), channel_id=1, source_target_pairs={{0,4},{1,5},{2,6},{3,7},{4,0},{5,1},{6,2},{7,3},{8,12},{9,13},{10,... | collective-permute-start | bytes 294920 | tf_op jit(solution)/shard_map/ppermute | solution.py:17
  85.6 1.4 %collective-permute-start.26 = (f32[256,96]{0,1:T(8,128)S(1)}, f32[256,96]{0,1:T(8,128)S(1)}, u32[]{:S(2)}, u32[]{:S(2)}) collective-permute-start(f32[256,96]{0,1:T(8,128)S(1)} %slice.281), channel_id=1, source_target_pairs={{0,1},{1,0},{2,3},{3,2},{4,5},{5,4},{6,7},{7,6},{8,9},{9,8},{10,11... | collective-permute-start | bytes 294920 | tf_op jit(solution)/shard_map/ppermute | solution.py:17
  87.0 4.2 %collective-permute-start.27 = (bf16[256,96]{0,1:T(8,128)(2,1)S(1)}, bf16[256,96]{0,1:T(8,128)(2,1)S(1)}, u32[]{:S(2)}, u32[]{:S(2)}) collective-permute-start(bf16[256,96]{0,1:T(8,128)(2,1)S(1)} %pad_maximum_fusion.13), channel_id=1, source_target_pairs={{0,2},{1,3},{2,0},{3,1},{4,6},{5,7},{6,4},{7,5},{8,10},{9,11},{10,... | collective-permute-start | bytes 147464 | tf_op jit(solution)/shard_map/ppermute | solution.py:17
  91.2 7.7 %collective-permute-start.30 = (bf16[256,96]{0,1:T(8,128)(2,1)S(1)}, bf16[256,96]{0,1:T(8,128)(2,1)S(1)}, u32[]{:S(2)}, u32[]{:S(2)}) collective-permute-start(bf16[256,96]{0,1:T(8,128)(2,1)S(1)} %get-tuple-element.53), channel_id=1, source_target_pairs={{0,12},{1,13},{2,14},{3,15},{4,8},{5,9},{6,10},{7,11},{8,4},{9,5},... | collective-permute-start | bytes 147464 | tf_op jit(solution)/shard_map/ppermute | solution.py:17
  93.3 5.5 %collective-permute-start.29 = (bf16[256,96]{0,1:T(8,128)(2,1)S(1)}, bf16[256,96]{0,1:T(8,128)(2,1)S(1)}, u32[]{:S(2)}, u32[]{:S(2)}) collective-permute-start(bf16[256,96]{0,1:T(8,128)(2,1)S(1)} %get-tuple-element.53), channel_id=1, source_target_pairs={{0,8},{1,9},{2,10},{3,11},{4,12},{5,13},{6,14},{7,15},{8,0},{9,1},... | collective-permute-start | bytes 147464 | tf_op jit(solution)/shard_map/ppermute | solution.py:17
  94.4 4.3 %collective-permute-start.28 = (bf16[256,96]{0,1:T(8,128)(2,1)S(1)}, bf16[256,96]{0,1:T(8,128)(2,1)S(1)}, u32[]{:S(2)}, u32[]{:S(2)}) collective-permute-start(bf16[256,96]{0,1:T(8,128)(2,1)S(1)} %get-tuple-element.53), channel_id=1, source_target_pairs={{0,4},{1,5},{2,6},{3,7},{4,0},{5,1},{6,2},{7,3},{8,12},{9,13},{10,... | collective-permute-start | bytes 147464 | tf_op jit(solution)/shard_map/ppermute | solution.py:17
  99.0 1.5 %collective-permute-start.31 = (bf16[1024,96]{0,1:T(8,128)(2,1)S(1)}, bf16[1024,96]{0,1:T(8,128)(2,1)S(1)}, u32[]{:S(2)}, u32[]{:S(2)}) collective-permute-start(bf16[1024,96]{0,1:T(8,128)(2,1)S(1)} %constant_dynamic-update-slice_fusion.8), channel_id=1, source_target_pairs={{0,1},{1,0},{2,3},{3,2},{4,5},{5,4},{6,7},{7,6},{8,9},{9,8},{10,11... | collective-permute-start | bytes 589832 | tf_op jit(solution)/shard_map/ppermute | solution.py:17
  101.5 11.1 %copy-start = (f32[1024,96]{0,1:T(8,128)}, f32[1024,96]{0,1:T(8,128)S(1)}, u32[]{:S(2)}) copy-start(f32[1024,96]{0,1:T(8,128)S(1)} %fusion.3) | copy-start | bytes 1179652
  102.2 9.9 %all-to-all-start = ((f32[16,1,96]{2,1,0:T(1,128)}), f32[16,1,96]{2,1,0:T(1,128)S(1)}, u32[]{:S(2)}, u32[]{:S(2)}) async-start(f32[16,1,96]{2,1,0:T(1,128)} %broadcast_in_dim.23), calls=%async_computation | async-start | bytes 16384 | tf_op jit(solution)/shard_map/all_to_all | solution.py:181

commit v9 on v8

--- a/solution.py
+++ b/solution.py
@@ -154,7 +154,7 @@
         part = lax.dot_general(inverse_low, pair, contract, preferred_element_type=WIDE)
         part = part[:, :classes] + part[:, classes:]
         keep, send = halved(part)
-        part = keep + swapped(send, "rows", 1)
+        part = keep + swapped(send.astype(LOW), "rows", 1).astype(WIDE)
         top, bottom = halved(part)
         delta = part + swapped(jnp.concatenate([bottom, top]).astype(LOW), "rows", 2).astype(WIDE)
         delta_low = delta.astype(LOW)

time: 113 us -> 113 us (level)
  no operation moved by 1% of the time
where the time goes in v9:
time: 113 us; the launch traced here: 112 us
  waiting for transfers between devices  57.7 us (51%)
  starting transfers between devices  37.7 us (33%)
  matrix products  7.31 us (6%)
  local copies, waits for them, and re-layouts  3.27 us (3%)
  other arithmetic  2.96 us (3%)
  Pallas kernels  2.41 us (2%)
  between operations  1.14 us (1%)
    ppermute x31, waiting for transfers between devices, swapped(): return lax.ppermute(shard, axis, [(i, i ^ bit) for i in range(peers)])  46.5 us
    ppermute x31, starting transfers between devices, swapped(): return lax.ppermute(shard, axis, [(i, i ^ bit) for i in range(peers)])  32.7 us
    all_to_all x1, waiting for transfers between devices, on_device(): lax.all_to_all(jnp.broadcast_to(squares[None], (nrows, 1, classes)), 'row...  5.74 us
    ppermute x1, waiting for transfers between devices, on_device(): got = lax.ppermute(sent.astype(LOW), 'feat', along).astype(WIDE)  5.45 us
    all_to_all x1, starting transfers between devices, on_device(): lax.all_to_all(jnp.broadcast_to(squares[None], (nrows, 1, classes)), 'row...  3.48 us
    pallas_call x1, Pallas kernels, reordered(): pl.pallas_call(functools.partial(reorder_kernel, order, own), out_shape=[...  2.41 us
    dot_general x3, matrix products, product(): return first + jnp.dot(sending, far, preferred_element_type=WIDE)  2.36 us
    dot_general x3, matrix products, product(): first, far = tied(jnp.dot(keeping, rows, preferred_element_type=WIDE), far)  2.33 us
  transfers between devices with their start and end apart: 33, of which 24 were waited for; matrix products, arithmetic and copies ran while one was open for 6% of the time, Pallas kernels for 2%

profile of v9, /device:TPU:0, one launch (start us, length us, event | category | flops | bytes accessed | tf_op | source)
XLA Modules:
  0.0 112.4 jit_solution(7250778603802830023)
XLA Ops:
  0.6 0.8 convert.122
  1.4 4.0 %collective-permute-start.1 = (bf16[128,96]{0,1:T(8,128)(2,1)S(1)}, bf16[128,96]{0,1:T(8,128)(2,1)S(1)}, u32[]{:S(2)}, u32[]{:S(2)}) collective-permute-start(bf16[128,96]{0,1:T(8,128)(2,1)S(1)} %convert.122), channel_id=1, source_target_pairs={{0,8},{1,9},{2,10},{3,11},{4,12},{5,13},{6,14},{7,15},{8,0},{9,1},... | collective-permute-start | bytes 73736 | tf_op jit(solution)/shard_map/ppermute | solution.py:17
  5.5 1.3 %collective-permute-start.2 = (bf16[128,96]{0,1:T(8,128)(2,1)S(1)}, bf16[128,96]{0,1:T(8,128)(2,1)S(1)}, u32[]{:S(2)}, u32[]{:S(2)}) collective-permute-start(bf16[128,96]{0,1:T(8,128)(2,1)S(1)} %convert.122), channel_id=1, source_target_pairs={{0,12},{1,13},{2,14},{3,15},{4,8},{5,9},{6,10},{7,11},{8,4},{9,5},... | collective-permute-start | bytes 73736 | tf_op jit(solution)/shard_map/ppermute | solution.py:17
  7.1 1.3 %dynamic-slice_convert_fusion.3 = (bf16[128,128]{1,0:T(8,128)(2,1)S(1)}, bf16[128,128]{1,0:T(8,128)(2,1)S(1)}, bf16[128,128]{1,0:T(8,128)(2,1)S(1)}, bf16[128,12...) fusion(f32[128,2048]{1,0:T(8,128)} %param.6, ...), kind=kLoop, calls=%fused_computation.69 | loop fusion | bytes 1048640 | tf_op jit(solution)/shard_map/convert.12
  8.5 2.4 %shard_map.67 = (bf16[1024,1024]{1,0:T(8,128)(2,1)S(1)}, bf16[1024,1024]{1,0:T(8,128)(2,1)S(1)}) custom-call(s32[1]{0:T(128)} %bitcast.me_ref, bf16[1024,2048]{1,0:T(8,128)(2,1)} %given.1), custom_call_target="tpu_custom_call" | custom-call | bytes 8388608 | tf_op jit(solution)/shard_map/pallas_call | solution.py:58
  11.1 1.6 %collective-permute-start.3 = (bf16[512,96]{0,1:T(8,128)(2,1)S(1)}, bf16[512,96]{0,1:T(8,128)(2,1)S(1)}, u32[]{:S(2)}, u32[]{:S(2)}) collective-permute-start(bf16[512,96]{0,1:T(8,128)(2,1)S(1)} %pad_maximum_fusion.6), channel_id=1, source_target_pairs={{0,2},{1,3},{2,0},{3,1},{4,6},{5,7},{6,4},{7,5},{8,10},{9,11},{10,... | collective-permute-start | bytes 294920 | tf_op jit(solution)/shard_map/ppermute | solution.py:17
  12.7 1.7 %collective-permute-start.6 = (bf16[128,512]{1,0:T(8,128)(2,1)S(1)}, bf16[128,512]{1,0:T(8,128)(2,1)S(1)}, u32[]{:S(2)}, u32[]{:S(2)}) collective-permute-start(bf16[128,512]{1,0:T(8,128)(2,1)S(1)} %get-tuple-element.38), channel_id=1, source_target_pairs={{0,4},{1,5},{2,6},{3,7},{4,0},{5,1},{6,2},{7,3},{8,12},{9,13},{10,... | collective-permute-start | bytes 393224 | tf_op jit(solution)/shard_map/ppermute | solution.py:17
  14.4 1.7 %collective-permute-start.7 = (bf16[128,512]{1,0:T(8,128)(2,1)S(1)}, bf16[128,512]{1,0:T(8,128)(2,1)S(1)}, u32[]{:S(2)}, u32[]{:S(2)}) collective-permute-start(bf16[128,512]{1,0:T(8,128)(2,1)S(1)} %get-tuple-element.39), channel_id=1, source_target_pairs={{0,8},{1,9},{2,10},{3,11},{4,12},{5,13},{6,14},{7,15},{8,0},{9,1},... | collective-permute-start | bytes 393224 | tf_op jit(solution)/shard_map/ppermute | solution.py:17
  16.1 1.0 collective-permute-start.8
  17.2 0.8 fusion.34
  18.0 0.6 collective-permute-done.4
  18.6 0.8 reduce-precision_convert_fusion
  19.4 1.6 %collective-permute-start.5 = (bf16[1024,96]{0,1:T(8,128)(2,1)S(1)}, bf16[1024,96]{0,1:T(8,128)(2,1)S(1)}, u32[]{:S(2)}, u32[]{:S(2)}) collective-permute-start(bf16[1024,96]{0,1:T(8,128)(2,1)S(1)} %get-tuple-element.36), channel_id=1, source_target_pairs={{0,16},{16,0},{1,17},{17,1},{2,18},{18,2},{3,19},{19,3},{4,20},{20... | collective-permute-start | bytes 589832 | tf_op jit(solution)/shard_map/ppermute | solution.py:17
  21.0 5.2 %collective-permute-done.7 = bf16[128,512]{1,0:T(8,128)(2,1)S(1)} collective-permute-done((bf16[128,512]{1,0:T(8,128)(2,1)S(1)}, bf16[128,512]{1,0:T(8,128)(2,1)S(1)}, u32[]{:S(2)}, u32[]{:S(2)}) %collective-permute-start.7) | collective-permute-done | bytes 131104 | tf_op jit(solution)/shard_map/ppermute | solution.py:17
  27.6 0.9 collective-permute-done.9
  29.2 1.0 constant_dynamic-slice_fusion.3
  30.1 3.4 %collective-permute-done.10 = bf16[512,96]{0,1:T(8,128)(2,1)S(1)} collective-permute-done((bf16[512,96]{0,1:T(8,128)(2,1)S(1)}, bf16[512,96]{0,1:T(8,128)(2,1)S(1)}, u32[]{:S(2)}, u32[]{:S(2)}) %collective-permute-start.10) | collective-permute-done | bytes 98336 | tf_op jit(solution)/shard_map/ppermute | solution.py:17
  33.5 2.8 %collective-permute-start.12 = (bf16[512,96]{0,1:T(8,128)(2,1)S(1)}, bf16[512,96]{0,1:T(8,128)(2,1)S(1)}, u32[]{:S(2)}, u32[]{:S(2)}) collective-permute-start(bf16[512,96]{0,1:T(8,128)(2,1)S(1)} %fusion.20), channel_id=1, source_target_pairs={{0,8},{1,9},{2,10},{3,11},{4,12},{5,13},{6,14},{7,15},{8,0},{9,1},... | collective-permute-start | bytes 294920 | tf_op jit(solution)/shard_map/ppermute | solution.py:17
  36.4 1.4 %collective-permute-start.13 = (bf16[512,96]{0,1:T(8,128)(2,1)S(1)}, bf16[512,96]{0,1:T(8,128)(2,1)S(1)}, u32[]{:S(2)}, u32[]{:S(2)}) collective-permute-start(bf16[512,96]{0,1:T(8,128)(2,1)S(1)} %fusion.20), channel_id=1, source_target_pairs={{0,12},{1,13},{2,14},{3,15},{4,8},{5,9},{6,10},{7,11},{8,4},{9,5},... | collective-permute-start | bytes 294920 | tf_op jit(solution)/shard_map/ppermute | solution.py:17
  37.8 6.1 %collective-permute-done.12 = bf16[512,96]{0,1:T(8,128)(2,1)S(1)} collective-permute-done((bf16[512,96]{0,1:T(8,128)(2,1)S(1)}, bf16[512,96]{0,1:T(8,128)(2,1)S(1)}, u32[]{:S(2)}, u32[]{:S(2)}) %collective-permute-start.12) | collective-permute-done | bytes 98336 | tf_op jit(solution)/shard_map/ppermute | solution.py:17
  44.9 1.2 %collective-permute-done.14 = bf16[256,96]{0,1:T(8,128)(2,1)S(1)} collective-permute-done((bf16[256,96]{0,1:T(8,128)(2,1)S(1)}, bf16[256,96]{0,1:T(8,128)(2,1)S(1)}, u32[]{:S(2)}, u32[]{:S(2)}) %collective-permute-start.14) | collective-permute-done | bytes 49184 | tf_op jit(solution)/shard_map/ppermute | solution.py:17
  46.7 3.6 %collective-permute-done.15 = bf16[256,96]{0,1:T(8,128)(2,1)S(1)} collective-permute-done((bf16[256,96]{0,1:T(8,128)(2,1)S(1)}, bf16[256,96]{0,1:T(8,128)(2,1)S(1)}, u32[]{:S(2)}, u32[]{:S(2)}) %collective-permute-start.15) | collective-permute-done | bytes 49184 | tf_op jit(solution)/shard_map/ppermute | solution.py:17
  50.3 2.5 %collective-permute-start.18 = (bf16[256,96]{0,1:T(8,128)(2,1)S(1)}, bf16[256,96]{0,1:T(8,128)(2,1)S(1)}, u32[]{:S(2)}, u32[]{:S(2)}) collective-permute-start(bf16[256,96]{0,1:T(8,128)(2,1)S(1)} %get-tuple-element.55), channel_id=1, source_target_pairs={{0,12},{1,13},{2,14},{3,15},{4,8},{5,9},{6,10},{7,11},{8,4},{9,5},... | collective-permute-start | bytes 147464 | tf_op jit(solution)/shard_map/ppermute | solution.py:17
  53.1 1.6 %collective-permute-start.16 = (bf16[256,96]{0,1:T(8,128)(2,1)S(1)}, bf16[256,96]{0,1:T(8,128)(2,1)S(1)}, u32[]{:S(2)}, u32[]{:S(2)}) collective-permute-start(bf16[256,96]{0,1:T(8,128)(2,1)S(1)} %get-tuple-element.55), channel_id=1, source_target_pairs={{0,4},{1,5},{2,6},{3,7},{4,0},{5,1},{6,2},{7,3},{8,12},{9,13},{10,... | collective-permute-start | bytes 147464 | tf_op jit(solution)/shard_map/ppermute | solution.py:17
  54.8 2.5 %collective-permute-done.16 = bf16[256,96]{0,1:T(8,128)(2,1)S(1)} collective-permute-done((bf16[256,96]{0,1:T(8,128)(2,1)S(1)}, bf16[256,96]{0,1:T(8,128)(2,1)S(1)}, u32[]{:S(2)}, u32[]{:S(2)}) %collective-permute-start.16) | collective-permute-done | bytes 49184 | tf_op jit(solution)/shard_map/ppermute | solution.py:17
  57.3 1.0 collective-permute-done.17
  58.5 0.8 fusion.46
  59.3 0.6 collective-permute-done.19
  60.0 0.8 fusion.5
  60.8 1.6 %collective-permute-start.20 = (bf16[1024,96]{0,1:T(8,128)(2,1)S(1)}, bf16[1024,96]{0,1:T(8,128)(2,1)S(1)}, u32[]{:S(2)}, u32[]{:S(2)}) collective-permute-start(bf16[1024,96]{0,1:T(8,128)(2,1)S(1)} %get-tuple-element.110), channel_id=1, source_target_pairs={{0,16},{16,0},{1,17},{17,1},{2,18},{18,2},{3,19},{19,3},{4,20},{20... | collective-permute-start | bytes 589832 | tf_op jit(solution)/shard_map/ppermute | solution.py:169
  62.3 5.4 %collective-permute-done.20 = bf16[1024,96]{0,1:T(8,128)(2,1)S(1)} collective-permute-done((bf16[1024,96]{0,1:T(8,128)(2,1)S(1)}, bf16[1024,96]{0,1:T(8,128)(2,1)S(1)}, u32[]{:S(2)}, u32[]{:S(2)}) %collective-permute-start.20) | collective-permute-done | bytes 196640 | tf_op jit(solution)/shard_map/ppermute | solution.py:169
  68.9 0.9 collective-permute-done.21
  70.4 4.3 %collective-permute-done.22 = bf16[512,96]{0,1:T(8,128)(2,1)S(1)} collective-permute-done((bf16[512,96]{0,1:T(8,128)(2,1)S(1)}, bf16[512,96]{0,1:T(8,128)(2,1)S(1)}, u32[]{:S(2)}, u32[]{:S(2)}) %collective-permute-start.22) | collective-permute-done | bytes 98336 | tf_op jit(solution)/shard_map/ppermute | solution.py:17
  74.8 1.6 %collective-permute-start.24 = (bf16[512,96]{0,1:T(8,128)(2,1)S(1)}, bf16[512,96]{0,1:T(8,128)(2,1)S(1)}, u32[]{:S(2)}, u32[]{:S(2)}) collective-permute-start(bf16[512,96]{0,1:T(8,128)(2,1)S(1)} %fusion.21), channel_id=1, source_target_pairs={{0,8},{1,9},{2,10},{3,11},{4,12},{5,13},{6,14},{7,15},{8,0},{9,1},... | collective-permute-start | bytes 294920 | tf_op jit(solution)/shard_map/ppermute | solution.py:17
  76.4 1.4 %collective-permute-start.25 = (bf16[512,96]{0,1:T(8,128)(2,1)S(1)}, bf16[512,96]{0,1:T(8,128)(2,1)S(1)}, u32[]{:S(2)}, u32[]{:S(2)}) collective-permute-start(bf16[512,96]{0,1:T(8,128)(2,1)S(1)} %fusion.21), channel_id=1, source_target_pairs={{0,12},{1,13},{2,14},{3,15},{4,8},{5,9},{6,10},{7,11},{8,4},{9,5},... | collective-permute-start | bytes 294920 | tf_op jit(solution)/shard_map/ppermute | solution.py:17
  78.3 6.3 %collective-permute-done.24 = bf16[512,96]{0,1:T(8,128)(2,1)S(1)} collective-permute-done((bf16[512,96]{0,1:T(8,128)(2,1)S(1)}, bf16[512,96]{0,1:T(8,128)(2,1)S(1)}, u32[]{:S(2)}, u32[]{:S(2)}) %collective-permute-start.24) | collective-permute-done | bytes 98336 | tf_op jit(solution)/shard_map/ppermute | solution.py:17
  85.6 1.2 %collective-permute-done.26 = bf16[256,96]{0,1:T(8,128)(2,1)S(1)} collective-permute-done((bf16[256,96]{0,1:T(8,128)(2,1)S(1)}, bf16[256,96]{0,1:T(8,128)(2,1)S(1)}, u32[]{:S(2)}, u32[]{:S(2)}) %collective-permute-start.26) | collective-permute-done | bytes 49184 | tf_op jit(solution)/shard_map/ppermute | solution.py:17
  87.4 3.6 %collective-permute-done.27 = bf16[256,96]{0,1:T(8,128)(2,1)S(1)} collective-permute-done((bf16[256,96]{0,1:T(8,128)(2,1)S(1)}, bf16[256,96]{0,1:T(8,128)(2,1)S(1)}, u32[]{:S(2)}, u32[]{:S(2)}) %collective-permute-start.27) | collective-permute-done | bytes 49184 | tf_op jit(solution)/shard_map/ppermute | solution.py:17
  91.0 2.2 %collective-permute-start.30 = (bf16[256,96]{0,1:T(8,128)(2,1)S(1)}, bf16[256,96]{0,1:T(8,128)(2,1)S(1)}, u32[]{:S(2)}, u32[]{:S(2)}) collective-permute-start(bf16[256,96]{0,1:T(8,128)(2,1)S(1)} %get-tuple-element.53), channel_id=1, source_target_pairs={{0,12},{1,13},{2,14},{3,15},{4,8},{5,9},{6,10},{7,11},{8,4},{9,5},... | collective-permute-start | bytes 147464 | tf_op jit(solution)/shard_map/ppermute | solution.py:17
  93.2 1.0 collective-permute-start.29
  94.2 1.3 %collective-permute-start.28 = (bf16[256,96]{0,1:T(8,128)(2,1)S(1)}, bf16[256,96]{0,1:T(8,128)(2,1)S(1)}, u32[]{:S(2)}, u32[]{:S(2)}) collective-permute-start(bf16[256,96]{0,1:T(8,128)(2,1)S(1)} %get-tuple-element.53), channel_id=1, source_target_pairs={{0,4},{1,5},{2,6},{3,7},{4,0},{5,1},{6,2},{7,3},{8,12},{9,13},{10,... | collective-permute-start | bytes 147464 | tf_op jit(solution)/shard_map/ppermute | solution.py:17
  95.5 3.0 %collective-permute-done.28 = bf16[256,96]{0,1:T(8,128)(2,1)S(1)} collective-permute-done((bf16[256,96]{0,1:T(8,128)(2,1)S(1)}, bf16[256,96]{0,1:T(8,128)(2,1)S(1)}, u32[]{:S(2)}, u32[]{:S(2)}) %collective-permute-start.28) | collective-permute-done | bytes 49184 | tf_op jit(solution)/shard_map/ppermute | solution.py:17
  98.9 0.8 fusion.47
  99.7 0.6 collective-permute-done.31
  100.3 0.8 fusion.48
  102.1 3.5 %all-to-all-start = ((f32[16,1,96]{2,1,0:T(1,128)}), f32[16,1,96]{2,1,0:T(1,128)S(1)}, u32[]{:S(2)}, u32[]{:S(2)}) async-start(f32[16,1,96]{2,1,0:T(1,128)} %broadcast_in_dim.23), calls=%async_computation | async-start | bytes 16384 | tf_op jit(solution)/shard_map/all_to_all | solution.py:181
  105.5 0.6 fusion.28
  106.2 5.7 %all-to-all-done = f32[16,1,96]{2,1,0:T(1,128)S(1)} async-done(((f32[16,1,96]{2,1,0:T(1,128)}), f32[16,1,96]{2,1,0:T(1,128)S(1)}, u32[]{:S(2)}, u32[]{:S(2)}) %all-to-all-start) | async-done | bytes 6176 | tf_op jit(solution)/shard_map/all_to_all | solution.py:181
  (98 shorter events, 10.3 us)
Async XLA Ops:
  1.4 9.5 %collective-permute-start.1 = (bf16[128,96]{0,1:T(8,128)(2,1)S(1)}, bf16[128,96]{0,1:T(8,128)(2,1)S(1)}, u32[]{:S(2)}, u32[]{:S(2)}) collective-permute-start(bf16[128,96]{0,1:T(8,128)(2,1)S(1)} %convert.122), channel_id=1, source_target_pairs={{0,8},{1,9},{2,10},{3,11},{4,12},{5,13},{6,14},{7,15},{8,0},{9,1},... | collective-permute-start | bytes 73736 | tf_op jit(solution)/shard_map/ppermute | solution.py:17
  5.5 5.6 %collective-permute-start.2 = (bf16[128,96]{0,1:T(8,128)(2,1)S(1)}, bf16[128,96]{0,1:T(8,128)(2,1)S(1)}, u32[]{:S(2)}, u32[]{:S(2)}) collective-permute-start(bf16[128,96]{0,1:T(8,128)(2,1)S(1)} %convert.122), channel_id=1, source_target_pairs={{0,12},{1,13},{2,14},{3,15},{4,8},{5,9},{6,10},{7,11},{8,4},{9,5},... | collective-permute-start | bytes 73736 | tf_op jit(solution)/shard_map/ppermute | solution.py:17
  6.8 4.3 %collective-permute-start = (bf16[128,96]{0,1:T(8,128)(2,1)S(1)}, bf16[128,96]{0,1:T(8,128)(2,1)S(1)}, u32[]{:S(2)}, u32[]{:S(2)}) collective-permute-start(bf16[128,96]{0,1:T(8,128)(2,1)S(1)} %convert.122), channel_id=1, source_target_pairs={{0,4},{1,5},{2,6},{3,7},{4,0},{5,1},{6,2},{7,3},{8,12},{9,13},{10,... | collective-permute-start | bytes 73736 | tf_op jit(solution)/shard_map/ppermute | solution.py:17
  8.5 2.6 %copy-start.1 = (f32[128,96]{0,1:T(8,128)S(1)}, f32[128,96]{0,1:T(8,128)}, u32[]{:S(2)}) copy-start(f32[128,96]{0,1:T(8,128)} %param.5) | copy-start | bytes 147460
  11.1 6.0 %collective-permute-start.3 = (bf16[512,96]{0,1:T(8,128)(2,1)S(1)}, bf16[512,96]{0,1:T(8,128)(2,1)S(1)}, u32[]{:S(2)}, u32[]{:S(2)}) collective-permute-start(bf16[512,96]{0,1:T(8,128)(2,1)S(1)} %pad_maximum_fusion.6), channel_id=1, source_target_pairs={{0,2},{1,3},{2,0},{3,1},{4,6},{5,7},{6,4},{7,5},{8,10},{9,11},{10,... | collective-permute-start | bytes 294920 | tf_op jit(solution)/shard_map/ppermute | solution.py:17
  12.7 8.3 %collective-permute-start.6 = (bf16[128,512]{1,0:T(8,128)(2,1)S(1)}, bf16[128,512]{1,0:T(8,128)(2,1)S(1)}, u32[]{:S(2)}, u32[]{:S(2)}) collective-permute-start(bf16[128,512]{1,0:T(8,128)(2,1)S(1)} %get-tuple-element.38), channel_id=1, source_target_pairs={{0,4},{1,5},{2,6},{3,7},{4,0},{5,1},{6,2},{7,3},{8,12},{9,13},{10,... | collective-permute-start | bytes 393224 | tf_op jit(solution)/shard_map/ppermute | solution.py:17
  14.4 11.8 %collective-permute-start.7 = (bf16[128,512]{1,0:T(8,128)(2,1)S(1)}, bf16[128,512]{1,0:T(8,128)(2,1)S(1)}, u32[]{:S(2)}, u32[]{:S(2)}) collective-permute-start(bf16[128,512]{1,0:T(8,128)(2,1)S(1)} %get-tuple-element.39), channel_id=1, source_target_pairs={{0,8},{1,9},{2,10},{3,11},{4,12},{5,13},{6,14},{7,15},{8,0},{9,1},... | collective-permute-start | bytes 393224 | tf_op jit(solution)/shard_map/ppermute | solution.py:17
  16.1 10.1 %collective-permute-start.8 = (bf16[128,512]{1,0:T(8,128)(2,1)S(1)}, bf16[128,512]{1,0:T(8,128)(2,1)S(1)}, u32[]{:S(2)}, u32[]{:S(2)}) collective-permute-start(bf16[128,512]{1,0:T(8,128)(2,1)S(1)} %get-tuple-element.40), channel_id=1, source_target_pairs={{0,12},{1,13},{2,14},{3,15},{4,8},{5,9},{6,10},{7,11},{8,4},{9,5},... | collective-permute-start | bytes 393224 | tf_op jit(solution)/shard_map/ppermute | solution.py:17
  17.1 1.5 %collective-permute-start.4 = (bf16[1024,96]{0,1:T(8,128)(2,1)S(1)}, bf16[1024,96]{0,1:T(8,128)(2,1)S(1)}, u32[]{:S(2)}, u32[]{:S(2)}) collective-permute-start(bf16[1024,96]{0,1:T(8,128)(2,1)S(1)} %pad_maximum_fusion.7), channel_id=1, source_target_pairs={{0,1},{1,0},{2,3},{3,2},{4,5},{5,4},{6,7},{7,6},{8,9},{9,8},{10,11... | collective-permute-start | bytes 589832 | tf_op jit(solution)/shard_map/ppermute | solution.py:17
  18.6 7.8 %copy-start.2 = (s32[1024]{0:T(1024)S(1)}, s32[1024]{0:T(1024)}, u32[]{:S(2)}) copy-start(s32[1024]{0:T(1024)} %param.7) | copy-start | bytes 12292
  19.4 7.0 %collective-permute-start.5 = (bf16[1024,96]{0,1:T(8,128)(2,1)S(1)}, bf16[1024,96]{0,1:T(8,128)(2,1)S(1)}, u32[]{:S(2)}, u32[]{:S(2)}) collective-permute-start(bf16[1024,96]{0,1:T(8,128)(2,1)S(1)} %get-tuple-element.36), channel_id=1, source_target_pairs={{0,16},{16,0},{1,17},{17,1},{2,18},{18,2},{3,19},{19,3},{4,20},{20... | collective-permute-start | bytes 589832 | tf_op jit(solution)/shard_map/ppermute | solution.py:17
  27.0 1.5 %collective-permute-start.9 = (bf16[1024,96]{0,1:T(8,128)(2,1)S(1)}, bf16[1024,96]{0,1:T(8,128)(2,1)S(1)}, u32[]{:S(2)}, u32[]{:S(2)}) collective-permute-start(bf16[1024,96]{0,1:T(8,128)(2,1)S(1)} %convolution_convert_fusion.1), channel_id=1, source_target_pairs={{0,1},{1,0},{2,3},{3,2},{4,5},{5,4},{6,7},{7,6},{8,9},{9,8},{10,11... | collective-permute-start | bytes 589832 | tf_op jit(solution)/shard_map/ppermute | solution.py:17
  28.6 4.9 %collective-permute-start.10 = (bf16[512,96]{0,1:T(8,128)(2,1)S(1)}, bf16[512,96]{0,1:T(8,128)(2,1)S(1)}, u32[]{:S(2)}, u32[]{:S(2)}) collective-permute-start(bf16[512,96]{0,1:T(8,128)(2,1)S(1)} %slice.347), channel_id=1, source_target_pairs={{0,2},{1,3},{2,0},{3,1},{4,6},{5,7},{6,4},{7,5},{8,10},{9,11},{10,... | collective-permute-start | bytes 294920 | tf_op jit(solution)/shard_map/ppermute | solution.py:17
  33.5 10.4 %collective-permute-start.12 = (bf16[512,96]{0,1:T(8,128)(2,1)S(1)}, bf16[512,96]{0,1:T(8,128)(2,1)S(1)}, u32[]{:S(2)}, u32[]{:S(2)}) collective-permute-start(bf16[512,96]{0,1:T(8,128)(2,1)S(1)} %fusion.20), channel_id=1, source_target_pairs={{0,8},{1,9},{2,10},{3,11},{4,12},{5,13},{6,14},{7,15},{8,0},{9,1},... | collective-permute-start | bytes 294920 | tf_op jit(solution)/shard_map/ppermute | solution.py:17
  36.4 7.6 %collective-permute-start.13 = (bf16[512,96]{0,1:T(8,128)(2,1)S(1)}, bf16[512,96]{0,1:T(8,128)(2,1)S(1)}, u32[]{:S(2)}, u32[]{:S(2)}) collective-permute-start(bf16[512,96]{0,1:T(8,128)(2,1)S(1)} %fusion.20), channel_id=1, source_target_pairs={{0,12},{1,13},{2,14},{3,15},{4,8},{5,9},{6,10},{7,11},{8,4},{9,5},... | collective-permute-start | bytes 294920 | tf_op jit(solution)/shard_map/ppermute | solution.py:17
  37.8 6.5 %collective-permute-start.11 = (bf16[512,96]{0,1:T(8,128)(2,1)S(1)}, bf16[512,96]{0,1:T(8,128)(2,1)S(1)}, u32[]{:S(2)}, u32[]{:S(2)}) collective-permute-start(bf16[512,96]{0,1:T(8,128)(2,1)S(1)} %fusion.20), channel_id=1, source_target_pairs={{0,4},{1,5},{2,6},{3,7},{4,0},{5,1},{6,2},{7,3},{8,12},{9,13},{10,... | collective-permute-start | bytes 294920 | tf_op jit(solution)/shard_map/ppermute | solution.py:17
  44.8 1.3 %collective-permute-start.14 = (bf16[256,96]{0,1:T(8,128)(2,1)S(1)}, bf16[256,96]{0,1:T(8,128)(2,1)S(1)}, u32[]{:S(2)}, u32[]{:S(2)}) collective-permute-start(bf16[256,96]{0,1:T(8,128)(2,1)S(1)} %slice.349), channel_id=1, source_target_pairs={{0,1},{1,0},{2,3},{3,2},{4,5},{5,4},{6,7},{7,6},{8,9},{9,8},{10,11... | collective-permute-start | bytes 147464 | tf_op jit(solution)/shard_map/ppermute | solution.py:17
  46.1 4.2 %collective-permute-start.15 = (bf16[256,96]{0,1:T(8,128)(2,1)S(1)}, bf16[256,96]{0,1:T(8,128)(2,1)S(1)}, u32[]{:S(2)}, u32[]{:S(2)}) collective-permute-start(bf16[256,96]{0,1:T(8,128)(2,1)S(1)} %pad_maximum_fusion.12), channel_id=1, source_target_pairs={{0,2},{1,3},{2,0},{3,1},{4,6},{5,7},{6,4},{7,5},{8,10},{9,11},{10,... | collective-permute-start | bytes 147464 | tf_op jit(solution)/shard_map/ppermute | solution.py:17
  50.3 8.1 %collective-permute-start.18 = (bf16[256,96]{0,1:T(8,128)(2,1)S(1)}, bf16[256,96]{0,1:T(8,128)(2,1)S(1)}, u32[]{:S(2)}, u32[]{:S(2)}) collective-permute-start(bf16[256,96]{0,1:T(8,128)(2,1)S(1)} %get-tuple-element.55), channel_id=1, source_target_pairs={{0,12},{1,13},{2,14},{3,15},{4,8},{5,9},{6,10},{7,11},{8,4},{9,5},... | collective-permute-start | bytes 147464 | tf_op jit(solution)/shard_map/ppermute | solution.py:17
  52.8 5.5 %collective-permute-start.17 = (bf16[256,96]{0,1:T(8,128)(2,1)S(1)}, bf16[256,96]{0,1:T(8,128)(2,1)S(1)}, u32[]{:S(2)}, u32[]{:S(2)}) collective-permute-start(bf16[256,96]{0,1:T(8,128)(2,1)S(1)} %get-tuple-element.55), channel_id=1, source_target_pairs={{0,8},{1,9},{2,10},{3,11},{4,12},{5,13},{6,14},{7,15},{8,0},{9,1},... | collective-permute-start | bytes 147464 | tf_op jit(solution)/shard_map/ppermute | solution.py:17
  53.1 4.2 %collective-permute-start.16 = (bf16[256,96]{0,1:T(8,128)(2,1)S(1)}, bf16[256,96]{0,1:T(8,128)(2,1)S(1)}, u32[]{:S(2)}, u32[]{:S(2)}) collective-permute-start(bf16[256,96]{0,1:T(8,128)(2,1)S(1)} %get-tuple-element.55), channel_id=1, source_target_pairs={{0,4},{1,5},{2,6},{3,7},{4,0},{5,1},{6,2},{7,3},{8,12},{9,13},{10,... | collective-permute-start | bytes 147464 | tf_op jit(solution)/shard_map/ppermute | solution.py:17
  58.5 1.5 %collective-permute-start.19 = (bf16[1024,96]{0,1:T(8,128)(2,1)S(1)}, bf16[1024,96]{0,1:T(8,128)(2,1)S(1)}, u32[]{:S(2)}, u32[]{:S(2)}) collective-permute-start(bf16[1024,96]{0,1:T(8,128)(2,1)S(1)} %constant_dynamic-update-slice_fusion), channel_id=1, source_target_pairs={{0,1},{1,0},{2,3},{3,2},{4,5},{5,4},{6,7},{7,6},{8,9},{9,8},{10,11... | collective-permute-start | bytes 589832 | tf_op jit(solution)/shard_map/ppermute | solution.py:17
  60.8 7.0 %collective-permute-start.20 = (bf16[1024,96]{0,1:T(8,128)(2,1)S(1)}, bf16[1024,96]{0,1:T(8,128)(2,1)S(1)}, u32[]{:S(2)}, u32[]{:S(2)}) collective-permute-start(bf16[1024,96]{0,1:T(8,128)(2,1)S(1)} %get-tuple-element.110), channel_id=1, source_target_pairs={{0,16},{16,0},{1,17},{17,1},{2,18},{18,2},{3,19},{19,3},{4,20},{20... | collective-permute-start | bytes 589832 | tf_op jit(solution)/shard_map/ppermute | solution.py:169
  68.3 1.5 %collective-permute-start.21 = (bf16[1024,96]{0,1:T(8,128)(2,1)S(1)}, bf16[1024,96]{0,1:T(8,128)(2,1)S(1)}, u32[]{:S(2)}, u32[]{:S(2)}) collective-permute-start(bf16[1024,96]{0,1:T(8,128)(2,1)S(1)} %convolution_convert_fusion), channel_id=1, source_target_pairs={{0,1},{1,0},{2,3},{3,2},{4,5},{5,4},{6,7},{7,6},{8,9},{9,8},{10,11... | collective-permute-start | bytes 589832 | tf_op jit(solution)/shard_map/ppermute | solution.py:17
  69.9 4.9 %collective-permute-start.22 = (bf16[512,96]{0,1:T(8,128)(2,1)S(1)}, bf16[512,96]{0,1:T(8,128)(2,1)S(1)}, u32[]{:S(2)}, u32[]{:S(2)}) collective-permute-start(bf16[512,96]{0,1:T(8,128)(2,1)S(1)} %slice.346), channel_id=1, source_target_pairs={{0,2},{1,3},{2,0},{3,1},{4,6},{5,7},{6,4},{7,5},{8,10},{9,11},{10,... | collective-permute-start | bytes 294920 | tf_op jit(solution)/shard_map/ppermute | solution.py:17
  74.8 9.8 %collective-permute-start.24 = (bf16[512,96]{0,1:T(8,128)(2,1)S(1)}, bf16[512,96]{0,1:T(8,128)(2,1)S(1)}, u32[]{:S(2)}, u32[]{:S(2)}) collective-permute-start(bf16[512,96]{0,1:T(8,128)(2,1)S(1)} %fusion.21), channel_id=1, source_target_pairs={{0,8},{1,9},{2,10},{3,11},{4,12},{5,13},{6,14},{7,15},{8,0},{9,1},... | collective-permute-start | bytes 294920 | tf_op jit(solution)/shard_map/ppermute | solution.py:17
  76.4 8.3 %collective-permute-start.25 = (bf16[512,96]{0,1:T(8,128)(2,1)S(1)}, bf16[512,96]{0,1:T(8,128)(2,1)S(1)}, u32[]{:S(2)}, u32[]{:S(2)}) collective-permute-start(bf16[512,96]{0,1:T(8,128)(2,1)S(1)} %fusion.21), channel_id=1, source_target_pairs={{0,12},{1,13},{2,14},{3,15},{4,8},{5,9},{6,10},{7,11},{8,4},{9,5},... | collective-permute-start | bytes 294920 | tf_op jit(solution)/shard_map/ppermute | solution.py:17
  77.7 7.2 %collective-permute-start.23 = (bf16[512,96]{0,1:T(8,128)(2,1)S(1)}, bf16[512,96]{0,1:T(8,128)(2,1)S(1)}, u32[]{:S(2)}, u32[]{:S(2)}) collective-permute-start(bf16[512,96]{0,1:T(8,128)(2,1)S(1)} %fusion.21), channel_id=1, source_target_pairs={{0,4},{1,5},{2,6},{3,7},{4,0},{5,1},{6,2},{7,3},{8,12},{9,13},{10,... | collective-permute-start | bytes 294920 | tf_op jit(solution)/shard_map/ppermute | solution.py:17
  85.5 1.3 %collective-permute-start.26 = (bf16[256,96]{0,1:T(8,128)(2,1)S(1)}, bf16[256,96]{0,1:T(8,128)(2,1)S(1)}, u32[]{:S(2)}, u32[]{:S(2)}) collective-permute-start(bf16[256,96]{0,1:T(8,128)(2,1)S(1)} %slice.348), channel_id=1, source_target_pairs={{0,1},{1,0},{2,3},{3,2},{4,5},{5,4},{6,7},{7,6},{8,9},{9,8},{10,11... | collective-permute-start | bytes 147464 | tf_op jit(solution)/shard_map/ppermute | solution.py:17
  86.9 4.2 %collective-permute-start.27 = (bf16[256,96]{0,1:T(8,128)(2,1)S(1)}, bf16[256,96]{0,1:T(8,128)(2,1)S(1)}, u32[]{:S(2)}, u32[]{:S(2)}) collective-permute-start(bf16[256,96]{0,1:T(8,128)(2,1)S(1)} %pad_maximum_fusion.13), channel_id=1, source_target_pairs={{0,2},{1,3},{2,0},{3,1},{4,6},{5,7},{6,4},{7,5},{8,10},{9,11},{10,... | collective-permute-start | bytes 147464 | tf_op jit(solution)/shard_map/ppermute | solution.py:17
  91.0 7.7 %collective-permute-start.30 = (bf16[256,96]{0,1:T(8,128)(2,1)S(1)}, bf16[256,96]{0,1:T(8,128)(2,1)S(1)}, u32[]{:S(2)}, u32[]{:S(2)}) collective-permute-start(bf16[256,96]{0,1:T(8,128)(2,1)S(1)} %get-tuple-element.53), channel_id=1, source_target_pairs={{0,12},{1,13},{2,14},{3,15},{4,8},{5,9},{6,10},{7,11},{8,4},{9,5},... | collective-permute-start | bytes 147464 | tf_op jit(solution)/shard_map/ppermute | solution.py:17
  93.2 5.5 %collective-permute-start.29 = (bf16[256,96]{0,1:T(8,128)(2,1)S(1)}, bf16[256,96]{0,1:T(8,128)(2,1)S(1)}, u32[]{:S(2)}, u32[]{:S(2)}) collective-permute-start(bf16[256,96]{0,1:T(8,128)(2,1)S(1)} %get-tuple-element.53), channel_id=1, source_target_pairs={{0,8},{1,9},{2,10},{3,11},{4,12},{5,13},{6,14},{7,15},{8,0},{9,1},... | collective-permute-start | bytes 147464 | tf_op jit(solution)/shard_map/ppermute | solution.py:17
  94.2 4.3 %collective-permute-start.28 = (bf16[256,96]{0,1:T(8,128)(2,1)S(1)}, bf16[256,96]{0,1:T(8,128)(2,1)S(1)}, u32[]{:S(2)}, u32[]{:S(2)}) collective-permute-start(bf16[256,96]{0,1:T(8,128)(2,1)S(1)} %get-tuple-element.53), channel_id=1, source_target_pairs={{0,4},{1,5},{2,6},{3,7},{4,0},{5,1},{6,2},{7,3},{8,12},{9,13},{10,... | collective-permute-start | bytes 147464 | tf_op jit(solution)/shard_map/ppermute | solution.py:17
  98.8 1.5 %collective-permute-start.31 = (bf16[1024,96]{0,1:T(8,128)(2,1)S(1)}, bf16[1024,96]{0,1:T(8,128)(2,1)S(1)}, u32[]{:S(2)}, u32[]{:S(2)}) collective-permute-start(bf16[1024,96]{0,1:T(8,128)(2,1)S(1)} %constant_dynamic-update-slice_fusion.8), channel_id=1, source_target_pairs={{0,1},{1,0},{2,3},{3,2},{4,5},{5,4},{6,7},{7,6},{8,9},{9,8},{10,11... | collective-permute-start | bytes 589832 | tf_op jit(solution)/shard_map/ppermute | solution.py:17
  101.3 11.1 %copy-start = (f32[1024,96]{0,1:T(8,128)}, f32[1024,96]{0,1:T(8,128)S(1)}, u32[]{:S(2)}) copy-start(f32[1024,96]{0,1:T(8,128)S(1)} %fusion.3) | copy-start | bytes 1179652
  102.1 9.9 %all-to-all-start = ((f32[16,1,96]{2,1,0:T(1,128)}), f32[16,1,96]{2,1,0:T(1,128)S(1)}, u32[]{:S(2)}, u32[]{:S(2)}) async-start(f32[16,1,96]{2,1,0:T(1,128)} %broadcast_in_dim.23), calls=%async_computation | async-start | bytes 16384 | tf_op jit(solution)/shard_map/all_to_all | solution.py:181

commit v10 on v8

--- a/solution.py
+++ b/solution.py
@@ -155,8 +155,8 @@
         part = part[:, :classes] + part[:, classes:]
         keep, send = halved(part)
         part = keep + swapped(send, "rows", 1)
-        top, bottom = halved(part)
-        delta = part + swapped(jnp.concatenate([bottom, top]).astype(LOW), "rows", 2).astype(WIDE)
+        top, bottom = halved(swapped(part.astype(LOW), "rows", 2))
+        delta = part + jnp.concatenate([bottom, top]).astype(WIDE)
         delta_low = delta.astype(LOW)
         slots = [delta_low] + [swapped(delta_low, "rows", z) for z in near[1:]]
         delta_low = jnp.concatenate([s[:own] for s in slots] + [s[own:] for s in slots], axis=0)

time: 113 us -> 113 us (level)
  no operation moved by 1% of the time
where the time goes in v10:
time: 113 us
  waiting for transfers between devices  57.8 us (51%)
  starting transfers between devices  37.7 us (33%)
  matrix products  7.31 us (6%)
  local copies, waits for them, and re-layouts  3.27 us (3%)
  other arithmetic  2.95 us (3%)
  Pallas kernels  2.41 us (2%)
    ppermute x31, waiting for transfers between devices, swapped(): return lax.ppermute(shard, axis, [(i, i ^ bit) for i in range(peers)])  46.6 us
    ppermute x31, starting transfers between devices, swapped(): return lax.ppermute(shard, axis, [(i, i ^ bit) for i in range(peers)])  32.7 us
    all_to_all x1, waiting for transfers between devices, on_device(): lax.all_to_all(jnp.broadcast_to(squares[None], (nrows, 1, classes)), 'row...  5.74 us
    ppermute x1, waiting for transfers between devices, on_device(): got = lax.ppermute(sent.astype(LOW), 'feat', along).astype(WIDE)  5.45 us
    all_to_all x1, starting transfers between devices, on_device(): lax.all_to_all(jnp.broadcast_to(squares[None], (nrows, 1, classes)), 'row...  3.48 us
    pallas_call x1, Pallas kernels, reordered(): pl.pallas_call(functools.partial(reorder_kernel, order, own), out_shape=[...  2.41 us
    dot_general x3, matrix products, product(): return first + jnp.dot(sending, far, preferred_element_type=WIDE)  2.36 us
    dot_general x3, matrix products, product(): first, far = tied(jnp.dot(keeping, rows, preferred_element_type=WIDE), far)  2.33 us
  transfers between devices with their start and end apart: 33, of which 24 were waited for; matrix products, arithmetic and copies ran while one was open for 6% of the time, Pallas kernels for 2%

profile of v10, /device:TPU:0, one launch (start us, length us, event | category | flops | bytes accessed | tf_op | source)
XLA Modules:
  0.0 112.5 jit_solution(17709767808013766364)
XLA Ops:
  0.6 0.8 convert.96
  1.4 4.0 %collective-permute-start.1 = (bf16[128,96]{0,1:T(8,128)(2,1)S(1)}, bf16[128,96]{0,1:T(8,128)(2,1)S(1)}, u32[]{:S(2)}, u32[]{:S(2)}) collective-permute-start(bf16[128,96]{0,1:T(8,128)(2,1)S(1)} %convert.96), channel_id=1, source_target_pairs={{0,8},{1,9},{2,10},{3,11},{4,12},{5,13},{6,14},{7,15},{8,0},{9,1},... | collective-permute-start | bytes 73736 | tf_op jit(solution)/shard_map/ppermute | solution.py:17
  5.5 1.3 %collective-permute-start.2 = (bf16[128,96]{0,1:T(8,128)(2,1)S(1)}, bf16[128,96]{0,1:T(8,128)(2,1)S(1)}, u32[]{:S(2)}, u32[]{:S(2)}) collective-permute-start(bf16[128,96]{0,1:T(8,128)(2,1)S(1)} %convert.96), channel_id=1, source_target_pairs={{0,12},{1,13},{2,14},{3,15},{4,8},{5,9},{6,10},{7,11},{8,4},{9,5},... | collective-permute-start | bytes 73736 | tf_op jit(solution)/shard_map/ppermute | solution.py:17
  7.1 1.3 %dynamic-slice_convert_fusion.3 = (bf16[128,128]{1,0:T(8,128)(2,1)S(1)}, bf16[128,128]{1,0:T(8,128)(2,1)S(1)}, bf16[128,128]{1,0:T(8,128)(2,1)S(1)}, bf16[128,12...) fusion(f32[128,2048]{1,0:T(8,128)} %param.6, ...), kind=kLoop, calls=%fused_computation.67 | loop fusion | bytes 1048640 | tf_op jit(solution)/shard_map/convert.2
  8.5 2.4 %shard_map.67 = (bf16[1024,1024]{1,0:T(8,128)(2,1)S(1)}, bf16[1024,1024]{1,0:T(8,128)(2,1)S(1)}) custom-call(s32[1]{0:T(128)} %bitcast.me_ref, bf16[1024,2048]{1,0:T(8,128)(2,1)} %given.1), custom_call_target="tpu_custom_call" | custom-call | bytes 8388608 | tf_op jit(solution)/shard_map/pallas_call | solution.py:58
  11.1 1.6 %collective-permute-start.3 = (bf16[512,96]{0,1:T(8,128)(2,1)S(1)}, bf16[512,96]{0,1:T(8,128)(2,1)S(1)}, u32[]{:S(2)}, u32[]{:S(2)}) collective-permute-start(bf16[512,96]{0,1:T(8,128)(2,1)S(1)} %pad_maximum_fusion.6), channel_id=1, source_target_pairs={{0,2},{1,3},{2,0},{3,1},{4,6},{5,7},{6,4},{7,5},{8,10},{9,11},{10,... | collective-permute-start | bytes 294920 | tf_op jit(solution)/shard_map/ppermute | solution.py:17
  12.7 1.7 %collective-permute-start.6 = (bf16[128,512]{1,0:T(8,128)(2,1)S(1)}, bf16[128,512]{1,0:T(8,128)(2,1)S(1)}, u32[]{:S(2)}, u32[]{:S(2)}) collective-permute-start(bf16[128,512]{1,0:T(8,128)(2,1)S(1)} %get-tuple-element.38), channel_id=1, source_target_pairs={{0,4},{1,5},{2,6},{3,7},{4,0},{5,1},{6,2},{7,3},{8,12},{9,13},{10,... | collective-permute-start | bytes 393224 | tf_op jit(solution)/shard_map/ppermute | solution.py:17
  14.4 1.7 %collective-permute-start.7 = (bf16[128,512]{1,0:T(8,128)(2,1)S(1)}, bf16[128,512]{1,0:T(8,128)(2,1)S(1)}, u32[]{:S(2)}, u32[]{:S(2)}) collective-permute-start(bf16[128,512]{1,0:T(8,128)(2,1)S(1)} %get-tuple-element.39), channel_id=1, source_target_pairs={{0,8},{1,9},{2,10},{3,11},{4,12},{5,13},{6,14},{7,15},{8,0},{9,1},... | collective-permute-start | bytes 393224 | tf_op jit(solution)/shard_map/ppermute | solution.py:17
  16.1 1.0 collective-permute-start.8
  17.2 0.8 fusion.34
  18.0 0.6 collective-permute-done.4
  18.6 0.8 reduce-precision_convert_fusion
  19.4 1.6 %collective-permute-start.5 = (bf16[1024,96]{0,1:T(8,128)(2,1)S(1)}, bf16[1024,96]{0,1:T(8,128)(2,1)S(1)}, u32[]{:S(2)}, u32[]{:S(2)}) collective-permute-start(bf16[1024,96]{0,1:T(8,128)(2,1)S(1)} %get-tuple-element.36), channel_id=1, source_target_pairs={{0,16},{16,0},{1,17},{17,1},{2,18},{18,2},{3,19},{19,3},{4,20},{20... | collective-permute-start | bytes 589832 | tf_op jit(solution)/shard_map/ppermute | solution.py:17
  21.0 5.2 %collective-permute-done.7 = bf16[128,512]{1,0:T(8,128)(2,1)S(1)} collective-permute-done((bf16[128,512]{1,0:T(8,128)(2,1)S(1)}, bf16[128,512]{1,0:T(8,128)(2,1)S(1)}, u32[]{:S(2)}, u32[]{:S(2)}) %collective-permute-start.7) | collective-permute-done | bytes 131104 | tf_op jit(solution)/shard_map/ppermute | solution.py:17
  27.6 0.9 collective-permute-done.9
  29.2 1.0 constant_dynamic-slice_fusion.3
  30.1 3.4 %collective-permute-done.10 = bf16[512,96]{0,1:T(8,128)(2,1)S(1)} collective-permute-done((bf16[512,96]{0,1:T(8,128)(2,1)S(1)}, bf16[512,96]{0,1:T(8,128)(2,1)S(1)}, u32[]{:S(2)}, u32[]{:S(2)}) %collective-permute-start.10) | collective-permute-done | bytes 98336 | tf_op jit(solution)/shard_map/ppermute | solution.py:17
  33.5 2.8 %collective-permute-start.12 = (bf16[512,96]{0,1:T(8,128)(2,1)S(1)}, bf16[512,96]{0,1:T(8,128)(2,1)S(1)}, u32[]{:S(2)}, u32[]{:S(2)}) collective-permute-start(bf16[512,96]{0,1:T(8,128)(2,1)S(1)} %fusion.20), channel_id=1, source_target_pairs={{0,8},{1,9},{2,10},{3,11},{4,12},{5,13},{6,14},{7,15},{8,0},{9,1},... | collective-permute-start | bytes 294920 | tf_op jit(solution)/shard_map/ppermute | solution.py:17
  36.4 1.4 %collective-permute-start.13 = (bf16[512,96]{0,1:T(8,128)(2,1)S(1)}, bf16[512,96]{0,1:T(8,128)(2,1)S(1)}, u32[]{:S(2)}, u32[]{:S(2)}) collective-permute-start(bf16[512,96]{0,1:T(8,128)(2,1)S(1)} %fusion.20), channel_id=1, source_target_pairs={{0,12},{1,13},{2,14},{3,15},{4,8},{5,9},{6,10},{7,11},{8,4},{9,5},... | collective-permute-start | bytes 294920 | tf_op jit(solution)/shard_map/ppermute | solution.py:17
  37.8 6.1 %collective-permute-done.12 = bf16[512,96]{0,1:T(8,128)(2,1)S(1)} collective-permute-done((bf16[512,96]{0,1:T(8,128)(2,1)S(1)}, bf16[512,96]{0,1:T(8,128)(2,1)S(1)}, u32[]{:S(2)}, u32[]{:S(2)}) %collective-permute-start.12) | collective-permute-done | bytes 98336 | tf_op jit(solution)/shard_map/ppermute | solution.py:17
  44.9 1.3 %collective-permute-done.14 = f32[256,96]{0,1:T(8,128)S(1)} collective-permute-done((f32[256,96]{0,1:T(8,128)S(1)}, f32[256,96]{0,1:T(8,128)S(1)}, u32[]{:S(2)}, u32[]{:S(2)}) %collective-permute-start.14) | collective-permute-done | bytes 98336 | tf_op jit(solution)/shard_map/ppermute | solution.py:17
  46.7 3.6 %collective-permute-done.15 = bf16[256,96]{0,1:T(8,128)(2,1)S(1)} collective-permute-done((bf16[256,96]{0,1:T(8,128)(2,1)S(1)}, bf16[256,96]{0,1:T(8,128)(2,1)S(1)}, u32[]{:S(2)}, u32[]{:S(2)}) %collective-permute-start.15) | collective-permute-done | bytes 49184 | tf_op jit(solution)/shard_map/ppermute | solution.py:17
  50.3 2.5 %collective-permute-start.18 = (bf16[256,96]{0,1:T(8,128)(2,1)S(1)}, bf16[256,96]{0,1:T(8,128)(2,1)S(1)}, u32[]{:S(2)}, u32[]{:S(2)}) collective-permute-start(bf16[256,96]{0,1:T(8,128)(2,1)S(1)} %get-tuple-element.55), channel_id=1, source_target_pairs={{0,12},{1,13},{2,14},{3,15},{4,8},{5,9},{6,10},{7,11},{8,4},{9,5},... | collective-permute-start | bytes 147464 | tf_op jit(solution)/shard_map/ppermute | solution.py:17
  53.2 1.6 %collective-permute-start.16 = (bf16[256,96]{0,1:T(8,128)(2,1)S(1)}, bf16[256,96]{0,1:T(8,128)(2,1)S(1)}, u32[]{:S(2)}, u32[]{:S(2)}) collective-permute-start(bf16[256,96]{0,1:T(8,128)(2,1)S(1)} %get-tuple-element.55), channel_id=1, source_target_pairs={{0,4},{1,5},{2,6},{3,7},{4,0},{5,1},{6,2},{7,3},{8,12},{9,13},{10,... | collective-permute-start | bytes 147464 | tf_op jit(solution)/shard_map/ppermute | solution.py:17
  54.8 2.5 %collective-permute-done.16 = bf16[256,96]{0,1:T(8,128)(2,1)S(1)} collective-permute-done((bf16[256,96]{0,1:T(8,128)(2,1)S(1)}, bf16[256,96]{0,1:T(8,128)(2,1)S(1)}, u32[]{:S(2)}, u32[]{:S(2)}) %collective-permute-start.16) | collective-permute-done | bytes 49184 | tf_op jit(solution)/shard_map/ppermute | solution.py:17
  57.4 1.0 collective-permute-done.17
  58.6 0.8 fusion.46
  59.4 0.6 collective-permute-done.19
  60.0 0.8 fusion.5
  60.8 1.6 %collective-permute-start.20 = (bf16[1024,96]{0,1:T(8,128)(2,1)S(1)}, bf16[1024,96]{0,1:T(8,128)(2,1)S(1)}, u32[]{:S(2)}, u32[]{:S(2)}) collective-permute-start(bf16[1024,96]{0,1:T(8,128)(2,1)S(1)} %get-tuple-element.110), channel_id=1, source_target_pairs={{0,16},{16,0},{1,17},{17,1},{2,18},{18,2},{3,19},{19,3},{4,20},{20... | collective-permute-start | bytes 589832 | tf_op jit(solution)/shard_map/ppermute | solution.py:169
  62.4 5.4 %collective-permute-done.20 = bf16[1024,96]{0,1:T(8,128)(2,1)S(1)} collective-permute-done((bf16[1024,96]{0,1:T(8,128)(2,1)S(1)}, bf16[1024,96]{0,1:T(8,128)(2,1)S(1)}, u32[]{:S(2)}, u32[]{:S(2)}) %collective-permute-start.20) | collective-permute-done | bytes 196640 | tf_op jit(solution)/shard_map/ppermute | solution.py:169
  68.9 0.9 collective-permute-done.21
  70.5 4.3 %collective-permute-done.22 = bf16[512,96]{0,1:T(8,128)(2,1)S(1)} collective-permute-done((bf16[512,96]{0,1:T(8,128)(2,1)S(1)}, bf16[512,96]{0,1:T(8,128)(2,1)S(1)}, u32[]{:S(2)}, u32[]{:S(2)}) %collective-permute-start.22) | collective-permute-done | bytes 98336 | tf_op jit(solution)/shard_map/ppermute | solution.py:17
  74.8 1.6 %collective-permute-start.24 = (bf16[512,96]{0,1:T(8,128)(2,1)S(1)}, bf16[512,96]{0,1:T(8,128)(2,1)S(1)}, u32[]{:S(2)}, u32[]{:S(2)}) collective-permute-start(bf16[512,96]{0,1:T(8,128)(2,1)S(1)} %fusion.21), channel_id=1, source_target_pairs={{0,8},{1,9},{2,10},{3,11},{4,12},{5,13},{6,14},{7,15},{8,0},{9,1},... | collective-permute-start | bytes 294920 | tf_op jit(solution)/shard_map/ppermute | solution.py:17
  76.4 1.4 %collective-permute-start.25 = (bf16[512,96]{0,1:T(8,128)(2,1)S(1)}, bf16[512,96]{0,1:T(8,128)(2,1)S(1)}, u32[]{:S(2)}, u32[]{:S(2)}) collective-permute-start(bf16[512,96]{0,1:T(8,128)(2,1)S(1)} %fusion.21), channel_id=1, source_target_pairs={{0,12},{1,13},{2,14},{3,15},{4,8},{5,9},{6,10},{7,11},{8,4},{9,5},... | collective-permute-start | bytes 294920 | tf_op jit(solution)/shard_map/ppermute | solution.py:17
  78.4 6.3 %collective-permute-done.24 = bf16[512,96]{0,1:T(8,128)(2,1)S(1)} collective-permute-done((bf16[512,96]{0,1:T(8,128)(2,1)S(1)}, bf16[512,96]{0,1:T(8,128)(2,1)S(1)}, u32[]{:S(2)}, u32[]{:S(2)}) %collective-permute-start.24) | collective-permute-done | bytes 98336 | tf_op jit(solution)/shard_map/ppermute | solution.py:17
  85.6 1.3 %collective-permute-done.26 = f32[256,96]{0,1:T(8,128)S(1)} collective-permute-done((f32[256,96]{0,1:T(8,128)S(1)}, f32[256,96]{0,1:T(8,128)S(1)}, u32[]{:S(2)}, u32[]{:S(2)}) %collective-permute-start.26) | collective-permute-done | bytes 98336 | tf_op jit(solution)/shard_map/ppermute | solution.py:17
  87.5 3.6 %collective-permute-done.27 = bf16[256,96]{0,1:T(8,128)(2,1)S(1)} collective-permute-done((bf16[256,96]{0,1:T(8,128)(2,1)S(1)}, bf16[256,96]{0,1:T(8,128)(2,1)S(1)}, u32[]{:S(2)}, u32[]{:S(2)}) %collective-permute-start.27) | collective-permute-done | bytes 49184 | tf_op jit(solution)/shard_map/ppermute | solution.py:17
  91.1 2.2 %collective-permute-start.30 = (bf16[256,96]{0,1:T(8,128)(2,1)S(1)}, bf16[256,96]{0,1:T(8,128)(2,1)S(1)}, u32[]{:S(2)}, u32[]{:S(2)}) collective-permute-start(bf16[256,96]{0,1:T(8,128)(2,1)S(1)} %get-tuple-element.53), channel_id=1, source_target_pairs={{0,12},{1,13},{2,14},{3,15},{4,8},{5,9},{6,10},{7,11},{8,4},{9,5},... | collective-permute-start | bytes 147464 | tf_op jit(solution)/shard_map/ppermute | solution.py:17
  93.3 1.0 collective-permute-start.29
  94.3 1.3 %collective-permute-start.28 = (bf16[256,96]{0,1:T(8,128)(2,1)S(1)}, bf16[256,96]{0,1:T(8,128)(2,1)S(1)}, u32[]{:S(2)}, u32[]{:S(2)}) collective-permute-start(bf16[256,96]{0,1:T(8,128)(2,1)S(1)} %get-tuple-element.53), channel_id=1, source_target_pairs={{0,4},{1,5},{2,6},{3,7},{4,0},{5,1},{6,2},{7,3},{8,12},{9,13},{10,... | collective-permute-start | bytes 147464 | tf_op jit(solution)/shard_map/ppermute | solution.py:17
  95.6 3.0 %collective-permute-done.28 = bf16[256,96]{0,1:T(8,128)(2,1)S(1)} collective-permute-done((bf16[256,96]{0,1:T(8,128)(2,1)S(1)}, bf16[256,96]{0,1:T(8,128)(2,1)S(1)}, u32[]{:S(2)}, u32[]{:S(2)}) %collective-permute-start.28) | collective-permute-done | bytes 49184 | tf_op jit(solution)/shard_map/ppermute | solution.py:17
  99.0 0.8 fusion.47
  99.8 0.6 collective-permute-done.31
  100.4 0.8 fusion.48
  102.2 3.5 %all-to-all-start = ((f32[16,1,96]{2,1,0:T(1,128)}), f32[16,1,96]{2,1,0:T(1,128)S(1)}, u32[]{:S(2)}, u32[]{:S(2)}) async-start(f32[16,1,96]{2,1,0:T(1,128)} %broadcast_in_dim.23), calls=%async_computation | async-start | bytes 16384 | tf_op jit(solution)/shard_map/all_to_all | solution.py:181
  105.6 0.6 fusion.26
  106.3 5.7 %all-to-all-done = f32[16,1,96]{2,1,0:T(1,128)S(1)} async-done(((f32[16,1,96]{2,1,0:T(1,128)}), f32[16,1,96]{2,1,0:T(1,128)S(1)}, u32[]{:S(2)}, u32[]{:S(2)}) %all-to-all-start) | async-done | bytes 6176 | tf_op jit(solution)/shard_map/all_to_all | solution.py:181
  (96 shorter events, 10.2 us)
Async XLA Ops:
  1.4 9.5 %collective-permute-start.1 = (bf16[128,96]{0,1:T(8,128)(2,1)S(1)}, bf16[128,96]{0,1:T(8,128)(2,1)S(1)}, u32[]{:S(2)}, u32[]{:S(2)}) collective-permute-start(bf16[128,96]{0,1:T(8,128)(2,1)S(1)} %convert.96), channel_id=1, source_target_pairs={{0,8},{1,9},{2,10},{3,11},{4,12},{5,13},{6,14},{7,15},{8,0},{9,1},... | collective-permute-start | bytes 73736 | tf_op jit(solution)/shard_map/ppermute | solution.py:17
  5.5 5.6 %collective-permute-start.2 = (bf16[128,96]{0,1:T(8,128)(2,1)S(1)}, bf16[128,96]{0,1:T(8,128)(2,1)S(1)}, u32[]{:S(2)}, u32[]{:S(2)}) collective-permute-start(bf16[128,96]{0,1:T(8,128)(2,1)S(1)} %convert.96), channel_id=1, source_target_pairs={{0,12},{1,13},{2,14},{3,15},{4,8},{5,9},{6,10},{7,11},{8,4},{9,5},... | collective-permute-start | bytes 73736 | tf_op jit(solution)/shard_map/ppermute | solution.py:17
  6.8 4.3 %collective-permute-start = (bf16[128,96]{0,1:T(8,128)(2,1)S(1)}, bf16[128,96]{0,1:T(8,128)(2,1)S(1)}, u32[]{:S(2)}, u32[]{:S(2)}) collective-permute-start(bf16[128,96]{0,1:T(8,128)(2,1)S(1)} %convert.96), channel_id=1, source_target_pairs={{0,4},{1,5},{2,6},{3,7},{4,0},{5,1},{6,2},{7,3},{8,12},{9,13},{10,... | collective-permute-start | bytes 73736 | tf_op jit(solution)/shard_map/ppermute | solution.py:17
  8.5 2.6 %copy-start.1 = (f32[128,96]{0,1:T(8,128)S(1)}, f32[128,96]{0,1:T(8,128)}, u32[]{:S(2)}) copy-start(f32[128,96]{0,1:T(8,128)} %param.5) | copy-start | bytes 147460
  11.1 6.0 %collective-permute-start.3 = (bf16[512,96]{0,1:T(8,128)(2,1)S(1)}, bf16[512,96]{0,1:T(8,128)(2,1)S(1)}, u32[]{:S(2)}, u32[]{:S(2)}) collective-permute-start(bf16[512,96]{0,1:T(8,128)(2,1)S(1)} %pad_maximum_fusion.6), channel_id=1, source_target_pairs={{0,2},{1,3},{2,0},{3,1},{4,6},{5,7},{6,4},{7,5},{8,10},{9,11},{10,... | collective-permute-start | bytes 294920 | tf_op jit(solution)/shard_map/ppermute | solution.py:17
  12.7 8.3 %collective-permute-start.6 = (bf16[128,512]{1,0:T(8,128)(2,1)S(1)}, bf16[128,512]{1,0:T(8,128)(2,1)S(1)}, u32[]{:S(2)}, u32[]{:S(2)}) collective-permute-start(bf16[128,512]{1,0:T(8,128)(2,1)S(1)} %get-tuple-element.38), channel_id=1, source_target_pairs={{0,4},{1,5},{2,6},{3,7},{4,0},{5,1},{6,2},{7,3},{8,12},{9,13},{10,... | collective-permute-start | bytes 393224 | tf_op jit(solution)/shard_map/ppermute | solution.py:17
  14.4 11.8 %collective-permute-start.7 = (bf16[128,512]{1,0:T(8,128)(2,1)S(1)}, bf16[128,512]{1,0:T(8,128)(2,1)S(1)}, u32[]{:S(2)}, u32[]{:S(2)}) collective-permute-start(bf16[128,512]{1,0:T(8,128)(2,1)S(1)} %get-tuple-element.39), channel_id=1, source_target_pairs={{0,8},{1,9},{2,10},{3,11},{4,12},{5,13},{6,14},{7,15},{8,0},{9,1},... | collective-permute-start | bytes 393224 | tf_op jit(solution)/shard_map/ppermute | solution.py:17
  16.1 10.1 %collective-permute-start.8 = (bf16[128,512]{1,0:T(8,128)(2,1)S(1)}, bf16[128,512]{1,0:T(8,128)(2,1)S(1)}, u32[]{:S(2)}, u32[]{:S(2)}) collective-permute-start(bf16[128,512]{1,0:T(8,128)(2,1)S(1)} %get-tuple-element.40), channel_id=1, source_target_pairs={{0,12},{1,13},{2,14},{3,15},{4,8},{5,9},{6,10},{7,11},{8,4},{9,5},... | collective-permute-start | bytes 393224 | tf_op jit(solution)/shard_map/ppermute | solution.py:17
  17.1 1.5 %collective-permute-start.4 = (bf16[1024,96]{0,1:T(8,128)(2,1)S(1)}, bf16[1024,96]{0,1:T(8,128)(2,1)S(1)}, u32[]{:S(2)}, u32[]{:S(2)}) collective-permute-start(bf16[1024,96]{0,1:T(8,128)(2,1)S(1)} %pad_maximum_fusion.7), channel_id=1, source_target_pairs={{0,1},{1,0},{2,3},{3,2},{4,5},{5,4},{6,7},{7,6},{8,9},{9,8},{10,11... | collective-permute-start | bytes 589832 | tf_op jit(solution)/shard_map/ppermute | solution.py:17
  18.6 7.8 %copy-start.2 = (s32[1024]{0:T(1024)S(1)}, s32[1024]{0:T(1024)}, u32[]{:S(2)}) copy-start(s32[1024]{0:T(1024)} %param.7) | copy-start | bytes 12292
  19.4 7.0 %collective-permute-start.5 = (bf16[1024,96]{0,1:T(8,128)(2,1)S(1)}, bf16[1024,96]{0,1:T(8,128)(2,1)S(1)}, u32[]{:S(2)}, u32[]{:S(2)}) collective-permute-start(bf16[1024,96]{0,1:T(8,128)(2,1)S(1)} %get-tuple-element.36), channel_id=1, source_target_pairs={{0,16},{16,0},{1,17},{17,1},{2,18},{18,2},{3,19},{19,3},{4,20},{20... | collective-permute-start | bytes 589832 | tf_op jit(solution)/shard_map/ppermute | solution.py:17
  27.0 1.5 %collective-permute-start.9 = (bf16[1024,96]{0,1:T(8,128)(2,1)S(1)}, bf16[1024,96]{0,1:T(8,128)(2,1)S(1)}, u32[]{:S(2)}, u32[]{:S(2)}) collective-permute-start(bf16[1024,96]{0,1:T(8,128)(2,1)S(1)} %convolution_convert_fusion.1), channel_id=1, source_target_pairs={{0,1},{1,0},{2,3},{3,2},{4,5},{5,4},{6,7},{7,6},{8,9},{9,8},{10,11... | collective-permute-start | bytes 589832 | tf_op jit(solution)/shard_map/ppermute | solution.py:17
  28.6 4.9 %collective-permute-start.10 = (bf16[512,96]{0,1:T(8,128)(2,1)S(1)}, bf16[512,96]{0,1:T(8,128)(2,1)S(1)}, u32[]{:S(2)}, u32[]{:S(2)}) collective-permute-start(bf16[512,96]{0,1:T(8,128)(2,1)S(1)} %slice.339), channel_id=1, source_target_pairs={{0,2},{1,3},{2,0},{3,1},{4,6},{5,7},{6,4},{7,5},{8,10},{9,11},{10,... | collective-permute-start | bytes 294920 | tf_op jit(solution)/shard_map/ppermute | solution.py:17
  33.5 10.4 %collective-permute-start.12 = (bf16[512,96]{0,1:T(8,128)(2,1)S(1)}, bf16[512,96]{0,1:T(8,128)(2,1)S(1)}, u32[]{:S(2)}, u32[]{:S(2)}) collective-permute-start(bf16[512,96]{0,1:T(8,128)(2,1)S(1)} %fusion.20), channel_id=1, source_target_pairs={{0,8},{1,9},{2,10},{3,11},{4,12},{5,13},{6,14},{7,15},{8,0},{9,1},... | collective-permute-start | bytes 294920 | tf_op jit(solution)/shard_map/ppermute | solution.py:17
  36.4 7.6 %collective-permute-start.13 = (bf16[512,96]{0,1:T(8,128)(2,1)S(1)}, bf16[512,96]{0,1:T(8,128)(2,1)S(1)}, u32[]{:S(2)}, u32[]{:S(2)}) collective-permute-start(bf16[512,96]{0,1:T(8,128)(2,1)S(1)} %fusion.20), channel_id=1, source_target_pairs={{0,12},{1,13},{2,14},{3,15},{4,8},{5,9},{6,10},{7,11},{8,4},{9,5},... | collective-permute-start | bytes 294920 | tf_op jit(solution)/shard_map/ppermute | solution.py:17
  37.8 6.5 %collective-permute-start.11 = (bf16[512,96]{0,1:T(8,128)(2,1)S(1)}, bf16[512,96]{0,1:T(8,128)(2,1)S(1)}, u32[]{:S(2)}, u32[]{:S(2)}) collective-permute-start(bf16[512,96]{0,1:T(8,128)(2,1)S(1)} %fusion.20), channel_id=1, source_target_pairs={{0,4},{1,5},{2,6},{3,7},{4,0},{5,1},{6,2},{7,3},{8,12},{9,13},{10,... | collective-permute-start | bytes 294920 | tf_op jit(solution)/shard_map/ppermute | solution.py:17
  44.8 1.4 %collective-permute-start.14 = (f32[256,96]{0,1:T(8,128)S(1)}, f32[256,96]{0,1:T(8,128)S(1)}, u32[]{:S(2)}, u32[]{:S(2)}) collective-permute-start(f32[256,96]{0,1:T(8,128)S(1)} %slice.250), channel_id=1, source_target_pairs={{0,1},{1,0},{2,3},{3,2},{4,5},{5,4},{6,7},{7,6},{8,9},{9,8},{10,11... | collective-permute-start | bytes 294920 | tf_op jit(solution)/shard_map/ppermute | solution.py:17
  46.2 4.2 %collective-permute-start.15 = (bf16[256,96]{0,1:T(8,128)(2,1)S(1)}, bf16[256,96]{0,1:T(8,128)(2,1)S(1)}, u32[]{:S(2)}, u32[]{:S(2)}) collective-permute-start(bf16[256,96]{0,1:T(8,128)(2,1)S(1)} %fusion.27), channel_id=1, source_target_pairs={{0,2},{1,3},{2,0},{3,1},{4,6},{5,7},{6,4},{7,5},{8,10},{9,11},{10,... | collective-permute-start | bytes 147464 | tf_op jit(solution)/shard_map/ppermute | solution.py:17
  50.3 8.1 %collective-permute-start.18 = (bf16[256,96]{0,1:T(8,128)(2,1)S(1)}, bf16[256,96]{0,1:T(8,128)(2,1)S(1)}, u32[]{:S(2)}, u32[]{:S(2)}) collective-permute-start(bf16[256,96]{0,1:T(8,128)(2,1)S(1)} %get-tuple-element.55), channel_id=1, source_target_pairs={{0,12},{1,13},{2,14},{3,15},{4,8},{5,9},{6,10},{7,11},{8,4},{9,5},... | collective-permute-start | bytes 147464 | tf_op jit(solution)/shard_map/ppermute | solution.py:17
  52.9 5.5 %collective-permute-start.17 = (bf16[256,96]{0,1:T(8,128)(2,1)S(1)}, bf16[256,96]{0,1:T(8,128)(2,1)S(1)}, u32[]{:S(2)}, u32[]{:S(2)}) collective-permute-start(bf16[256,96]{0,1:T(8,128)(2,1)S(1)} %get-tuple-element.55), channel_id=1, source_target_pairs={{0,8},{1,9},{2,10},{3,11},{4,12},{5,13},{6,14},{7,15},{8,0},{9,1},... | collective-permute-start | bytes 147464 | tf_op jit(solution)/shard_map/ppermute | solution.py:17
  53.2 4.2 %collective-permute-start.16 = (bf16[256,96]{0,1:T(8,128)(2,1)S(1)}, bf16[256,96]{0,1:T(8,128)(2,1)S(1)}, u32[]{:S(2)}, u32[]{:S(2)}) collective-permute-start(bf16[256,96]{0,1:T(8,128)(2,1)S(1)} %get-tuple-element.55), channel_id=1, source_target_pairs={{0,4},{1,5},{2,6},{3,7},{4,0},{5,1},{6,2},{7,3},{8,12},{9,13},{10,... | collective-permute-start | bytes 147464 | tf_op jit(solution)/shard_map/ppermute | solution.py:17
  58.5 1.5 %collective-permute-start.19 = (bf16[1024,96]{0,1:T(8,128)(2,1)S(1)}, bf16[1024,96]{0,1:T(8,128)(2,1)S(1)}, u32[]{:S(2)}, u32[]{:S(2)}) collective-permute-start(bf16[1024,96]{0,1:T(8,128)(2,1)S(1)} %constant_dynamic-update-slice_fusion), channel_id=1, source_target_pairs={{0,1},{1,0},{2,3},{3,2},{4,5},{5,4},{6,7},{7,6},{8,9},{9,8},{10,11... | collective-permute-start | bytes 589832 | tf_op jit(solution)/shard_map/ppermute | solution.py:17
  60.8 7.0 %collective-permute-start.20 = (bf16[1024,96]{0,1:T(8,128)(2,1)S(1)}, bf16[1024,96]{0,1:T(8,128)(2,1)S(1)}, u32[]{:S(2)}, u32[]{:S(2)}) collective-permute-start(bf16[1024,96]{0,1:T(8,128)(2,1)S(1)} %get-tuple-element.110), channel_id=1, source_target_pairs={{0,16},{16,0},{1,17},{17,1},{2,18},{18,2},{3,19},{19,3},{4,20},{20... | collective-permute-start | bytes 589832 | tf_op jit(solution)/shard_map/ppermute | solution.py:169
  68.3 1.5 %collective-permute-start.21 = (bf16[1024,96]{0,1:T(8,128)(2,1)S(1)}, bf16[1024,96]{0,1:T(8,128)(2,1)S(1)}, u32[]{:S(2)}, u32[]{:S(2)}) collective-permute-start(bf16[1024,96]{0,1:T(8,128)(2,1)S(1)} %convolution_convert_fusion), channel_id=1, source_target_pairs={{0,1},{1,0},{2,3},{3,2},{4,5},{5,4},{6,7},{7,6},{8,9},{9,8},{10,11... | collective-permute-start | bytes 589832 | tf_op jit(solution)/shard_map/ppermute | solution.py:17
  69.9 4.9 %collective-permute-start.22 = (bf16[512,96]{0,1:T(8,128)(2,1)S(1)}, bf16[512,96]{0,1:T(8,128)(2,1)S(1)}, u32[]{:S(2)}, u32[]{:S(2)}) collective-permute-start(bf16[512,96]{0,1:T(8,128)(2,1)S(1)} %slice.338), channel_id=1, source_target_pairs={{0,2},{1,3},{2,0},{3,1},{4,6},{5,7},{6,4},{7,5},{8,10},{9,11},{10,... | collective-permute-start | bytes 294920 | tf_op jit(solution)/shard_map/ppermute | solution.py:17
  74.8 9.8 %collective-permute-start.24 = (bf16[512,96]{0,1:T(8,128)(2,1)S(1)}, bf16[512,96]{0,1:T(8,128)(2,1)S(1)}, u32[]{:S(2)}, u32[]{:S(2)}) collective-permute-start(bf16[512,96]{0,1:T(8,128)(2,1)S(1)} %fusion.21), channel_id=1, source_target_pairs={{0,8},{1,9},{2,10},{3,11},{4,12},{5,13},{6,14},{7,15},{8,0},{9,1},... | collective-permute-start | bytes 294920 | tf_op jit(solution)/shard_map/ppermute | solution.py:17
  76.4 8.3 %collective-permute-start.25 = (bf16[512,96]{0,1:T(8,128)(2,1)S(1)}, bf16[512,96]{0,1:T(8,128)(2,1)S(1)}, u32[]{:S(2)}, u32[]{:S(2)}) collective-permute-start(bf16[512,96]{0,1:T(8,128)(2,1)S(1)} %fusion.21), channel_id=1, source_target_pairs={{0,12},{1,13},{2,14},{3,15},{4,8},{5,9},{6,10},{7,11},{8,4},{9,5},... | collective-permute-start | bytes 294920 | tf_op jit(solution)/shard_map/ppermute | solution.py:17
  77.8 7.2 %collective-permute-start.23 = (bf16[512,96]{0,1:T(8,128)(2,1)S(1)}, bf16[512,96]{0,1:T(8,128)(2,1)S(1)}, u32[]{:S(2)}, u32[]{:S(2)}) collective-permute-start(bf16[512,96]{0,1:T(8,128)(2,1)S(1)} %fusion.21), channel_id=1, source_target_pairs={{0,4},{1,5},{2,6},{3,7},{4,0},{5,1},{6,2},{7,3},{8,12},{9,13},{10,... | collective-permute-start | bytes 294920 | tf_op jit(solution)/shard_map/ppermute | solution.py:17
  85.6 1.4 %collective-permute-start.26 = (f32[256,96]{0,1:T(8,128)S(1)}, f32[256,96]{0,1:T(8,128)S(1)}, u32[]{:S(2)}, u32[]{:S(2)}) collective-permute-start(f32[256,96]{0,1:T(8,128)S(1)} %slice.277), channel_id=1, source_target_pairs={{0,1},{1,0},{2,3},{3,2},{4,5},{5,4},{6,7},{7,6},{8,9},{9,8},{10,11... | collective-permute-start | bytes 294920 | tf_op jit(solution)/shard_map/ppermute | solution.py:17
  86.9 4.2 %collective-permute-start.27 = (bf16[256,96]{0,1:T(8,128)(2,1)S(1)}, bf16[256,96]{0,1:T(8,128)(2,1)S(1)}, u32[]{:S(2)}, u32[]{:S(2)}) collective-permute-start(bf16[256,96]{0,1:T(8,128)(2,1)S(1)} %fusion.28), channel_id=1, source_target_pairs={{0,2},{1,3},{2,0},{3,1},{4,6},{5,7},{6,4},{7,5},{8,10},{9,11},{10,... | collective-permute-start | bytes 147464 | tf_op jit(solution)/shard_map/ppermute | solution.py:17
  91.1 7.7 %collective-permute-start.30 = (bf16[256,96]{0,1:T(8,128)(2,1)S(1)}, bf16[256,96]{0,1:T(8,128)(2,1)S(1)}, u32[]{:S(2)}, u32[]{:S(2)}) collective-permute-start(bf16[256,96]{0,1:T(8,128)(2,1)S(1)} %get-tuple-element.53), channel_id=1, source_target_pairs={{0,12},{1,13},{2,14},{3,15},{4,8},{5,9},{6,10},{7,11},{8,4},{9,5},... | collective-permute-start | bytes 147464 | tf_op jit(solution)/shard_map/ppermute | solution.py:17
  93.3 5.5 %collective-permute-start.29 = (bf16[256,96]{0,1:T(8,128)(2,1)S(1)}, bf16[256,96]{0,1:T(8,128)(2,1)S(1)}, u32[]{:S(2)}, u32[]{:S(2)}) collective-permute-start(bf16[256,96]{0,1:T(8,128)(2,1)S(1)} %get-tuple-element.53), channel_id=1, source_target_pairs={{0,8},{1,9},{2,10},{3,11},{4,12},{5,13},{6,14},{7,15},{8,0},{9,1},... | collective-permute-start | bytes 147464 | tf_op jit(solution)/shard_map/ppermute | solution.py:17
  94.3 4.3 %collective-permute-start.28 = (bf16[256,96]{0,1:T(8,128)(2,1)S(1)}, bf16[256,96]{0,1:T(8,128)(2,1)S(1)}, u32[]{:S(2)}, u32[]{:S(2)}) collective-permute-start(bf16[256,96]{0,1:T(8,128)(2,1)S(1)} %get-tuple-element.53), channel_id=1, source_target_pairs={{0,4},{1,5},{2,6},{3,7},{4,0},{5,1},{6,2},{7,3},{8,12},{9,13},{10,... | collective-permute-start | bytes 147464 | tf_op jit(solution)/shard_map/ppermute | solution.py:17
  98.9 1.5 %collective-permute-start.31 = (bf16[1024,96]{0,1:T(8,128)(2,1)S(1)}, bf16[1024,96]{0,1:T(8,128)(2,1)S(1)}, u32[]{:S(2)}, u32[]{:S(2)}) collective-permute-start(bf16[1024,96]{0,1:T(8,128)(2,1)S(1)} %constant_dynamic-update-slice_fusion.8), channel_id=1, source_target_pairs={{0,1},{1,0},{2,3},{3,2},{4,5},{5,4},{6,7},{7,6},{8,9},{9,8},{10,11... | collective-permute-start | bytes 589832 | tf_op jit(solution)/shard_map/ppermute | solution.py:17
  101.4 11.1 %copy-start = (f32[1024,96]{0,1:T(8,128)}, f32[1024,96]{0,1:T(8,128)S(1)}, u32[]{:S(2)}) copy-start(f32[1024,96]{0,1:T(8,128)S(1)} %fusion.3) | copy-start | bytes 1179652
  102.2 9.9 %all-to-all-start = ((f32[16,1,96]{2,1,0:T(1,128)}), f32[16,1,96]{2,1,0:T(1,128)S(1)}, u32[]{:S(2)}, u32[]{:S(2)}) async-start(f32[16,1,96]{2,1,0:T(1,128)} %broadcast_in_dim.23), calls=%async_computation | async-start | bytes 16384 | tf_op jit(solution)/shard_map/all_to_all | solution.py:181
